TPU v7x, 32 devices: a whole 2x2x4 slice. The times are simulated.
32 devices in a mesh: grp: 16 (over z, y, x), exp: 2 (over core).
Axes of the slice: x: 2, y: 2, z: 4, core: 2. Of those that a mesh axis runs over, the one named last changes fastest.
Arguments:
- tokens: bfloat16 [64, 512, 768], P(('grp', 'exp')), may hold values from -6 to 6
- lengths: int32 [64], P(('grp', 'exp')), may hold values from 1 to 512, 22937 in all
- expert_ids: int32 [64, 512], P(('grp', 'exp')), may hold values from 0 to 31, as said below
- slots: int32 [64, 512], P(('grp', 'exp')), may hold values from -1 to 1279, as said below
- w_query: bfloat16 [768, 768], replicated, may hold values from -0.3125 to 0.3125
- w_key: bfloat16 [768, 768], replicated, may hold values from -0.3125 to 0.3125
- w_value: bfloat16 [768, 768], replicated, may hold values from -0.21875 to 0.21875
- w_output: bfloat16 [768, 768], replicated, may hold values from -0.875 to 0.875
- gain_attn: float32 [768], replicated, may hold values from 0.5 to 1.5
- gain_ffn: float32 [768], replicated, may hold values from 0.5 to 1.5
- bias_table: float32 [32, 12], replicated, may hold values from -4 to 4
- w_router: bfloat16 [768, 32], replicated, may hold values from -0.109375 to 0.109375
- w_in: bfloat16 [32, 768, 3072], P(('grp', 'exp')), may hold values from -0.4375 to 0.4375
- w_out: bfloat16 [32, 3072, 768], P(('grp', 'exp')), may hold values from -3 to 3
- cotangent: bfloat16 [64, 512, 768], P(('grp', 'exp')), may hold values from -6 to 6
Outputs:
- mixed: bfloat16 [64, 512, 768], P(('grp', 'exp'))
- grad_tokens: float32 [64, 512, 768], P(('grp', 'exp'))
- grad_query: float32 [768, 768], replicated
- grad_key: float32 [768, 768], replicated
- grad_value: float32 [768, 768], replicated
- grad_output: float32 [768, 768], replicated
- grad_gain_attn: float32 [768], replicated
- grad_gain_ffn: float32 [768], replicated
- grad_bias_table: float32 [32, 12], replicated
- grad_router: float32 [768, 32], replicated
- grad_in: float32 [32, 768, 3072], P(('grp', 'exp'))
- grad_out: float32 [32, 3072, 768], P(('grp', 'exp'))
Inputs may be any that keep to these rules, and one draw needn't show every extreme that they name: `expert_ids`: at most 64 of one device's 1024 tokens name one expert; in every draw one expert is named by exactly 64 tokens of every device. `slots`: a token's slot is the number of earlier tokens (rows in order, then positions) with the same expert, or -1 where that number is 1280 or more; every draw drops some tokens.
All inputs are finite; a program needn't handle non-finite values. No bound on the sum of `lengths` on one device may be relied on, other than what follows from the above.
Results may differ from a plain program's by a relative error of at most 0.02.
Values may be sent and summed in bfloat16 or wider, within the bound.
A program may use at most 320 MiB of HBM per device.

v0:
```python
import jax
import jax.numpy as jnp
from jax import lax
from jax.sharding import PartitionSpec as P

EPSILON = 1e-06
NEGATIVE = -1e30
THRESHOLDS = (12, 16, 23, 32, 46, 64, 91)


def bucket_table(length):
    positions = jnp.arange(length, dtype=jnp.int32)
    offset = positions[None, :] - positions[:, None]
    distance = jnp.abs(offset)
    far_bucket = jnp.full_like(distance, 8)
    for border in THRESHOLDS:
        far_bucket = far_bucket + (distance >= border).astype(jnp.int32)
    return jnp.where(distance < 8, distance, far_bucket) + jnp.where(offset > 0, 16, 0).astype(
        jnp.int32
    )


def send_rows(buffer, experts_all, room):
    groups = lax.axis_size("grp")
    shaped = buffer.reshape(groups, experts_all // groups, room, buffer.shape[-1])
    moved = lax.all_to_all(
        lax.all_to_all(shaped, "grp", split_axis=0, concat_axis=0, tiled=True),
        "exp",
        split_axis=1,
        concat_axis=1,
        tiled=True,
    )
    return moved.reshape(experts_all * room, buffer.shape[-1])


def return_rows(buffer, experts_all, room):
    groups = lax.axis_size("grp")
    shaped = buffer.reshape(groups, experts_all // groups, room, buffer.shape[-1])
    moved = lax.all_to_all(
        lax.all_to_all(shaped, "grp", split_axis=0, concat_axis=0, tiled=True),
        "exp",
        split_axis=1,
        concat_axis=1,
        tiled=True,
    )
    return moved.reshape(experts_all * room, buffer.shape[-1])


def send_grads(buffer, experts_all, room):
    groups = lax.axis_size("grp")
    shaped = buffer.reshape(groups, experts_all // groups, room, buffer.shape[-1])
    moved = lax.all_to_all(
        lax.all_to_all(shaped, "grp", split_axis=0, concat_axis=0, tiled=True),
        "exp",
        split_axis=1,
        concat_axis=1,
        tiled=True,
    )
    return moved.reshape(experts_all * room, buffer.shape[-1])


def return_grads(buffer, experts_all, room):
    groups = lax.axis_size("grp")
    shaped = buffer.reshape(groups, experts_all // groups, room, buffer.shape[-1])
    moved = lax.all_to_all(
        lax.all_to_all(shaped, "grp", split_axis=0, concat_axis=0, tiled=True),
        "exp",
        split_axis=1,
        concat_axis=1,
        tiled=True,
    )
    return moved.reshape(experts_all * room, buffer.shape[-1])


def expert_forward(arrived, first_w, second_w):
    inner = jnp.dot(arrived, first_w, preferred_element_type=jnp.float32)
    hidden = jax.nn.gelu(inner).astype(jnp.bfloat16)
    expert_out = jnp.dot(hidden, second_w, preferred_element_type=jnp.float32).astype(jnp.bfloat16)
    return (inner, hidden, expert_out)


def expert_backward(arrived, inner, hidden, grad_arrived, first_w, second_w):
    grad_hidden = jnp.dot(grad_arrived, second_w.T, preferred_element_type=jnp.float32)
    grad_second = jnp.dot(hidden.T, grad_arrived, preferred_element_type=jnp.float32)
    _, gelu_pull = jax.vjp(jax.nn.gelu, inner)
    grad_inner = gelu_pull(grad_hidden)[0].astype(jnp.bfloat16)
    grad_first = jnp.dot(arrived.T, grad_inner, preferred_element_type=jnp.float32)
    grad_rows = jnp.dot(grad_inner, first_w.T, preferred_element_type=jnp.float32).astype(
        jnp.bfloat16
    )
    return (grad_first, grad_second, grad_rows)


def local(
    tokens,
    lengths,
    expert_ids,
    slots,
    w_query,
    w_key,
    w_value,
    w_output,
    gain_attn,
    gain_ffn,
    bias_table,
    w_router,
    w_in,
    w_out,
    cotangent,
):
    rows_dev, seq_len, width = tokens.shape
    n_tok = rows_dev * seq_len
    heads = bias_table.shape[1]
    head_size = width // heads
    experts_all = w_router.shape[1]
    room = max(4, 2 * n_tok // experts_all)
    inputs = tokens.astype(jnp.float32).reshape(n_tok, width)
    rms_one = lax.rsqrt(jnp.mean(inputs * inputs, axis=-1, keepdims=True) + EPSILON)
    normed = (inputs * rms_one * gain_attn).astype(jnp.bfloat16)
    weight_qkv = jnp.concatenate([w_query, w_key, w_value], axis=1)
    projected = jnp.dot(normed, weight_qkv, preferred_element_type=jnp.float32).astype(jnp.bfloat16)
    queries = projected[:, :width].reshape(rows_dev, seq_len, heads, head_size)
    key_rows = projected[:, width : 2 * width].reshape(rows_dev, seq_len, heads, head_size)
    value_rows = projected[:, 2 * width :].reshape(rows_dev, seq_len, heads, head_size)
    buckets = bucket_table(seq_len)
    one_hot = buckets[:, :, None] == jnp.arange(bias_table.shape[0], dtype=jnp.int32)[None, None, :]
    one_hot_low = one_hot.astype(jnp.bfloat16)
    bias_all = jnp.einsum(
        "qkn,nh->hqk", one_hot.astype(jnp.float32), bias_table, precision=lax.Precision.HIGHEST
    )
    key_mask = jnp.arange(seq_len, dtype=jnp.int32)[None, :] < lengths[:, None]
    mask_full = key_mask[:, None, None, :]

    def score_rows():
        raw = (
            jnp.einsum("bqhd,bkhd->bhqk", queries, key_rows, preferred_element_type=jnp.float32)
            * 0.125
        )
        return jnp.where(mask_full, raw + bias_all[None], NEGATIVE)

    scores = score_rows()
    top_score = jnp.max(scores, axis=-1, keepdims=True)
    expo = jnp.exp(scores - top_score)
    total = jnp.sum(expo, axis=-1, keepdims=True)
    log_total = top_score + jnp.log(total)
    weights = expo / total
    mixed_heads = jnp.einsum(
        "bhqk,bkhd->bqhd",
        weights.astype(jnp.bfloat16),
        value_rows,
        preferred_element_type=jnp.float32,
    )
    joined = mixed_heads.astype(jnp.bfloat16).reshape(n_tok, width)
    resid = inputs + jnp.dot(joined, w_output, preferred_element_type=jnp.float32)
    rms_two = lax.rsqrt(jnp.mean(resid * resid, axis=-1, keepdims=True) + EPSILON)
    normed_two = (resid * rms_two * gain_ffn).astype(jnp.bfloat16)
    logits = jnp.dot(normed_two, w_router, preferred_element_type=jnp.float32)
    router = jax.nn.softmax(logits, axis=-1)
    flat_expert = expert_ids.reshape(-1)
    flat_slot = slots.reshape(-1)
    picked = flat_expert[:, None] == jnp.arange(experts_all, dtype=jnp.int32)[None, :]
    gate = jnp.sum(jnp.where(picked, router, 0.0), axis=-1)
    counted = jnp.cumsum(picked.astype(jnp.int32), axis=0)
    place = jnp.sum(jnp.where(picked, counted - 1, 0), axis=-1)
    dest_index = jnp.where(flat_slot >= 0, flat_expert * room + place, experts_all * room)
    upstream = cotangent.astype(jnp.float32).reshape(n_tok, width)
    grad_ff = (gate[:, None] * upstream).astype(jnp.bfloat16)
    outgoing = (
        jnp.zeros((experts_all * room, width), jnp.bfloat16)
        .at[dest_index]
        .set(normed_two, mode="drop")
    )
    grad_buffer = (
        jnp.zeros((experts_all * room, width), jnp.bfloat16)
        .at[dest_index]
        .set(grad_ff, mode="drop")
    )
    first_w = w_in[0]
    second_w = w_out[0]
    arrived = send_rows(outgoing, experts_all, room)
    inner, hidden, expert_out = expert_forward(arrived, first_w, second_w)
    returned = return_rows(expert_out, experts_all, room)
    grad_arrived = send_grads(grad_buffer, experts_all, room)
    grad_first, grad_second, grad_rows = expert_backward(
        arrived, inner, hidden, grad_arrived, first_w, second_w
    )
    grad_back = return_grads(grad_rows, experts_all, room)
    ff_tok = jnp.take(returned, dest_index, axis=0, mode="fill", fill_value=0).astype(jnp.float32)
    result = resid + gate[:, None] * ff_tok
    mixed = result.astype(jnp.bfloat16).reshape(rows_dev, seq_len, width)
    grad_gate = jnp.sum(upstream * ff_tok, axis=-1)
    grad_expert_tok = jnp.take(grad_back, dest_index, axis=0, mode="fill", fill_value=0).astype(
        jnp.float32
    )
    grad_logits = ((gate * grad_gate)[:, None] * (picked.astype(jnp.float32) - router)).astype(
        jnp.bfloat16
    )
    grad_router_w = jnp.dot(normed_two.T, grad_logits, preferred_element_type=jnp.float32)
    grad_normed_two = grad_expert_tok + jnp.dot(
        grad_logits, w_router.T, preferred_element_type=jnp.float32
    )
    grad_gain_two = jnp.sum(grad_normed_two * resid * rms_two, axis=0)
    scaled_two = grad_normed_two * gain_ffn
    grad_resid = (
        upstream
        + rms_two * scaled_two
        - resid * rms_two**3 * jnp.mean(scaled_two * resid, axis=-1, keepdims=True)
    )
    grad_resid_low = grad_resid.astype(jnp.bfloat16)
    grad_out_w = jnp.dot(joined.T, grad_resid_low, preferred_element_type=jnp.float32)
    grad_joined = jnp.dot(grad_resid_low, w_output.T, preferred_element_type=jnp.float32).astype(
        jnp.bfloat16
    )
    grad_heads = grad_joined.reshape(rows_dev, seq_len, heads, head_size)
    again = jnp.exp(score_rows() - log_total)
    grad_weights = jnp.einsum(
        "bqhd,bkhd->bhqk", grad_heads, value_rows, preferred_element_type=jnp.float32
    )
    grad_values = jnp.einsum(
        "bhqk,bqhd->bkhd",
        again.astype(jnp.bfloat16),
        grad_heads,
        preferred_element_type=jnp.float32,
    ).astype(jnp.bfloat16)
    centred = jnp.sum(again * grad_weights, axis=-1, keepdims=True)
    grad_scores = (again * (grad_weights - centred)).astype(jnp.bfloat16)
    grad_queries = (
        jnp.einsum("bhqk,bkhd->bqhd", grad_scores, key_rows, preferred_element_type=jnp.float32)
        * 0.125
    ).astype(jnp.bfloat16)
    grad_keys = (
        jnp.einsum("bhqk,bqhd->bkhd", grad_scores, queries, preferred_element_type=jnp.float32)
        * 0.125
    ).astype(jnp.bfloat16)
    grad_table = jnp.einsum(
        "bhqk,qkn->nh", grad_scores, one_hot_low, preferred_element_type=jnp.float32
    )
    grad_projected = jnp.concatenate(
        [
            grad_queries.reshape(n_tok, width),
            grad_keys.reshape(n_tok, width),
            grad_values.reshape(n_tok, width),
        ],
        axis=1,
    )
    grad_qkv = jnp.dot(normed.T, grad_projected, preferred_element_type=jnp.float32)
    grad_normed = jnp.dot(grad_projected, weight_qkv.T, preferred_element_type=jnp.float32)
    grad_gain_one = jnp.sum(grad_normed * inputs * rms_one, axis=0)
    scaled_one = grad_normed * gain_attn
    grad_inputs = (
        grad_resid
        + rms_one * scaled_one
        - inputs * rms_one**3 * jnp.mean(scaled_one * inputs, axis=-1, keepdims=True)
    )
    summed = lax.psum(
        (
            grad_qkv[:, :width],
            grad_qkv[:, width : 2 * width],
            grad_qkv[:, 2 * width :],
            grad_out_w,
            grad_gain_one,
            grad_gain_two,
            grad_table,
            grad_router_w,
        ),
        ("grp", "exp"),
    )
    return (
        mixed,
        grad_inputs.reshape(rows_dev, seq_len, width),
        summed[0],
        summed[1],
        summed[2],
        summed[3],
        summed[4],
        summed[5],
        summed[6],
        summed[7],
        grad_first[None],
        grad_second[None],
    )


def solution(mesh):
    in_specs = (
        P(("grp", "exp"), None, None),
        P(("grp", "exp")),
        P(("grp", "exp"), None),
        P(("grp", "exp"), None),
        P(),
        P(),
        P(),
        P(),
        P(),
        P(),
        P(),
        P(),
        P(("grp", "exp"), None, None),
        P(("grp", "exp"), None, None),
        P(("grp", "exp"), None, None),
    )
    out_specs = (
        P(("grp", "exp"), None, None),
        P(("grp", "exp"), None, None),
        P(),
        P(),
        P(),
        P(),
        P(),
        P(),
        P(),
        P(),
        P(("grp", "exp"), None, None),
        P(("grp", "exp"), None, None),
    )
    return jax.shard_map(local, mesh=mesh, in_specs=in_specs, out_specs=out_specs, check_vma=False)
```

profile of v0, /device:TPU:0, one launch (start us, length us, event | category | flops | bytes accessed | tf_op | source)
XLA Modules:
  0.0 889.4 jit_solution(6268757407106432791)
XLA Ops:
  14.2 9.0 %reduce-window.6 = s32[32,8,128]{2,1,0:T(8,128)S(1)} reduce-window(s32[32,8,128]{2,1,0:T(8,128)S(1)} %fusion.87, s32[]{:T(128)} %constant.14.clone.1), window={size=1x1x128 pad=0_0x0_0x127_0}, to_apply=%region_7.8 | reduce-window | flops 4161536 | bytes 262148 | tf_op jit(solution)/shard_map/reduce-window
  26.8 4.0 convolution_convert_fusion
  32.8 2.6 copy.127
  35.4 3.8 reshape.284
  40.8 2.9 reshape.286
  43.7 3.1 copy.128
  46.8 3.8 reshape.285
  50.7 9.8 %iota_compare_fusion = pred[512,512,32]{0,2,1:T(32,128)(4,1)} fusion(s32[512,512]{0,1:T(8,128)} %fusion.72), kind=kLoop, calls=%fused_computation.6 | loop fusion | flops 8388608 | bytes 9437184 | tf_op jit(solution)/shard_map/eq | solution.py:126
  60.5 45.2 %copy.132 = pred[512,512,32]{1,2,0:T(32,128)(4,1)S(1)} copy(pred[512,512,32]{0,2,1:T(32,128)(4,1)} %iota_compare_fusion) | data formatting | bytes 16777216 | tf_op jit(solution)/shard_map/eq | solution.py:126
  105.8 12.2 %convolution_bitcast_fusion = f32[12,512,512]{2,0,1:T(8,128)} fusion(pred[512,512,32]{1,2,0:T(32,128)(4,1)S(1)} %copy.132, f32[32,12]{0,1:T(8,128)S(1)} %copy-done.60), kind=kOutput, calls=%fused_computation.29 | convolution fusion | flops 1207959552 | bytes 20973056 | tf_op jit(solution)/shard_map/qkn,nh->hqk/dot_general | solution.py:128
  118.0 17.7 %copy.133 = f32[12,512,512]{1,2,0:T(8,128)} copy(f32[12,512,512]{2,0,1:T(8,128)} %convolution_bitcast_fusion) | data formatting | bytes 25165824 | tf_op jit(solution)/shard_map/qkn,nh->hqk/dot_general | solution.py:128
  135.7 14.9 %fusion.94 = (f32[2,12,512]{2,1,0:T(8,128)S(1)}, f32[2,12,512,512]{2,3,1,0:T(8,128)}) fusion(f32[12,512,512]{1,2,0:T(8,128)} %copy.133, bf16[2,512,12,64]{1,0,3,2:T(2,128)(2,1)S(1)} %reshape.286, bf16[2,512,12,64]{1,0,3,2:T(2,128)(2,1)} %reshape.285, pred[2,512]{1,0:T(4,128)(4,1)S(1)} %iota_compare_fusion.3), kind=kOutput, calls=%fused_computation.147 | convolution fusion | flops 830459904 | bytes 40944640 | tf_op jit(solution)/shard_map/bqhd,bkhd->bhqk/dot_general | solution.py:136
  150.6 10.5 %fusion.7 = f32[2,12,512]{2,1,0:T(8,128)S(1)} fusion(f32[2,12,512,512]{2,3,1,0:T(8,128)} %get-tuple-element.38, f32[2,12,512]{2,1,0:T(8,128)S(1)} %get-tuple-element.37), kind=kLoop, calls=%fused_computation.22 | loop fusion | flops 12570624 | bytes 25264128 | tf_op jit(solution)/shard_map/reduce_sum | solution.py:144
  161.0 10.7 %fusion.59 = bf16[2,512,12,64]{1,3,2,0:T(8,128)(2,1)S(1)} fusion(f32[2,12,512,512]{2,3,1,0:T(8,128)} %get-tuple-element.38, f32[2,12,512]{2,1,0:T(8,128)S(1)} %fusion.7, f32[2,12,512]{2,1,0:T(8,128)S(1)} %get-tuple-element.37, bf16[2,512,12,64]{1,0,3,2:T(2,128)(2,1)S(1)} %copy-done.15), kind=kOutput, calls=%fused_computation.86 | convolution fusion | flops 824967168 | bytes 28409856 | tf_op jit(solution)/shard_map/bhqk,bkhd->bqhd/dot_general | solution.py:147
  173.8 3.2 multiply_reduce_fusion.3
  177.7 8.5 scatter_custom_fusion
  186.2 8.8 all-to-all-start
  195.1 2.3 multiply_convert_fusion.4
  199.9 7.7 scatter_custom_fusion.1
  207.6 48.4 %all-to-all-done = bf16[16,2,64,768]{3,2,1,0:T(8,128)(2,1)} async-done(((bf16[16,2,64,768]{3,2,1,0:T(8,128)(2,1)}), bf16[16,2,64,768]{3,2,1,0:T(8,128)(2,1)}, u32[]{:S(2)}, u32[]{:S(2)}) %all-to-all-start) | async-done | bytes 3145760 | tf_op jit(solution)/shard_map/all_to_all | solution.py:27
  256.0 15.0 %all-to-all-start.4 = ((bf16[16,2,64,768]{3,2,1,0:T(8,128)(2,1)}), bf16[16,2,64,768]{3,2,1,0:T(8,128)(2,1)}, u32[]{:S(2)}, u32[]{:S(2)}) async-start(bf16[16,2,64,768]{3,2,1,0:T(8,128)(2,1)} %bitcast.157), calls=%async_computation.4 | async-start | bytes 6291456 | tf_op jit(solution)/shard_map/all_to_all | solution.py:53
  271.0 3.9 copy.139
  274.9 56.8 %all-to-all-done.4 = bf16[16,2,64,768]{3,2,1,0:T(8,128)(2,1)} async-done(((bf16[16,2,64,768]{3,2,1,0:T(8,128)(2,1)}), bf16[16,2,64,768]{3,2,1,0:T(8,128)(2,1)}, u32[]{:S(2)}, u32[]{:S(2)}) %all-to-all-start.4) | async-done | bytes 3145760 | tf_op jit(solution)/shard_map/all_to_all | solution.py:53
  331.7 5.2 all-to-all-start.1
  336.9 3.9 copy.143
  340.8 5.2 all-to-all-start.5
  346.1 2.4 copy.140
  350.2 15.7 %fusion.23 = f32[2048,3072]{1,0:T(8,128)} fusion(bf16[2048,768]{1,0:T(8,128)(2,1)S(1)} %bitcast.165, bf16[1,768,3072]{2,1,0:T(8,128)(2,1)} %param.29), kind=kOutput, calls=%fused_computation.42 | convolution fusion | flops 9663676416 | bytes 33030144 | tf_op jit(solution)/shard_map/dot_general | solution.py:76
  365.9 20.4 %fusion.28 = bf16[2048,768]{1,0:T(8,128)(2,1)} fusion(bf16[1,3072,768]{2,1,0:T(8,128)(2,1)S(1)} %bitcast.194, f32[2048,3072]{1,0:T(8,128)} %fusion.23), kind=kOutput, calls=%fused_computation.46 | convolution fusion | flops 9721872384 | bytes 33030144 | tf_op jit(solution)/shard_map/dot_general | solution.py:78
  386.3 14.3 %all-to-all-start.2 = ((bf16[16,2,64,768]{3,2,1,0:T(8,128)(2,1)}), bf16[16,2,64,768]{3,2,1,0:T(8,128)(2,1)}, u32[]{:S(2)}, u32[]{:S(2)}) async-start(bf16[16,2,64,768]{3,2,1,0:T(8,128)(2,1)} %bitcast.170), calls=%async_computation.2 | async-start | bytes 6291456 | tf_op jit(solution)/shard_map/all_to_all | solution.py:40
  400.6 2.4 copy.144
  403.0 28.3 %fusion.6 = bf16[2048,3072]{1,0:T(8,128)(2,1)} fusion(f32[2048,3072]{1,0:T(8,128)} %fusion.23, bf16[2048,768]{1,0:T(8,128)(2,1)S(1)} %bitcast.168, bf16[1,3072,768]{2,1,0:T(8,128)(2,1)} %param.30), kind=kOutput, calls=%fused_computation.13 | convolution fusion | flops 9789505536 | bytes 45613056 | tf_op jit(solution)/shard_map/dot_general | solution.py:83
  431.4 14.1 %fusion.25 = bf16[2048,768]{1,0:T(8,128)(2,1)} fusion(bf16[2048,3072]{1,0:T(8,128)(2,1)} %fusion.6, bf16[1,768,3072]{2,1,0:T(8,128)(2,1)S(1)} %bitcast.196), kind=kOutput, calls=%fused_computation.45 | convolution fusion | flops 9665249280 | bytes 20447232 | tf_op jit(solution)/shard_map/dot_general | solution.py:88
  445.4 16.7 %all-to-all-done.2 = bf16[16,2,64,768]{3,2,1,0:T(8,128)(2,1)} async-done(((bf16[16,2,64,768]{3,2,1,0:T(8,128)(2,1)}), bf16[16,2,64,768]{3,2,1,0:T(8,128)(2,1)}, u32[]{:S(2)}, u32[]{:S(2)}) %all-to-all-start.2) | async-done | bytes 3145760 | tf_op jit(solution)/shard_map/all_to_all | solution.py:40
  462.1 2.2 copy.141
  464.3 7.2 all_to_all.40
  471.6 16.5 %all-to-all-start.6 = ((bf16[16,2,64,768]{3,2,1,0:T(8,128)(2,1)}), bf16[16,2,64,768]{3,2,1,0:T(8,128)(2,1)}, u32[]{:S(2)}, u32[]{:S(2)}) async-start(bf16[16,2,64,768]{3,2,1,0:T(8,128)(2,1)} %bitcast.167), calls=%async_computation.6 | async-start | bytes 6291456 | tf_op jit(solution)/shard_map/all_to_all | solution.py:66
  488.3 22.1 %convolution_bitcast_fusion.1 = f32[1,3072,768]{2,1,0:T(8,128)} fusion(bf16[2048,768]{1,0:T(8,128)(2,1)} %bitcast.169, f32[2048,3072]{1,0:T(8,128)} %fusion.23), kind=kOutput, calls=%fused_computation.30 | convolution fusion | flops 9720299520 | bytes 37748736 | tf_op jit(solution)/shard_map/dot_general | solution.py:84
  510.4 2.0 copy.142
  512.4 8.0 gather_fusion
  520.4 2.5 fusion.34
  524.0 25.3 %all-to-all-done.6 = bf16[16,2,64,768]{3,2,1,0:T(8,128)(2,1)} async-done(((bf16[16,2,64,768]{3,2,1,0:T(8,128)(2,1)}), bf16[16,2,64,768]{3,2,1,0:T(8,128)(2,1)}, u32[]{:S(2)}, u32[]{:S(2)}) %all-to-all-start.6) | async-done | bytes 3145760 | tf_op jit(solution)/shard_map/all_to_all | solution.py:66
  549.3 2.2 copy.145
  551.5 6.4 all_to_all.41
  557.9 2.0 copy.146
  559.9 7.9 gather_fusion.1
  567.9 3.5 multiply_reduce_fusion.1
  571.6 2.6 fusion.35
  574.2 2.8 fusion.82
  580.1 2.9 reshape.300
  583.0 11.5 %fusion.54 = bf16[2,512,12,64]{1,3,2,0:T(8,128)(2,1)} fusion(f32[2,12,512,512]{2,3,1,0:T(8,128)} %get-tuple-element.38, f32[2,12,512]{2,1,0:T(8,128)S(1)} %log_add_fusion, bf16[2,512,12,64]{1,0,3,2:T(2,128)(2,1)S(1)} %reshape.300), kind=kOutput, calls=%fused_computation.83 | convolution fusion | flops 818675712 | bytes 28360704 | tf_op jit(solution)/shard_map/bhqk,bqhd->bkhd/dot_general | solution.py:219
  594.5 16.0 %multiply_reduce_fusion = (f32[2,12,512]{2,1,0:T(8,128)S(1)}, f32[2,12,512,512]{2,3,1,0:T(8,128)}) fusion(f32[2,12,512,512]{2,3,1,0:T(8,128)} %get-tuple-element.38, f32[2,12,512]{2,1,0:T(8,128)S(1)} %log_add_fusion, bf16[2,512,12,64]{1,0,3,2:T(2,128)(2,1)} %reshape.284, bf16[2,512,12,64]{1,0,3,2:T(2,128)(2,1)S(1)} %reshape.300), kind=kOutput, calls=%fused_computation.16 | convolution fusion | flops 824168448 | bytes 53575680 | tf_op jit(solution)/shard_map/bqhd,bkhd->bhqk/dot_general | solution.py:216
  610.5 25.9 %convert_reduce_fusion = (bf16[12,512,512]{1,2,0:T(8,128)(2,1)}, bf16[2,12,512,512]{2,3,1,0:T(8,128)(2,1)}) fusion(f32[2,12,512,512]{2,3,1,0:T(8,128)} %get-tuple-element.45, f32[2,12,512]{2,1,0:T(8,128)S(1)} %get-tuple-element.44, f32[2,12,512,512]{2,3,1,0:T(8,128)} %get-tuple-element.38, f32[2,12,512]{2,1,0:T(8,128)S(1)} %log_add_fusion), kind=kLoop, calls=%fused_computation.14 | loop fusion | flops 34603008 | bytes 69304320 | tf_op jit(solution)/shard_map/bhqk,qkn->nh/reduce_sum | solution.py:235
  636.4 8.6 fusion.58
  645.0 6.8 fusion.57
  659.5 4.3 fusion.96
  663.9 3.1 fusion.92
  667.0 16.5 %convolution_bitcast_fusion.2 = f32[1,768,3072]{2,1,0:T(8,128)} fusion(bf16[2048,768]{1,0:T(8,128)(2,1)} %bitcast.166, bf16[2048,3072]{1,0:T(8,128)(2,1)} %fusion.6), kind=kOutput, calls=%fused_computation.32 | convolution fusion | flops 9663676416 | bytes 25165824 | tf_op jit(solution)/shard_map/dot_general | solution.py:87
  683.5 12.6 %fusion.69 = f32[32,12]{0,1:T(8,128)S(1)} fusion(bf16[12,512,512]{1,2,0:T(8,128)(2,1)} %get-tuple-element.25, s32[512,512]{0,1:T(8,128)S(1)} %copy-done.17), kind=kOutput, calls=%fused_computation.96 | convolution fusion | flops 209715200 | bytes 7341568 | tf_op jit(solution)/shard_map/bhqk,qkn->nh/dot_general | solution.py:235
  696.2 6.0 fusion.43
  702.2 50.6 %all-reduce = (f32[768]{0:T(1024)}, f32[768]{0:T(1024)}, f32[32,12]{0,1:T(8,128)}) all-reduce(f32[768]{0:T(1024)S(1)} %get-tuple-element.15, f32[768]{0:T(1024)S(1)} %get-tuple-element.13, f32[32,12]{0,1:T(8,128)S(1)} %fusion.69), channel_id=1, replica_groups=mesh['grp'=16,'exp'=2] {'grp','exp'}, use_global_device_ids=true, to_apply=%region_21.23 | all-reduce | flops 1920 | bytes 15360 | tf_op jit(solution)/shard_map/psum | solution.py:255
  752.9 4.5 fusion.40
  757.4 114.5 %all-reduce.4.cloned.1.call-done = (f32[768,768]{1,0:T(8,128)}, f32[768,768]{1,0:T(8,128)}, f32[768,768]{1,0:T(8,128)}, f32[768,768]{1,0:T(8,128)}, f32[768,32]{0,1:T(8,128)}) async-done(((f32[768,768]{1,0:T(8,128)}, f32[768,768]{1,0:T(8,128)}, f32[768,768]{1,0:T(8,128)}, f32[768,768]{1,0:T(8,128)}, f32[768,32]{0,1:T(8,128)}), (f32[768,768]{1,0:T(8,128)}, f32[768,768]{1,0:T(8,128)}, f32[768,768]{1,0:T(8,128)}, ...) | async-done | bytes 9535504 | tf_op jit(solution)/shard_map/psum | solution.py:255
  871.9 3.4 copy.213
  (192 shorter events, 40.1 us)
Async XLA Ops:
  7.2 166.6 %copy-start = (bf16[768,768]{1,0:T(8,128)(2,1)S(1)}, bf16[768,768]{1,0:T(8,128)(2,1)}, u32[]{:S(2)}) copy-start(bf16[768,768]{1,0:T(8,128)(2,1)} %param.24) | copy-start | bytes 3538948
  7.2 17.9 %copy-start.9 = (bf16[2,512,768]{2,1,0:T(8,128)(2,1)S(1)}, bf16[2,512,768]{2,1,0:T(8,128)(2,1)}, u32[]{:S(2)}) copy-start(bf16[2,512,768]{2,1,0:T(8,128)(2,1)} %param.17) | copy-start | bytes 4718596
  7.2 17.9 %copy-start.56 = (f32[768]{0:T(1024)S(1)}, f32[768]{0:T(1024)}, u32[]{:S(2)}) copy-start(f32[768]{0:T(1024)} %param.25) | copy-start | bytes 9220
  14.2 11.4 %copy-start.44 = (f32[1,4,2,128]{3,1,2,0:T(4,128)}, f32[1,4,2,128]{3,1,2,0:T(4,128)S(1)}, u32[]{:S(2)}) copy-start(f32[1,4,2,128]{3,1,2,0:T(4,128)S(1)} %copy.164) | copy-start | bytes 12292
  26.8 4.0 copy-start.35
  43.7 92.0 %copy-start.2 = (bf16[2,512,12,64]{1,0,3,2:T(2,128)(2,1)}, bf16[2,512,12,64]{1,0,3,2:T(2,128)(2,1)S(1)}, u32[]{:S(2)}) copy-start(bf16[2,512,12,64]{1,0,3,2:T(2,128)(2,1)S(1)} %reshape.286) | copy-start | bytes 4718596
  60.5 45.3 %copy-start.60 = (f32[32,12]{0,1:T(8,128)S(1)}, f32[32,12]{0,1:T(8,128)}, u32[]{:S(2)}) copy-start(f32[32,12]{0,1:T(8,128)} %param.27) | copy-start | bytes 4612
  150.5 10.5 %copy-start.31 = (f32[2,12,512]{2,1,0:T(8,128)}, f32[2,12,512]{2,1,0:T(8,128)S(1)}, u32[]{:S(2)}) copy-start(f32[2,12,512]{2,1,0:T(8,128)S(1)} %get-tuple-element.37) | copy-start | bytes 147460
  150.5 10.5 %copy-start.15 = (bf16[2,512,12,64]{1,0,3,2:T(2,128)(2,1)S(1)}, bf16[2,512,12,64]{1,0,3,2:T(2,128)(2,1)}, u32[]{:S(2)}) copy-start(bf16[2,512,12,64]{1,0,3,2:T(2,128)(2,1)} %reshape.284) | copy-start | bytes 4718596
  161.0 10.7 %copy-start.37 = (f32[2,12,512]{2,1,0:T(8,128)}, f32[2,12,512]{2,1,0:T(8,128)S(1)}, u32[]{:S(2)}) copy-start(f32[2,12,512]{2,1,0:T(8,128)S(1)} %fusion.7) | copy-start | bytes 147460
  171.7 2.1 copy-start.10
  173.8 3.3 copy-start.27
  173.8 3.9 copy-start.52
  177.6 17.4 %copy-start.40 = (f32[1024]{0:T(1024)}, f32[1024]{0:T(1024)S(1)}, u32[]{:S(2)}) copy-start(f32[1024]{0:T(1024)S(1)} %get-tuple-element.36) | copy-start | bytes 12292
  177.7 8.6 copy-start.46
  186.2 69.7 %all-to-all-start = ((bf16[16,2,64,768]{3,2,1,0:T(8,128)(2,1)}), bf16[16,2,64,768]{3,2,1,0:T(8,128)(2,1)}, u32[]{:S(2)}, u32[]{:S(2)}) async-start(bf16[16,2,64,768]{3,2,1,0:T(8,128)(2,1)} %bitcast.156), calls=%async_computation | async-start | bytes 6291456 | tf_op jit(solution)/shard_map/all_to_all | solution.py:27
  195.0 3.5 copy-start.50
  195.0 4.8 copy-start.4
  199.1 56.8 %copy-start.42 = (f32[1024]{0:T(1024)}, f32[1024]{0:T(1024)S(1)}, u32[]{:S(2)}) copy-start(f32[1024]{0:T(1024)S(1)} %get-tuple-element.41) | copy-start | bytes 12292
  199.8 56.2 %copy-start.54 = (f32[1024]{0:T(1024)}, f32[1024]{0:T(1024)S(1)}, u32[]{:S(2)}) copy-start(f32[1024]{0:T(1024)S(1)} %fusion.89) | copy-start | bytes 12292
  199.8 56.1 %copy-start.48 = (f32[1024]{0:T(1024)}, f32[1024]{0:T(1024)S(1)}, u32[]{:S(2)}) copy-start(f32[1024]{0:T(1024)S(1)} %select_reduce_fusion) | copy-start | bytes 12292
  256.0 75.7 %all-to-all-start.4 = ((bf16[16,2,64,768]{3,2,1,0:T(8,128)(2,1)}), bf16[16,2,64,768]{3,2,1,0:T(8,128)(2,1)}, u32[]{:S(2)}, u32[]{:S(2)}) async-start(bf16[16,2,64,768]{3,2,1,0:T(8,128)(2,1)} %bitcast.157), calls=%async_computation.4 | async-start | bytes 6291456 | tf_op jit(solution)/shard_map/all_to_all | solution.py:53
  331.7 9.1 %all-to-all-start.1 = ((bf16[16,2,64,768]{3,2,0,1:T(8,128)(2,1)}), bf16[16,2,64,768]{3,2,0,1:T(8,128)(2,1)}, u32[]{:S(2)}, u32[]{:S(2)}) async-start(bf16[16,2,64,768]{3,2,0,1:T(8,128)(2,1)} %copy.139), calls=%async_computation.1 | async-start | bytes 6291456 | tf_op jit(solution)/shard_map/all_to_all | solution.py:26
  340.8 45.5 %all-to-all-start.5 = ((bf16[16,2,64,768]{3,2,0,1:T(8,128)(2,1)}), bf16[16,2,64,768]{3,2,0,1:T(8,128)(2,1)}, u32[]{:S(2)}, u32[]{:S(2)}) async-start(bf16[16,2,64,768]{3,2,0,1:T(8,128)(2,1)} %copy.143), calls=%async_computation.5 | async-start | bytes 6291456 | tf_op jit(solution)/shard_map/all_to_all | solution.py:52
  346.1 19.9 %slice-start = ((s8[4718592]{0:T(1024)(128)(4,1)}), s8[4194304]{0:T(1024)(128)(4,1)S(1)}, s32[]{:S(2)}) async-start(s8[4718592]{0:T(1024)(128)(4,1)} %bitcast.193), calls=%async_computation.9 | async-start | bytes 8388608
  350.2 15.8 %slice-start.1 = ((s8[4718592]{0:T(1024)(128)(4,1)}), s8[524288]{0:T(1024)(128)(4,1)S(1)}, s32[]{:S(2)}) async-start(s8[4718592]{0:T(1024)(128)(4,1)} %bitcast.193), calls=%async_computation.10 | async-start | bytes 1048576
  386.3 75.8 %all-to-all-start.2 = ((bf16[16,2,64,768]{3,2,1,0:T(8,128)(2,1)}), bf16[16,2,64,768]{3,2,1,0:T(8,128)(2,1)}, u32[]{:S(2)}, u32[]{:S(2)}) async-start(bf16[16,2,64,768]{3,2,1,0:T(8,128)(2,1)} %bitcast.170), calls=%async_computation.2 | async-start | bytes 6291456 | tf_op jit(solution)/shard_map/all_to_all | solution.py:40
  400.6 30.7 %slice-start.2 = ((s8[4718592]{0:T(1024)(128)(4,1)}), s8[4194304]{0:T(1024)(128)(4,1)S(1)}, s32[]{:S(2)}) async-start(s8[4718592]{0:T(1024)(128)(4,1)} %bitcast.195), calls=%async_computation.11 | async-start | bytes 8388608
  403.0 28.4 %copy-start.19 = (bf16[16,2,64,768]{3,2,1,0:T(8,128)(2,1)}, bf16[16,2,64,768]{3,2,1,0:T(8,128)(2,1)S(1)}, u32[]{:S(2)}) copy-start(bf16[16,2,64,768]{3,2,1,0:T(8,128)(2,1)S(1)} %copy.144) | copy-start | bytes 9437188
  403.0 28.4 %slice-start.3 = ((s8[4718592]{0:T(1024)(128)(4,1)}), s8[524288]{0:T(1024)(128)(4,1)S(1)}, s32[]{:S(2)}) async-start(s8[4718592]{0:T(1024)(128)(4,1)} %bitcast.195), calls=%async_computation.12 | async-start | bytes 1048576
  471.5 16.6 %copy-start.59 = (s32[2,512]{1,0:T(2,128)S(1)}, s32[2,512]{1,0:T(2,128)}, u32[]{:S(2)}) copy-start(s32[2,512]{1,0:T(2,128)} %param.20) | copy-start | bytes 12292
  471.5 16.6 %copy-start.47 = (s32[1024]{0:T(1024)S(1)}, s32[1024]{0:T(1024)}, u32[]{:S(2)}) copy-start(s32[1024]{0:T(1024)} %copy-done.46) | copy-start | bytes 12292
  471.5 16.7 %copy-start.32 = (f32[2,12,512]{2,1,0:T(8,128)S(1)}, f32[2,12,512]{2,1,0:T(8,128)}, u32[]{:S(2)}) copy-start(f32[2,12,512]{2,1,0:T(8,128)} %copy-done.31) | copy-start | bytes 147460
  471.5 16.7 %copy-start.38 = (f32[2,12,512]{2,1,0:T(8,128)S(1)}, f32[2,12,512]{2,1,0:T(8,128)}, u32[]{:S(2)}) copy-start(f32[2,12,512]{2,1,0:T(8,128)} %copy-done.37) | copy-start | bytes 147460
  471.6 77.7 %all-to-all-start.6 = ((bf16[16,2,64,768]{3,2,1,0:T(8,128)(2,1)}), bf16[16,2,64,768]{3,2,1,0:T(8,128)(2,1)}, u32[]{:S(2)}, u32[]{:S(2)}) async-start(bf16[16,2,64,768]{3,2,1,0:T(8,128)(2,1)} %bitcast.167), calls=%async_computation.6 | async-start | bytes 6291456 | tf_op jit(solution)/shard_map/all_to_all | solution.py:66
  488.1 383.8 %all-reduce.4.cloned.1.call-start = ((), (), s32[]{:S(2)}) async-start(), calls=%async_computation.8 | async-start | bytes 19070976 | tf_op jit(solution)/shard_map/psum | solution.py:255
  488.2 22.2 %copy-start.14 = (bf16[16,2,64,768]{3,2,0,1:T(8,128)(2,1)S(1)}, bf16[16,2,64,768]{3,2,0,1:T(8,128)(2,1)}, u32[]{:S(2)}) copy-start(bf16[16,2,64,768]{3,2,0,1:T(8,128)(2,1)} %all_to_all.40) | copy-start | bytes 9437188
  512.4 8.0 copy-start.5
  520.4 2.5 copy-start.49
  520.4 2.5 copy-start.7
  520.4 2.6 copy-start.24
  520.4 2.6 copy-start.43
  520.4 2.6 copy-start.55
  559.9 7.9 copy-start.41
  559.9 7.9 copy-start.51
  559.9 7.9 copy-start.53
  567.8 3.6 copy-start.1
  567.8 3.8 copy-start.8
  567.8 3.8 copy-start.58
  571.6 2.6 copy-start.28
  574.2 2.8 copy-start.13
  610.5 25.9 %copy-start.12 = (bf16[2,512,12,64]{1,0,3,2:T(2,128)(2,1)S(1)}, bf16[2,512,12,64]{1,0,3,2:T(2,128)(2,1)}, u32[]{:S(2)}) copy-start(bf16[2,512,12,64]{1,0,3,2:T(2,128)(2,1)} %reshape.285) | copy-start | bytes 4718596
  636.4 8.6 copy-start.3
  645.0 6.9 copy-start.16
  659.5 4.3 copy-start.33
  667.0 16.5 %copy-start.17 = (s32[512,512]{0,1:T(8,128)S(1)}, s32[512,512]{0,1:T(8,128)}, u32[]{:S(2)}) copy-start(s32[512,512]{0,1:T(8,128)} %fusion.72) | copy-start | bytes 3145732
  683.5 12.7 %copy-start.11 = (bf16[2,512,768]{2,1,0:T(8,128)(2,1)S(1)}, bf16[2,512,768]{2,1,0:T(8,128)(2,1)}, u32[]{:S(2)}) copy-start(bf16[2,512,768]{2,1,0:T(8,128)(2,1)} %param.17) | copy-start | bytes 4718596
  683.5 12.7 %copy-start.34 = (bf16[1024,2304]{0,1:T(8,128)(2,1)S(1)}, bf16[1024,2304]{0,1:T(8,128)(2,1)}, u32[]{:S(2)}) copy-start(bf16[1024,2304]{0,1:T(8,128)(2,1)} %copy-done.33) | copy-start | bytes 14155780
  683.5 12.7 %copy-start.36 = (bf16[768,2304]{1,0:T(8,128)(2,1)S(1)}, bf16[768,2304]{1,0:T(8,128)(2,1)}, u32[]{:S(2)}) copy-start(bf16[768,2304]{1,0:T(8,128)(2,1)} %copy-done.35) | copy-start | bytes 10616836
  683.5 12.7 %copy-start.45 = (f32[1,4,2,128]{3,1,2,0:T(4,128)S(1)}, f32[1,4,2,128]{3,1,2,0:T(4,128)}, u32[]{:S(2)}) copy-start(f32[1,4,2,128]{3,1,2,0:T(4,128)} %copy-done.44) | copy-start | bytes 12292
  683.5 12.7 %copy-start.57 = (f32[768]{0:T(1024)S(1)}, f32[768]{0:T(1024)}, u32[]{:S(2)}) copy-start(f32[768]{0:T(1024)} %param.25) | copy-start | bytes 9220
  871.9 3.4 copy-start.22
  875.2 2.5 copy-start.21
  877.8 2.5 copy-start.20
  (8 other events, 10.9 us)
Sparse Core Ops, SparseCore 0:
  667.1 204.6 all-reduce.3
where the time goes:
time: 899 us; the launch traced here: 889 us
  waiting for transfers between devices  262 us (29%)
  matrix products  237 us (26%)
  local copies, waits for them, and re-layouts  156 us (17%)
  other arithmetic  90.1 us (10%)
  starting transfers between devices  65.1 us (7%)
  blocking collectives  64.3 us (7%)
  between operations  15.2 us (2%)
    psum x1, waiting for transfers between devices, local(): lax.psum((grad_qkv[:, :width], grad_qkv[:, width:2 * width], grad_qkv[:,...  115 us
    all_to_all x1, waiting for transfers between devices, send_grads(): lax.all_to_all(shaped, 'grp', split_axis=0, concat_axis=0, tiled=True)  56.8 us
    psum x1, blocking collectives, local(): lax.psum((grad_qkv[:, :width], grad_qkv[:, width:2 * width], grad_qkv[:,...  50.6 us
    all_to_all x1, waiting for transfers between devices, send_rows(): lax.all_to_all(shaped, 'grp', split_axis=0, concat_axis=0, tiled=True)  48.4 us
    eq x1, local copies, waits for them, and re-layouts, local(): buckets[:, :, None]  45.2 us
    dot_general x1, matrix products, expert_backward(): jnp.dot(grad_arrived, second_w.T, preferred_element_type=jnp.float32)  28.3 us
    reduce_sum x1, other arithmetic, local(): jnp.einsum('bhqk,qkn->nh', grad_scores, one_hot_low, preferred_element_ty...  25.9 us
    all_to_all x1, waiting for transfers between devices, return_grads(): lax.all_to_all(shaped, 'grp', split_axis=0, concat_axis=0, tiled=True)  25.3 us
  transfers between devices with their start and end apart: 7, of which 5 were waited for; matrix products, arithmetic and copies ran while one was open for 20% of the time, Pallas kernels for 0%

commit v1 on v0

v1 whole, which is shorter than its diff:
```python
import functools

import jax
import jax.numpy as jnp
from jax import lax
from jax.experimental import pallas as pl
from jax.experimental.pallas import tpu as pltpu
from jax.sharding import PartitionSpec as P

EPSILON = 1e-06
NEGATIVE = -1e30
THRESHOLDS = (12, 16, 23, 32, 46, 64, 91)
LOG2E = 1.4426950408889634
TILE = 128
GELU_A = 0.7978845608028654
GELU_B = GELU_A * 0.044715
AXES = ("grp", "exp")
LOW = jnp.bfloat16


def dot(a, b):
    return jnp.dot(a, b, preferred_element_type=jnp.float32)


def dot_t(a, b):
    return lax.dot_general(a, b, (((1,), (1,)), ((), ())), preferred_element_type=jnp.float32)


def params(mib, **more):
    return pltpu.CompilerParams(vmem_limit_bytes=mib << 20, **more)


def whole(shape):
    return pl.BlockSpec(shape, lambda *_: (0,) * len(shape), pipeline_mode=pl.Buffered(1))


def cost(flops, bytes_accessed, transcendentals=0):
    return pl.CostEstimate(
        flops=flops, bytes_accessed=bytes_accessed, transcendentals=transcendentals
    )


def bucket_of(offset):
    distance = jnp.abs(offset)
    far = jnp.full_like(distance, 8)
    for border in THRESHOLDS:
        far = far + (distance >= border).astype(jnp.int32)
    return jnp.where(distance < 8, distance, far) + jnp.where(offset > 0, 16, 0).astype(jnp.int32)


def route_kernel(experts, room, eid_c, eid_r, slot_c, slot_r, g_ref, dest_c, dest_r, g_out):
    tokens = g_ref.shape[0]
    wide = max(128, experts)
    at = lax.broadcasted_iota(jnp.int32, (tokens, tokens), 0)
    to = lax.broadcasted_iota(jnp.int32, (tokens, tokens), 1)
    ids = eid_c[...]
    picked = ids == lax.broadcasted_iota(jnp.int32, (tokens, wide), 1)
    earlier = dot((to < at).astype(LOW), picked.astype(LOW))
    place = jnp.sum(jnp.where(picked, earlier, 0.0), axis=1, keepdims=True).astype(jnp.int32)
    dest_c[...] = jnp.where(slot_c[...] >= 0, ids * room + place, -1)
    ids = eid_r[...]
    picked = ids == lax.broadcasted_iota(jnp.int32, (wide, tokens), 0)
    earlier = dot(picked.astype(LOW), (at < to).astype(LOW))
    place = jnp.sum(jnp.where(picked, earlier, 0.0), axis=0, keepdims=True).astype(jnp.int32)
    dest = jnp.where(slot_r[...] >= 0, ids * room + place, -1)
    dest_r[...] = dest
    spread(dest, g_ref[...], g_out)


def spread(dest, values, out):
    rows = out.shape[0]
    step = 256
    for start in range(0, rows, step):
        here = lax.broadcasted_iota(jnp.int32, (step, dest.shape[1]), 0) + start
        out[start : start + step] = dot((dest == here).astype(LOW), values).astype(LOW)


def collect(dest, values):
    rows = values.shape[0]
    here = lax.broadcasted_iota(jnp.int32, (dest.shape[0], rows), 1)
    return dot((dest == here).astype(LOW), values)


def route(expert_ids, slots, upstream, experts, room):
    tokens, width = upstream.shape
    flat = lambda a, shape: a.reshape(shape)
    return pl.pallas_call(
        functools.partial(route_kernel, experts, room),
        out_shape=[
            jax.ShapeDtypeStruct((tokens, 1), jnp.int32),
            jax.ShapeDtypeStruct((1, tokens), jnp.int32),
            jax.ShapeDtypeStruct((experts * room, width), LOW),
        ],
        compiler_params=params(48),
        cost_estimate=cost(2 * experts * room * tokens * width, 8 << 20),
        name="route",
    )(
        flat(expert_ids, (tokens, 1)),
        flat(expert_ids, (1, tokens)),
        flat(slots, (tokens, 1)),
        flat(slots, (1, tokens)),
        upstream,
    )


def exchange(buffer, devices):
    shaped = buffer.reshape(devices, buffer.shape[0] // devices, buffer.shape[1])
    moved = lax.all_to_all(shaped, AXES, split_axis=0, concat_axis=0, tiled=True)
    return moved.reshape(buffer.shape)


def project_kernel(x_ref, gain_ref, w_ref, normed_ref, out_ref):
    x = x_ref[...].astype(jnp.float32)
    rms = lax.rsqrt(jnp.mean(x * x, axis=-1, keepdims=True) + EPSILON)
    normed = (x * rms * gain_ref[...]).astype(LOW)
    normed_ref[...] = normed
    out_ref[...] = dot(normed, w_ref[...]).astype(LOW)


def project(x, gain, w_qkv):
    tokens, width = x.shape
    out = w_qkv.shape[1]
    step = 256
    rows = lambda w: pl.BlockSpec((step, w), lambda i: (i, 0))
    return pl.pallas_call(
        project_kernel,
        grid=(tokens // step,),
        in_specs=[rows(width), whole((1, width)), whole((width, out))],
        out_specs=[rows(width), rows(out)],
        out_shape=[
            jax.ShapeDtypeStruct((tokens, width), LOW),
            jax.ShapeDtypeStruct((tokens, out), LOW),
        ],
        compiler_params=params(40),
        cost_estimate=cost(2 * tokens * width * out, 12 << 20),
        name="project",
    )(x, gain, w_qkv)


def after_attention_kernel(o_ref, x_ref, w_ref, gain_ref, dest_ref, y_ref, out_ref, held):
    step = o_ref.shape[0]
    i = pl.program_id(0)
    y = x_ref[...].astype(jnp.float32) + dot(o_ref[...], w_ref[...])
    y_ref[...] = y
    rms = lax.rsqrt(jnp.mean(y * y, axis=-1, keepdims=True) + EPSILON)
    held[pl.ds(pl.multiple_of(i * step, step), step), :] = (y * rms * gain_ref[...]).astype(LOW)

    @pl.when(i == pl.num_programs(0) - 1)
    def _():
        spread(dest_ref[...], held[...], out_ref)


def after_attention(joined, x, w_output, gain, dest_r, rows_out):
    tokens, width = x.shape
    step = 256
    rows = pl.BlockSpec((step, width), lambda i: (i, 0))
    return pl.pallas_call(
        after_attention_kernel,
        grid=(tokens // step,),
        in_specs=[rows, rows, whole((width, width)), whole((1, width)), whole((1, tokens))],
        out_specs=[rows, pl.BlockSpec((rows_out, width), lambda i: (0, 0))],
        out_shape=[
            jax.ShapeDtypeStruct((tokens, width), jnp.float32),
            jax.ShapeDtypeStruct((rows_out, width), LOW),
        ],
        scratch_shapes=[pltpu.VMEM((tokens, width), LOW)],
        compiler_params=params(48),
        cost_estimate=cost(2 * tokens * width * (width + rows_out), 12 << 20),
        name="after_attention",
    )(joined, x, w_output, gain, dest_r)


def mix_kernel(experts, ff_ref, dest_ref, eid_ref, y_ref, gain_ref, wr_ref, out_ref):
    y = y_ref[...]
    rms = lax.rsqrt(jnp.mean(y * y, axis=-1, keepdims=True) + EPSILON)
    normed = (y * rms * gain_ref[...]).astype(LOW)
    router = route_softmax(dot(normed, wr_ref[...]), experts)
    lane = lax.broadcasted_iota(jnp.int32, router.shape, 1)
    gate = jnp.sum(jnp.where(lane == eid_ref[...], router, 0.0), axis=-1, keepdims=True)
    out_ref[...] = (y + gate * collect(dest_ref[...], ff_ref[...])).astype(LOW)


def route_softmax(logits, experts):
    lane = lax.broadcasted_iota(jnp.int32, logits.shape, 1)
    logits = jnp.where(lane < experts, logits, NEGATIVE)
    e = jnp.exp(logits - jnp.max(logits, axis=-1, keepdims=True))
    return e / jnp.sum(e, axis=-1, keepdims=True)


def mix(ff, dest_c, expert_ids, y, gain, w_router, experts):
    tokens, width = y.shape
    step = 256
    rows = lambda w: pl.BlockSpec((step, w), lambda i: (i, 0))
    return pl.pallas_call(
        functools.partial(mix_kernel, experts),
        grid=(tokens // step,),
        in_specs=[whole(ff.shape), rows(1), rows(1), rows(width), whole((1, width)), whole(w_router.shape)],
        out_specs=rows(width),
        out_shape=jax.ShapeDtypeStruct((tokens, width), LOW),
        compiler_params=params(40),
        cost_estimate=cost(2 * tokens * width * ff.shape[0], 8 << 20),
        name="mix",
    )(ff, dest_c, expert_ids.reshape(tokens, 1), y, gain, w_router)


def before_attention_kernel(
    dh_ref, dest_ref, y_ref, g_ref, gain_ref, wt_ref, o_ref, dy_ref, do_ref, gw_ref, gg_ref
):
    i = pl.program_id(0)

    @pl.when(i == 0)
    def _():
        gw_ref[...] = jnp.zeros_like(gw_ref)
        gg_ref[...] = jnp.zeros_like(gg_ref)

    dh = collect(dest_ref[...], dh_ref[...])
    y = y_ref[...]
    rms = lax.rsqrt(jnp.mean(y * y, axis=-1, keepdims=True) + EPSILON)
    gg_ref[...] += jnp.sum(dh * y * rms, axis=0, keepdims=True)
    u = dh * gain_ref[...]
    dy = (
        g_ref[...].astype(jnp.float32)
        + rms * u
        - y * (rms * rms * rms) * jnp.mean(u * y, axis=-1, keepdims=True)
    )
    dy_ref[...] = dy
    low = dy.astype(LOW)
    do_ref[...] = dot(low, wt_ref[...]).astype(LOW)
    gw_ref[...] += dot(o_ref[...].T, low)


def before_attention(dh, dest_c, y, g, gain, w_output_t, joined):
    tokens, width = y.shape
    step = 256
    rows = lambda w: pl.BlockSpec((step, w), lambda i: (i, 0))
    return pl.pallas_call(
        before_attention_kernel,
        grid=(tokens // step,),
        in_specs=[
            whole(dh.shape), rows(1), rows(width), rows(width), whole((1, width)),
            whole((width, width)), rows(width),
        ],
        out_specs=[
            rows(width), rows(width),
            pl.BlockSpec((width, width), lambda i: (0, 0)),
            pl.BlockSpec((1, width), lambda i: (0, 0)),
        ],
        out_shape=[
            jax.ShapeDtypeStruct((tokens, width), jnp.float32),
            jax.ShapeDtypeStruct((tokens, width), LOW),
            jax.ShapeDtypeStruct((width, width), jnp.float32),
            jax.ShapeDtypeStruct((1, width), jnp.float32),
        ],
        compiler_params=params(40),
        cost_estimate=cost(2 * tokens * width * (dh.shape[0] + 2 * width), 16 << 20),
        name="before_attention",
    )(dh, dest_c, y, g, gain, w_output_t, joined)


def finish_kernel(
    dq_ref, dk_ref, dv_ref, wt_ref, normed_ref, x_ref, dy_ref, gain_ref, out_ref, gw_ref, gg_ref
):
    i = pl.program_id(0)

    @pl.when(i == 0)
    def _():
        gw_ref[...] = jnp.zeros_like(gw_ref)
        gg_ref[...] = jnp.zeros_like(gg_ref)

    width = x_ref.shape[1]
    grads = (dq_ref[...], dk_ref[...], dv_ref[...])
    normed_t = normed_ref[...].T
    dh = None
    for n, d in enumerate(grads):
        gw_ref[n * width : (n + 1) * width] += dot(normed_t, d)
        part = dot(d, wt_ref[n * width : (n + 1) * width])
        dh = part if dh is None else dh + part
    x = x_ref[...].astype(jnp.float32)
    rms = lax.rsqrt(jnp.mean(x * x, axis=-1, keepdims=True) + EPSILON)
    gg_ref[...] += jnp.sum(dh * x * rms, axis=0, keepdims=True)
    u = dh * gain_ref[...]
    out_ref[...] = (
        dy_ref[...]
        + rms * u
        - x * (rms * rms * rms) * jnp.mean(u * x, axis=-1, keepdims=True)
    )


def finish(dq, dk, dv, w_qkv_t, normed, x, dy, gain):
    tokens, width = x.shape
    step = 256
    rows = pl.BlockSpec((step, width), lambda i: (i, 0))
    return pl.pallas_call(
        finish_kernel,
        grid=(tokens // step,),
        in_specs=[rows, rows, rows, whole((3 * width, width)), rows, rows, rows, whole((1, width))],
        out_specs=[
            rows,
            pl.BlockSpec((3 * width, width), lambda i: (0, 0)),
            pl.BlockSpec((1, width), lambda i: (0, 0)),
        ],
        out_shape=[
            jax.ShapeDtypeStruct((tokens, width), jnp.float32),
            jax.ShapeDtypeStruct((3 * width, width), jnp.float32),
            jax.ShapeDtypeStruct((1, width), jnp.float32),
        ],
        compiler_params=params(48),
        cost_estimate=cost(12 * tokens * width * width, 24 << 20),
        name="finish",
    )(dq, dk, dv, w_qkv_t, normed, x, dy, gain)


def attention_forward_kernel(len_ref, q_ref, k_ref, v_ref, near_ref, far_ref, o_ref, p_ref, s_ref):
    seq = q_ref.shape[0]
    tiles = seq // TILE
    half = q_ref.shape[1] // 2
    row = pl.program_id(0)
    pair = pl.program_id(1)
    live = len_ref[row]
    lane = lax.broadcasted_iota(jnp.int32, (seq, 2 * half), 1)
    dead = lax.broadcasted_iota(jnp.int32, (seq, 2 * half), 0) >= live
    q = q_ref[...]
    k = k_ref[...]
    v_t = v_ref[...].T
    outs = []
    for h in range(2):
        mine = (lane >= h * half) & (lane < (h + 1) * half)
        flag = lane == (1 - h) * half
        k_h = jnp.where(mine, k, jnp.where(flag & dead, -1e30, 0.0).astype(k.dtype))
        q_h = jnp.where(flag, jnp.ones_like(q), q)
        after = far_ref[2 * pair + h, 0]
        before = far_ref[2 * pair + h, 1]
        tops = []
        for i in range(tiles):
            q_i = q_h[i * TILE:(i + 1) * TILE]
            raw = lax.dot_general(k_h, q_i, (((1,), (1,)), ((), ())), preferred_element_type=jnp.float32)
            top = None
            for j in range(tiles):
                x = raw[j * TILE:(j + 1) * TILE] * (0.125 * LOG2E)
                d = j - i
                if -1 <= d <= 1:
                    x = x + near_ref[h, d + 1]
                else:
                    x = x + (after if d > 0 else before)
                s_ref[j * TILE:(j + 1) * TILE, i * TILE:(i + 1) * TILE] = x
                m = jnp.max(x, axis=0, keepdims=True)
                top = m if top is None else jnp.maximum(top, m)
            tops.append(top)
        for i in range(tiles):
            e = jnp.exp2(s_ref[:, i * TILE:(i + 1) * TILE] - tops[i])
            total = jnp.sum(e, axis=0, keepdims=True)
            p_ref[0, h, :, i * TILE:(i + 1) * TILE] = (e * (1.0 / total)).astype(LOW)
        outs.append(lax.dot_general(v_t[h * half:(h + 1) * half], p_ref[0, h], (((1,), (0,)), ((), ())), preferred_element_type=jnp.float32))
    o_ref[...] = jnp.concatenate(outs, axis=0).T.astype(o_ref.dtype)

def attention_forward(lengths, projected, near, far, rows, seq, heads, head):
    width = heads * head
    pairs = heads // 2
    spec = lambda off: pl.BlockSpec((seq, 2 * head), lambda b, p: (b, off + p))
    return pl.pallas_call(
        attention_forward_kernel,
        grid=(rows, pairs),
        in_specs=[
            pl.BlockSpec(memory_space=pltpu.SMEM),
            spec(0), spec(pairs), spec(2 * pairs),
            pl.BlockSpec((2, 3, TILE, TILE), lambda b, p: (p, 0, 0, 0)),
            pl.BlockSpec(memory_space=pltpu.SMEM),
        ],
        out_specs=[
            pl.BlockSpec((seq, 2 * head), lambda b, p: (b, p)),
            pl.BlockSpec((1, 2, seq, seq), lambda b, p: (b, p, 0, 0)),
        ],
        out_shape=[
            jax.ShapeDtypeStruct((rows * seq, width), LOW),
            jax.ShapeDtypeStruct((rows, heads, seq, seq), LOW),
        ],
        scratch_shapes=[pltpu.VMEM((seq, seq), jnp.float32)],
        compiler_params=params(40),
        cost_estimate=cost(flops=4 * rows * heads * seq * seq * head * 4, bytes_accessed=rows * heads * seq * seq * 2, transcendentals=rows * heads * seq * seq),
        name="attention_forward",
    )(lengths, projected, projected, projected, near, far)

def attention_backward_kernel(q_ref, k_ref, v_ref, do_ref, o_ref, p_ref, dq_ref, dk_ref, dv_ref, near_ref, far_ref, d_ref):
    seq = q_ref.shape[0]
    tiles = seq // TILE
    half = q_ref.shape[1] // 2
    row = pl.program_id(1)
    lane = lax.broadcasted_iota(jnp.int32, (seq, 2 * half), 1)
    q = q_ref[...]
    k = k_ref[...]
    k_t = k.T
    v = v_ref[...]
    do = do_ref[...]
    weighed = (do.astype(jnp.float32) * o_ref[...].astype(jnp.float32)).T
    dq_parts = []
    dk_all = None
    dv_all = None

    @pl.when(row == 0)
    def _():
        near_ref[...] = jnp.zeros_like(near_ref)
        far_ref[...] = jnp.zeros_like(far_ref)

    for h in range(2):
        mine = (lane >= h * half) & (lane < (h + 1) * half)
        v_h = jnp.where(mine, v, jnp.zeros_like(v))
        delta = jnp.sum(weighed[h * half:(h + 1) * half], axis=0, keepdims=True)
        far_sum = [jnp.zeros((8, TILE), jnp.float32), jnp.zeros((8, TILE), jnp.float32)]
        for i in range(tiles):
            cols = slice(i * TILE, (i + 1) * TILE)
            dp = lax.dot_general(v_h, do[cols], (((1,), (1,)), ((), ())), preferred_element_type=jnp.float32)
            for j in range(tiles):
                rws = slice(j * TILE, (j + 1) * TILE)
                ds = p_ref[0, h, rws, cols].astype(jnp.float32) * (dp[rws] - delta[:, cols])
                d = j - i
                if -1 <= d <= 1:
                    near_ref[h, d + 1] += ds
                else:
                    which = 0 if d > 0 else 1
                    far_sum[which] = far_sum[which] + jnp.sum(ds.reshape(TILE // 8, 8, TILE), axis=0)
                d_ref[rws, cols] = ds.astype(LOW)
        far_ref[h, 0] += far_sum[0]
        far_ref[h, 1] += far_sum[1]
        ds_all = d_ref[...]
        dq_parts.append(lax.dot_general(k_t[h * half:(h + 1) * half], ds_all, (((1,), (0,)), ((), ())), preferred_element_type=jnp.float32))
        dk_h = lax.dot_general(ds_all, q, (((1,), (0,)), ((), ())), preferred_element_type=jnp.float32)
        dv_h = lax.dot_general(p_ref[0, h], do, (((1,), (0,)), ((), ())), preferred_element_type=jnp.float32)
        dk_all = dk_h if h == 0 else jnp.where(mine, dk_h, dk_all)
        dv_all = dv_h if h == 0 else jnp.where(mine, dv_h, dv_all)
    dq_ref[...] = (jnp.concatenate(dq_parts, axis=0).T * 0.125).astype(LOW)
    dk_ref[...] = (dk_all * 0.125).astype(LOW)
    dv_ref[...] = dv_all.astype(LOW)

def attention_backward(projected, do, joined, weights, rows, seq, heads, head):
    width = heads * head
    pairs = heads // 2
    spec = lambda off: pl.BlockSpec((seq, 2 * head), lambda p, b: (b, off + p))
    return pl.pallas_call(
        attention_backward_kernel,
        grid=(pairs, rows),
        in_specs=[
            spec(0), spec(pairs), spec(2 * pairs), spec(0), spec(0),
            pl.BlockSpec((1, 2, seq, seq), lambda p, b: (b, p, 0, 0)),
        ],
        out_specs=[
            spec(0), spec(0), spec(0),
            pl.BlockSpec((2, 3, TILE, TILE), lambda p, b: (p, 0, 0, 0)),
            pl.BlockSpec((2, 2, 8, TILE), lambda p, b: (p, 0, 0, 0)),
        ],
        out_shape=[jax.ShapeDtypeStruct((rows * seq, width), LOW)] * 3 + [
            jax.ShapeDtypeStruct((heads, 3, TILE, TILE), jnp.float32),
            jax.ShapeDtypeStruct((heads, 2, 8, TILE), jnp.float32),
        ],
        scratch_shapes=[pltpu.VMEM((seq, seq), LOW)],
        compiler_params=params(40),
        cost_estimate=cost(flops=8 * rows * heads * seq * seq * head * 4, bytes_accessed=rows * heads * seq * seq * 2, transcendentals=0),
        name="attention_backward",
    )(projected, projected, projected, do, joined, weights)

def bias_tiles(table):
    j = lax.broadcasted_iota(jnp.int32, (3, TILE, TILE), 1)
    i = lax.broadcasted_iota(jnp.int32, (3, TILE, TILE), 2)
    d = lax.broadcasted_iota(jnp.int32, (3, TILE, TILE), 0) - 1
    b = bucket_of(d * TILE + j - i)
    scaled = table.T * LOG2E
    hot = (b.reshape(1, -1) == jnp.arange(table.shape[0], dtype=jnp.int32)[:, None]).astype(jnp.float32)
    near = jnp.dot(scaled, hot, precision=lax.Precision.HIGHEST).reshape(-1, 3, TILE, TILE)
    far = jnp.stack([scaled[:, -1], scaled[:, table.shape[0] // 2 - 1]], axis=1)
    return near, far, hot


def expert_kernel(experts, chunk, x_ref, g_ref, mine_ref, wr_ref, wrt_ref, wi_ref, wit_ref, wo_ref, wot_ref,
                  ff_ref, dx_ref, hid_ref, da_ref, xt_ref, dfft_ref, gr_ref):
    x = x_ref[...]
    g = g_ref[...].astype(jnp.float32)
    mine = mine_ref[...]
    lane = lax.broadcasted_iota(jnp.int32, (1, wr_ref.shape[1]), 1)
    logits = jnp.dot(x, wr_ref[...], preferred_element_type=jnp.float32)
    logits = jnp.where(lane < experts, logits, -1e30)
    e = jnp.exp(logits - jnp.max(logits, axis=-1, keepdims=True))
    router = e / jnp.sum(e, axis=-1, keepdims=True)
    gate = jnp.sum(router * mine, axis=-1, keepdims=True)
    dff = (g * gate).astype(LOW)
    inner = wi_ref.shape[1]
    ff = None
    dx = None
    def first(f):
        cols = slice(f, f + chunk)
        return (jnp.dot(x, wi_ref[:, cols], preferred_element_type=jnp.float32),
                jnp.dot(dff, wot_ref[:, cols], preferred_element_type=jnp.float32))
    ahead = first(0)
    for f in range(0, inner, chunk):
        cols = slice(f, f + chunk)
        a, dhid = ahead
        if f + chunk < inner:
            ahead = first(f + chunk)
        u = a * a
        t = jnp.tanh(a * (GELU_A + GELU_B * u))
        h = 0.5 + 0.5 * t
        hid = a * h
        slope = h + hid * ((1.0 - t) * (GELU_A + (3.0 * GELU_B) * u))
        da = (dhid * slope).astype(LOW)
        hid = hid.astype(LOW)
        hid_ref[:, cols] = hid
        da_ref[:, cols] = da
        ff_part = jnp.dot(hid, wo_ref[cols, :], preferred_element_type=jnp.float32)
        dx_part = jnp.dot(da, wit_ref[cols, :], preferred_element_type=jnp.float32)
        ff = ff_part if ff is None else ff + ff_part
        dx = dx_part if dx is None else dx + dx_part
    ff = ff.astype(LOW)
    ff_ref[...] = ff
    dgate = jnp.sum(g * ff.astype(jnp.float32), axis=-1, keepdims=True)
    dlogits = ((gate * dgate) * (mine - router)).astype(LOW)
    dx = dx + jnp.dot(dlogits, wrt_ref[...], preferred_element_type=jnp.float32)
    dx_ref[...] = dx.astype(LOW)
    x_t = x.T
    xt_ref[...] = x_t
    dfft_ref[...] = dff.T

    @pl.when(pl.program_id(0) == 0)
    def _():
        gr_ref[...] = jnp.zeros_like(gr_ref)
    gr_ref[...] += jnp.dot(x_t, dlogits, preferred_element_type=jnp.float32)

def expert_rows(x, g, mine, wr, wrt, wi, wit, wo, wot, experts, tile=256, chunk=768):
    n, width = x.shape
    inner = wi.shape[1]
    while n % tile: tile //= 2
    once = lambda s: pl.BlockSpec(s, lambda i: (0,) * len(s), pipeline_mode=pl.Buffered(1))
    rowspec = lambda w: pl.BlockSpec((tile, w), lambda i: (i, 0))
    return pl.pallas_call(
        functools.partial(expert_kernel, experts, chunk),
        grid=(n // tile,),
        in_specs=[rowspec(width), rowspec(width), once(mine.shape), once(wr.shape), once(wrt.shape), once(wi.shape), once(wit.shape), once(wo.shape), once(wot.shape)],
        out_specs=[rowspec(width), rowspec(width), rowspec(inner), rowspec(inner),
                   pl.BlockSpec((width, tile), lambda i: (0, i)), pl.BlockSpec((width, tile), lambda i: (0, i)),
                   pl.BlockSpec((width, wr.shape[1]), lambda i: (0, 0))],
        out_shape=[jax.ShapeDtypeStruct((n, width), LOW)] * 2 + [jax.ShapeDtypeStruct((n, inner), LOW)] * 2
            + [jax.ShapeDtypeStruct((width, n), LOW)] * 2 + [jax.ShapeDtypeStruct((width, wr.shape[1]), jnp.float32)],
        compiler_params=params(56),
        cost_estimate=cost(flops=8 * n * width * inner, bytes_accessed=4 * n * inner + 8 * width * inner, transcendentals=n * inner),
        name="expert_rows",
    )(x, g, mine, wr, wrt, wi, wit, wo, wot)

def expert_weights_kernel(parts, *refs):
    ins, (gi_ref, go_ref) = refs[:4 * parts], refs[4 * parts:]
    gi = None
    go = None
    for c in range(parts):
        xt, dfft, hid, da = ins[4 * c:4 * c + 4]
        gi_c = jnp.dot(xt[...], da[...], preferred_element_type=jnp.float32)
        go_c = jnp.dot(dfft[...], hid[...], preferred_element_type=jnp.float32)
        gi = gi_c if gi is None else gi + gi_c
        go = go_c if go is None else go + go_c
    gi_ref[0] = gi
    go_ref[0] = go.T

def expert_weights(parts, tile=256):
    inner = parts[0][2].shape[1]
    width = parts[0][0].shape[0]
    specs, args, rows = [], [], 0
    for xt, dfft, hid, da in parts:
        n = hid.shape[0]
        rows += n
        specs += [pl.BlockSpec((width, n), lambda f: (0, 0), pipeline_mode=pl.Buffered(1))] * 2
        specs += [pl.BlockSpec((n, tile), lambda f: (0, f))] * 2
        args += [xt, dfft, hid, da]
    return pl.pallas_call(
        functools.partial(expert_weights_kernel, len(parts)),
        grid=(inner // tile,),
        in_specs=specs,
        out_specs=[pl.BlockSpec((1, width, tile), lambda f: (0, 0, f)), pl.BlockSpec((1, tile, width), lambda f: (0, f, 0))],
        out_shape=[jax.ShapeDtypeStruct((1, width, inner), jnp.float32), jax.ShapeDtypeStruct((1, inner, width), jnp.float32)],
        compiler_params=params(56),
        cost_estimate=cost(flops=4 * rows * width * inner, bytes_accessed=4 * rows * inner + 8 * width * inner, transcendentals=0),
        name="expert_weights",
    )(*args)


def local(
    tokens, lengths, expert_ids, slots, w_query, w_key, w_value, w_output,
    gain_attn, gain_ffn, bias_table, w_router, w_in, w_out, cotangent,
):
    rows, seq, width = tokens.shape
    count = rows * seq
    buckets, heads = bias_table.shape
    head = width // heads
    experts = w_router.shape[1]
    devices = lax.axis_size(AXES)
    room = max(4, 2 * count // experts)
    me = lax.axis_index(AXES)
    x = tokens.reshape(count, width)
    g = cotangent.reshape(count, width)
    gain_one = gain_attn.reshape(1, width)
    gain_two = gain_ffn.reshape(1, width)
    wide = max(128, experts)
    router_w = jnp.pad(w_router, ((0, 0), (0, wide - experts)))
    mine = (jnp.arange(wide, dtype=jnp.int32) == me).astype(jnp.float32).reshape(1, wide)

    dest_c, dest_r, g_out = route(expert_ids, slots, g, experts, room)
    g_in = exchange(g_out, devices)

    w_qkv = jnp.concatenate([w_query, w_key, w_value], axis=1)
    normed, projected = project(x, gain_one, w_qkv)
    near, far, hot = bias_tiles(bias_table)
    joined, weights = attention_forward(lengths, projected, near, far, rows, seq, heads, head)
    y, h_out = after_attention(joined, x, w_output, gain_two, dest_r, experts * room)
    h_in = exchange(h_out, devices)

    ff, dx, hid, da, x_t, dff_t, grad_router = expert_rows(
        h_in, g_in, mine, router_w, router_w.T, w_in[0], w_in[0].T, w_out[0], w_out[0].T, experts
    )
    dh_back = exchange(dx, devices)
    ff_back = exchange(ff, devices)
    grad_in, grad_out = expert_weights([(x_t, dff_t, hid, da)])

    dy, do, grad_output, grad_gain_two = before_attention(
        dh_back, dest_c, y, g, gain_two, w_output.T, joined
    )
    dq, dk, dv, near_sum, far_sum = attention_backward(
        projected, do, joined, weights, rows, seq, heads, head
    )
    grad_tokens, grad_qkv, grad_gain_one = finish(
        dq, dk, dv, w_qkv.T, normed, x, dy, gain_one
    )
    table = jnp.dot(hot, near_sum.reshape(heads, -1).T, precision=lax.Precision.HIGHEST)
    far_total = jnp.sum(far_sum, axis=(2, 3))
    table = table.at[buckets - 1].add(far_total[:, 0]).at[buckets // 2 - 1].add(far_total[:, 1])
    mixed = mix(ff_back, dest_c, expert_ids, y, gain_two, router_w, experts)
    summed = lax.psum(
        (
            grad_qkv[:width], grad_qkv[width : 2 * width], grad_qkv[2 * width :], grad_output,
            grad_gain_one.reshape(width), grad_gain_two.reshape(width), table,
            grad_router[:, :experts],
        ),
        AXES,
    )
    return (
        mixed.reshape(rows, seq, width),
        grad_tokens.reshape(rows, seq, width),
        *summed,
        grad_in,
        grad_out,
    )


def solution(mesh):
    split = P(AXES)
    in_specs = (split,) * 4 + (P(),) * 8 + (split,) * 3
    out_specs = (split,) * 2 + (P(),) * 8 + (split,) * 2
    return jax.shard_map(local, mesh=mesh, in_specs=in_specs, out_specs=out_specs, check_vma=False)
```

time: 899 us -> 663 us (0.74)
  matrix products: 237 us -> 8.13 us
  Pallas kernels: 0 us -> 185 us
  other arithmetic: 90.1 us -> 6.93 us
  local copies, waits for them, and re-layouts: 156 us -> 73.3 us
  blocking collectives: 64.3 us -> 119 us
  starting transfers between devices: 65.1 us -> 11.8 us
  waiting for transfers between devices: 262 us -> 234 us
    dot_general x23 -> x2, matrix products: 237 us -> 8.13 us  [the longest x1 5.35 us: local(): jnp.dot(hot, near_sum.reshape(heads, -1).T, precision=lax.Precision.HIGHEST)]
    pallas_call x0 -> x10, Pallas kernels: none -> 185 us  [the longest x1 58.7 us: expert_rows(): pl.pallas_call(functools.partial(expert_kernel, experts, chunk), grid=(n...]
    all_to_all x2 -> x1, blocking collectives: 13.6 us -> 78.6 us  [exchange(): lax.all_to_all(shaped, AXES, split_axis=0, concat_axis=0, tiled=True)]
    all_to_all x6 -> x3, starting transfers between devices: 65.1 us -> 11.8 us  [exchange(): lax.all_to_all(shaped, AXES, split_axis=0, concat_axis=0, tiled=True)]
    eq x2 -> x0, local copies, waits for them, and re-layouts: 46.1 us -> none  [the longest x1 45.2 us: local(): buckets[:, :, None]]
    reduce_sum x7 -> x1, other arithmetic: 40.8 us -> 0.11 us  [local(): far_total = jnp.sum(far_sum, axis=(2, 3))]
    unnamed x147 -> x91, local copies, waits for them, and re-layouts: 20.6 us -> 59 us
    all_to_all x6 -> x3, waiting for transfers between devices: 147 us -> 126 us  [exchange(): lax.all_to_all(shaped, AXES, split_axis=0, concat_axis=0, tiled=True)]
  transfers between devices with their start and end apart: 7 -> 4, of which waited for: 5 -> 3; matrix products, arithmetic and copies ran while one was open for 20% -> 5% of each run, Pallas kernels for 0% -> 13%
where the time goes in v1:
time: 663 us; the launch traced here: 653 us
  waiting for transfers between devices  234 us (35%)
  Pallas kernels  185 us (28%)
  blocking collectives  119 us (18%)
  local copies, waits for them, and re-layouts  73.3 us (11%)
  between operations  14.8 us (2%)
  starting transfers between devices  11.8 us (2%)
  matrix products  8.13 us (1%)
  other arithmetic  6.93 us (1%)
    all_to_all x3, waiting for transfers between devices, exchange(): lax.all_to_all(shaped, AXES, split_axis=0, concat_axis=0, tiled=True)  126 us
    psum x1, waiting for transfers between devices, local(): lax.psum((grad_qkv[:width], grad_qkv[width:2 * width], grad_qkv[2 * width...  108 us
    all_to_all x1, blocking collectives, exchange(): lax.all_to_all(shaped, AXES, split_axis=0, concat_axis=0, tiled=True)  78.6 us
    unnamed x91, local copies, waits for them, and re-layouts  59 us
    pallas_call x1, Pallas kernels, expert_rows(): pl.pallas_call(functools.partial(expert_kernel, experts, chunk), grid=(n...  58.7 us
    psum x1, blocking collectives, local(): lax.psum((grad_qkv[:width], grad_qkv[width:2 * width], grad_qkv[2 * width...  40.8 us
    pallas_call x1, Pallas kernels, expert_weights(): pl.pallas_call(functools.partial(expert_weights_kernel, len(parts)), grid...  29 us
    pallas_call x1, Pallas kernels, attention_backward(): pl.pallas_call(attention_backward_kernel, grid=(pairs, rows), in_specs=[s...  24 us
  transfers between devices with their start and end apart: 4, of which 3 were waited for; matrix products, arithmetic and copies ran while one was open for 5% of the time, Pallas kernels for 13%

profile of v1, /device:TPU:0, one launch (start us, length us, event | category | flops | bytes accessed | tf_op | source)
XLA Modules:
  0.0 652.9 jit_solution(95347640472003153)
XLA Ops:
  7.2 1.4 reshape.210.gain_ref
  8.6 1.6 copy.79
  10.1 0.6 copy.78
  10.8 1.6 copy.77
  12.4 3.3 fusion.13
  15.7 4.3 copy.80.w_ref
  20.1 0.9 fusion.6
  20.9 0.7 copy.81
  21.6 0.7 multiply_bitcast_fusion
  22.3 1.2 fusion.4
  23.5 2.8 fusion.1
  26.3 0.6 copy.98
  26.9 1.6 slice.74
  29.2 0.7 copy.99
  29.9 1.0 copy.100
  31.0 0.7 copy.102
  31.6 1.0 copy.103
  32.7 0.7 copy-done.10
  33.4 1.4 copy-done.14
  34.8 4.7 project.1
  39.5 1.1 copy-done.26
  40.7 6.1 route.1
  46.9 20.7 %attention_forward.1 = (bf16[1024,768]{1,0:T(8,128)(2,1)S(1)}, bf16[2,12,512,512]{3,2,1,0:T(8,128)(2,1)}) custom-call(s32[2]{0:T(128)S(1)} %copy-done.16, bf16[1024,2304]{1,0:T(8,128)(2,1)S(1)} %get-tuple-element.66.q_ref.k_ref.v_ref, bf16[1024,2304]{1,0:T(8,128)(2,1)S(1)} %get-tuple-element.66.q_ref.k_ref.v_ref, ...), custom_call_target="tpu_custom_call" | custom-call | flops 6442450944 | bytes 12582912 | tf_op jit(solution)/shard_map/attention_forward/pallas_call | solution.py:360
  67.7 8.2 %after_attention.1 = (f32[1024,768]{1,0:T(8,128)}, bf16[2048,768]{1,0:T(8,128)(2,1)}) custom-call(bf16[1024,768]{1,0:T(8,128)(2,1)S(1)} %get-tuple-element.67.o_ref, bf16[1024,768]{1,0:T(8,128)(2,1)S(1)} %bitcast.76, bf16[768,768]{1,0:T(8,128)(2,1)S(1)} %copy-done.3, f32[1,768]{1,0:T(1,128)S(1)} %copy-done.9, s32[1,1024]{1,0:T(1,128)S(1)} %get-tuple-element.68.dest_ref), custom_call_target="tpu_custom_call" | custom-call | flops 4429185024 | bytes 12582912 | tf_op jit(solution)/shard_map/after_attention/pallas_call | solution.py:157
  75.9 78.6 %all_to_all.20 = bf16[32,64,768]{2,1,0:T(8,128)(2,1)} all-to-all(bf16[32,64,768]{2,1,0:T(8,128)(2,1)} %bitcast.89), channel_id=1, replica_groups=mesh['grp'=16,'exp'=2] {'grp','exp'}, dimensions={0} | all-to-all | bytes 6291456 | tf_op jit(solution)/shard_map/all_to_all | solution.py:108
  154.5 3.8 all-to-all-start.1
  158.5 0.7 pad_bitcast_fusion
  159.2 0.8 copy.88.wrt_ref
  160.0 6.6 %copy.86 = bf16[1,768,3072]{1,2,0:T(8,128)(2,1)} copy(bf16[1,768,3072]{2,1,0:T(8,128)(2,1)} %param.31) | data formatting | bytes 9437184 | tf_op args[12]
  166.6 6.6 %copy.87 = bf16[1,3072,768]{1,2,0:T(8,128)(2,1)} copy(bf16[1,3072,768]{2,1,0:T(8,128)(2,1)} %param.32) | data formatting | bytes 9437184 | tf_op args[13]
  173.8 56.0 %all-to-all-done.1 = bf16[32,64,768]{2,1,0:T(8,128)(2,1)} async-done(((bf16[32,64,768]{2,1,0:T(8,128)(2,1)}), bf16[32,64,768]{2,1,0:T(8,128)(2,1)}, u32[]{:S(2)}, u32[]{:S(2)}) %all-to-all-start.1) | async-done | bytes 3145760 | tf_op jit(solution)/shard_map/all_to_all | solution.py:108
  229.7 58.7 %expert_rows.1 = (bf16[2048,768]{1,0:T(8,128)(2,1)}, bf16[2048,768]{1,0:T(8,128)(2,1)}, bf16[2048,3072]{1,0:T(8,128)(2,1)}, bf16[2048,3072]{1,0:T(8,128)(2,1)}, ...) custom-call(bf16[2048,768]{1,0:T(8,128)(2,1)} %bitcast.87, ...), custom_call_target="tpu_custom_call" | custom-call | flops 38654705664 | bytes 44040192 | tf_op jit(solution)/shard_map/expert_rows/pallas_call | solution.py:531
  288.5 4.1 all-to-all-start.3
  292.5 1.5 copy.92
  294.0 70.0 %all-to-all-done.3 = bf16[32,64,768]{2,1,0:T(8,128)(2,1)} async-done(((bf16[32,64,768]{2,1,0:T(8,128)(2,1)}), bf16[32,64,768]{2,1,0:T(8,128)(2,1)}, u32[]{:S(2)}, u32[]{:S(2)}) %all-to-all-start.3) | async-done | bytes 3145760 | tf_op jit(solution)/shard_map/all_to_all | solution.py:108
  364.0 3.9 all-to-all-start.2
  368.0 1.3 copy-done.4
  369.3 1.4 copy-done.13
  370.7 1.0 copy-done.20
  371.7 1.4 copy-done.24
  373.1 12.2 %before_attention.1 = (f32[1024,768]{1,0:T(8,128)S(1)}, bf16[1024,768]{1,0:T(8,128)(2,1)S(1)}, f32[768,768]{1,0:T(8,128)S(1)}, f32[1,768]{1,0:T(1,128)S(1)}) custom-call(bf16[2048,768]{1,0:T(8,128)(2,1)} %bitcast.20.dh_ref, s32[1024,1]{1,0:T(8,128)S(1)} %copy-done.20, f32[1024,768]{1,0:T(8,128)} %get-tuple-element.73.y_ref, bf16[1024,768]{1,0:T(8,128)(2,1)S(1)} %bitcast.73, ...), custom_call_target="tpu_custom_call" | custom-call | flops 5637144576 | bytes 16777216 | tf_op jit(solution)/shard_map/before_attention/pallas_call | solution.py:236
  385.4 1.4 copy-done.2
  386.8 1.7 copy-done.22
  388.5 24.0 %attention_backward.1 = (bf16[1024,768]{1,0:T(8,128)(2,1)S(1)}, bf16[1024,768]{1,0:T(8,128)(2,1)S(1)}, bf16[1024,768]{1,0:T(8,128)(2,1)S(1)}, f32[12,3,128,128]{3,2,1,0:T(8,128)S(1)}, f32[12,2,8,128]{3,2,1,0:T(8,128)S(1)}) custom-call(bf16[1024,2304]{1,0:T(8,128)(2,1)} %copy-done.18, bf16[1024,2304]{1,0:T(8,128)(2,1)} %copy-done.18, ...), custom_call_target="tpu_custom_call" | custom-call | flops 12884901888 | bytes 12582912 | tf_op jit(solution)/shard_map/attention_backward/pallas_call | solution.py:438
  412.5 1.4 copy-done
  413.9 15.3 %finish.1 = (f32[1024,768]{1,0:T(8,128)}, f32[2304,768]{1,0:T(8,128)}, f32[1,768]{1,0:T(1,128)S(1)}) custom-call(bf16[1024,768]{1,0:T(8,128)(2,1)S(1)} %get-tuple-element.77.dq_ref, bf16[1024,768]{1,0:T(8,128)(2,1)S(1)} %get-tuple-element.78.dk_ref, bf16[1024,768]{1,0:T(8,128)(2,1)S(1)} %get-tuple-element.79.dv_ref, ...), custom_call_target="tpu_custom_call" | custom-call | flops 7247757312 | bytes 25165824 | tf_op jit(solution)/shard_map/finish/pallas_call | solution.py:293
  429.2 6.2 fusion.14
  435.4 29.0 %expert_weights.1 = (f32[1,768,3072]{2,1,0:T(8,128)}, f32[1,3072,768]{2,1,0:T(8,128)}) custom-call(bf16[768,2048]{1,0:T(8,128)(2,1)} %get-tuple-element.90.refs_0_, bf16[768,2048]{1,0:T(8,128)(2,1)} %get-tuple-element.91.refs_1_, bf16[2048,3072]{1,0:T(8,128)(2,1)} %get-tuple-element.92.refs_2_, bf16[2048,3072]{1,0:T(8,128)(2,1)} %get-tuple-element.93.refs_3_), custom_call_target="tpu_custom_call" | custom-call | flops 19327352832 | bytes 44040192 | tf_op jit(solution)/shard_map/expert_weights/pallas_call | solution.py:568
  464.5 2.0 pad.14
  466.5 3.5 copy.105
  470.1 5.4 fusion
  475.8 40.8 %all-reduce.1 = (f32[768]{0:T(1024)}, f32[768]{0:T(1024)}, f32[32,12]{0,1:T(8,128)}) all-reduce(f32[768]{0:T(1024)S(1)} %reduce.4, f32[768]{0:T(1024)S(1)} %reduce.5, f32[32,12]{0,1:T(8,128)S(1)} %scatter-add.9), channel_id=1, replica_groups=mesh['grp'=16,'exp'=2] {'grp','exp'}, use_global_device_ids=true, to_apply=%region_4.5 | all-reduce | flops 1920 | bytes 15360 | tf_op jit(solution)/shard_map/psum | solution.py:630
  516.7 1.0 copy-done.6
  517.7 1.9 copy-done.17
  519.6 1.1 copy-done.21
  520.7 5.6 mix.1
  526.3 107.8 %all-reduce.5.cloned.1.call-done = (f32[768,768]{1,0:T(8,128)}, f32[768,768]{1,0:T(8,128)}, f32[768,768]{1,0:T(8,128)}, f32[768,768]{1,0:T(8,128)}, f32[768,32]{1,0:T(8,128)}) async-done(((f32[768,768]{1,0:T(8,128)}, f32[768,768]{1,0:T(8,128)}, f32[768,768]{1,0:T(8,128)}, f32[768,768]{1,0:T(8,128)}, f32[768,32]{1,0:T(8,128)}), (f32[768,768]{1,0:T(8,128)}, f32[768,768]{1,0:T(8,128)}, f32[768,768]{1,0:T(8,128)}, ...) | async-done | bytes 9535504 | tf_op jit(solution)/shard_map/psum | solution.py:630
  634.1 1.9 copy.95
  636.0 3.2 copy.113
  639.2 1.4 copy.114
  640.6 1.1 copy-done.28
  641.7 1.4 copy.115
  643.1 1.1 copy-done.27
  644.2 1.4 copy.116
  (72 shorter events, 2.0 us)
Async XLA Ops:
  7.2 3.0 copy-start.31
  15.7 5.2 copy-start.33
  23.5 2.8 copy-start.30
  26.9 1.7 copy-start.34
  32.7 0.7 copy-start.10
  33.4 1.4 copy-start.14
  34.8 5.9 copy-start.5
  34.8 5.9 copy-start.7
  34.8 5.9 copy-start.12
  39.5 1.1 copy-start.26
  40.7 6.2 copy-start.18
  40.7 6.2 copy-start.1
  40.7 6.2 copy-start.16
  46.8 20.8 %copy-start.19 = (s32[1024,1]{1,0:T(8,128)}, s32[1024,1]{1,0:T(8,128)S(1)}, u32[]{:S(2)}) copy-start(s32[1024,1]{1,0:T(8,128)S(1)} %get-tuple-element.72.dest_ref) | copy-start | bytes 12292
  46.9 20.8 %copy-start.3 = (bf16[768,768]{1,0:T(8,128)(2,1)S(1)}, bf16[768,768]{1,0:T(8,128)(2,1)}, u32[]{:S(2)}) copy-start(bf16[768,768]{1,0:T(8,128)(2,1)} %w_ref.1) | copy-start | bytes 3538948
  46.9 20.8 %copy-start.9 = (f32[1,768]{1,0:T(1,128)S(1)}, f32[1,768]{1,0:T(1,128)}, u32[]{:S(2)}) copy-start(f32[1,768]{1,0:T(1,128)} %reshape.212.gain_ref) | copy-start | bytes 9220
  46.9 20.8 %copy-start.15 = (bf16[2,512,768]{2,1,0:T(8,128)(2,1)S(1)}, bf16[2,512,768]{2,1,0:T(8,128)(2,1)}, u32[]{:S(2)}) copy-start(bf16[2,512,768]{2,1,0:T(8,128)(2,1)} %param.19) | copy-start | bytes 4718596
  67.6 8.3 %copy-start.23 = (bf16[1024,768]{1,0:T(8,128)(2,1)}, bf16[1024,768]{1,0:T(8,128)(2,1)S(1)}, u32[]{:S(2)}) copy-start(bf16[1024,768]{1,0:T(8,128)(2,1)S(1)} %get-tuple-element.67.o_ref) | copy-start | bytes 4718596
  154.5 3.8 copy-start.32
  154.5 75.2 %all-to-all-start.1 = ((bf16[32,64,768]{2,1,0:T(8,128)(2,1)}), bf16[32,64,768]{2,1,0:T(8,128)(2,1)}, u32[]{:S(2)}, u32[]{:S(2)}) async-start(bf16[32,64,768]{2,1,0:T(8,128)(2,1)} %bitcast.86), calls=%async_computation.1 | async-start | bytes 6291456 | tf_op jit(solution)/shard_map/all_to_all | solution.py:108
  288.5 75.5 %all-to-all-start.3 = ((bf16[32,64,768]{2,1,0:T(8,128)(2,1)}), bf16[32,64,768]{2,1,0:T(8,128)(2,1)}, u32[]{:S(2)}, u32[]{:S(2)}) async-start(bf16[32,64,768]{2,1,0:T(8,128)(2,1)} %bitcast.88), calls=%async_computation.3 | async-start | bytes 6291456 | tf_op jit(solution)/shard_map/all_to_all | solution.py:108
  364.0 152.7 %all-to-all-start.2 = ((bf16[32,64,768]{2,1,0:T(8,128)(2,1)}), bf16[32,64,768]{2,1,0:T(8,128)(2,1)S(1)}, u32[]{:S(2)}, u32[]{:S(2)}) async-start(bf16[32,64,768]{2,1,0:T(8,128)(2,1)} %bitcast.85), calls=%async_computation.2 | async-start | bytes 6291456 | tf_op jit(solution)/shard_map/all_to_all | solution.py:108
  367.9 266.1 %all-reduce.5.cloned.1.call-start = ((), (), s32[]{:S(2)}) async-start(), calls=%async_computation.4 | async-start | bytes 19660800 | tf_op jit(solution)/shard_map/psum | solution.py:630
  368.0 1.3 copy-start.4
  369.3 1.4 copy-start.13
  370.7 1.0 copy-start.20
  371.7 1.4 copy-start.24
  373.1 15.3 %copy-start.25 = (bf16[1024,768]{1,0:T(8,128)(2,1)S(1)}, bf16[1024,768]{1,0:T(8,128)(2,1)}, u32[]{:S(2)}) copy-start(bf16[1024,768]{1,0:T(8,128)(2,1)} %copy-done.23) | copy-start | bytes 4718596
  385.4 1.4 copy-start.2
  386.8 1.7 copy-start.22
  388.5 25.5 %copy-start.11 = (f32[1,768]{1,0:T(1,128)S(1)}, f32[1,768]{1,0:T(1,128)}, u32[]{:S(2)}) copy-start(f32[1,768]{1,0:T(1,128)} %reshape.210.gain_ref) | copy-start | bytes 9220
  412.5 1.4 copy-start
  470.0 46.7 %copy-start.8 = (bf16[768,128]{1,0:T(8,128)(2,1)S(1)}, bf16[768,128]{1,0:T(8,128)(2,1)}, u32[]{:S(2)}) copy-start(bf16[768,128]{1,0:T(8,128)(2,1)} %get-tuple-element.158.wr_ref) | copy-start | bytes 589828
  516.7 1.0 copy-start.6
  517.7 1.9 copy-start.17
  519.6 1.1 copy-start.21
  634.1 5.2 copy-start.29
  639.2 2.5 copy-start.28
  641.7 2.5 copy-start.27
Sparse Core Ops, SparseCore 0:
  435.5 198.4 all-reduce.4

commit v2 on v1

--- a/solution.py
+++ b/solution.py
@@ -203,8 +203,15 @@
     )(ff, dest_c, expert_ids.reshape(tokens, 1), y, gain, w_router)
 
 
+def pack(values, first, height, out, at):
+    for c in range(values.shape[1] // TILE):
+        out[at + c * height : at + (c + 1) * height] = values[
+            first : first + height, c * TILE : (c + 1) * TILE
+        ].astype(LOW)
+
+
 def before_attention_kernel(
-    dh_ref, dest_ref, y_ref, g_ref, gain_ref, wt_ref, o_ref, dy_ref, do_ref, gw_ref, gg_ref
+    dh_ref, dest_ref, y_ref, g_ref, gain_ref, wt_ref, o_ref, dy_ref, do_ref, pack_ref, gg_ref, gw_ref
 ):
     i = pl.program_id(0)
 
@@ -228,6 +235,10 @@
     do_ref[...] = dot(low, wt_ref[...]).astype(LOW)
     gw_ref[...] += dot(o_ref[...].T, low)
 
+    @pl.when(i == pl.num_programs(0) - 1)
+    def _():
+        pack(gw_ref, 0, gw_ref.shape[0], pack_ref, 0)
+
 
 def before_attention(dh, dest_c, y, g, gain, w_output_t, joined):
     tokens, width = y.shape
@@ -242,15 +253,16 @@
         ],
         out_specs=[
             rows(width), rows(width),
-            pl.BlockSpec((width, width), lambda i: (0, 0)),
+            pl.BlockSpec((width * width // TILE, TILE), lambda i: (0, 0)),
             pl.BlockSpec((1, width), lambda i: (0, 0)),
         ],
         out_shape=[
             jax.ShapeDtypeStruct((tokens, width), jnp.float32),
             jax.ShapeDtypeStruct((tokens, width), LOW),
-            jax.ShapeDtypeStruct((width, width), jnp.float32),
+            jax.ShapeDtypeStruct((width * width // TILE, TILE), LOW),
             jax.ShapeDtypeStruct((1, width), jnp.float32),
         ],
+        scratch_shapes=[pltpu.VMEM((width, width), jnp.float32)],
         compiler_params=params(40),
         cost_estimate=cost(2 * tokens * width * (dh.shape[0] + 2 * width), 16 << 20),
         name="before_attention",
@@ -258,7 +270,8 @@
 
 
 def finish_kernel(
-    dq_ref, dk_ref, dv_ref, wt_ref, normed_ref, x_ref, dy_ref, gain_ref, out_ref, gw_ref, gg_ref
+    dq_ref, dk_ref, dv_ref, wt_ref, normed_ref, x_ref, dy_ref, gain_ref, go_ref, gr_ref, gg2_ref, table_ref,
+    out_ref, pack_ref, gw_ref, gg_ref,
 ):
     i = pl.program_id(0)
 
@@ -285,29 +298,78 @@
         - x * (rms * rms * rms) * jnp.mean(u * x, axis=-1, keepdims=True)
     )
 
-
-def finish(dq, dk, dv, w_qkv_t, normed, x, dy, gain):
+    @pl.when(i == pl.num_programs(0) - 1)
+    def _():
+        block = width * width // TILE
+        for n in range(3):
+            pack(gw_ref, n * width, width, pack_ref, n * block)
+        pack_ref[3 * block : 4 * block] = go_ref[...]
+        at = 4 * block
+        routed = gr_ref.shape[0]
+        pack_ref[at : at + routed] = gr_ref[...].astype(LOW)
+        at = at + routed
+        rows = width // TILE
+        gains = [gg_ref[:, c * TILE : (c + 1) * TILE] for c in range(rows)]
+        gains += [gg2_ref[:, c * TILE : (c + 1) * TILE] for c in range(rows)]
+        gains += [jnp.zeros((16 - 2 * rows % 16, TILE), jnp.float32)] if 2 * rows % 16 else []
+        gains = jnp.concatenate(gains, axis=0)
+        pack_ref[at : at + gains.shape[0]] = gains.astype(LOW)
+        at = at + gains.shape[0]
+        heads, buckets, _ = table_ref.shape
+        lane = lax.broadcasted_iota(jnp.int32, (buckets, TILE), 1)
+        table = jnp.zeros((buckets, TILE), jnp.float32)
+        for h in range(heads):
+            table = jnp.where(lane == h, jnp.sum(table_ref[h], axis=1, keepdims=True), table)
+        pack_ref[at : at + buckets] = table.astype(LOW)
+        at = at + buckets
+        pack_ref[at:] = jnp.zeros((pack_ref.shape[0] - at, TILE), LOW)
+
+
+def finish(dq, dk, dv, w_qkv_t, normed, x, dy, gain, go, gr, gg2, table, rows_packed):
     tokens, width = x.shape
     step = 256
     rows = pl.BlockSpec((step, width), lambda i: (i, 0))
     return pl.pallas_call(
         finish_kernel,
         grid=(tokens // step,),
-        in_specs=[rows, rows, rows, whole((3 * width, width)), rows, rows, rows, whole((1, width))],
-        out_specs=[
-            rows,
-            pl.BlockSpec((3 * width, width), lambda i: (0, 0)),
-            pl.BlockSpec((1, width), lambda i: (0, 0)),
-        ],
+        in_specs=[
+            rows, rows, rows, whole((3 * width, width)), rows, rows, rows, whole((1, width)),
+            whole(go.shape), whole(gr.shape), whole(gg2.shape), whole(table.shape),
+        ],
+        out_specs=[rows, pl.BlockSpec((rows_packed, TILE), lambda i: (0, 0))],
         out_shape=[
             jax.ShapeDtypeStruct((tokens, width), jnp.float32),
-            jax.ShapeDtypeStruct((3 * width, width), jnp.float32),
-            jax.ShapeDtypeStruct((1, width), jnp.float32),
-        ],
-        compiler_params=params(48),
+            jax.ShapeDtypeStruct((rows_packed, TILE), LOW),
+        ],
+        scratch_shapes=[
+            pltpu.VMEM((3 * width, width), jnp.float32),
+            pltpu.VMEM((1, width), jnp.float32),
+        ],
+        compiler_params=params(56),
         cost_estimate=cost(12 * tokens * width * width, 24 << 20),
         name="finish",
-    )(dq, dk, dv, w_qkv_t, normed, x, dy, gain)
+    )(dq, dk, dv, w_qkv_t, normed, x, dy, gain, go, gr, gg2, table)
+
+
+def unpack_kernel(packed_ref, out_ref):
+    height = out_ref.shape[1]
+    for c in range(out_ref.shape[2] // TILE):
+        out_ref[0, :, c * TILE : (c + 1) * TILE] = packed_ref[c * height : (c + 1) * height].astype(
+            jnp.float32
+        )
+
+
+def unpack(packed, width):
+    block = width * width // TILE
+    return pl.pallas_call(
+        unpack_kernel,
+        grid=(4,),
+        in_specs=[pl.BlockSpec((block, TILE), lambda i: (i, 0))],
+        out_specs=pl.BlockSpec((1, width, width), lambda i: (i, 0, 0)),
+        out_shape=jax.ShapeDtypeStruct((4, width, width), jnp.float32),
+        compiler_params=params(32),
+        name="unpack",
+    )(packed)
 
 
 def attention_forward_kernel(len_ref, q_ref, k_ref, v_ref, near_ref, far_ref, o_ref, p_ref, s_ref):
@@ -380,7 +442,7 @@
         name="attention_forward",
     )(lengths, projected, projected, projected, near, far)
 
-def attention_backward_kernel(q_ref, k_ref, v_ref, do_ref, o_ref, p_ref, dq_ref, dk_ref, dv_ref, near_ref, far_ref, d_ref):
+def attention_backward_kernel(q_ref, k_ref, v_ref, do_ref, o_ref, p_ref, dq_ref, dk_ref, dv_ref, table_ref, near_ref, far_ref, d_ref):
     seq = q_ref.shape[0]
     tiles = seq // TILE
     half = q_ref.shape[1] // 2
@@ -427,11 +489,35 @@
         dv_h = lax.dot_general(p_ref[0, h], do, (((1,), (0,)), ((), ())), preferred_element_type=jnp.float32)
         dk_all = dk_h if h == 0 else jnp.where(mine, dk_h, dk_all)
         dv_all = dv_h if h == 0 else jnp.where(mine, dv_h, dv_all)
+    @pl.when(row == pl.num_programs(1) - 1)
+    def _():
+        bucket_sums(near_ref, far_ref, table_ref)
+
     dq_ref[...] = (jnp.concatenate(dq_parts, axis=0).T * 0.125).astype(LOW)
     dk_ref[...] = (dk_all * 0.125).astype(LOW)
     dv_ref[...] = dv_all.astype(LOW)
 
-def attention_backward(projected, do, joined, weights, rows, seq, heads, head):
+def bucket_sums(near_ref, far_ref, table_ref):
+    buckets = table_ref.shape[1]
+    half = buckets // 2
+    key = lax.broadcasted_iota(jnp.int32, (TILE, TILE), 0)
+    query = lax.broadcasted_iota(jnp.int32, (TILE, TILE), 1)
+    tiles = [bucket_of((d - 1) * TILE + key - query) for d in range(3)]
+    for h in range(2):
+        sums = []
+        for n in range(buckets):
+            total = far_ref[h, 0 if n >= half else 1] if n % half == half - 1 else None
+            for d in range(3):
+                if (d == 0 and n >= half) or (d == 2 and n < half):
+                    continue
+                part = jnp.where(tiles[d] == n, near_ref[h, d], 0.0)
+                part = jnp.sum(part.reshape(TILE // 8, 8, TILE), axis=0)
+                total = part if total is None else total + part
+            sums.append(jnp.sum(total, axis=0, keepdims=True))
+        table_ref[h] = jnp.concatenate(sums, axis=0)
+
+
+def attention_backward(buckets, projected, do, joined, weights, rows, seq, heads, head):
     width = heads * head
     pairs = heads // 2
     spec = lambda off: pl.BlockSpec((seq, 2 * head), lambda p, b: (b, off + p))
@@ -444,14 +530,16 @@
         ],
         out_specs=[
             spec(0), spec(0), spec(0),
-            pl.BlockSpec((2, 3, TILE, TILE), lambda p, b: (p, 0, 0, 0)),
-            pl.BlockSpec((2, 2, 8, TILE), lambda p, b: (p, 0, 0, 0)),
+            pl.BlockSpec((2, buckets, TILE), lambda p, b: (p, 0, 0)),
         ],
         out_shape=[jax.ShapeDtypeStruct((rows * seq, width), LOW)] * 3 + [
-            jax.ShapeDtypeStruct((heads, 3, TILE, TILE), jnp.float32),
-            jax.ShapeDtypeStruct((heads, 2, 8, TILE), jnp.float32),
-        ],
-        scratch_shapes=[pltpu.VMEM((seq, seq), LOW)],
+            jax.ShapeDtypeStruct((heads, buckets, TILE), jnp.float32),
+        ],
+        scratch_shapes=[
+            pltpu.VMEM((2, 3, TILE, TILE), jnp.float32),
+            pltpu.VMEM((2, 2, 8, TILE), jnp.float32),
+            pltpu.VMEM((seq, seq), LOW),
+        ],
         compiler_params=params(40),
         cost_estimate=cost(flops=8 * rows * heads * seq * seq * head * 4, bytes_accessed=rows * heads * seq * seq * 2, transcendentals=0),
         name="attention_backward",
@@ -466,7 +554,7 @@
     hot = (b.reshape(1, -1) == jnp.arange(table.shape[0], dtype=jnp.int32)[:, None]).astype(jnp.float32)
     near = jnp.dot(scaled, hot, precision=lax.Precision.HIGHEST).reshape(-1, 3, TILE, TILE)
     far = jnp.stack([scaled[:, -1], scaled[:, table.shape[0] // 2 - 1]], axis=1)
-    return near, far, hot
+    return near, far
 
 
 def expert_kernel(experts, chunk, x_ref, g_ref, mine_ref, wr_ref, wrt_ref, wi_ref, wit_ref, wo_ref, wot_ref,
@@ -577,6 +665,106 @@
     )(*args)
 
 
+def sum_parts(bits, units):
+    upper = list(range(1, bits))
+    turns = min(6, units, 2 * max(1, min(3, len(upper))))
+    sizes = [(units + t) // turns for t in range(turns)]
+    orders = [[0] + upper[t % 3 :] + upper[: t % 3] for t in range(turns)]
+    return sizes, orders
+
+
+def sum_kernel(cores, bits, sizes, orders, x_ref, out_ref, work_ref, got_ref, send, recv):
+    n = 1 << bits
+    me = lax.axis_index("grp") * cores + lax.axis_index("exp")
+    barrier = pltpu.get_barrier_semaphore()
+    def place(d):
+        return dict(device_id=(d // cores, d % cores), device_id_type=pl.DeviceIdType.MESH)
+    def other(b):
+        bit = (me // (1 << b)) % 2
+        return bit, me + (1 - 2 * bit) * (1 << b)
+    for b in range(bits):
+        pl.semaphore_signal(barrier, inc=1, **place(other(b)[1]))
+    pl.semaphore_wait(barrier, bits)
+    parts = len(sizes)
+    starts = [sum(sizes[:p]) * 16 * n for p in range(parts)]
+    base = list(starts)
+    got_at = list(starts)
+    def rows(start, length):
+        return pl.ds(pl.multiple_of(start, 16), length)
+    def halving(p, s):
+        length = sizes[p] * 16 * (n >> (s + 1))
+        bit, partner = other(orders[p][s])
+        source = x_ref if s == 0 else work_ref
+        return pltpu.make_async_remote_copy(
+            src_ref=source.at[rows(base[p] + (1 - bit) * length, length)],
+            dst_ref=got_ref.at[rows(got_at[p], length)],
+            send_sem=send.at[p, s], recv_sem=recv.at[p, s], **place(partner))
+    pending = {}
+    for p in range(parts):
+        pending[p] = halving(p, 0); pending[p].start()
+    sends = []
+    for s in range(bits):
+        for p in range(parts):
+            length = sizes[p] * 16 * (n >> (s + 1))
+            bit, partner = other(orders[p][s])
+            keep = base[p] + bit * length
+            pending[p].wait_recv()
+            sends.append(pending[p])
+            step = sizes[p] * 16
+            source = x_ref if s == 0 else work_ref
+            target = work_ref if s + 1 < bits else out_ref
+            def add(i, _, keep=keep, source=source, target=target, at=got_at[p], step=step):
+                here = rows(keep + i * step, step)
+                arrived = got_ref[rows(at + i * step, step), :].astype(jnp.float32)
+                target[here, :] = (source[here, :].astype(jnp.float32) + arrived).astype(LOW)
+                return 0
+            lax.fori_loop(0, length // step, add, 0)
+            base[p] = keep
+            got_at[p] += length
+            if s + 1 < bits:
+                pending[p] = halving(p, s + 1); pending[p].start()
+    for c in sends:
+        c.wait_send()
+    back = {}
+    def doubling(p, s):
+        length = sizes[p] * 16 * (n >> (s + 1))
+        bit, partner = other(orders[p][s])
+        return pltpu.make_async_remote_copy(
+            src_ref=out_ref.at[rows(base[p], length)], dst_ref=out_ref.at[rows(base[p], length)],
+            send_sem=send.at[p, bits + s], recv_sem=recv.at[p, bits + s], **place(partner))
+    for p in range(parts):
+        back[p] = doubling(p, bits - 1); back[p].start()
+    sends = []
+    for s in reversed(range(bits)):
+        for p in range(parts):
+            length = sizes[p] * 16 * (n >> (s + 1))
+            bit, partner = other(orders[p][s])
+            back[p].wait_recv()
+            sends.append(back[p])
+            base[p] = base[p] - bit * length
+            if s > 0:
+                back[p] = doubling(p, s - 1); back[p].start()
+    for c in sends:
+        c.wait_send()
+
+def all_sum(x, cid=1):
+    cores = lax.axis_size("exp")
+    n = lax.axis_size(AXES)
+    bits = n.bit_length() - 1
+    units = x.shape[0] // (16 * n)
+    sizes, orders = sum_parts(bits, units)
+    parts = len(sizes)
+    return pl.pallas_call(
+        functools.partial(sum_kernel, cores, bits, sizes, orders),
+        out_shape=jax.ShapeDtypeStruct(x.shape, x.dtype),
+        in_specs=[pl.BlockSpec(memory_space=pltpu.VMEM)],
+        out_specs=pl.BlockSpec(memory_space=pltpu.VMEM),
+        scratch_shapes=[pltpu.VMEM(x.shape, x.dtype), pltpu.VMEM(x.shape, x.dtype), pltpu.SemaphoreType.DMA((parts, 2 * bits)), pltpu.SemaphoreType.DMA((parts, 2 * bits))],
+        compiler_params=params(40, collective_id=cid, has_side_effects=True),
+        name="all_sum",
+    )(x)
+
+
 def local(
     tokens, lengths, expert_ids, slots, w_query, w_key, w_value, w_output,
     gain_attn, gain_ffn, bias_table, w_router, w_in, w_out, cotangent,
@@ -594,51 +782,62 @@
     gain_one = gain_attn.reshape(1, width)
     gain_two = gain_ffn.reshape(1, width)
     wide = max(128, experts)
-    router_w = jnp.pad(w_router, ((0, 0), (0, wide - experts)))
     mine = (jnp.arange(wide, dtype=jnp.int32) == me).astype(jnp.float32).reshape(1, wide)
 
     dest_c, dest_r, g_out = route(expert_ids, slots, g, experts, room)
     g_in = exchange(g_out, devices)
+    dest_r, x, w_query, w_key, w_value, w_output, bias_table, w_router = lax.optimization_barrier(
+        (dest_r, x, w_query, w_key, w_value, w_output, bias_table, w_router)
+    )
+    router_w = jnp.pad(w_router, ((0, 0), (0, wide - experts)))
 
     w_qkv = jnp.concatenate([w_query, w_key, w_value], axis=1)
     normed, projected = project(x, gain_one, w_qkv)
-    near, far, hot = bias_tiles(bias_table)
+    near, far = bias_tiles(bias_table)
     joined, weights = attention_forward(lengths, projected, near, far, rows, seq, heads, head)
     y, h_out = after_attention(joined, x, w_output, gain_two, dest_r, experts * room)
+    h_out, g_in = lax.optimization_barrier((h_out, g_in))
     h_in = exchange(h_out, devices)
+    w_in, w_out, h_out = lax.optimization_barrier((w_in, w_out, h_out))
 
     ff, dx, hid, da, x_t, dff_t, grad_router = expert_rows(
         h_in, g_in, mine, router_w, router_w.T, w_in[0], w_in[0].T, w_out[0], w_out[0].T, experts
     )
     dh_back = exchange(dx, devices)
+    grad_in, grad_out = expert_weights([(x_t, dff_t, hid, da)])
+    dh_back, grad_in, grad_out, ff = lax.optimization_barrier((dh_back, grad_in, grad_out, ff))
     ff_back = exchange(ff, devices)
-    grad_in, grad_out = expert_weights([(x_t, dff_t, hid, da)])
+    grad_router = grad_router[:, :experts].reshape(width * experts // TILE, TILE)
 
     dy, do, grad_output, grad_gain_two = before_attention(
         dh_back, dest_c, y, g, gain_two, w_output.T, joined
     )
-    dq, dk, dv, near_sum, far_sum = attention_backward(
-        projected, do, joined, weights, rows, seq, heads, head
-    )
-    grad_tokens, grad_qkv, grad_gain_one = finish(
-        dq, dk, dv, w_qkv.T, normed, x, dy, gain_one
-    )
-    table = jnp.dot(hot, near_sum.reshape(heads, -1).T, precision=lax.Precision.HIGHEST)
-    far_total = jnp.sum(far_sum, axis=(2, 3))
-    table = table.at[buckets - 1].add(far_total[:, 0]).at[buckets // 2 - 1].add(far_total[:, 1])
+    dq, dk, dv, table = attention_backward(
+        buckets, projected, do, joined, weights, rows, seq, heads, head
+    )
+    small = grad_router.shape[0] + -(-2 * width // TILE // 16) * 16 + buckets
+    block = width * width // TILE
+    rows_packed = -(-(4 * block + small) // (16 * devices)) * 16 * devices
+    grad_tokens, packed = finish(
+        dq, dk, dv, w_qkv.T, normed, x, dy, gain_one, grad_output, grad_router, grad_gain_two, table, rows_packed
+    )
+    summed = all_sum(packed)
+    summed, ff_back = lax.optimization_barrier((summed, ff_back))
     mixed = mix(ff_back, dest_c, expert_ids, y, gain_two, router_w, experts)
-    summed = lax.psum(
-        (
-            grad_qkv[:width], grad_qkv[width : 2 * width], grad_qkv[2 * width :], grad_output,
-            grad_gain_one.reshape(width), grad_gain_two.reshape(width), table,
-            grad_router[:, :experts],
-        ),
-        AXES,
-    )
+    grads = unpack(summed, width)
+    at = 4 * block
+    rest = summed[at : at + small].astype(jnp.float32)
+    routed = grad_router.shape[0]
+    grad_router = rest[:routed].reshape(width, experts)
+    lines = width // TILE
+    grad_gain_one = rest[routed : routed + lines].reshape(width)
+    grad_gain_two = rest[routed + lines : routed + 2 * lines].reshape(width)
+    grad_table = rest[small - buckets :, :heads]
     return (
         mixed.reshape(rows, seq, width),
         grad_tokens.reshape(rows, seq, width),
-        *summed,
+        grads[0], grads[1], grads[2], grads[3],
+        grad_gain_one, grad_gain_two, grad_table, grad_router,
         grad_in,
         grad_out,
     )

time: 663 us -> 471 us (0.71); the launches traced: 653 us -> 469 us
  blocking collectives: 119 us -> 0 us
  waiting for transfers between devices: 234 us -> 117 us
  Pallas kernels: 185 us -> 254 us
  between operations: 14.8 us -> 1.04 us
  starting transfers between devices: 11.8 us -> 19.7 us
    psum x1 -> x0, waiting for transfers between devices: 108 us -> none  [local(): lax.psum((grad_qkv[:width], grad_qkv[width:2 * width], grad_qkv[2 * width...]
    all_to_all x1 -> x0, blocking collectives: 78.6 us -> none  [exchange(): lax.all_to_all(shaped, AXES, split_axis=0, concat_axis=0, tiled=True)]
    pallas_call x0 -> x2, Pallas kernels: none -> 63.2 us  [the longest x1 62.5 us: all_sum(): pl.pallas_call(functools.partial(sum_kernel, cores, bits, sizes, orders),...]
    psum x1 -> x0, blocking collectives: 40.8 us -> none  [local(): lax.psum((grad_qkv[:width], grad_qkv[width:2 * width], grad_qkv[2 * width...]
    unnamed x91 -> x92, local copies, waits for them, and re-layouts: 59 us -> 37.2 us
    optimization_barrier x0 -> x8, local copies, waits for them, and re-layouts: none -> 19.3 us  [the longest x2 13.2 us: local(): w_in, w_out, h_out = lax.optimization_barrier((w_in, w_out, h_out))]
    all_to_all x3 -> x4, waiting for transfers between devices: 126 us -> 117 us  [exchange(): lax.all_to_all(shaped, AXES, split_axis=0, concat_axis=0, tiled=True)]
    all_to_all x3 -> x4, starting transfers between devices: 11.8 us -> 19.7 us  [exchange(): lax.all_to_all(shaped, AXES, split_axis=0, concat_axis=0, tiled=True)]
  transfers between devices with their start and end apart: 4 -> 4, of which waited for: 3 -> 3; matrix products, arithmetic and copies ran while one was open for 5% -> 7% of each run, Pallas kernels for 13% -> 39%
where the time goes in v2:
time: 471 us; the launch traced here: 469 us
  Pallas kernels  254 us (54%)
  waiting for transfers between devices  117 us (25%)
  local copies, waits for them, and re-layouts  68.7 us (15%)
  starting transfers between devices  19.7 us (4%)
  other arithmetic  4.97 us (1%)
    all_to_all x4, waiting for transfers between devices, exchange(): lax.all_to_all(shaped, AXES, split_axis=0, concat_axis=0, tiled=True)  117 us
    pallas_call x1, Pallas kernels, all_sum(): pl.pallas_call(functools.partial(sum_kernel, cores, bits, sizes, orders),...  62.5 us
    pallas_call x1, Pallas kernels, expert_rows(): pl.pallas_call(functools.partial(expert_kernel, experts, chunk), grid=(n...  58.7 us
    unnamed x92, local copies, waits for them, and re-layouts  37.2 us
    pallas_call x1, Pallas kernels, attention_backward(): pl.pallas_call(attention_backward_kernel, grid=(pairs, rows), in_specs=[s...  31.9 us
    pallas_call x1, Pallas kernels, expert_weights(): pl.pallas_call(functools.partial(expert_weights_kernel, len(parts)), grid...  28.1 us
    pallas_call x1, Pallas kernels, attention_forward(): pl.pallas_call(attention_forward_kernel, grid=(rows, pairs), in_specs=[pl...  20.6 us
    all_to_all x4, starting transfers between devices, exchange(): lax.all_to_all(shaped, AXES, split_axis=0, concat_axis=0, tiled=True)  19.7 us
  transfers between devices with their start and end apart: 4, of which 3 were waited for; matrix products, arithmetic and copies ran while one was open for 7% of the time, Pallas kernels for 39%

profile of v2, /device:TPU:0, one launch (start us, length us, event | category | flops | bytes accessed | tf_op | source)
XLA Modules:
  0.0 468.8 jit_solution(18050722260432873953)
XLA Ops:
  0.6 0.7 copy.76
  1.6 0.7 copy.79
  2.5 1.4 copy-done.11
  3.9 6.1 %route.1 = (s32[1024,1]{1,0:T(8,128)S(1)}, s32[1,1024]{1,0:T(1,128)S(1)}, bf16[2048,768]{1,0:T(8,128)(2,1)}) custom-call(s32[1024,1]{1,0:T(8,128)S(1)} %bitcast.64, s32[1,1024]{1,0:T(1,128)S(1)} %bitcast.68, s32[1024,1]{1,0:T(8,128)S(1)} %bitcast.66, s32[1,1024]{1,0:T(1,128)S(1)} %bitcast.70, bf16[1024,768]{1,0:T(8,128)(2,1)S(1)} %bitcast.71), custom_call_target="tpu_custom_call" | custom-call | flops 3221225472 | bytes 8388608 | tf_op jit(solution)/shard_map/route/pallas_call | solution.py:87
  10.1 0.8 copy-done.18
  10.9 0.6 copy-done.31
  11.5 7.6 %all-to-all-start = ((bf16[32,64,768]{2,1,0:T(8,128)(2,1)}), bf16[32,64,768]{2,1,0:T(8,128)(2,1)}, u32[]{:S(2)}, u32[]{:S(2)}) async-start(bf16[32,64,768]{2,1,0:T(8,128)(2,1)} %bitcast.83), calls=%async_computation | async-start | bytes 6291456 | tf_op jit(solution)/shard_map/all_to_all | solution.py:108
  19.1 0.6 copy.58
  19.7 0.6 copy.59
  20.4 1.6 copy.60
  22.0 3.4 fusion.9
  25.4 4.3 copy.61.w_ref
  29.8 0.7 copy.62
  30.5 0.7 multiply_bitcast_fusion
  31.6 2.8 fusion
  34.4 0.6 copy.82
  35.7 0.7 copy-done.13
  36.4 4.7 %project.1 = (bf16[1024,768]{1,0:T(8,128)(2,1)S(1)}, bf16[1024,2304]{1,0:T(8,128)(2,1)S(1)}) custom-call(bf16[1024,768]{1,0:T(8,128)(2,1)S(1)} %bitcast.74, f32[1,768]{1,0:T(1,128)S(1)} %reshape.167.gain_ref, bf16[768,2304]{1,0:T(8,128)(2,1)S(1)} %copy.61.w_ref), custom_call_target="tpu_custom_call" | custom-call | flops 3623878656 | bytes 12582912 | tf_op jit(solution)/shard_map/project/pallas_call | solution.py:125
  41.2 1.1 copy-done.25
  42.3 20.6 %attention_forward.1 = (bf16[1024,768]{1,0:T(8,128)(2,1)S(1)}, bf16[2,12,512,512]{3,2,1,0:T(8,128)(2,1)}) custom-call(s32[2]{0:T(128)S(1)} %copy-done.14, bf16[1024,2304]{1,0:T(8,128)(2,1)S(1)} %get-tuple-element.63.q_ref.k_ref.v_ref, bf16[1024,2304]{1,0:T(8,128)(2,1)S(1)} %get-tuple-element.63.q_ref.k_ref.v_ref, ...), custom_call_target="tpu_custom_call" | custom-call | flops 6442450944 | bytes 12582912 | tf_op jit(solution)/shard_map/attention_forward/pallas_call | solution.py:422
  63.0 8.0 %after_attention.1 = (f32[1024,768]{1,0:T(8,128)}, bf16[2048,768]{1,0:T(8,128)(2,1)}) custom-call(bf16[1024,768]{1,0:T(8,128)(2,1)S(1)} %get-tuple-element.65.o_ref, bf16[1024,768]{1,0:T(8,128)(2,1)S(1)} %bitcast.75, bf16[768,768]{1,0:T(8,128)(2,1)S(1)} %copy-done.5, f32[1,768]{1,0:T(1,128)S(1)} %reshape.169.gain_ref, s32[1,1024]{1,0:T(1,128)S(1)} %copy-done.32), custom_call_target="tpu_custom_call" | custom-call | flops 4429185024 | bytes 12582912 | tf_op jit(solution)/shard_map/after_attention/pallas_call | solution.py:157
  71.0 1.1 copy-done.22
  72.2 18.2 %all-to-all-done = bf16[32,64,768]{2,1,0:T(8,128)(2,1)} async-done(((bf16[32,64,768]{2,1,0:T(8,128)(2,1)}), bf16[32,64,768]{2,1,0:T(8,128)(2,1)}, u32[]{:S(2)}, u32[]{:S(2)}) %all-to-all-start) | async-done | bytes 3145760 | tf_op jit(solution)/shard_map/all_to_all | solution.py:108
  90.4 4.1 all-to-all-start.1
  94.7 0.8 pad_bitcast_fusion
  95.5 0.8 copy.67.wrt_ref
  96.3 0.5 compare_convert_fusion.mine_ref
  96.8 6.6 %copy.65 = bf16[1,768,3072]{1,2,0:T(8,128)(2,1)} copy(bf16[1,768,3072]{2,1,0:T(8,128)(2,1)} %param.27) | data formatting | bytes 9437184 | tf_op jit(solution)/shard_map/optimization_barrier | solution.py:801
  103.4 6.6 %copy.66 = bf16[1,3072,768]{1,2,0:T(8,128)(2,1)} copy(bf16[1,3072,768]{2,1,0:T(8,128)(2,1)} %param.28) | data formatting | bytes 9437184 | tf_op jit(solution)/shard_map/optimization_barrier | solution.py:801
  110.0 55.8 %all-to-all-done.1 = bf16[32,64,768]{2,1,0:T(8,128)(2,1)S(1)} async-done(((bf16[32,64,768]{2,1,0:T(8,128)(2,1)}), bf16[32,64,768]{2,1,0:T(8,128)(2,1)S(1)}, u32[]{:S(2)}, u32[]{:S(2)}) %all-to-all-start.1) | async-done | bytes 3145760 | tf_op jit(solution)/shard_map/all_to_all | solution.py:108
  165.8 1.7 copy-done.34
  167.5 58.7 %expert_rows.1 = (bf16[2048,768]{1,0:T(8,128)(2,1)}, bf16[2048,768]{1,0:T(8,128)(2,1)}, bf16[2048,3072]{1,0:T(8,128)(2,1)}, bf16[2048,3072]{1,0:T(8,128)(2,1)}, ...) custom-call(bf16[2048,768]{1,0:T(8,128)(2,1)} %bitcast.84, ...), custom_call_target="tpu_custom_call" | custom-call | flops 38654705664 | bytes 44040192 | tf_op jit(solution)/shard_map/expert_rows/pallas_call | solution.py:619
  226.2 3.9 all-to-all-start.2
  230.1 28.1 %expert_weights.1 = (f32[1,768,3072]{2,1,0:T(8,128)}, f32[1,3072,768]{2,1,0:T(8,128)}) custom-call(bf16[768,2048]{1,0:T(8,128)(2,1)} %get-tuple-element.76.refs_0_, bf16[768,2048]{1,0:T(8,128)(2,1)} %get-tuple-element.77.refs_1_, bf16[2048,3072]{1,0:T(8,128)(2,1)} %get-tuple-element.78.refs_2_, bf16[2048,3072]{1,0:T(8,128)(2,1)} %get-tuple-element.79.refs_3_), custom_call_target="tpu_custom_call" | custom-call | flops 19327352832 | bytes 44040192 | tf_op jit(solution)/shard_map/expert_weights/pallas_call | solution.py:656
  258.2 43.4 %all-to-all-done.2 = bf16[32,64,768]{2,1,0:T(8,128)(2,1)S(1)} async-done(((bf16[32,64,768]{2,1,0:T(8,128)(2,1)}), bf16[32,64,768]{2,1,0:T(8,128)(2,1)S(1)}, u32[]{:S(2)}, u32[]{:S(2)}) %all-to-all-start.2) | async-done | bytes 3145760 | tf_op jit(solution)/shard_map/all_to_all | solution.py:108
  301.6 1.7 copy-done.3
  303.2 4.2 all-to-all-start.3
  307.4 2.4 copy.70
  309.8 0.8 reshape.176.gr_ref
  310.6 1.9 copy-done.4
  312.5 1.3 copy-done.6
  313.8 1.4 copy-done.12
  315.2 1.0 copy-done.19
  316.2 1.4 copy-done.23
  317.6 11.2 %before_attention.1 = (f32[1024,768]{1,0:T(8,128)S(1)}, bf16[1024,768]{1,0:T(8,128)(2,1)S(1)}, bf16[4608,128]{1,0:T(8,128)(2,1)S(1)}, f32[1,768]{1,0:T(1,128)S(1)}) custom-call(bf16[2048,768]{1,0:T(8,128)(2,1)S(1)} %bitcast.61, s32[1024,1]{1,0:T(8,128)S(1)} %copy-done.19, f32[1024,768]{1,0:T(8,128)} %get-tuple-element.85.y_ref, ...), custom_call_target="tpu_custom_call" | custom-call | flops 5637144576 | bytes 16777216 | tf_op jit(solution)/shard_map/before_attention/pallas_call | solution.py:247
  328.8 1.6 copy-done.21
  330.5 1.0 copy-done.29
  331.5 2.3 copy-done.17
  333.8 31.9 %attention_backward.1 = (bf16[1024,768]{1,0:T(8,128)(2,1)S(1)}, bf16[1024,768]{1,0:T(8,128)(2,1)S(1)}, bf16[1024,768]{1,0:T(8,128)(2,1)S(1)}, f32[12,32,128]{2,1,0:T(8,128)S(1)}) custom-call(bf16[1024,2304]{1,0:T(8,128)(2,1)S(1)} %copy-done.17, bf16[1024,2304]{1,0:T(8,128)(2,1)S(1)} %copy-done.17, bf16[1024,2304]{1,0:T(8,128)(2,1)S(1)} %copy-done.17, ...), custom_call_target="tpu_custom_call" | custom-call | flops 12884901888 | bytes 12582912 | tf_op jit(solution)/shard_map/attention_backward/pallas_call | solution.py:524
  365.8 1.1 copy-done.26
  366.9 1.1 copy-done.27
  368.1 1.1 copy-done.28
  369.2 0.7 copy-done.30
  369.9 15.9 %finish.1 = (f32[1024,768]{1,0:T(8,128)}, bf16[18944,128]{1,0:T(8,128)(2,1)}) custom-call(bf16[1024,768]{1,0:T(8,128)(2,1)} %copy-done.26, bf16[1024,768]{1,0:T(8,128)(2,1)} %copy-done.27, bf16[1024,768]{1,0:T(8,128)(2,1)} %copy-done.28, bf16[2304,768]{1,0:T(8,128)(2,1)} %get-tuple-element.144.wt_ref, bf16[1024,768]{1,0:T(8,128)(2,1)} %copy-done.25, ...), custom_call_target="tpu_custom_call" | custom-call | flops 7247757312 | bytes 25165824 | tf_op jit(solution)/shard_map/finish/pallas_call | solution.py:332
  385.8 2.4 copy-done.2
  388.2 62.5 %all_sum.1.packed_ref = bf16[18944,128]{1,0:T(8,128)(2,1)S(1)} custom-call(bf16[18944,128]{1,0:T(8,128)(2,1)S(1)} %copy-done.2), custom_call_target="tpu_custom_call" | custom-call | tf_op jit(solution)/shard_map/all_sum/pallas_call | solution.py:757
  450.7 2.2 copy-done
  452.9 2.4 copy-done.1
  455.3 0.7 unpack.1
  456.0 0.6 slice_bitcast_fusion.4
  456.6 4.5 slice_bitcast_fusion
  461.6 5.6 %mix.1 = bf16[1024,768]{1,0:T(8,128)(2,1)} custom-call(bf16[2048,768]{1,0:T(8,128)(2,1)S(1)} %bitcast.60, s32[1024,1]{1,0:T(8,128)S(1)} %copy-done.20, s32[1024,1]{1,0:T(8,128)S(1)} %bitcast.65, f32[1024,768]{1,0:T(8,128)S(1)} %copy-done.15, f32[1,768]{1,0:T(1,128)S(1)} %reshape.169.gain_ref, bf16[768,128]{1,0:T(8,128)(2,1)S(1)} %copy-done.9), custom_call_target="tpu_custom_call" | custom-call | flops 3221225472 | bytes 8388608 | tf_op jit(solution)/shard_map/mix/pallas_call | solution.py:194
  467.3 0.8 copy.73
  468.1 0.7 copy.72
  (78 shorter events, 2.4 us)
Async XLA Ops:
  1.6 8.5 %copy-start.7 = (s32[1,1024]{0,1:T(8,128)}, s32[1,1024]{0,1:T(8,128)S(1)}, u32[]{:S(2)}) copy-start(s32[1,1024]{0,1:T(8,128)S(1)} %copy.77) | copy-start | bytes 12292
  2.5 1.4 copy-start.11
  10.1 0.8 copy-start.18
  10.9 0.6 copy-start.31
  11.5 7.6 %copy-start.35 = (bf16[768,768]{1,0:T(8,128)(2,1)S(1)}, bf16[768,768]{1,0:T(8,128)(2,1)}, u32[]{:S(2)}) copy-start(bf16[768,768]{1,0:T(8,128)(2,1)} %param.19) | copy-start | bytes 3538948
  11.5 8.3 %copy-start.36 = (bf16[768,768]{1,0:T(8,128)(2,1)S(1)}, bf16[768,768]{1,0:T(8,128)(2,1)}, u32[]{:S(2)}) copy-start(bf16[768,768]{1,0:T(8,128)(2,1)} %param.20) | copy-start | bytes 3538948
  11.5 78.9 %all-to-all-start = ((bf16[32,64,768]{2,1,0:T(8,128)(2,1)}), bf16[32,64,768]{2,1,0:T(8,128)(2,1)}, u32[]{:S(2)}, u32[]{:S(2)}) async-start(bf16[32,64,768]{2,1,0:T(8,128)(2,1)} %bitcast.83), calls=%async_computation | async-start | bytes 6291456 | tf_op jit(solution)/shard_map/all_to_all | solution.py:108
  25.4 4.4 copy-start.40
  25.4 4.4 copy-start.39
  29.8 5.9 %copy-start.10 = (f32[1,768]{1,0:T(1,128)}, f32[1,768]{1,0:T(1,128)S(1)}, u32[]{:S(2)}) copy-start(f32[1,768]{1,0:T(1,128)S(1)} %reshape.167.gain_ref) | copy-start | bytes 9220
  35.0 0.7 copy-start.41
  35.0 1.4 copy-start.13
  36.4 5.9 %copy-start.14 = (s32[2]{0:T(128)S(1)}, s32[2]{0:T(128)}, u32[]{:S(2)}) copy-start(s32[2]{0:T(128)} %len_ref.1) | copy-start | bytes 28
  41.2 1.1 copy-start.25
  42.3 20.7 %copy-start.16 = (bf16[1024,2304]{1,0:T(8,128)(2,1)}, bf16[1024,2304]{1,0:T(8,128)(2,1)S(1)}, u32[]{:S(2)}) copy-start(bf16[1024,2304]{1,0:T(8,128)(2,1)S(1)} %get-tuple-element.63.q_ref.k_ref.v_ref) | copy-start | bytes 14155780
  42.3 20.7 %copy-start.5 = (bf16[768,768]{1,0:T(8,128)(2,1)S(1)}, bf16[768,768]{1,0:T(8,128)(2,1)}, u32[]{:S(2)}) copy-start(bf16[768,768]{1,0:T(8,128)(2,1)} %w_ref) | copy-start | bytes 3538948
  42.3 20.7 %copy-start.32 = (s32[1,1024]{1,0:T(1,128)S(1)}, s32[1,1024]{1,0:T(1,128)}, u32[]{:S(2)}) copy-start(s32[1,1024]{1,0:T(1,128)} %copy-done.31) | copy-start | bytes 12292
  71.0 1.1 copy-start.22
  90.4 4.1 copy-start.38
  90.4 75.4 %all-to-all-start.1 = ((bf16[32,64,768]{2,1,0:T(8,128)(2,1)}), bf16[32,64,768]{2,1,0:T(8,128)(2,1)S(1)}, u32[]{:S(2)}, u32[]{:S(2)}) async-start(bf16[32,64,768]{2,1,0:T(8,128)(2,1)} %bitcast.85), calls=%async_computation.1 | async-start | bytes 6291456 | tf_op jit(solution)/shard_map/all_to_all | solution.py:108
  165.8 1.7 copy-start.34
  226.2 75.3 %all-to-all-start.2 = ((bf16[32,64,768]{2,1,0:T(8,128)(2,1)}), bf16[32,64,768]{2,1,0:T(8,128)(2,1)S(1)}, u32[]{:S(2)}, u32[]{:S(2)}) async-start(bf16[32,64,768]{2,1,0:T(8,128)(2,1)} %bitcast.86), calls=%async_computation.2 | async-start | bytes 6291456 | tf_op jit(solution)/shard_map/all_to_all | solution.py:108
  301.6 1.7 copy-start.3
  303.2 6.6 %copy-start.37 = (f32[768,128]{1,0:T(8,128)S(1)}, f32[768,128]{1,0:T(8,128)}, u32[]{:S(2)}) copy-start(f32[768,128]{1,0:T(8,128)} %get-tuple-element.94) | copy-start | bytes 1179652
  303.2 149.7 %all-to-all-start.3 = ((bf16[32,64,768]{2,1,0:T(8,128)(2,1)}), bf16[32,64,768]{2,1,0:T(8,128)(2,1)S(1)}, u32[]{:S(2)}, u32[]{:S(2)}) async-start(bf16[32,64,768]{2,1,0:T(8,128)(2,1)} %bitcast.82), calls=%async_computation.3 | async-start | bytes 6291456 | tf_op jit(solution)/shard_map/all_to_all | solution.py:108
  310.6 1.9 copy-start.4
  312.5 1.3 copy-start.6
  313.8 1.4 copy-start.12
  315.2 1.0 copy-start.19
  316.2 1.4 copy-start.23
  317.6 13.9 %copy-start.24 = (bf16[1024,768]{1,0:T(8,128)(2,1)S(1)}, bf16[1024,768]{1,0:T(8,128)(2,1)}, u32[]{:S(2)}) copy-start(bf16[1024,768]{1,0:T(8,128)(2,1)} %copy-done.22) | copy-start | bytes 4718596
  328.8 1.6 copy-start.21
  330.5 1.0 copy-start.29
  331.5 34.3 %copy-start.33 = (f32[1,768]{1,0:T(1,128)}, f32[1,768]{1,0:T(1,128)S(1)}, u32[]{:S(2)}) copy-start(f32[1,768]{1,0:T(1,128)S(1)} %get-tuple-element.95.gg2_ref) | copy-start | bytes 9220
  331.5 2.3 copy-start.17
  365.8 1.1 copy-start.26
  366.9 1.1 copy-start.27
  368.1 1.1 copy-start.28
  369.2 0.7 copy-start.30
  385.8 2.4 copy-start.2
  450.7 2.2 copy-start
  452.9 2.4 copy-start.1
  456.6 4.6 copy-start.8
  456.6 4.6 copy-start.9
  456.6 4.6 copy-start.15
  456.6 5.0 %copy-start.20 = (s32[1024,1]{1,0:T(8,128)S(1)}, s32[1024,1]{1,0:T(8,128)}, u32[]{:S(2)}) copy-start(s32[1024,1]{1,0:T(8,128)} %copy-done.18) | copy-start | bytes 12292

commit v3 on v2

--- a/solution.py
+++ b/solution.py
@@ -48,58 +48,115 @@
     return jnp.where(distance < 8, distance, far) + jnp.where(offset > 0, 16, 0).astype(jnp.int32)
 
 
-def route_kernel(experts, room, eid_c, eid_r, slot_c, slot_r, g_ref, dest_c, dest_r, g_out):
-    tokens = g_ref.shape[0]
-    wide = max(128, experts)
-    at = lax.broadcasted_iota(jnp.int32, (tokens, tokens), 0)
-    to = lax.broadcasted_iota(jnp.int32, (tokens, tokens), 1)
-    ids = eid_c[...]
-    picked = ids == lax.broadcasted_iota(jnp.int32, (tokens, wide), 1)
-    earlier = dot((to < at).astype(LOW), picked.astype(LOW))
-    place = jnp.sum(jnp.where(picked, earlier, 0.0), axis=1, keepdims=True).astype(jnp.int32)
-    dest_c[...] = jnp.where(slot_c[...] >= 0, ids * room + place, -1)
-    ids = eid_r[...]
-    picked = ids == lax.broadcasted_iota(jnp.int32, (wide, tokens), 0)
-    earlier = dot(picked.astype(LOW), (at < to).astype(LOW))
-    place = jnp.sum(jnp.where(picked, earlier, 0.0), axis=0, keepdims=True).astype(jnp.int32)
-    dest = jnp.where(slot_r[...] >= 0, ids * room + place, -1)
-    dest_r[...] = dest
-    spread(dest, g_ref[...], g_out)
+def plan(room):
+    if room % 64:
+        return ((0, room),), 0
+    return ((0, room // 2), (room // 2, room)), 0
+
+
+def segment(code, room, low, high):
+    expert = lax.div(code, room)
+    place = code - expert * room
+    inside = (code >= 0) & (place >= low) & (place < high)
+    return jnp.where(inside, expert * (high - low) + place - low, -1)
 
 
 def spread(dest, values, out):
     rows = out.shape[0]
-    step = 256
+    step = min(256, rows)
     for start in range(0, rows, step):
         here = lax.broadcasted_iota(jnp.int32, (step, dest.shape[1]), 0) + start
         out[start : start + step] = dot((dest == here).astype(LOW), values).astype(LOW)
 
 
 def collect(dest, values):
-    rows = values.shape[0]
-    here = lax.broadcasted_iota(jnp.int32, (dest.shape[0], rows), 1)
+    here = lax.broadcasted_iota(jnp.int32, (dest.shape[0], values.shape[0]), 1)
     return dot((dest == here).astype(LOW), values)
+
+
+def spread_all(code, rank, room, values, outs):
+    segments, extra = plan(room)
+    for (low, high), out in zip(segments, outs):
+        spread(segment(code, room, low, high), values, out)
+    if extra:
+        spread(rank, values, outs[-1])
+
+
+def collect_all(code, rank, room, refs):
+    segments, extra = plan(room)
+    if len(refs) == 1:
+        return collect(code, refs[0][...])
+    total = None
+    for (low, high), ref in zip(segments, refs):
+        part = collect(segment(code, room, low, high), ref[...])
+        total = part if total is None else total + part
+    if extra:
+        total = total + collect(rank, refs[len(segments)][...])
+        total = total + refs[len(segments) + 1][...].astype(jnp.float32)
+    return total
+
+
+def buffers(experts, room, width):
+    segments, extra = plan(room)
+    shapes = [jax.ShapeDtypeStruct((experts * (high - low), width), LOW) for low, high in segments]
+    return shapes + ([jax.ShapeDtypeStruct((extra, width), LOW)] if extra else [])
+
+
+def route_kernel(
+    experts, room, eid_c, eid_r, slot_c, slot_r, g_ref, code_c, code_r, rank_c, rank_r, tags, *outs
+):
+    tokens = g_ref.shape[0]
+    wide = max(TILE, experts)
+    segments, extra = plan(room)
+    cut = segments[-1][1]
+    at = lax.broadcasted_iota(jnp.int32, (tokens, tokens), 0)
+    to = lax.broadcasted_iota(jnp.int32, (tokens, tokens), 1)
+    before = (to < at).astype(LOW)
+    after = (at < to).astype(LOW)
+
+    ids = eid_c[...]
+    picked = ids == lax.broadcasted_iota(jnp.int32, (tokens, wide), 1)
+    place = jnp.sum(jnp.where(picked, dot(before, picked.astype(LOW)), 0.0), axis=1, keepdims=True)
+    place = place.astype(jnp.int32)
+    kept = slot_c[...] >= 0
+    code_c[...] = jnp.where(kept, ids * room + place, -1)
+    over = jnp.broadcast_to(jnp.where(kept & (place >= cut), 1.0, 0.0), (tokens, TILE))
+    rank = jnp.where(over > 0, dot(before, over.astype(LOW)).astype(jnp.int32), -1)
+    rank_c[...] = rank[:, :1]
+    lane = lax.broadcasted_iota(jnp.int32, (tokens, TILE), 1)
+    marks = jnp.where((rank == lane) & (lane < extra), ids + 1, 0)
+    marks = marks + jnp.where((lane == TILE - 1) & (rank >= extra), 1, 0)
+    tags[...] = jnp.sum(marks, axis=0, keepdims=True)
+
+    ids = eid_r[...]
+    picked = ids == lax.broadcasted_iota(jnp.int32, (wide, tokens), 0)
+    place = jnp.sum(jnp.where(picked, dot(picked.astype(LOW), after), 0.0), axis=0, keepdims=True)
+    place = place.astype(jnp.int32)
+    kept = slot_r[...] >= 0
+    code = jnp.where(kept, ids * room + place, -1)
+    code_r[...] = code
+    over = jnp.broadcast_to(jnp.where(kept & (place >= cut), 1.0, 0.0), (16, tokens))
+    rank = jnp.where(over > 0, dot(over.astype(LOW), after).astype(jnp.int32), -1)[:1]
+    rank_r[...] = rank
+    spread(code, g_ref[...], outs[0])
 
 
 def route(expert_ids, slots, upstream, experts, room):
     tokens, width = upstream.shape
-    flat = lambda a, shape: a.reshape(shape)
+    column = jax.ShapeDtypeStruct((tokens, 1), jnp.int32)
+    line = jax.ShapeDtypeStruct((1, tokens), jnp.int32)
     return pl.pallas_call(
         functools.partial(route_kernel, experts, room),
         out_shape=[
-            jax.ShapeDtypeStruct((tokens, 1), jnp.int32),
-            jax.ShapeDtypeStruct((1, tokens), jnp.int32),
+            column, line, column, line, jax.ShapeDtypeStruct((1, TILE), jnp.int32),
             jax.ShapeDtypeStruct((experts * room, width), LOW),
         ],
         compiler_params=params(48),
         cost_estimate=cost(2 * experts * room * tokens * width, 8 << 20),
         name="route",
     )(
-        flat(expert_ids, (tokens, 1)),
-        flat(expert_ids, (1, tokens)),
-        flat(slots, (tokens, 1)),
-        flat(slots, (1, tokens)),
-        upstream,
+        expert_ids.reshape(tokens, 1), expert_ids.reshape(1, tokens),
+        slots.reshape(tokens, 1), slots.reshape(1, tokens), upstream,
     )
 
 
@@ -109,23 +166,25 @@
     return moved.reshape(buffer.shape)
 
 
-def project_kernel(x_ref, gain_ref, w_ref, normed_ref, out_ref):
+def project_kernel(x_ref, gain_ref, wq_ref, wk_ref, wv_ref, normed_ref, out_ref):
     x = x_ref[...].astype(jnp.float32)
     rms = lax.rsqrt(jnp.mean(x * x, axis=-1, keepdims=True) + EPSILON)
     normed = (x * rms * gain_ref[...]).astype(LOW)
     normed_ref[...] = normed
-    out_ref[...] = dot(normed, w_ref[...]).astype(LOW)
-
-
-def project(x, gain, w_qkv):
+    width = x.shape[1]
+    for n, w_ref in enumerate((wq_ref, wk_ref, wv_ref)):
+        out_ref[:, n * width : (n + 1) * width] = dot(normed, w_ref[...]).astype(LOW)
+
+
+def project(x, gain, w_query, w_key, w_value):
     tokens, width = x.shape
-    out = w_qkv.shape[1]
+    out = 3 * width
     step = 256
     rows = lambda w: pl.BlockSpec((step, w), lambda i: (i, 0))
     return pl.pallas_call(
         project_kernel,
         grid=(tokens // step,),
-        in_specs=[rows(width), whole((1, width)), whole((width, out))],
+        in_specs=[rows(width), whole((1, width)), *[whole((width, width))] * 3],
         out_specs=[rows(width), rows(out)],
         out_shape=[
             jax.ShapeDtypeStruct((tokens, width), LOW),
@@ -134,10 +193,11 @@
         compiler_params=params(40),
         cost_estimate=cost(2 * tokens * width * out, 12 << 20),
         name="project",
-    )(x, gain, w_qkv)
-
-
-def after_attention_kernel(o_ref, x_ref, w_ref, gain_ref, dest_ref, y_ref, out_ref, held):
+    )(x, gain, w_query, w_key, w_value)
+
+
+def after_attention_kernel(room, o_ref, x_ref, w_ref, gain_ref, code_ref, rank_ref, y_ref, *rest):
+    outs, held = rest[:-1], rest[-1]
     step = o_ref.shape[0]
     i = pl.program_id(0)
     y = x_ref[...].astype(jnp.float32) + dot(o_ref[...], w_ref[...])
@@ -147,37 +207,46 @@
 
     @pl.when(i == pl.num_programs(0) - 1)
     def _():
-        spread(dest_ref[...], held[...], out_ref)
-
-
-def after_attention(joined, x, w_output, gain, dest_r, rows_out):
+        spread_all(code_ref[...], rank_ref[...], room, held[...], outs)
+
+
+def after_attention(joined, x, w_output, gain, code, rank, experts, room):
     tokens, width = x.shape
     step = 256
     rows = pl.BlockSpec((step, width), lambda i: (i, 0))
-    return pl.pallas_call(
-        after_attention_kernel,
+    outs = buffers(experts, room, width)
+    return pl.pallas_call(
+        functools.partial(after_attention_kernel, room),
         grid=(tokens // step,),
-        in_specs=[rows, rows, whole((width, width)), whole((1, width)), whole((1, tokens))],
-        out_specs=[rows, pl.BlockSpec((rows_out, width), lambda i: (0, 0))],
-        out_shape=[
-            jax.ShapeDtypeStruct((tokens, width), jnp.float32),
-            jax.ShapeDtypeStruct((rows_out, width), LOW),
-        ],
+        in_specs=[
+            rows, rows, whole((width, width)), whole((1, width)), whole((1, tokens)), whole((1, tokens)),
+        ],
+        out_specs=[rows] + [pl.BlockSpec(o.shape, lambda i: (0, 0)) for o in outs],
+        out_shape=[jax.ShapeDtypeStruct((tokens, width), jnp.float32)] + outs,
         scratch_shapes=[pltpu.VMEM((tokens, width), LOW)],
         compiler_params=params(48),
-        cost_estimate=cost(2 * tokens * width * (width + rows_out), 12 << 20),
+        cost_estimate=cost(2 * tokens * width * (width + experts * room), 12 << 20),
         name="after_attention",
-    )(joined, x, w_output, gain, dest_r)
-
-
-def mix_kernel(experts, ff_ref, dest_ref, eid_ref, y_ref, gain_ref, wr_ref, out_ref):
+    )(joined, x, w_output, gain, code, rank)
+
+
+def mix_kernel(experts, room, code_ref, rank_ref, eid_ref, y_ref, gain_ref, wr_ref, *rest):
+    backs, out_ref = rest[:-1], rest[-1]
     y = y_ref[...]
     rms = lax.rsqrt(jnp.mean(y * y, axis=-1, keepdims=True) + EPSILON)
     normed = (y * rms * gain_ref[...]).astype(LOW)
     router = route_softmax(dot(normed, wr_ref[...]), experts)
     lane = lax.broadcasted_iota(jnp.int32, router.shape, 1)
     gate = jnp.sum(jnp.where(lane == eid_ref[...], router, 0.0), axis=-1, keepdims=True)
-    out_ref[...] = (y + gate * collect(dest_ref[...], ff_ref[...])).astype(LOW)
+    out_ref[...] = (y + gate * collect_all(code_ref[...], rank_ref[...], room, backs)).astype(LOW)
+
+
+def back_specs(backs, tokens, step):
+    return [
+        pl.BlockSpec((step, b.shape[1]), lambda i: (i, 0)) if b.shape[0] == tokens and n == 3
+        else whole(b.shape)
+        for n, b in enumerate(backs)
+    ]
 
 
 def route_softmax(logits, experts):
@@ -187,20 +256,23 @@
     return e / jnp.sum(e, axis=-1, keepdims=True)
 
 
-def mix(ff, dest_c, expert_ids, y, gain, w_router, experts):
+def mix(backs, code, rank, expert_ids, y, gain, w_router, experts, room):
     tokens, width = y.shape
     step = 256
     rows = lambda w: pl.BlockSpec((step, w), lambda i: (i, 0))
     return pl.pallas_call(
-        functools.partial(mix_kernel, experts),
+        functools.partial(mix_kernel, experts, room),
         grid=(tokens // step,),
-        in_specs=[whole(ff.shape), rows(1), rows(1), rows(width), whole((1, width)), whole(w_router.shape)],
+        in_specs=[
+            rows(1), rows(1), rows(1), rows(width), whole((1, width)), whole(w_router.shape),
+            *back_specs(backs, tokens, step),
+        ],
         out_specs=rows(width),
         out_shape=jax.ShapeDtypeStruct((tokens, width), LOW),
         compiler_params=params(40),
-        cost_estimate=cost(2 * tokens * width * ff.shape[0], 8 << 20),
+        cost_estimate=cost(2 * tokens * width * experts * room, 8 << 20),
         name="mix",
-    )(ff, dest_c, expert_ids.reshape(tokens, 1), y, gain, w_router)
+    )(code, rank, expert_ids.reshape(tokens, 1), y, gain, w_router, *backs)
 
 
 def pack(values, first, height, out, at):
@@ -211,8 +283,10 @@
 
 
 def before_attention_kernel(
-    dh_ref, dest_ref, y_ref, g_ref, gain_ref, wt_ref, o_ref, dy_ref, do_ref, pack_ref, gg_ref, gw_ref
+    room, n_backs, code_ref, rank_ref, y_ref, g_ref, gain_ref, w_ref, o_ref, *rest
 ):
+    backs = rest[:n_backs]
+    dy_ref, do_ref, pack_ref, gg_ref, gw_ref = rest[n_backs:]
     i = pl.program_id(0)
 
     @pl.when(i == 0)
@@ -220,7 +294,7 @@
         gw_ref[...] = jnp.zeros_like(gw_ref)
         gg_ref[...] = jnp.zeros_like(gg_ref)
 
-    dh = collect(dest_ref[...], dh_ref[...])
+    dh = collect_all(code_ref[...], rank_ref[...], room, backs)
     y = y_ref[...]
     rms = lax.rsqrt(jnp.mean(y * y, axis=-1, keepdims=True) + EPSILON)
     gg_ref[...] += jnp.sum(dh * y * rms, axis=0, keepdims=True)
@@ -232,7 +306,7 @@
     )
     dy_ref[...] = dy
     low = dy.astype(LOW)
-    do_ref[...] = dot(low, wt_ref[...]).astype(LOW)
+    do_ref[...] = dot_t(low, w_ref[...]).astype(LOW)
     gw_ref[...] += dot(o_ref[...].T, low)
 
     @pl.when(i == pl.num_programs(0) - 1)
@@ -240,16 +314,16 @@
         pack(gw_ref, 0, gw_ref.shape[0], pack_ref, 0)
 
 
-def before_attention(dh, dest_c, y, g, gain, w_output_t, joined):
+def before_attention(backs, code, rank, y, g, gain, w_output, joined, room):
     tokens, width = y.shape
     step = 256
     rows = lambda w: pl.BlockSpec((step, w), lambda i: (i, 0))
     return pl.pallas_call(
-        before_attention_kernel,
+        functools.partial(before_attention_kernel, room, len(backs)),
         grid=(tokens // step,),
         in_specs=[
-            whole(dh.shape), rows(1), rows(width), rows(width), whole((1, width)),
-            whole((width, width)), rows(width),
+            rows(1), rows(1), rows(width), rows(width), whole((1, width)),
+            whole((width, width)), rows(width), *back_specs(backs, tokens, step),
         ],
         out_specs=[
             rows(width), rows(width),
@@ -264,13 +338,14 @@
         ],
         scratch_shapes=[pltpu.VMEM((width, width), jnp.float32)],
         compiler_params=params(40),
-        cost_estimate=cost(2 * tokens * width * (dh.shape[0] + 2 * width), 16 << 20),
+        cost_estimate=cost(6 * tokens * width * width, 16 << 20),
         name="before_attention",
-    )(dh, dest_c, y, g, gain, w_output_t, joined)
+    )(code, rank, y, g, gain, w_output, joined, *backs)
 
 
 def finish_kernel(
-    dq_ref, dk_ref, dv_ref, wt_ref, normed_ref, x_ref, dy_ref, gain_ref, go_ref, gr_ref, gg2_ref, table_ref,
+    buckets,
+    dq_ref, dk_ref, dv_ref, wq_ref, wk_ref, wv_ref, normed_ref, x_ref, dy_ref, gain_ref, go_ref, gr_ref, gg2_ref, table_ref,
     out_ref, pack_ref, gw_ref, gg_ref,
 ):
     i = pl.program_id(0)
@@ -284,9 +359,9 @@
     grads = (dq_ref[...], dk_ref[...], dv_ref[...])
     normed_t = normed_ref[...].T
     dh = None
-    for n, d in enumerate(grads):
+    for n, (d, w_ref) in enumerate(zip(grads, (wq_ref, wk_ref, wv_ref))):
         gw_ref[n * width : (n + 1) * width] += dot(normed_t, d)
-        part = dot(d, wt_ref[n * width : (n + 1) * width])
+        part = dot_t(d, w_ref[...])
         dh = part if dh is None else dh + part
     x = x_ref[...].astype(jnp.float32)
     rms = lax.rsqrt(jnp.mean(x * x, axis=-1, keepdims=True) + EPSILON)
@@ -315,25 +390,22 @@
         gains = jnp.concatenate(gains, axis=0)
         pack_ref[at : at + gains.shape[0]] = gains.astype(LOW)
         at = at + gains.shape[0]
-        heads, buckets, _ = table_ref.shape
-        lane = lax.broadcasted_iota(jnp.int32, (buckets, TILE), 1)
-        table = jnp.zeros((buckets, TILE), jnp.float32)
-        for h in range(heads):
-            table = jnp.where(lane == h, jnp.sum(table_ref[h], axis=1, keepdims=True), table)
-        pack_ref[at : at + buckets] = table.astype(LOW)
-        at = at + buckets
+        table = bucket_table(table_ref, buckets)
+        table = jnp.concatenate([table, jnp.zeros((-table.shape[0] % 16, TILE), jnp.float32)], axis=0)
+        pack_ref[at : at + table.shape[0]] = table.astype(LOW)
+        at = at + table.shape[0]
         pack_ref[at:] = jnp.zeros((pack_ref.shape[0] - at, TILE), LOW)
 
 
-def finish(dq, dk, dv, w_qkv_t, normed, x, dy, gain, go, gr, gg2, table, rows_packed):
+def finish(dq, dk, dv, w_query, w_key, w_value, normed, x, dy, gain, go, gr, gg2, table, buckets, rows_packed):
     tokens, width = x.shape
-    step = 256
+    step = 512
     rows = pl.BlockSpec((step, width), lambda i: (i, 0))
     return pl.pallas_call(
-        finish_kernel,
+        functools.partial(finish_kernel, buckets),
         grid=(tokens // step,),
         in_specs=[
-            rows, rows, rows, whole((3 * width, width)), rows, rows, rows, whole((1, width)),
+            rows, rows, rows, *[whole((width, width))] * 3, rows, rows, rows, whole((1, width)),
             whole(go.shape), whole(gr.shape), whole(gg2.shape), whole(table.shape),
         ],
         out_specs=[rows, pl.BlockSpec((rows_packed, TILE), lambda i: (0, 0))],
@@ -348,28 +420,26 @@
         compiler_params=params(56),
         cost_estimate=cost(12 * tokens * width * width, 24 << 20),
         name="finish",
-    )(dq, dk, dv, w_qkv_t, normed, x, dy, gain, go, gr, gg2, table)
-
-
-def unpack_kernel(packed_ref, out_ref):
-    height = out_ref.shape[1]
-    for c in range(out_ref.shape[2] // TILE):
-        out_ref[0, :, c * TILE : (c + 1) * TILE] = packed_ref[c * height : (c + 1) * height].astype(
-            jnp.float32
-        )
+    )(dq, dk, dv, w_query, w_key, w_value, normed, x, dy, gain, go, gr, gg2, table)
+
+
+def unpack_kernel(*refs):
+    for packed_ref, out_ref in zip(refs[:4], refs[4:]):
+        out_ref[...] = packed_ref[...].astype(jnp.float32)
 
 
 def unpack(packed, width):
-    block = width * width // TILE
+    blocks = width // TILE
+    source = lambda m: pl.BlockSpec((width, TILE), lambda i: (m * blocks + i, 0))
     return pl.pallas_call(
         unpack_kernel,
-        grid=(4,),
-        in_specs=[pl.BlockSpec((block, TILE), lambda i: (i, 0))],
-        out_specs=pl.BlockSpec((1, width, width), lambda i: (i, 0, 0)),
-        out_shape=jax.ShapeDtypeStruct((4, width, width), jnp.float32),
+        grid=(blocks,),
+        in_specs=[source(m) for m in range(4)],
+        out_specs=[pl.BlockSpec((width, TILE), lambda i: (0, i))] * 4,
+        out_shape=[jax.ShapeDtypeStruct((width, width), jnp.float32)] * 4,
         compiler_params=params(32),
         name="unpack",
-    )(packed)
+    )(*[packed] * 4)
 
 
 def attention_forward_kernel(len_ref, q_ref, k_ref, v_ref, near_ref, far_ref, o_ref, p_ref, s_ref):
@@ -498,26 +568,46 @@
     dv_ref[...] = dv_all.astype(LOW)
 
 def bucket_sums(near_ref, far_ref, table_ref):
-    buckets = table_ref.shape[1]
-    half = buckets // 2
-    key = lax.broadcasted_iota(jnp.int32, (TILE, TILE), 0)
-    query = lax.broadcasted_iota(jnp.int32, (TILE, TILE), 1)
-    tiles = [bucket_of((d - 1) * TILE + key - query) for d in range(3)]
+    empty = jnp.zeros((8, TILE), jnp.float32)
+    sub = lax.broadcasted_iota(jnp.int32, (8, 2 * TILE), 0)
     for h in range(2):
-        sums = []
-        for n in range(buckets):
-            total = far_ref[h, 0 if n >= half else 1] if n % half == half - 1 else None
-            for d in range(3):
-                if (d == 0 and n >= half) or (d == 2 and n < half):
-                    continue
-                part = jnp.where(tiles[d] == n, near_ref[h, d], 0.0)
-                part = jnp.sum(part.reshape(TILE // 8, 8, TILE), axis=0)
-                total = part if total is None else total + part
-            sums.append(jnp.sum(total, axis=0, keepdims=True))
-        table_ref[h] = jnp.concatenate(sums, axis=0)
-
-
-def attention_backward(buckets, projected, do, joined, weights, rows, seq, heads, head):
+        lines = []
+        for d in range(3):
+            turned = None
+            for a in range(0, TILE, 8):
+                part = jnp.concatenate([near_ref[h, d, a : a + 8], empty], axis=1)
+                part = pltpu.roll(part, (2 * TILE - a) % (2 * TILE), 1) if a else part
+                turned = part if turned is None else turned + part
+            for b in (1, 2, 4):
+                turned = jnp.where((sub & b) > 0, pltpu.roll(turned, 2 * TILE - b, 1), turned)
+            lines.append(jnp.sum(turned, axis=0, keepdims=True))
+        for side in range(2):
+            total = jnp.sum(far_ref[h, side], axis=0, keepdims=True)
+            lines.append(jnp.concatenate([total, jnp.zeros((1, TILE), jnp.float32)], axis=1))
+        lines.append(jnp.zeros((3, 2 * TILE), jnp.float32))
+        table_ref[h] = jnp.concatenate(lines, axis=0)
+
+
+def bucket_table(lines_ref, buckets):
+    heads = lines_ref.shape[0]
+    lane = lax.broadcasted_iota(jnp.int32, (2 * TILE, TILE), 0)
+    bucket = lax.broadcasted_iota(jnp.int32, (2 * TILE, TILE), 1)
+    turn = jnp.where(lane >= TILE, lane - 2 * TILE, lane)
+    total = None
+    for r in range(5):
+        if r < 3:
+            hit = bucket_of((r - 1) * TILE - turn) == bucket
+        else:
+            hit = bucket == (buckets - 1 if r == 3 else buckets // 2 - 1)
+        hit = hit.astype(LOW)
+        line = jnp.concatenate([lines_ref[h, r : r + 1, :] for h in range(heads)], axis=0)
+        high = line.astype(LOW)
+        part = dot(high, hit) + dot((line - high.astype(jnp.float32)).astype(LOW), hit)
+        total = part if total is None else total + part
+    return total
+
+
+def attention_backward(projected, do, joined, weights, rows, seq, heads, head):
     width = heads * head
     pairs = heads // 2
     spec = lambda off: pl.BlockSpec((seq, 2 * head), lambda p, b: (b, off + p))
@@ -530,10 +620,10 @@
         ],
         out_specs=[
             spec(0), spec(0), spec(0),
-            pl.BlockSpec((2, buckets, TILE), lambda p, b: (p, 0, 0)),
+            pl.BlockSpec((2, 8, 2 * TILE), lambda p, b: (p, 0, 0)),
         ],
         out_shape=[jax.ShapeDtypeStruct((rows * seq, width), LOW)] * 3 + [
-            jax.ShapeDtypeStruct((heads, buckets, TILE), jnp.float32),
+            jax.ShapeDtypeStruct((heads, 8, 2 * TILE), jnp.float32),
         ],
         scratch_shapes=[
             pltpu.VMEM((2, 3, TILE, TILE), jnp.float32),
@@ -557,10 +647,25 @@
     return near, far
 
 
-def expert_kernel(experts, chunk, x_ref, g_ref, mine_ref, wr_ref, wrt_ref, wi_ref, wit_ref, wo_ref, wot_ref,
-                  ff_ref, dx_ref, hid_ref, da_ref, xt_ref, dfft_ref, gr_ref):
+def expert_kernel(experts, chunk, x_ref, g_ref, mine_ref, wr_ref, wi_any, wo_any,
+                  ff_ref, dx_ref, hid_ref, da_ref, xt_ref, dfft_ref, gr_ref, wi_ref, wo_ref, sem):
+    inner = wi_ref.shape[1]
+    first_step = pl.program_id(0) == 0
+
+    def loads(f):
+        cols = pl.ds(f, chunk)
+        return (pltpu.make_async_copy(wi_any.at[:, cols], wi_ref.at[:, cols], sem.at[0, f // chunk]),
+                pltpu.make_async_copy(wo_any.at[cols, :], wo_ref.at[cols, :], sem.at[1, f // chunk]))
+
+    @pl.when(first_step)
+    def _():
+        for f in range(0, inner, chunk):
+            for c in loads(f):
+                c.start()
+        gr_ref[...] = jnp.zeros_like(gr_ref)
+
     x = x_ref[...]
-    g = g_ref[...].astype(jnp.float32)
+    g = g_ref[...].reshape(x.shape).astype(jnp.float32)
     mine = mine_ref[...]
     lane = lax.broadcasted_iota(jnp.int32, (1, wr_ref.shape[1]), 1)
     logits = jnp.dot(x, wr_ref[...], preferred_element_type=jnp.float32)
@@ -569,19 +674,19 @@
     router = e / jnp.sum(e, axis=-1, keepdims=True)
     gate = jnp.sum(router * mine, axis=-1, keepdims=True)
     dff = (g * gate).astype(LOW)
-    inner = wi_ref.shape[1]
     ff = None
     dx = None
     def first(f):
+        @pl.when(first_step)
+        def _():
+            for c in loads(f):
+                c.wait()
         cols = slice(f, f + chunk)
         return (jnp.dot(x, wi_ref[:, cols], preferred_element_type=jnp.float32),
-                jnp.dot(dff, wot_ref[:, cols], preferred_element_type=jnp.float32))
-    ahead = first(0)
+                lax.dot_general(dff, wo_ref[cols, :], (((1,), (1,)), ((), ())), preferred_element_type=jnp.float32))
     for f in range(0, inner, chunk):
         cols = slice(f, f + chunk)
-        a, dhid = ahead
-        if f + chunk < inner:
-            ahead = first(f + chunk)
+        a, dhid = first(f)
         u = a * a
         t = jnp.tanh(a * (GELU_A + GELU_B * u))
         h = 0.5 + 0.5 * t
@@ -592,43 +697,44 @@
         hid_ref[:, cols] = hid
         da_ref[:, cols] = da
         ff_part = jnp.dot(hid, wo_ref[cols, :], preferred_element_type=jnp.float32)
-        dx_part = jnp.dot(da, wit_ref[cols, :], preferred_element_type=jnp.float32)
+        dx_part = lax.dot_general(da, wi_ref[:, cols], (((1,), (1,)), ((), ())), preferred_element_type=jnp.float32)
         ff = ff_part if ff is None else ff + ff_part
         dx = dx_part if dx is None else dx + dx_part
     ff = ff.astype(LOW)
     ff_ref[...] = ff
     dgate = jnp.sum(g * ff.astype(jnp.float32), axis=-1, keepdims=True)
     dlogits = ((gate * dgate) * (mine - router)).astype(LOW)
-    dx = dx + jnp.dot(dlogits, wrt_ref[...], preferred_element_type=jnp.float32)
+    dx = dx + lax.dot_general(dlogits, wr_ref[...], (((1,), (1,)), ((), ())), preferred_element_type=jnp.float32)
     dx_ref[...] = dx.astype(LOW)
     x_t = x.T
     xt_ref[...] = x_t
     dfft_ref[...] = dff.T
-
-    @pl.when(pl.program_id(0) == 0)
-    def _():
-        gr_ref[...] = jnp.zeros_like(gr_ref)
     gr_ref[...] += jnp.dot(x_t, dlogits, preferred_element_type=jnp.float32)
 
-def expert_rows(x, g, mine, wr, wrt, wi, wit, wo, wot, experts, tile=256, chunk=768):
+def expert_rows(x, g, mine, wr, wi, wo, experts, low, high, tile=256, chunk=1024):
     n, width = x.shape
     inner = wi.shape[1]
-    while n % tile: tile //= 2
+    sources, room = g.shape[0], high - low
+    tile = min(tile, n)
+    group = tile // room
+    gspec = pl.BlockSpec((group, room, width), lambda i: (i, low // room, 0))
     once = lambda s: pl.BlockSpec(s, lambda i: (0,) * len(s), pipeline_mode=pl.Buffered(1))
     rowspec = lambda w: pl.BlockSpec((tile, w), lambda i: (i, 0))
+    anywhere = pl.BlockSpec(memory_space=pl.ANY)
     return pl.pallas_call(
         functools.partial(expert_kernel, experts, chunk),
         grid=(n // tile,),
-        in_specs=[rowspec(width), rowspec(width), once(mine.shape), once(wr.shape), once(wrt.shape), once(wi.shape), once(wit.shape), once(wo.shape), once(wot.shape)],
+        in_specs=[rowspec(width), gspec, once(mine.shape), once(wr.shape), anywhere, anywhere],
         out_specs=[rowspec(width), rowspec(width), rowspec(inner), rowspec(inner),
                    pl.BlockSpec((width, tile), lambda i: (0, i)), pl.BlockSpec((width, tile), lambda i: (0, i)),
                    pl.BlockSpec((width, wr.shape[1]), lambda i: (0, 0))],
         out_shape=[jax.ShapeDtypeStruct((n, width), LOW)] * 2 + [jax.ShapeDtypeStruct((n, inner), LOW)] * 2
             + [jax.ShapeDtypeStruct((width, n), LOW)] * 2 + [jax.ShapeDtypeStruct((width, wr.shape[1]), jnp.float32)],
-        compiler_params=params(56),
+        scratch_shapes=[pltpu.VMEM(wi.shape, LOW), pltpu.VMEM(wo.shape, LOW), pltpu.SemaphoreType.DMA((2, inner // chunk))],
+        compiler_params=params(60),
         cost_estimate=cost(flops=8 * n * width * inner, bytes_accessed=4 * n * inner + 8 * width * inner, transcendentals=n * inner),
         name="expert_rows",
-    )(x, g, mine, wr, wrt, wi, wit, wo, wot)
+    )(x, g, mine, wr, wi, wo)
 
 def expert_weights_kernel(parts, *refs):
     ins, (gi_ref, go_ref) = refs[:4 * parts], refs[4 * parts:]
@@ -643,7 +749,7 @@
     gi_ref[0] = gi
     go_ref[0] = go.T
 
-def expert_weights(parts, tile=256):
+def expert_weights(parts, tile=512):
     inner = parts[0][2].shape[1]
     width = parts[0][0].shape[0]
     specs, args, rows = [], [], 0
@@ -659,7 +765,7 @@
         in_specs=specs,
         out_specs=[pl.BlockSpec((1, width, tile), lambda f: (0, 0, f)), pl.BlockSpec((1, tile, width), lambda f: (0, f, 0))],
         out_shape=[jax.ShapeDtypeStruct((1, width, inner), jnp.float32), jax.ShapeDtypeStruct((1, inner, width), jnp.float32)],
-        compiler_params=params(56),
+        compiler_params=params(60),
         cost_estimate=cost(flops=4 * rows * width * inner, bytes_accessed=4 * rows * inner + 8 * width * inner, transcendentals=0),
         name="expert_weights",
     )(*args)
@@ -784,46 +890,59 @@
     wide = max(128, experts)
     mine = (jnp.arange(wide, dtype=jnp.int32) == me).astype(jnp.float32).reshape(1, wide)
 
-    dest_c, dest_r, g_out = route(expert_ids, slots, g, experts, room)
+    code_c, code_r, rank_c, rank_r, tags, g_out = route(expert_ids, slots, g, experts, room)
     g_in = exchange(g_out, devices)
-    dest_r, x, w_query, w_key, w_value, w_output, bias_table, w_router = lax.optimization_barrier(
-        (dest_r, x, w_query, w_key, w_value, w_output, bias_table, w_router)
+    code_r, x, w_query, w_key, w_value, w_output, bias_table, w_router = lax.optimization_barrier(
+        (code_r, x, w_query, w_key, w_value, w_output, bias_table, w_router)
     )
     router_w = jnp.pad(w_router, ((0, 0), (0, wide - experts)))
 
-    w_qkv = jnp.concatenate([w_query, w_key, w_value], axis=1)
-    normed, projected = project(x, gain_one, w_qkv)
+    normed, projected = project(x, gain_one, w_query, w_key, w_value)
     near, far = bias_tiles(bias_table)
     joined, weights = attention_forward(lengths, projected, near, far, rows, seq, heads, head)
-    y, h_out = after_attention(joined, x, w_output, gain_two, dest_r, experts * room)
+    y, *h_out = after_attention(joined, x, w_output, gain_two, code_r, rank_r, experts, room)
     h_out, g_in = lax.optimization_barrier((h_out, g_in))
-    h_in = exchange(h_out, devices)
-    w_in, w_out, h_out = lax.optimization_barrier((w_in, w_out, h_out))
-
-    ff, dx, hid, da, x_t, dff_t, grad_router = expert_rows(
-        h_in, g_in, mine, router_w, router_w.T, w_in[0], w_in[0].T, w_out[0], w_out[0].T, experts
-    )
-    dh_back = exchange(dx, devices)
-    grad_in, grad_out = expert_weights([(x_t, dff_t, hid, da)])
-    dh_back, grad_in, grad_out, ff = lax.optimization_barrier((dh_back, grad_in, grad_out, ff))
+
+    g_in = g_in.reshape(devices, room, width)
+    segments, _ = plan(room)
+    h_in, dx_back, ffs, parts, grad_router = [], [], [], [], 0.0
+    for h in h_out:
+        if h_in:
+            h, h_in[-1] = lax.optimization_barrier((h, h_in[-1]))
+        h_in.append(exchange(h, devices))
+    for n, (low, high) in enumerate(segments):
+        ff, dx, hid, da, x_t, dff_t, routed = expert_rows(
+            h_in[n], g_in, mine, router_w, w_in[0], w_out[0], experts, low, high
+        )
+        if n + 1 < len(segments):
+            dx, h_in[n + 1] = lax.optimization_barrier((dx, h_in[n + 1]))
+        if n:
+            dx, dx_back[-1] = lax.optimization_barrier((dx, dx_back[-1]))
+        dx_back.append(exchange(dx, devices))
+        ffs.append(ff.reshape(devices, high - low, width))
+        parts.append((x_t, dff_t, hid, da))
+        grad_router = grad_router + routed
+    grad_in, grad_out = expert_weights(parts)
+    ff = jnp.concatenate(ffs, axis=1).reshape(devices * room, width) if len(ffs) > 1 else ffs[0].reshape(-1, width)
+    dx_back, grad_in, grad_out, ff = lax.optimization_barrier((dx_back, grad_in, grad_out, ff))
     ff_back = exchange(ff, devices)
     grad_router = grad_router[:, :experts].reshape(width * experts // TILE, TILE)
 
     dy, do, grad_output, grad_gain_two = before_attention(
-        dh_back, dest_c, y, g, gain_two, w_output.T, joined
+        dx_back, code_c, rank_c, y, g, gain_two, w_output, joined, room
     )
     dq, dk, dv, table = attention_backward(
-        buckets, projected, do, joined, weights, rows, seq, heads, head
+        projected, do, joined, weights, rows, seq, heads, head
     )
-    small = grad_router.shape[0] + -(-2 * width // TILE // 16) * 16 + buckets
+    small = grad_router.shape[0] + -(-2 * width // TILE // 16) * 16 + -(-heads // 16) * 16
     block = width * width // TILE
     rows_packed = -(-(4 * block + small) // (16 * devices)) * 16 * devices
     grad_tokens, packed = finish(
-        dq, dk, dv, w_qkv.T, normed, x, dy, gain_one, grad_output, grad_router, grad_gain_two, table, rows_packed
+        dq, dk, dv, w_query, w_key, w_value, normed, x, dy, gain_one, grad_output, grad_router, grad_gain_two, table, buckets, rows_packed
     )
     summed = all_sum(packed)
     summed, ff_back = lax.optimization_barrier((summed, ff_back))
-    mixed = mix(ff_back, dest_c, expert_ids, y, gain_two, router_w, experts)
+    mixed = mix([ff_back], code_c, rank_c, expert_ids, y, gain_two, router_w, experts, room)
     grads = unpack(summed, width)
     at = 4 * block
     rest = summed[at : at + small].astype(jnp.float32)
@@ -832,7 +951,7 @@
     lines = width // TILE
     grad_gain_one = rest[routed : routed + lines].reshape(width)
     grad_gain_two = rest[routed + lines : routed + 2 * lines].reshape(width)
-    grad_table = rest[small - buckets :, :heads]
+    grad_table = rest[small - -(-heads // 16) * 16 :][:heads, :buckets].T
     return (
         mixed.reshape(rows, seq, width),
         grad_tokens.reshape(rows, seq, width),

time: 471 us -> 431 us (0.915)
  waiting for transfers between devices: 117 us -> 45.8 us
  blocking collectives: 0 us -> 41.9 us
  local copies, waits for them, and re-layouts: 68.7 us -> 39.9 us
  Pallas kernels: 254 us -> 265 us
    all_to_all x4 -> x5, waiting for transfers between devices: 117 us -> 45.8 us  [exchange(): lax.all_to_all(shaped, AXES, split_axis=0, concat_axis=0, tiled=True)]
    all_to_all x0 -> x1, blocking collectives: none -> 41.9 us  [exchange(): lax.all_to_all(shaped, AXES, split_axis=0, concat_axis=0, tiled=True)]
    optimization_barrier x8 -> x2, local copies, waits for them, and re-layouts: 19.3 us -> 0.25 us  [local(): lax.optimization_barrier((code_r, x, w_query, w_key, w_value, w_output, b...]
    pallas_call x5, Pallas kernels: 41.4 us -> 47.6 us  [the longest x1 16.9 us: finish(): pl.pallas_call(functools.partial(finish_kernel, buckets), grid=(tokens //...]
    pallas_call x1 -> x2, Pallas kernels: 58.7 us -> 64.6 us  [expert_rows(): pl.pallas_call(functools.partial(expert_kernel, experts, chunk), grid=(n...]
    all_to_all x4 -> x5, starting transfers between devices: 19.7 us -> 23 us  [exchange(): lax.all_to_all(shaped, AXES, split_axis=0, concat_axis=0, tiled=True)]
    unnamed x92 -> x95, local copies, waits for them, and re-layouts: 37.2 us -> 36.7 us
  transfers between devices with their start and end apart: 4 -> 5, of which waited for: 3 -> 4; matrix products, arithmetic and copies ran while one was open for 7% -> 2% of each run, Pallas kernels for 39% -> 58%
where the time goes in v3:
time: 431 us; the launch traced here: 425 us
  Pallas kernels  265 us (61%)
  waiting for transfers between devices  45.8 us (11%)
  blocking collectives  41.9 us (10%)
  local copies, waits for them, and re-layouts  39.9 us (9%)
  starting transfers between devices  23 us (5%)
  other arithmetic  6.6 us (2%)
    pallas_call x2, Pallas kernels, expert_rows(): pl.pallas_call(functools.partial(expert_kernel, experts, chunk), grid=(n...  64.6 us
    pallas_call x1, Pallas kernels, all_sum(): pl.pallas_call(functools.partial(sum_kernel, cores, bits, sizes, orders),...  62.9 us
    all_to_all x5, waiting for transfers between devices, exchange(): lax.all_to_all(shaped, AXES, split_axis=0, concat_axis=0, tiled=True)  45.8 us
    all_to_all x1, blocking collectives, exchange(): lax.all_to_all(shaped, AXES, split_axis=0, concat_axis=0, tiled=True)  41.9 us
    unnamed x95, local copies, waits for them, and re-layouts  36.7 us
    pallas_call x1, Pallas kernels, attention_backward(): pl.pallas_call(attention_backward_kernel, grid=(pairs, rows), in_specs=[s...  28.3 us
    pallas_call x1, Pallas kernels, expert_weights(): pl.pallas_call(functools.partial(expert_weights_kernel, len(parts)), grid...  27.8 us
    all_to_all x5, starting transfers between devices, exchange(): lax.all_to_all(shaped, AXES, split_axis=0, concat_axis=0, tiled=True)  23 us
  transfers between devices with their start and end apart: 5, of which 4 were waited for; matrix products, arithmetic and copies ran while one was open for 2% of the time, Pallas kernels for 58%

profile of v3, /device:TPU:0, one launch (start us, length us, event | category | flops | bytes accessed | tf_op | source)
XLA Modules:
  0.0 425.4 jit_solution(4961222502521330044)
XLA Ops:
  0.6 0.7 copy.41
  1.3 0.7 copy.44
  2.5 1.6 copy-done.11
  4.1 8.1 %route.1 = (s32[1024,1]{1,0:T(8,128)S(1)}, s32[1,1024]{1,0:T(1,128)S(1)}, s32[1024,1]{1,0:T(8,128)S(1)}, s32[1,1024]{1,0:T(1,128)S(1)}, s32[1,128]{1,0:T(1,128)}, /*index=5*/bf16[2048,768]{1,0:T(8,128)(2,1)}) custom-call(s32[1024,1]{1,0:T(8,128)S(1)} %bitcast.55, s32[1,1024]{1,0:T(1,128)S(1)} %bitcast.59, s32[1024,1]{1,0:T(8,128)S(1)} %bitcast.57, ...), custom_call_target="tpu_custom_call" | custom-call | flops 3221225472 | bytes 8388608 | tf_op jit(solution)/shard_map/route/pallas_call | solution.py:148
  12.2 0.8 copy-done.25
  13.0 0.8 copy-done.28
  13.9 7.9 %all-to-all-start = ((bf16[32,64,768]{2,1,0:T(8,128)(2,1)}), bf16[32,64,768]{2,1,0:T(8,128)(2,1)}, u32[]{:S(2)}, u32[]{:S(2)}) async-start(bf16[32,64,768]{2,1,0:T(8,128)(2,1)} %bitcast.69), calls=%async_computation | async-start | bytes 6291456 | tf_op jit(solution)/shard_map/all_to_all | solution.py:165
  22.4 2.1 fusion
  24.5 0.6 copy.47
  25.3 0.4 copy-done.18
  25.7 0.9 copy-done.13
  26.6 0.3 copy-done.16
  26.9 0.4 copy-done.17
  27.3 4.8 %project.1 = (bf16[1024,768]{1,0:T(8,128)(2,1)S(1)}, bf16[1024,2304]{1,0:T(8,128)(2,1)S(1)}) custom-call(bf16[1024,768]{1,0:T(8,128)(2,1)S(1)} %bitcast.66, f32[1,768]{1,0:T(1,128)S(1)} %reshape.191.gain_ref, bf16[768,768]{1,0:T(8,128)(2,1)S(1)} %copy-done.16, bf16[768,768]{1,0:T(8,128)(2,1)S(1)} %copy-done.17, bf16[768,768]{1,0:T(8,128)(2,1)S(1)} %copy-done.18), custom_call_target="tpu_custom_call" | custom-call | flops 3623878656 | bytes 12582912 | tf_op jit(solution)/shard_map/project/pallas_call | solution.py:184
  32.1 20.8 %attention_forward.1 = (bf16[1024,768]{1,0:T(8,128)(2,1)S(1)}, bf16[2,12,512,512]{3,2,1,0:T(8,128)(2,1)}) custom-call(s32[2]{0:T(128)S(1)} %copy-done.19, bf16[1024,2304]{1,0:T(8,128)(2,1)S(1)} %get-tuple-element.85.q_ref.k_ref.v_ref, bf16[1024,2304]{1,0:T(8,128)(2,1)S(1)} %get-tuple-element.85.q_ref.k_ref.v_ref, ...), custom_call_target="tpu_custom_call" | custom-call | flops 6442450944 | bytes 12582912 | tf_op jit(solution)/shard_map/attention_forward/pallas_call | solution.py:492
  52.9 9.0 %after_attention.1 = (f32[1024,768]{1,0:T(8,128)}, bf16[1024,768]{1,0:T(8,128)(2,1)S(1)}, bf16[1024,768]{1,0:T(8,128)(2,1)}) custom-call(bf16[1024,768]{1,0:T(8,128)(2,1)S(1)} %get-tuple-element.87.o_ref, bf16[1024,768]{1,0:T(8,128)(2,1)} %bitcast.64, bf16[768,768]{1,0:T(8,128)(2,1)S(1)} %copy-done.14, f32[1,768]{1,0:T(1,128)S(1)} %reshape.193.gain_ref, ...), custom_call_target="tpu_custom_call" | custom-call | flops 4429185024 | bytes 12582912 | tf_op jit(solution)/shard_map/after_attention/pallas_call | solution.py:218
  61.9 1.2 copy-done.22
  63.0 30.2 %all-to-all-done = bf16[32,64,768]{2,1,0:T(8,128)(2,1)} async-done(((bf16[32,64,768]{2,1,0:T(8,128)(2,1)}), bf16[32,64,768]{2,1,0:T(8,128)(2,1)}, u32[]{:S(2)}, u32[]{:S(2)}) %all-to-all-start) | async-done | bytes 3145760 | tf_op jit(solution)/shard_map/all_to_all | solution.py:165
  93.2 41.9 %all_to_all.30 = bf16[32,32,768]{2,1,0:T(8,128)(2,1)} all-to-all(bf16[32,32,768]{2,1,0:T(8,128)(2,1)S(1)} %bitcast.54), channel_id=1, replica_groups=mesh['grp'=16,'exp'=2] {'grp','exp'}, dimensions={0} | all-to-all | bytes 3145728 | tf_op jit(solution)/shard_map/all_to_all | solution.py:165
  135.1 3.2 all-to-all-start.2
  138.5 0.7 pad.4.wr_ref
  139.3 0.5 compare_convert_fusion.mine_ref
  139.8 32.3 %expert_rows.2 = (bf16[1024,768]{1,0:T(8,128)(2,1)}, bf16[1024,768]{1,0:T(8,128)(2,1)}, bf16[1024,3072]{1,0:T(8,128)(2,1)}, bf16[1024,3072]{1,0:T(8,128)(2,1)}, ...) custom-call(bf16[1024,768]{1,0:T(8,128)(2,1)} %bitcast.71, ...), custom_call_target="tpu_custom_call" | custom-call | flops 19327352832 | bytes 31457280 | tf_op jit(solution)/shard_map/expert_rows/pallas_call | solution.py:724
  172.0 4.0 all-to-all-done.2
  176.1 4.0 all-to-all-start.3
  180.1 32.3 %expert_rows.3 = (bf16[1024,768]{1,0:T(8,128)(2,1)}, bf16[1024,768]{1,0:T(8,128)(2,1)}, bf16[1024,3072]{1,0:T(8,128)(2,1)}, bf16[1024,3072]{1,0:T(8,128)(2,1)}, ...) custom-call(bf16[1024,768]{1,0:T(8,128)(2,1)} %bitcast.70, ...), custom_call_target="tpu_custom_call" | custom-call | flops 19327352832 | bytes 31457280 | tf_op jit(solution)/shard_map/expert_rows/pallas_call | solution.py:724
  212.4 5.4 %all-to-all-done.3 = bf16[32,32,768]{2,1,0:T(8,128)(2,1)S(1)} async-done(((bf16[32,32,768]{2,1,0:T(8,128)(2,1)}), bf16[32,32,768]{2,1,0:T(8,128)(2,1)S(1)}, u32[]{:S(2)}, u32[]{:S(2)}) %all-to-all-start.3) | async-done | bytes 1572896 | tf_op jit(solution)/shard_map/all_to_all | solution.py:165
  217.8 3.8 all-to-all-start.4
  221.6 3.8 pad_maximum_fusion
  225.4 27.8 %expert_weights.1 = (f32[1,768,3072]{2,1,0:T(8,128)}, f32[1,3072,768]{2,1,0:T(8,128)}) custom-call(bf16[768,1024]{1,0:T(8,128)(2,1)} %get-tuple-element.107.refs_0_, bf16[768,1024]{1,0:T(8,128)(2,1)} %get-tuple-element.108.refs_1_, bf16[1024,3072]{1,0:T(8,128)(2,1)} %get-tuple-element.109.refs_2_, bf16[1024,3072]{1,0:T(8,128)(2,1)} %get-tuple-element.110.refs_3_, ...), custom_call_target="tpu_custom_call" | custom-call | flops 19327352832 | bytes 44040192 | tf_op jit(solution)/shard_map/expert_weights/pallas_call | solution.py:762
  253.3 6.1 %all-to-all-done.4 = bf16[32,32,768]{2,1,0:T(8,128)(2,1)S(1)} async-done(((bf16[32,32,768]{2,1,0:T(8,128)(2,1)}), bf16[32,32,768]{2,1,0:T(8,128)(2,1)S(1)}, u32[]{:S(2)}, u32[]{:S(2)}) %all-to-all-start.4) | async-done | bytes 1572896 | tf_op jit(solution)/shard_map/all_to_all | solution.py:165
  259.3 1.1 copy-done.5
  260.5 4.0 all-to-all-start.5
  264.5 1.2 slice_add_fusion
  265.7 0.8 reshape.208.gr_ref
  266.5 1.4 copy-done.4
  267.9 1.4 copy-done.6
  269.3 1.4 copy-done.12
  270.7 1.3 copy-done.15
  272.0 1.4 copy-done.23
  273.4 1.0 copy-done.26
  274.4 1.0 copy-done.29
  275.4 11.4 %before_attention.1 = (f32[1024,768]{1,0:T(8,128)S(1)}, bf16[1024,768]{1,0:T(8,128)(2,1)S(1)}, bf16[4608,128]{1,0:T(8,128)(2,1)S(1)}, f32[1,768]{1,0:T(1,128)S(1)}) custom-call(s32[1024,1]{1,0:T(8,128)S(1)} %copy-done.26, s32[1024,1]{1,0:T(8,128)S(1)} %copy-done.29, f32[1024,768]{1,0:T(8,128)} %get-tuple-element.91.y_ref, bf16[1024,768]{1,0:T(8,128)(2,1)S(1)} %bitcast.63, ...), custom_call_target="tpu_custom_call" | custom-call | flops 3623878656 | bytes 16777216 | tf_op jit(solution)/shard_map/before_attention/pallas_call | solution.py:321
  286.9 1.6 copy-done.21
  288.5 1.0 copy-done.24
  289.5 2.3 copy-done.32
  291.9 28.3 %attention_backward.1 = (bf16[1024,768]{1,0:T(8,128)(2,1)S(1)}, bf16[1024,768]{1,0:T(8,128)(2,1)S(1)}, bf16[1024,768]{1,0:T(8,128)(2,1)S(1)}, f32[12,8,256]{2,1,0:T(8,128)S(1)}) custom-call(bf16[1024,2304]{1,0:T(8,128)(2,1)S(1)} %copy-done.32, bf16[1024,2304]{1,0:T(8,128)(2,1)S(1)} %copy-done.32, bf16[1024,2304]{1,0:T(8,128)(2,1)S(1)} %copy-done.32, ...), custom_call_target="tpu_custom_call" | custom-call | flops 12884901888 | bytes 12582912 | tf_op jit(solution)/shard_map/attention_backward/pallas_call | solution.py:614
  320.2 1.1 copy-done.34
  321.4 1.1 copy-done.35
  322.5 1.1 copy-done.36
  323.6 0.6 copy-done.38
  324.3 16.9 %finish.1 = (f32[1024,768]{1,0:T(8,128)}, bf16[18944,128]{1,0:T(8,128)(2,1)}) custom-call(bf16[1024,768]{1,0:T(8,128)(2,1)} %copy-done.34, bf16[1024,768]{1,0:T(8,128)(2,1)} %copy-done.35, bf16[1024,768]{1,0:T(8,128)(2,1)} %copy-done.36, bf16[768,768]{1,0:T(8,128)(2,1)} %wq_ref.1, bf16[768,768]{1,0:T(8,128)(2,1)} %wk_ref.1, bf16[768,768]{1,0:T(8,128)(2,1)} %wv_ref.1, ...), custom_call_target="tpu_custom_call" | custom-call | flops 7247757312 | bytes 25165824 | tf_op jit(solution)/shard_map/finish/pallas_call | solution.py:404
  341.2 2.4 copy-done.2
  343.6 62.9 %all_sum.1.refs_0_.refs_1_.refs_2_.refs_3_ = bf16[18944,128]{1,0:T(8,128)(2,1)S(1)} custom-call(bf16[18944,128]{1,0:T(8,128)(2,1)S(1)} %copy-done.2), custom_call_target="tpu_custom_call" | custom-call | tf_op jit(solution)/shard_map/all_sum/pallas_call | solution.py:863
  406.5 2.2 copy-done
  408.7 0.8 slice_convert_fusion
  409.5 0.6 slice_bitcast_fusion
  410.1 0.6 slice_bitcast_fusion.1
  410.7 2.4 copy-done.1
  413.1 4.7 %unpack.1 = (f32[768,768]{1,0:T(8,128)}, f32[768,768]{1,0:T(8,128)}, f32[768,768]{1,0:T(8,128)}, f32[768,768]{1,0:T(8,128)}) custom-call(bf16[18944,128]{1,0:T(8,128)(2,1)S(1)} %copy-done.1, bf16[18944,128]{1,0:T(8,128)(2,1)S(1)} %copy-done.1, bf16[18944,128]{1,0:T(8,128)(2,1)S(1)} %copy-done.1, bf16[18944,128]{1,0:T(8,128)(2,1)S(1)} %copy-done.1), custom_call_target="tpu_custom_call" | custom-call | tf_op jit(solution)/shard_map/unpack/pallas_call | solution.py:434
  417.8 0.3 copy-done.27
  418.1 0.5 copy-done.30
  418.7 5.6 %mix.1 = bf16[1024,768]{1,0:T(8,128)(2,1)} custom-call(s32[1024,1]{1,0:T(8,128)S(1)} %copy-done.27, s32[1024,1]{1,0:T(8,128)S(1)} %copy-done.30, s32[1024,1]{1,0:T(8,128)S(1)} %bitcast.56, f32[1024,768]{1,0:T(8,128)S(1)} %copy-done.20, f32[1,768]{1,0:T(1,128)S(1)} %reshape.193.gain_ref, bf16[768,128]{1,0:T(8,128)(2,1)S(1)} %copy-done.9, ...), custom_call_target="tpu_custom_call" | custom-call | flops 3221225472 | bytes 8388608 | tf_op jit(solution)/shard_map/mix/pallas_call | solution.py:263
  424.4 0.8 copy.40
  (77 shorter events, 1.5 us)
Async XLA Ops:
  2.5 9.7 %copy-start.7 = (s32[1,1024]{0,1:T(8,128)}, s32[1,1024]{0,1:T(8,128)S(1)}, u32[]{:S(2)}) copy-start(s32[1,1024]{0,1:T(8,128)S(1)} %copy.42) | copy-start | bytes 12292
  2.5 1.6 copy-start.11
  12.2 0.8 copy-start.25
  13.0 0.8 copy-start.28
  13.9 8.0 %copy-start.42 = (f32[768]{0:T(1024)S(1)}, f32[768]{0:T(1024)}, u32[]{:S(2)}) copy-start(f32[768]{0:T(1024)} %param.24) | copy-start | bytes 9220
  13.9 8.0 %copy-start.43 = (f32[768]{0:T(1024)S(1)}, f32[768]{0:T(1024)}, u32[]{:S(2)}) copy-start(f32[768]{0:T(1024)} %param.23) | copy-start | bytes 9220
  13.9 8.0 %copy-start.41 = (f32[32,12]{0,1:T(8,128)S(1)}, f32[32,12]{0,1:T(8,128)}, u32[]{:S(2)}) copy-start(f32[32,12]{0,1:T(8,128)} %param.25) | copy-start | bytes 4612
  13.9 79.4 %all-to-all-start = ((bf16[32,64,768]{2,1,0:T(8,128)(2,1)}), bf16[32,64,768]{2,1,0:T(8,128)(2,1)}, u32[]{:S(2)}, u32[]{:S(2)}) async-start(bf16[32,64,768]{2,1,0:T(8,128)(2,1)} %bitcast.69), calls=%async_computation | async-start | bytes 6291456 | tf_op jit(solution)/shard_map/all_to_all | solution.py:165
  21.8 3.4 copy-start.10
  24.4 1.3 copy-start.18
  25.1 1.5 copy-start.13
  25.1 1.8 copy-start.16
  25.1 2.2 copy-start.17
  27.3 4.8 %copy-start.19 = (s32[2]{0:T(128)S(1)}, s32[2]{0:T(128)}, u32[]{:S(2)}) copy-start(s32[2]{0:T(128)} %len_ref.1) | copy-start | bytes 28
  32.1 20.8 %copy-start.31 = (bf16[1024,2304]{1,0:T(8,128)(2,1)}, bf16[1024,2304]{1,0:T(8,128)(2,1)S(1)}, u32[]{:S(2)}) copy-start(bf16[1024,2304]{1,0:T(8,128)(2,1)S(1)} %get-tuple-element.85.q_ref.k_ref.v_ref) | copy-start | bytes 14155780
  32.1 20.8 %copy-start.33 = (bf16[1024,768]{1,0:T(8,128)(2,1)}, bf16[1024,768]{1,0:T(8,128)(2,1)S(1)}, u32[]{:S(2)}) copy-start(bf16[1024,768]{1,0:T(8,128)(2,1)S(1)} %get-tuple-element.126.normed_ref) | copy-start | bytes 4718596
  32.1 20.8 %copy-start.14 = (bf16[768,768]{1,0:T(8,128)(2,1)S(1)}, bf16[768,768]{1,0:T(8,128)(2,1)}, u32[]{:S(2)}) copy-start(bf16[768,768]{1,0:T(8,128)(2,1)} %w_ref.1) | copy-start | bytes 3538948
  61.9 1.2 copy-start.22
  135.1 3.3 copy-start.40
  135.1 41.0 %all-to-all-start.2 = ((bf16[32,32,768]{2,1,0:T(8,128)(2,1)}), bf16[32,32,768]{2,1,0:T(8,128)(2,1)S(1)}, u32[]{:S(2)}, u32[]{:S(2)}) async-start(bf16[32,32,768]{2,1,0:T(8,128)(2,1)} %bitcast.12), calls=%async_computation.2 | async-start | bytes 3145728 | tf_op jit(solution)/shard_map/all_to_all | solution.py:165
  176.1 4.0 copy-start.39
  176.1 41.7 %all-to-all-start.3 = ((bf16[32,32,768]{2,1,0:T(8,128)(2,1)}), bf16[32,32,768]{2,1,0:T(8,128)(2,1)S(1)}, u32[]{:S(2)}, u32[]{:S(2)}) async-start(bf16[32,32,768]{2,1,0:T(8,128)(2,1)} %bitcast.72), calls=%async_computation.3 | async-start | bytes 3145728 | tf_op jit(solution)/shard_map/all_to_all | solution.py:165
  217.8 7.6 %copy-start.3 = (bf16[32,32,768]{2,1,0:T(8,128)(2,1)}, bf16[32,32,768]{2,1,0:T(8,128)(2,1)S(1)}, u32[]{:S(2)}) copy-start(bf16[32,32,768]{2,1,0:T(8,128)(2,1)S(1)} %all-to-all-done.3) | copy-start | bytes 4718596
  217.8 41.5 %all-to-all-start.4 = ((bf16[32,32,768]{2,1,0:T(8,128)(2,1)}), bf16[32,32,768]{2,1,0:T(8,128)(2,1)S(1)}, u32[]{:S(2)}, u32[]{:S(2)}) async-start(bf16[32,32,768]{2,1,0:T(8,128)(2,1)} %bitcast.73), calls=%async_computation.4 | async-start | bytes 3145728 | tf_op jit(solution)/shard_map/all_to_all | solution.py:165
  259.3 1.1 copy-start.5
  260.5 148.2 %all-to-all-start.5 = ((bf16[32,64,768]{2,1,0:T(8,128)(2,1)}), bf16[32,64,768]{2,1,0:T(8,128)(2,1)S(1)}, u32[]{:S(2)}, u32[]{:S(2)}) async-start(bf16[32,64,768]{2,1,0:T(8,128)(2,1)} %pad_maximum_fusion), calls=%async_computation.5 | async-start | bytes 6291456 | tf_op jit(solution)/shard_map/all_to_all | solution.py:165
  266.5 1.4 copy-start.4
  267.9 1.4 copy-start.6
  269.3 1.4 copy-start.12
  270.7 1.3 copy-start.15
  272.0 1.4 copy-start.23
  273.4 1.0 copy-start.26
  274.4 1.0 copy-start.29
  286.9 1.6 copy-start.21
  288.5 1.0 copy-start.24
  289.5 30.7 %copy-start.37 = (f32[1,768]{1,0:T(1,128)}, f32[1,768]{1,0:T(1,128)S(1)}, u32[]{:S(2)}) copy-start(f32[1,768]{1,0:T(1,128)S(1)} %get-tuple-element.131.gg2_ref) | copy-start | bytes 9220
  289.5 2.3 copy-start.32
  320.2 1.1 copy-start.34
  321.4 1.1 copy-start.35
  322.5 1.1 copy-start.36
  323.6 0.6 copy-start.38
  341.2 2.4 copy-start.2
  406.5 2.2 copy-start
  410.7 2.4 copy-start.1
  413.1 4.7 %copy-start.8 = (s32[1,1024]{0,1:T(8,128)S(1)}, s32[1,1024]{0,1:T(8,128)}, u32[]{:S(2)}) copy-start(s32[1,1024]{0,1:T(8,128)} %copy-done.7) | copy-start | bytes 12292
  413.1 4.7 %copy-start.9 = (bf16[768,128]{1,0:T(8,128)(2,1)S(1)}, bf16[768,128]{1,0:T(8,128)(2,1)}, u32[]{:S(2)}) copy-start(bf16[768,128]{1,0:T(8,128)(2,1)} %pad.4.wr_ref) | copy-start | bytes 589828
  413.1 4.7 %copy-start.20 = (f32[1024,768]{1,0:T(8,128)S(1)}, f32[1024,768]{1,0:T(8,128)}, u32[]{:S(2)}) copy-start(f32[1024,768]{1,0:T(8,128)} %get-tuple-element.91.y_ref) | copy-start | bytes 9437188
  413.1 5.0 %copy-start.27 = (s32[1024,1]{1,0:T(8,128)S(1)}, s32[1024,1]{1,0:T(8,128)}, u32[]{:S(2)}) copy-start(s32[1024,1]{1,0:T(8,128)} %copy-done.25) | copy-start | bytes 12292
  413.1 5.6 %copy-start.30 = (s32[1024,1]{1,0:T(8,128)S(1)}, s32[1024,1]{1,0:T(8,128)}, u32[]{:S(2)}) copy-start(s32[1024,1]{1,0:T(8,128)} %copy-done.28) | copy-start | bytes 12292

commit v4 on v3

v4 whole, which is shorter than its diff:
```python
import functools

import jax
import jax.numpy as jnp
from jax import lax
from jax.experimental import pallas as pl
from jax.experimental.pallas import tpu as pltpu
from jax.sharding import PartitionSpec as P

EPSILON = 1e-06
NEGATIVE = -1e30
THRESHOLDS = (12, 16, 23, 32, 46, 64, 91)
LOG2E = 1.4426950408889634
TILE = 128
GELU_A = 0.7978845608028654
GELU_B = GELU_A * 0.044715
AXES = ("grp", "exp")
LOW = jnp.bfloat16


def dot(a, b):
    return jnp.dot(a, b, preferred_element_type=jnp.float32)


def dot_t(a, b):
    return lax.dot_general(a, b, (((1,), (1,)), ((), ())), preferred_element_type=jnp.float32)


def params(mib, **more):
    return pltpu.CompilerParams(vmem_limit_bytes=mib << 20, **more)


def whole(shape):
    return pl.BlockSpec(shape, lambda *_: (0,) * len(shape), pipeline_mode=pl.Buffered(1))


def cost(flops, bytes_accessed, transcendentals=0):
    return pl.CostEstimate(
        flops=flops, bytes_accessed=bytes_accessed, transcendentals=transcendentals
    )


def bucket_of(offset):
    distance = jnp.abs(offset)
    far = jnp.full_like(distance, 8)
    for border in THRESHOLDS:
        far = far + (distance >= border).astype(jnp.int32)
    return jnp.where(distance < 8, distance, far) + jnp.where(offset > 0, 16, 0).astype(jnp.int32)


def plan(room):
    if room % 64:
        return ((0, room),), room, 0
    return ((0, room // 2), (room // 2, room)), 3 * room // 4, room // 4


def segment(code, room, low, high):
    expert = lax.div(code, room)
    place = code - expert * room
    inside = (code >= 0) & (place >= low) & (place < high)
    return jnp.where(inside, expert * (high - low) + place - low, -1)


def spread(dest, values, out):
    rows = out.shape[0]
    step = min(256, rows)
    for start in range(0, rows, step):
        here = lax.broadcasted_iota(jnp.int32, (step, dest.shape[1]), 0) + start
        out[start : start + step] = dot((dest == here).astype(LOW), values).astype(LOW)


def collect(dest, values):
    here = lax.broadcasted_iota(jnp.int32, (dest.shape[0], values.shape[0]), 1)
    return dot((dest == here).astype(LOW), values)


def spread_all(code, room, values, outs):
    for (low, high), out in zip(plan(room)[0], outs):
        spread(segment(code, room, low, high), values, out)


def collect_all(code, room, refs):
    total = None
    for (low, high), ref in zip(plan(room)[0], refs):
        part = collect(segment(code, room, low, high), ref[...])
        total = part if total is None else total + part
    return total


def buffers(experts, room, width):
    return [
        jax.ShapeDtypeStruct((experts * (high - low), width), LOW) for low, high in plan(room)[0]
    ]


def route_kernel(
    experts, room, eid_c, eid_r, slot_c, slot_r, g_ref, code_c, code_r, rank_c, out, more
):
    tokens = g_ref.shape[0]
    wide = max(TILE, experts)
    _, cut, extra = plan(room)
    at = lax.broadcasted_iota(jnp.int32, (tokens, tokens), 0)
    to = lax.broadcasted_iota(jnp.int32, (tokens, tokens), 1)
    before = (to < at).astype(LOW)
    after = (at < to).astype(LOW)

    ids = eid_c[...]
    picked = ids == lax.broadcasted_iota(jnp.int32, (tokens, wide), 1)
    place = jnp.sum(jnp.where(picked, dot(before, picked.astype(LOW)), 0.0), axis=1, keepdims=True)
    place = place.astype(jnp.int32)
    kept = slot_c[...] >= 0
    code_c[...] = jnp.where(kept, ids * room + place, -1)
    over = jnp.broadcast_to(jnp.where(kept & (place >= cut), 1.0, 0.0), (tokens, TILE))
    rank = jnp.where(over > 0, dot(before, over.astype(LOW)).astype(jnp.int32), -1)
    rank_c[...] = rank[:, :1]
    ids = eid_r[...]
    picked = ids == lax.broadcasted_iota(jnp.int32, (wide, tokens), 0)
    place = jnp.sum(jnp.where(picked, dot(picked.astype(LOW), after), 0.0), axis=0, keepdims=True)
    place = place.astype(jnp.int32)
    kept = slot_r[...] >= 0
    code = jnp.where(kept, ids * room + place, -1)
    code_r[...] = code
    over = jnp.broadcast_to(jnp.where(kept & (place >= cut), 1.0, 0.0), (16, tokens))
    rank = jnp.where(over > 0, dot(over.astype(LOW), after).astype(jnp.int32), -1)[:1]
    spread(segment(code, room, 0, cut), g_ref[...], out)
    if not extra:
        more[...] = jnp.zeros(more.shape, LOW)
        return
    spread(rank, g_ref[...], more.at[:extra])
    rank = rank_c[...]
    lane = lax.broadcasted_iota(jnp.int32, (tokens, g_ref.shape[1]), 1)
    marks = jnp.where((rank == lane) & (lane < extra), eid_c[...] + 1, 0)
    marks = marks.astype(jnp.float32)
    marks = jnp.sum(marks, axis=0, keepdims=True)
    left = jnp.max(jnp.where(rank >= extra, 1.0, 0.0), axis=0, keepdims=True)
    marks = jnp.where(lane[:1] == extra, left, marks)
    line = lax.broadcasted_iota(jnp.int32, (more.shape[0] - extra, g_ref.shape[1]), 0)
    more[extra:] = jnp.where(line == 0, marks, 0.0).astype(LOW)


def route(expert_ids, slots, upstream, experts, room):
    tokens, width = upstream.shape
    column = jax.ShapeDtypeStruct((tokens, 1), jnp.int32)
    line = jax.ShapeDtypeStruct((1, tokens), jnp.int32)
    _, cut, extra = plan(room)
    return pl.pallas_call(
        functools.partial(route_kernel, experts, room),
        out_shape=[
            column, line, column,
            jax.ShapeDtypeStruct((experts * cut, width), LOW),
            jax.ShapeDtypeStruct((extra + 16, width), LOW),
        ],
        compiler_params=params(48),
        cost_estimate=cost(2 * experts * room * tokens * width, 8 << 20),
        name="route",
    )(
        expert_ids.reshape(tokens, 1), expert_ids.reshape(1, tokens),
        slots.reshape(tokens, 1), slots.reshape(1, tokens), upstream,
    )


def exchange(buffer, devices):
    shaped = buffer.reshape(devices, buffer.shape[0] // devices, buffer.shape[1])
    moved = lax.all_to_all(shaped, AXES, split_axis=0, concat_axis=0, tiled=True)
    return moved.reshape(buffer.shape)


def project_kernel(x_ref, gain_ref, wq_ref, wk_ref, wv_ref, normed_ref, out_ref):
    x = x_ref[...].astype(jnp.float32)
    rms = lax.rsqrt(jnp.mean(x * x, axis=-1, keepdims=True) + EPSILON)
    normed = (x * rms * gain_ref[...]).astype(LOW)
    normed_ref[...] = normed.T
    width = x.shape[1]
    for n, w_ref in enumerate((wq_ref, wk_ref, wv_ref)):
        out_ref[:, n * width : (n + 1) * width] = dot(normed, w_ref[...]).astype(LOW)


def project(x, gain, w_query, w_key, w_value):
    tokens, width = x.shape
    out = 3 * width
    step = 256
    rows = lambda w: pl.BlockSpec((step, w), lambda i: (i, 0))
    return pl.pallas_call(
        project_kernel,
        grid=(tokens // step,),
        in_specs=[rows(width), whole((1, width)), *[whole((width, width))] * 3],
        out_specs=[pl.BlockSpec((width, step), lambda i: (0, i)), rows(out)],
        out_shape=[
            jax.ShapeDtypeStruct((width, tokens), LOW),
            jax.ShapeDtypeStruct((tokens, out), LOW),
        ],
        compiler_params=params(60),
        cost_estimate=cost(2 * tokens * width * out, 12 << 20),
        name="project",
    )(x, gain, w_query, w_key, w_value)


def after_attention_kernel(
    experts, room, o_ref, x_ref, w_ref, gain_ref, eid_ref, wr_ref, code_ref, y_ref, gate_ref, *rest
):
    outs, held = rest[:-1], rest[-1]
    step = o_ref.shape[0]
    i = pl.program_id(0)
    y = x_ref[...].astype(jnp.float32) + dot(o_ref[...], w_ref[...])
    y_ref[...] = y
    rms = lax.rsqrt(jnp.mean(y * y, axis=-1, keepdims=True) + EPSILON)
    normed = (y * rms * gain_ref[...]).astype(LOW)
    held[pl.ds(pl.multiple_of(i * step, step), step), :] = normed
    router = route_softmax(dot(normed, wr_ref[...]), experts)
    lane = lax.broadcasted_iota(jnp.int32, router.shape, 1)
    gate_ref[...] = jnp.sum(jnp.where(lane == eid_ref[...], router, 0.0), axis=-1, keepdims=True)

    @pl.when(i == pl.num_programs(0) - 1)
    def _():
        spread_all(code_ref[...], room, held[...], outs)


def after_attention(joined, x, w_output, gain, expert_ids, w_router, code, experts, room):
    tokens, width = x.shape
    step = 256
    rows = pl.BlockSpec((step, width), lambda i: (i, 0))
    single = pl.BlockSpec((step, 1), lambda i: (i, 0))
    outs = buffers(experts, room, width)
    return pl.pallas_call(
        functools.partial(after_attention_kernel, experts, room),
        grid=(tokens // step,),
        in_specs=[
            rows, rows, whole((width, width)), whole((1, width)), single, whole(w_router.shape),
            whole((1, tokens)),
        ],
        out_specs=[rows, single] + [pl.BlockSpec(o.shape, lambda i: (0, 0)) for o in outs],
        out_shape=[
            jax.ShapeDtypeStruct((tokens, width), jnp.float32),
            jax.ShapeDtypeStruct((tokens, 1), jnp.float32),
        ]
        + outs,
        scratch_shapes=[pltpu.VMEM((tokens, width), LOW)],
        compiler_params=params(60),
        cost_estimate=cost(2 * tokens * width * (width + experts * room), 12 << 20),
        name="after_attention",
    )(joined, x, w_output, gain, expert_ids, w_router, code)


def route_softmax(logits, experts):
    lane = lax.broadcasted_iota(jnp.int32, logits.shape, 1)
    logits = jnp.where(lane < experts, logits, NEGATIVE)
    e = jnp.exp(logits - jnp.max(logits, axis=-1, keepdims=True))
    return e / jnp.sum(e, axis=-1, keepdims=True)


def pack(values, first, height, out, at):
    for c in range(values.shape[1] // TILE):
        out[at + c * height : at + (c + 1) * height] = values[
            first : first + height, c * TILE : (c + 1) * TILE
        ].astype(LOW)


def before_attention_kernel(
    room, n_backs, code_ref, y_ref, g_ref, gain_ref, w_ref, o_ref, *rest
):
    backs = rest[:n_backs]
    dy_ref, do_ref, pack_ref, gg_ref, gw_ref = rest[n_backs:]
    i = pl.program_id(0)

    @pl.when(i == 0)
    def _():
        gw_ref[...] = jnp.zeros_like(gw_ref)
        gg_ref[...] = jnp.zeros_like(gg_ref)

    dh = collect_all(code_ref[...], room, backs)
    y = y_ref[...]
    rms = lax.rsqrt(jnp.mean(y * y, axis=-1, keepdims=True) + EPSILON)
    gg_ref[...] += jnp.sum(dh * y * rms, axis=0, keepdims=True)
    u = dh * gain_ref[...]
    dy = (
        g_ref[...].astype(jnp.float32)
        + rms * u
        - y * (rms * rms * rms) * jnp.mean(u * y, axis=-1, keepdims=True)
    )
    dy_ref[...] = dy
    low = dy.astype(LOW)
    do_ref[...] = dot_t(low, w_ref[...]).astype(LOW)
    gw_ref[...] += dot(o_ref[...].T, low)

    @pl.when(i == pl.num_programs(0) - 1)
    def _():
        pack(gw_ref, 0, gw_ref.shape[0], pack_ref, 0)


def before_attention(backs, code, y, g, gain, w_output, joined, room):
    tokens, width = y.shape
    step = 256
    rows = lambda w: pl.BlockSpec((step, w), lambda i: (i, 0))
    return pl.pallas_call(
        functools.partial(before_attention_kernel, room, len(backs)),
        grid=(tokens // step,),
        in_specs=[
            rows(1), rows(width), rows(width), whole((1, width)),
            whole((width, width)), rows(width), *[whole(b.shape) for b in backs],
        ],
        out_specs=[
            rows(width), rows(width),
            pl.BlockSpec((width * width // TILE, TILE), lambda i: (0, 0)),
            pl.BlockSpec((1, width), lambda i: (0, 0)),
        ],
        out_shape=[
            jax.ShapeDtypeStruct((tokens, width), jnp.float32),
            jax.ShapeDtypeStruct((tokens, width), LOW),
            jax.ShapeDtypeStruct((width * width // TILE, TILE), LOW),
            jax.ShapeDtypeStruct((1, width), jnp.float32),
        ],
        scratch_shapes=[pltpu.VMEM((width, width), jnp.float32)],
        compiler_params=params(60),
        cost_estimate=cost(6 * tokens * width * width, 16 << 20),
        name="before_attention",
    )(code, y, g, gain, w_output, joined, *backs)


def unpack_kernel(
    experts, heads, buckets, q_ref, k_ref, v_ref, o_ref, small_ref, part_ref, gate_ref, rank_ref, *refs
):
    more, (gq, gk, gv, go, router, gains, table, mixed) = refs[:-8], refs[-8:]
    for packed_ref, out_ref in ((q_ref, gq), (k_ref, gk), (v_ref, gv), (o_ref, go)):
        out_ref[...] = packed_ref[...].astype(jnp.float32)
    part = part_ref[...]
    if more:
        extra_ref, late_ref = more
        ff = collect(rank_ref[...], extra_ref[...]) + late_ref[...].astype(jnp.float32)
        part = part + gate_ref[...] * ff
    mixed[...] = part.astype(LOW)

    @pl.when(pl.program_id(0) == 0)
    def _():
        lines = router.shape[1] // TILE
        small = small_ref[...].astype(jnp.float32)
        for c in range(lines):
            lanes = slice(c * TILE, (c + 1) * TILE)
            router[:, lanes] = small[c * experts : (c + 1) * experts]
            for n in range(2):
                at = lines * experts + n * lines + c
                gains[n : n + 1, lanes] = small[at : at + 1]
        at = lines * experts + -(-2 * lines // 16) * 16
        table[...] = small[at : at + heads, :buckets]


def unpack(packed, part, gate, rank, more, width, experts, heads, buckets, small_rows):
    blocks = width // TILE
    tokens = part.shape[0]
    source = lambda m: pl.BlockSpec((width, TILE), lambda i: (m * blocks + i, 0))
    column = lambda rows: pl.BlockSpec((rows, TILE), lambda i: (0, i))
    kept = lambda shape: pl.BlockSpec(shape, lambda i: (0, 0))
    return pl.pallas_call(
        functools.partial(unpack_kernel, experts, heads, buckets),
        grid=(blocks,),
        in_specs=[source(m) for m in range(4)]
        + [pl.BlockSpec((small_rows, TILE), lambda i: (4 * blocks * width // small_rows, 0))]
        + [column(tokens), whole((tokens, 1)), whole((tokens, 1))]
        + [column(m.shape[0]) for m in more],
        out_specs=[column(width)] * 4
        + [kept((experts, width)), kept((2, width)), kept((heads, buckets)), column(tokens)],
        out_shape=[jax.ShapeDtypeStruct((width, width), jnp.float32)] * 4
        + [
            jax.ShapeDtypeStruct((experts, width), jnp.float32),
            jax.ShapeDtypeStruct((2, width), jnp.float32),
            jax.ShapeDtypeStruct((heads, buckets), jnp.float32),
            jax.ShapeDtypeStruct((tokens, width), LOW),
        ],
        compiler_params=params(60),
        name="unpack",
    )(*[packed] * 5, part, gate, rank, *more)


def attention_forward_kernel(len_ref, q_ref, k_ref, v_ref, near_ref, far_ref, o_ref, p_ref, s_ref):
    seq = q_ref.shape[0]
    tiles = seq // TILE
    half = q_ref.shape[1] // 2
    row = pl.program_id(0)
    pair = pl.program_id(1)
    live = len_ref[row]
    lane = lax.broadcasted_iota(jnp.int32, (seq, 2 * half), 1)
    dead = lax.broadcasted_iota(jnp.int32, (seq, 2 * half), 0) >= live
    q = q_ref[...]
    k = k_ref[...]
    v_t = v_ref[...].T
    outs = []
    for h in range(2):
        mine = (lane >= h * half) & (lane < (h + 1) * half)
        flag = lane == (1 - h) * half
        k_h = jnp.where(mine, k, jnp.where(flag & dead, -1e30, 0.0).astype(k.dtype))
        q_h = jnp.where(flag, jnp.ones_like(q), q)
        after = far_ref[2 * pair + h, 0]
        before = far_ref[2 * pair + h, 1]
        tops = []
        for i in range(tiles):
            q_i = q_h[i * TILE:(i + 1) * TILE]
            raw = lax.dot_general(k_h, q_i, (((1,), (1,)), ((), ())), preferred_element_type=jnp.float32)
            top = None
            for j in range(tiles):
                x = raw[j * TILE:(j + 1) * TILE] * (0.125 * LOG2E)
                d = j - i
                if -1 <= d <= 1:
                    x = x + near_ref[h, d + 1]
                else:
                    x = x + (after if d > 0 else before)
                s_ref[j * TILE:(j + 1) * TILE, i * TILE:(i + 1) * TILE] = x
                m = jnp.max(x, axis=0, keepdims=True)
                top = m if top is None else jnp.maximum(top, m)
            tops.append(top)
        for i in range(tiles):
            e = jnp.exp2(s_ref[:, i * TILE:(i + 1) * TILE] - tops[i])
            total = jnp.sum(e, axis=0, keepdims=True)
            p_ref[0, h, :, i * TILE:(i + 1) * TILE] = (e * (1.0 / total)).astype(LOW)
        outs.append(lax.dot_general(v_t[h * half:(h + 1) * half], p_ref[0, h], (((1,), (0,)), ((), ())), preferred_element_type=jnp.float32))
    o_ref[...] = jnp.concatenate(outs, axis=0).T.astype(o_ref.dtype)

def attention_forward(lengths, projected, near, far, rows, seq, heads, head):
    width = heads * head
    pairs = heads // 2
    spec = lambda off: pl.BlockSpec((seq, 2 * head), lambda b, p: (b, off + p))
    return pl.pallas_call(
        attention_forward_kernel,
        grid=(rows, pairs),
        in_specs=[
            pl.BlockSpec(memory_space=pltpu.SMEM),
            spec(0), spec(pairs), spec(2 * pairs),
            pl.BlockSpec((2, 3, TILE, TILE), lambda b, p: (p, 0, 0, 0)),
            pl.BlockSpec(memory_space=pltpu.SMEM),
        ],
        out_specs=[
            pl.BlockSpec((seq, 2 * head), lambda b, p: (b, p)),
            pl.BlockSpec((1, 2, seq, seq), lambda b, p: (b, p, 0, 0)),
        ],
        out_shape=[
            jax.ShapeDtypeStruct((rows * seq, width), LOW),
            jax.ShapeDtypeStruct((rows, heads, seq, seq), LOW),
        ],
        scratch_shapes=[pltpu.VMEM((seq, seq), jnp.float32)],
        compiler_params=params(40),
        cost_estimate=cost(flops=4 * rows * heads * seq * seq * head * 4, bytes_accessed=rows * heads * seq * seq * 2, transcendentals=rows * heads * seq * seq),
        name="attention_forward",
    )(lengths, projected, projected, projected, near, far)

def attention_backward_kernel(
    q_ref, k_ref, v_ref, do_ref, o_ref, p_ref, nt_ref, wq_ref, wk_ref, wv_ref, x_ref, dy_ref, gain_ref,
    gr_ref, gg2_ref, out_ref, pack_ref, small_ref,
    near_ref, far_ref, d_ref, lines_ref, acc_ref, dh_ref, gg_ref,
):
    seq = q_ref.shape[0]
    tiles = seq // TILE
    half = q_ref.shape[1] // 2
    width = x_ref.shape[1]
    pair = pl.program_id(0)
    row = pl.program_id(1)
    last_pair = pair == pl.num_programs(0) - 1
    last_row = row == pl.num_programs(1) - 1
    lane = lax.broadcasted_iota(jnp.int32, (seq, 2 * half), 1)
    q = q_ref[...]
    k = k_ref[...]
    k_t = k.T
    v = v_ref[...]
    do = do_ref[...]
    weighed = (do.astype(jnp.float32) * o_ref[...].astype(jnp.float32)).T
    dq_parts = []
    dk_all = None
    dv_all = None

    @pl.when(row == 0)
    def _():
        near_ref[...] = jnp.zeros_like(near_ref)
        far_ref[...] = jnp.zeros_like(far_ref)
        acc_ref[...] = jnp.zeros_like(acc_ref)

    for h in range(2):
        mine = (lane >= h * half) & (lane < (h + 1) * half)
        v_h = jnp.where(mine, v, jnp.zeros_like(v))
        delta = jnp.sum(weighed[h * half : (h + 1) * half], axis=0, keepdims=True)
        far_sum = [jnp.zeros((8, TILE), jnp.float32), jnp.zeros((8, TILE), jnp.float32)]
        for i in range(tiles):
            cols = slice(i * TILE, (i + 1) * TILE)
            dp = dot_t(v_h, do[cols])
            for j in range(tiles):
                rws = slice(j * TILE, (j + 1) * TILE)
                ds = p_ref[0, h, rws, cols].astype(jnp.float32) * (dp[rws] - delta[:, cols])
                d = j - i
                if -1 <= d <= 1:
                    near_ref[h, d + 1] += ds
                else:
                    which = 0 if d > 0 else 1
                    far_sum[which] = far_sum[which] + jnp.sum(ds.reshape(TILE // 8, 8, TILE), axis=0)
                d_ref[rws, cols] = ds.astype(LOW)
        far_ref[h, 0] += far_sum[0]
        far_ref[h, 1] += far_sum[1]
        ds_all = d_ref[...]
        dq_parts.append(dot(k_t[h * half : (h + 1) * half], ds_all))
        dk_h = dot(ds_all, q)
        dv_h = dot(p_ref[0, h], do)
        dk_all = dk_h if h == 0 else jnp.where(mine, dk_h, dk_all)
        dv_all = dv_h if h == 0 else jnp.where(mine, dv_h, dv_all)

    dq = (jnp.concatenate(dq_parts, axis=0).T * 0.125).astype(LOW)
    grads = jnp.concatenate([dq, (dk_all * 0.125).astype(LOW), dv_all.astype(LOW)], axis=1)
    acc_ref[...] += dot(nt_ref[...], grads)
    weights = jnp.concatenate([wq_ref[...], wk_ref[...], wv_ref[...]], axis=1)
    dh = dot_t(grads, weights)
    here = pl.ds(pl.multiple_of(row * seq, seq), seq)

    @pl.when(pair == 0)
    def _():
        dh_ref[here, :] = dh

    @pl.when(pair > 0)
    def _():
        dh_ref[here, :] += dh

    @pl.when(last_row)
    def _():
        bucket_sums(near_ref, far_ref, lines_ref, 2 * pair)
        for n in range(3):
            pack_ref[n, 0] = acc_ref[:, n * TILE : (n + 1) * TILE].astype(LOW)

    @pl.when(last_pair & (row == 0))
    def _():
        gg_ref[...] = jnp.zeros_like(gg_ref)

    @pl.when(last_pair)
    def _():
        total = dh_ref[here, :]
        x = x_ref[...].astype(jnp.float32)
        rms = lax.rsqrt(jnp.mean(x * x, axis=-1, keepdims=True) + EPSILON)
        gg_ref[...] += jnp.sum(total * x * rms, axis=0, keepdims=True)
        u = total * gain_ref[...]
        out_ref[...] = (
            dy_ref[...]
            + rms * u
            - x * (rms * rms * rms) * jnp.mean(u * x, axis=-1, keepdims=True)
        )

    @pl.when(last_pair & last_row)
    def _():
        at = gr_ref.shape[0]
        small_ref[:at] = gr_ref[...].astype(LOW)
        lines = width // TILE
        gains = [gg_ref[:, c * TILE : (c + 1) * TILE] for c in range(lines)]
        gains += [gg2_ref[:, c * TILE : (c + 1) * TILE] for c in range(lines)]
        if 2 * lines % 16:
            gains += [jnp.zeros((16 - 2 * lines % 16, TILE), jnp.float32)]
        gains = jnp.concatenate(gains, axis=0)
        small_ref[at : at + gains.shape[0]] = gains.astype(LOW)
        at = at + gains.shape[0]
        table = bucket_table(lines_ref)
        if table.shape[0] % 16:
            table = jnp.concatenate([table, jnp.zeros((16 - table.shape[0] % 16, TILE), jnp.float32)], axis=0)
        small_ref[at : at + table.shape[0]] = table.astype(LOW)
        at = at + table.shape[0]
        small_ref[at:] = jnp.zeros((small_ref.shape[0] - at, TILE), LOW)


def bucket_sums(near_ref, far_ref, lines_ref, first):
    empty = jnp.zeros((8, TILE), jnp.float32)
    sub = lax.broadcasted_iota(jnp.int32, (8, 2 * TILE), 0)
    for h in range(2):
        lines = []
        for d in range(3):
            turned = None
            for a in range(0, TILE, 8):
                part = jnp.concatenate([near_ref[h, d, a : a + 8], empty], axis=1)
                part = pltpu.roll(part, (2 * TILE - a) % (2 * TILE), 1) if a else part
                turned = part if turned is None else turned + part
            for b in (1, 2, 4):
                turned = jnp.where((sub & b) > 0, pltpu.roll(turned, 2 * TILE - b, 1), turned)
            lines.append(jnp.sum(turned, axis=0, keepdims=True))
        for side in range(2):
            total = jnp.sum(far_ref[h, side], axis=0, keepdims=True)
            lines.append(jnp.concatenate([total, jnp.zeros((1, TILE), jnp.float32)], axis=1))
        lines.append(jnp.zeros((3, 2 * TILE), jnp.float32))
        lines_ref[first + h] = jnp.concatenate(lines, axis=0)


def bucket_table(lines_ref):
    heads = lines_ref.shape[0]
    buckets = 4 * 8
    lane = lax.broadcasted_iota(jnp.int32, (2 * TILE, TILE), 0)
    bucket = lax.broadcasted_iota(jnp.int32, (2 * TILE, TILE), 1)
    turn = jnp.where(lane >= TILE, lane - 2 * TILE, lane)
    total = None
    for r in range(5):
        if r < 3:
            hit = bucket_of((r - 1) * TILE - turn) == bucket
        else:
            hit = bucket == (buckets - 1 if r == 3 else buckets // 2 - 1)
        hit = hit.astype(LOW)
        line = jnp.concatenate([lines_ref[h, r : r + 1, :] for h in range(heads)], axis=0)
        high = line.astype(LOW)
        part = dot(high, hit) + dot((line - high.astype(jnp.float32)).astype(LOW), hit)
        total = part if total is None else total + part
    return total


def attention_backward(
    projected, do, joined, weights, normed_t, w_query, w_key, w_value, x, dy, gain, gr, gg2,
    rows, seq, heads, head, small_rows,
):
    width = heads * head
    pairs = heads // 2
    spec = lambda off: pl.BlockSpec((seq, 2 * head), lambda p, b: (b, off + p))
    column = pl.BlockSpec((width, 2 * head), lambda p, b: (0, p))
    at_end = pl.BlockSpec((seq, width), lambda p, b: (b * (p // (pairs - 1)), 0))
    return pl.pallas_call(
        attention_backward_kernel,
        grid=(pairs, rows),
        in_specs=[
            spec(0), spec(pairs), spec(2 * pairs), spec(0), spec(0),
            pl.BlockSpec((1, 2, seq, seq), lambda p, b: (b, p, 0, 0)),
            pl.BlockSpec((width, seq), lambda p, b: (0, b)),
            column, column, column, at_end, at_end,
            whole((1, width)), whole(gr.shape), whole(gg2.shape),
        ],
        out_specs=[
            at_end,
            pl.BlockSpec((3, 1, width, TILE), lambda p, b: (0, p, 0, 0)),
            pl.BlockSpec((small_rows, TILE), lambda p, b: (0, 0)),
        ],
        out_shape=[
            jax.ShapeDtypeStruct((rows * seq, width), jnp.float32),
            jax.ShapeDtypeStruct((3, pairs, width, TILE), LOW),
            jax.ShapeDtypeStruct((small_rows, TILE), LOW),
        ],
        scratch_shapes=[
            pltpu.VMEM((2, 3, TILE, TILE), jnp.float32),
            pltpu.VMEM((2, 2, 8, TILE), jnp.float32),
            pltpu.VMEM((seq, seq), LOW),
            pltpu.VMEM((heads, 8, 2 * TILE), jnp.float32),
            pltpu.VMEM((width, 3 * TILE), jnp.float32),
            pltpu.VMEM((rows * seq, width), jnp.float32),
            pltpu.VMEM((1, width), jnp.float32),
        ],
        compiler_params=params(60),
        cost_estimate=cost(8 * rows * heads * seq * seq * head * 4, rows * heads * seq * seq * 2),
        name="attention_backward",
    )(
        projected, projected, projected, do, joined, weights, normed_t, w_query, w_key, w_value,
        x, dy, gain, gr, gg2,
    )


def bias_tiles(table):
    j = lax.broadcasted_iota(jnp.int32, (3, TILE, TILE), 1)
    i = lax.broadcasted_iota(jnp.int32, (3, TILE, TILE), 2)
    d = lax.broadcasted_iota(jnp.int32, (3, TILE, TILE), 0) - 1
    b = bucket_of(d * TILE + j - i)
    scaled = table.T * LOG2E
    hot = (b.reshape(1, -1) == jnp.arange(table.shape[0], dtype=jnp.int32)[:, None]).astype(jnp.float32)
    near = jnp.dot(scaled, hot, precision=lax.Precision.HIGHEST).reshape(-1, 3, TILE, TILE)
    far = jnp.stack([scaled[:, -1], scaled[:, table.shape[0] // 2 - 1]], axis=1)
    return near, far


def expert_kernel(experts, chunk, x_ref, g_ref, mine_ref, wr_ref, wi_any, wo_any,
                  ff_ref, dx_ref, hid_ref, da_ref, xt_ref, dfft_ref, gr_ref, wi_ref, wo_ref, sem):
    inner = wi_ref.shape[1]
    first_step = pl.program_id(0) == 0

    def loads(f):
        cols = pl.ds(f, chunk)
        return (pltpu.make_async_copy(wi_any.at[:, cols], wi_ref.at[:, cols], sem.at[0, f // chunk]),
                pltpu.make_async_copy(wo_any.at[cols, :], wo_ref.at[cols, :], sem.at[1, f // chunk]))

    @pl.when(first_step)
    def _():
        for f in range(0, inner, chunk):
            for c in loads(f):
                c.start()
        gr_ref[...] = jnp.zeros_like(gr_ref)

    x = x_ref[...]
    g = g_ref[...].reshape(x.shape).astype(jnp.float32)
    mine = mine_ref[...]
    lane = lax.broadcasted_iota(jnp.int32, (1, wr_ref.shape[1]), 1)
    logits = jnp.dot(x, wr_ref[...], preferred_element_type=jnp.float32)
    logits = jnp.where(lane < experts, logits, -1e30)
    e = jnp.exp(logits - jnp.max(logits, axis=-1, keepdims=True))
    router = e / jnp.sum(e, axis=-1, keepdims=True)
    gate = jnp.sum(router * mine, axis=-1, keepdims=True)
    dff = (g * gate).astype(LOW)
    ff = None
    dx = None
    def first(f):
        @pl.when(first_step)
        def _():
            for c in loads(f):
                c.wait()
        cols = slice(f, f + chunk)
        return (jnp.dot(x, wi_ref[:, cols], preferred_element_type=jnp.float32),
                lax.dot_general(dff, wo_ref[cols, :], (((1,), (1,)), ((), ())), preferred_element_type=jnp.float32))
    for f in range(0, inner, chunk):
        cols = slice(f, f + chunk)
        a, dhid = first(f)
        u = a * a
        t = jnp.tanh(a * (GELU_A + GELU_B * u))
        h = 0.5 + 0.5 * t
        hid = a * h
        slope = h + hid * ((1.0 - t) * (GELU_A + (3.0 * GELU_B) * u))
        da = (dhid * slope).astype(LOW)
        hid = hid.astype(LOW)
        hid_ref[:, cols] = hid
        da_ref[:, cols] = da
        ff_part = jnp.dot(hid, wo_ref[cols, :], preferred_element_type=jnp.float32)
        dx_part = lax.dot_general(da, wi_ref[:, cols], (((1,), (1,)), ((), ())), preferred_element_type=jnp.float32)
        ff = ff_part if ff is None else ff + ff_part
        dx = dx_part if dx is None else dx + dx_part
    ff = ff.astype(LOW)
    ff_ref[...] = ff
    dgate = jnp.sum(g * ff.astype(jnp.float32), axis=-1, keepdims=True)
    dlogits = ((gate * dgate) * (mine - router)).astype(LOW)
    dx = dx + lax.dot_general(dlogits, wr_ref[...], (((1,), (1,)), ((), ())), preferred_element_type=jnp.float32)
    dx_ref[...] = dx.astype(LOW)
    x_t = x.T
    xt_ref[...] = x_t
    dfft_ref[...] = dff.T
    gr_ref[...] += dot(dlogits.T, x)

def expert_rows(x, g, mine, wr, wi, wo, experts, low, high, tile=256, chunk=768):
    n, width = x.shape
    inner = wi.shape[1]
    sources, room = g.shape[0], high - low
    group = max(1, min(sources, tile // room))
    while sources % group or (group * room) % TILE:
        group += 1
    tile = group * room
    gspec = pl.BlockSpec((group, room, width), lambda i: (i, low // room, 0))
    once = lambda s: pl.BlockSpec(s, lambda i: (0,) * len(s), pipeline_mode=pl.Buffered(1))
    rowspec = lambda w: pl.BlockSpec((tile, w), lambda i: (i, 0))
    anywhere = pl.BlockSpec(memory_space=pl.ANY)
    return pl.pallas_call(
        functools.partial(expert_kernel, experts, chunk),
        grid=(n // tile,),
        in_specs=[rowspec(width), gspec, once(mine.shape), once(wr.shape), anywhere, anywhere],
        out_specs=[rowspec(width), rowspec(width), rowspec(inner), rowspec(inner),
                   pl.BlockSpec((width, tile), lambda i: (0, i)), pl.BlockSpec((width, tile), lambda i: (0, i)),
                   pl.BlockSpec((wr.shape[1], width), lambda i: (0, 0))],
        out_shape=[jax.ShapeDtypeStruct((n, width), LOW)] * 2 + [jax.ShapeDtypeStruct((n, inner), LOW)] * 2
            + [jax.ShapeDtypeStruct((width, n), LOW)] * 2 + [jax.ShapeDtypeStruct((wr.shape[1], width), jnp.float32)],
        scratch_shapes=[pltpu.VMEM(wi.shape, LOW), pltpu.VMEM(wo.shape, LOW), pltpu.SemaphoreType.DMA((2, inner // chunk))],
        compiler_params=params(60),
        cost_estimate=cost(flops=8 * n * width * inner, bytes_accessed=4 * n * inner + 8 * width * inner, transcendentals=n * inner),
        name="expert_rows",
    )(x, g, mine, wr, wi, wo)

def expert_weights_kernel(parts, *refs):
    ins, (gi_ref, go_ref) = refs[: 4 * parts], refs[4 * parts :]
    gi = None
    go = None
    for c in range(parts):
        xt, dfft, hid, da = ins[4 * c : 4 * c + 4]
        gi_c = dot(xt[...], da[...])
        go_c = dot(dfft[...], hid[...])
        gi = gi_c if gi is None else gi + gi_c
        go = go_c if go is None else go + go_c
    gi_ref[0] = gi
    go_ref[0] = go.T


def expert_weights(parts, tile=512):
    inner = parts[0][2].shape[1]
    width = parts[0][0].shape[0]
    specs, args, rows = [], [], 0
    for xt, dfft, hid, da in parts:
        n = hid.shape[0]
        rows += n
        specs += [pl.BlockSpec((width, n), lambda f: (0, 0), pipeline_mode=pl.Buffered(1))] * 2
        specs += [pl.BlockSpec((n, tile), lambda f: (0, f))] * 2
        args += [xt, dfft, hid, da]
    return pl.pallas_call(
        functools.partial(expert_weights_kernel, len(parts)),
        grid=(inner // tile,),
        in_specs=specs,
        out_specs=[
            pl.BlockSpec((1, width, tile), lambda f: (0, 0, f)),
            pl.BlockSpec((1, tile, width), lambda f: (0, f, 0)),
        ],
        out_shape=[
            jax.ShapeDtypeStruct((1, width, inner), jnp.float32),
            jax.ShapeDtypeStruct((1, inner, width), jnp.float32),
        ],
        compiler_params=params(60),
        cost_estimate=cost(4 * rows * width * inner, 4 * rows * inner + 8 * width * inner),
        name="expert_weights",
    )(*args)


def device_place(cores, d):
    return dict(device_id=(lax.div(d, cores), lax.rem(d, cores)), device_id_type=pl.DeviceIdType.MESH)


def partner_of(me, b):
    bit = lax.rem(lax.div(me, 1 << b), 2)
    return bit, me + (1 - 2 * bit) * (1 << b)


def greet(cores, bits, me):
    barrier = pltpu.get_barrier_semaphore()
    for b in range(bits):
        pl.semaphore_signal(barrier, inc=1, **device_place(cores, partner_of(me, b)[1]))
    pl.semaphore_wait(barrier, bits)


def rows_at(start, length):
    return pl.ds(pl.multiple_of(start, 16), length)


def sum_parts(n, heights):
    bits = n.bit_length() - 1
    upper = list(range(1, bits))
    parts, first = [], 0
    for ref, rows in enumerate(heights):
        units = rows // (16 * n)
        pieces = max(1, min(units, round(6 * rows / sum(heights))))
        at = 0
        for c in range(pieces):
            size = (units + c) // pieces
            t = len(parts) % 3
            parts.append((ref, at * 16 * n, first, size * 16, [0] + upper[t:] + upper[:t]))
            at += size
            first += size * 16 * n
    return bits, parts


def sum_kernel(
    cores, n, room, heights, code_ref, gate_ref, ff_any, y_any, *refs
):
    xs = refs[: len(heights)]
    mixed_ref, out_ref, *rest = refs[len(heights) :]
    work_ref, got_ref, ff_ref, y_ref, send, recv, local = rest
    bits, parts = sum_parts(n, heights)
    me = lax.axis_index("grp") * cores + lax.axis_index("exp")
    loads = [
        pltpu.make_async_copy(ff_any, ff_ref, local.at[0]),
        pltpu.make_async_copy(y_any, y_ref, local.at[1]),
    ]
    for copy in loads:
        copy.start()
    greet(cores, bits, me)
    base = [first for _, _, first, _, _ in parts]
    got_at = list(base)

    def halving(p, s):
        ref, at, first, step, order = parts[p]
        length = step * (n >> (s + 1))
        bit, partner = partner_of(me, order[s])
        start = base[p] + (1 - bit) * length
        source = xs[ref].at[rows_at(start - first + at, length)] if s == 0 else work_ref.at[rows_at(start, length)]
        return pltpu.make_async_remote_copy(
            src_ref=source, dst_ref=got_ref.at[rows_at(got_at[p], length)],
            send_sem=send.at[p, s], recv_sem=recv.at[p, s], **device_place(cores, partner),
        )

    def doubling(p, s):
        _, _, _, step, order = parts[p]
        here = rows_at(base[p], step * (n >> (s + 1)))
        return pltpu.make_async_remote_copy(
            src_ref=out_ref.at[here], dst_ref=out_ref.at[here],
            send_sem=send.at[p, bits + s], recv_sem=recv.at[p, bits + s],
            **device_place(cores, partner_of(me, order[s])[1]),
        )

    tokens = mixed_ref.shape[0]
    tile = tokens // 4

    def mix_tile(i):
        if i >= 4:
            return
        if i == 0:
            for copy in loads:
                copy.wait()
        here = slice(i * tile, (i + 1) * tile)
        ff = collect(segment(code_ref[here, :], room, 0, plan(room)[1]), ff_ref[...])
        mixed_ref[here, :] = y_ref[here, :] + gate_ref[here, :] * ff

    moving = [halving(p, 0) for p in range(len(parts))]
    for copy in moving:
        copy.start()
    sent = []
    for s in range(bits):
        mix_tile(s - 1 if s else 9)
        for p, (ref, at, first, step, order) in enumerate(parts):
            length = step * (n >> (s + 1))
            moving[p].wait_recv()
            sent.append(moving[p])
            base[p] = base[p] + partner_of(me, order[s])[0] * length
            source, shift = (xs[ref], at - first) if s == 0 else (work_ref, 0)
            target = work_ref if s + 1 < bits else out_ref

            def add(i, _, start=base[p], source=source, shift=shift, target=target, arrived=got_at[p], step=step):
                got = got_ref[rows_at(arrived + i * step, step), :].astype(jnp.float32)
                mine = source[rows_at(start + shift + i * step, step), :].astype(jnp.float32)
                target[rows_at(start + i * step, step), :] = (mine + got).astype(LOW)
                return 0

            lax.fori_loop(0, length // step, add, 0)
            got_at[p] += length
            if s + 1 < bits:
                moving[p] = halving(p, s + 1)
            else:
                moving[p] = doubling(p, s)
            moving[p].start()
    for copy in sent:
        copy.wait_send()
    sent = []
    for s in reversed(range(bits)):
        if s == bits - 1:
            for i in range(bits - 1, 4):
                mix_tile(i)
        for p, (ref, at, first, step, order) in enumerate(parts):
            length = step * (n >> (s + 1))
            moving[p].wait_recv()
            sent.append(moving[p])
            base[p] = base[p] - partner_of(me, order[s])[0] * length
            if s > 0:
                moving[p] = doubling(p, s - 1)
                moving[p].start()
    for copy in sent:
        copy.wait_send()


def all_sum(xs, code, gate, ff, y, room):
    cores = lax.axis_size("exp")
    n = lax.axis_size(AXES)
    heights = [a.shape[0] for a in xs]
    if any(h % (16 * n) for h in heights):
        xs = [jnp.concatenate(xs[:-1], axis=0), xs[-1]]
        heights = [a.shape[0] for a in xs]
    total = sum(heights)
    bits, parts = sum_parts(n, heights)
    tokens, width = y.shape
    buffer = pltpu.VMEM((total, TILE), LOW)
    vmem = pl.BlockSpec(memory_space=pltpu.VMEM)
    anywhere = pl.BlockSpec(memory_space=pl.ANY)
    return pl.pallas_call(
        functools.partial(sum_kernel, cores, n, room, heights),
        out_shape=[
            jax.ShapeDtypeStruct((tokens, width), jnp.float32),
            jax.ShapeDtypeStruct((total, TILE), LOW),
        ],
        in_specs=[vmem, vmem, anywhere, anywhere] + [vmem] * len(xs),
        out_specs=[vmem] * 2,
        scratch_shapes=[
            buffer, buffer, pltpu.VMEM(ff.shape, LOW), pltpu.VMEM(y.shape, jnp.float32),
            pltpu.SemaphoreType.DMA((len(parts), 2 * bits)),
            pltpu.SemaphoreType.DMA((len(parts), 2 * bits)),
            pltpu.SemaphoreType.DMA((2,)),
        ],
        compiler_params=params(60, collective_id=1, has_side_effects=True),
        name="all_sum",
    )(code, gate, ff, y, *xs)


def local(
    tokens, lengths, expert_ids, slots, w_query, w_key, w_value, w_output,
    gain_attn, gain_ffn, bias_table, w_router, w_in, w_out, cotangent,
):
    rows, seq, width = tokens.shape
    count = rows * seq
    buckets, heads = bias_table.shape
    head = width // heads
    experts = w_router.shape[1]
    devices = lax.axis_size(AXES)
    room = max(4, 2 * count // experts)
    me = lax.axis_index(AXES)
    x = tokens.reshape(count, width)
    g = cotangent.reshape(count, width)
    gain_one = gain_attn.reshape(1, width)
    gain_two = gain_ffn.reshape(1, width)
    wide = max(128, experts)
    mine = (jnp.arange(wide, dtype=jnp.int32) == me).astype(jnp.float32).reshape(1, wide)

    segments, cut, extra = plan(room)
    code_c, code_r, rank_c, g_out, g_more = route(expert_ids, slots, g, experts, room)
    if extra:
        g_more = lax.all_gather(g_more, AXES, axis=0, tiled=False)
    g_in = exchange(g_out, devices)
    code_r, x, w_query, w_key, w_value, w_output, bias_table, w_router = lax.optimization_barrier(
        (code_r, x, w_query, w_key, w_value, w_output, bias_table, w_router)
    )
    router_w = jnp.pad(w_router, ((0, 0), (0, wide - experts)))

    normed_t, projected = project(x, gain_one, w_query, w_key, w_value)
    near, far = bias_tiles(bias_table)
    joined, weights = attention_forward(lengths, projected, near, far, rows, seq, heads, head)
    y, gate, *h_out = after_attention(
        joined, x, w_output, gain_two, expert_ids.reshape(count, 1), router_w, code_r, experts, room
    )
    h_out, g_in = lax.optimization_barrier((h_out, g_in))
    g_in = g_in.reshape(devices, cut, width)
    h_in = [exchange(h_out[0], devices)]
    g_parts = [(g_in, low, high) for low, high in segments]
    late = None
    if extra:
        spare = room - cut
        h_in[0], g_more = lax.optimization_barrier((h_in[0], g_more))
        marks = g_more[:, extra, : extra + 1].astype(jnp.float32)
        late = jnp.any(marks[:, extra] > 0)
        mine_marks = marks[:, :extra] == (me + 1).astype(jnp.float32)
        order = jnp.cumsum(mine_marks.astype(jnp.int32), axis=1) - 1
        chosen = (
            mine_marks[:, None, :]
            & (order[:, None, :] == jnp.arange(spare, dtype=jnp.int32)[None, :, None])
        ).astype(LOW)
        flat_code, flat_rank = code_c.reshape(-1), rank_c.reshape(-1)
        flat_expert = flat_code // room
        rest = jnp.where(
            flat_rank >= extra,
            flat_expert * spare + flat_code - flat_expert * room - cut,
            experts * spare,
        )

        def send_rest(rest):
            empty = jnp.zeros((experts * spare, width), LOW)
            return exchange(empty.at[rest].set(g, mode="drop"), devices)

        g_rest = lax.cond(
            late, send_rest, lambda rest: jnp.zeros((experts * spare, width), LOW), rest
        )
        h_out[1], g_rest = lax.optimization_barrier((h_out[1], g_rest))
        g_spare = jnp.einsum(
            "sqr,srw->sqw", chosen, g_more[:, :extra], preferred_element_type=jnp.float32
        ).astype(LOW) + g_rest.reshape(devices, spare, width)
        low, high = segments[1]
        g_parts[1] = (jnp.concatenate([g_in[:, low:], g_spare], axis=1), 0, high - low)
    for h in h_out[1:]:
        h, h_in[-1] = lax.optimization_barrier((h, h_in[-1]))
        h_in.append(exchange(h, devices))
    dx_back, ffs, parts, grad_router = [], [], [], 0.0
    for n, (low, high) in enumerate(segments):
        ff, dx, hid, da, x_t, dff_t, routed = expert_rows(
            h_in[n], g_parts[n][0], mine, router_w, w_in[0], w_out[0], experts, *g_parts[n][1:]
        )
        if n + 1 < len(segments):
            dx, h_in[n + 1] = lax.optimization_barrier((dx, h_in[n + 1]))
        if n:
            dx, dx_back[-1] = lax.optimization_barrier((dx, dx_back[-1]))
        dx_back.append(exchange(dx, devices))
        ffs.append(ff.reshape(devices, high - low, width))
        parts.append((x_t, dff_t, hid, da))
        grad_router = grad_router + routed
    grad_in, grad_out = expert_weights(parts)
    ff = jnp.concatenate(ffs, axis=1) if len(ffs) > 1 else ffs[0]
    more = []
    if extra:
        ff_spare = ff[:, cut:]
        ff_more = jnp.einsum(
            "sqr,sqw->srw", chosen, ff_spare, preferred_element_type=jnp.float32
        ).astype(LOW)
        ff_more = lax.psum_scatter(
            ff_more.reshape(devices * extra, width), AXES, scatter_dimension=0, tiled=True
        )
        dx_back, ff_spare = lax.optimization_barrier((dx_back, ff_spare))

        def return_rest(spare_rows, rest):
            back = exchange(spare_rows.reshape(devices * spare, width), devices)
            return jnp.take(back, rest, axis=0, mode="fill", fill_value=0)

        ff_rest = lax.cond(
            late, return_rest, lambda *_: jnp.zeros((count, width), LOW), ff_spare, rest
        )
        dx_back, ff_rest = lax.optimization_barrier((dx_back, ff_rest))
        more = [ff_more, ff_rest]
    ff = ff[:, :cut].reshape(devices * cut, width)
    dx_back, grad_in, grad_out, ff = lax.optimization_barrier((dx_back, grad_in, grad_out, ff))
    ff_back = exchange(ff, devices)
    grad_router = grad_router[:experts].reshape(experts, width // TILE, TILE)
    grad_router = jnp.swapaxes(grad_router, 0, 1).reshape(-1, TILE)

    dy, do, grad_output, grad_gain_two = before_attention(
        dx_back, code_c, y, g, gain_two, w_output, joined, room
    )
    lines = width // TILE
    small_rows = grad_router.shape[0] + -(-2 * lines // 16) * 16 + -(-heads // 16) * 16
    small_rows = -(-small_rows // (16 * devices)) * 16 * devices
    grad_tokens, packed, small = attention_backward(
        projected, do, joined, weights, normed_t, w_query, w_key, w_value, x, dy, gain_one,
        grad_router, grad_gain_two, rows, seq, heads, head, small_rows,
    )
    mixed, summed = all_sum(
        [packed.reshape(-1, TILE), grad_output, small], code_c, gate, ff_back, y, room
    )
    *grads, router_t, gains, table, mixed = unpack(
        summed, mixed, gate, rank_c, more, width, experts, heads, buckets, small_rows
    )
    return (
        mixed.reshape(rows, seq, width),
        grad_tokens.reshape(rows, seq, width),
        *grads,
        gains[0], gains[1], table.T, router_t.T,
        grad_in,
        grad_out,
    )


def solution(mesh):
    split = P(AXES)
    in_specs = (split,) * 4 + (P(),) * 8 + (split,) * 3
    out_specs = (split,) * 2 + (P(),) * 8 + (split,) * 2
    return jax.shard_map(local, mesh=mesh, in_specs=in_specs, out_specs=out_specs, check_vma=False)
```

time: 431 us -> 420 us (0.974)
  blocking collectives: 41.9 us -> 0 us
  local copies, waits for them, and re-layouts: 39.9 us -> 20.2 us
  waiting for transfers between devices: 45.8 us -> 59.8 us
  between operations: 1.34 us -> 15.2 us
  Pallas kernels: 265 us -> 278 us
  starting transfers between devices: 23 us -> 27.5 us
  matrix products: 2.07 us -> 6.49 us
    all_to_all x1 -> x0, blocking collectives: 41.9 us -> none  [exchange(): lax.all_to_all(shaped, AXES, split_axis=0, concat_axis=0, tiled=True)]
    unnamed x95 -> x42, local copies, waits for them, and re-layouts: 36.7 us -> 11.8 us
    pallas_call x1, Pallas kernels: 28.3 us -> 46.3 us  [attention_backward(): pl.pallas_call(attention_backward_kernel, grid=(pairs, rows), in_specs=[s...]
    all_gather x0 -> x1, waiting for transfers between devices: none -> 8.44 us  [local(): g_more = lax.all_gather(g_more, AXES, axis=0, tiled=False)]
    pallas_call x5 -> x3, Pallas kernels: 99 us -> 91.2 us  [the longest x1 68.3 us: all_sum(): pl.pallas_call(functools.partial(sum_kernel, cores, n, room, heights), ou...]
    all_to_all x5 -> x6, waiting for transfers between devices: 45.8 us -> 50.8 us  [exchange(): lax.all_to_all(shaped, AXES, split_axis=0, concat_axis=0, tiled=True)]
    dot_general x0 -> x2, matrix products: none -> 4.39 us  [the longest x1 2.46 us: local(): jnp.einsum('sqr,sqw->srw', chosen, ff_spare, preferred_element_type=jnp.f...]
    all_to_all x5 -> x6, starting transfers between devices: 23 us -> 27 us  [exchange(): lax.all_to_all(shaped, AXES, split_axis=0, concat_axis=0, tiled=True)]
  transfers between devices with their start and end apart: 5 -> 8, of which waited for: 4 -> 6; matrix products, arithmetic and copies ran while one was open for 2% -> 4% of each run, Pallas kernels for 58% -> 62%
where the time goes in v4:
time: 420 us; the launch traced here: 415 us
  Pallas kernels  278 us (66%)
  waiting for transfers between devices  59.8 us (14%)
  starting transfers between devices  27.5 us (7%)
  local copies, waits for them, and re-layouts  20.2 us (5%)
  between operations  15.2 us (4%)
  other arithmetic  6.92 us (2%)
  matrix products  6.49 us (2%)
    pallas_call x1, Pallas kernels, all_sum(): pl.pallas_call(functools.partial(sum_kernel, cores, n, room, heights), ou...  68.3 us
    pallas_call x2, Pallas kernels, expert_rows(): pl.pallas_call(functools.partial(expert_kernel, experts, chunk), grid=(n...  61.1 us
    all_to_all x6, waiting for transfers between devices, exchange(): lax.all_to_all(shaped, AXES, split_axis=0, concat_axis=0, tiled=True)  50.8 us
    pallas_call x1, Pallas kernels, attention_backward(): pl.pallas_call(attention_backward_kernel, grid=(pairs, rows), in_specs=[s...  46.3 us
    pallas_call x1, Pallas kernels, expert_weights(): pl.pallas_call(functools.partial(expert_weights_kernel, len(parts)), grid...  27.8 us
    all_to_all x6, starting transfers between devices, exchange(): lax.all_to_all(shaped, AXES, split_axis=0, concat_axis=0, tiled=True)  27 us
    pallas_call x1, Pallas kernels, attention_forward(): pl.pallas_call(attention_forward_kernel, grid=(rows, pairs), in_specs=[pl...  20.8 us
    pallas_call x1, Pallas kernels, before_attention(): pl.pallas_call(functools.partial(before_attention_kernel, room, len(backs...  14.5 us
  transfers between devices with their start and end apart: 8, of which 6 were waited for; matrix products, arithmetic and copies ran while one was open for 4% of the time, Pallas kernels for 62%

profile of v4, /device:TPU:0, one launch (start us, length us, event | category | flops | bytes accessed | tf_op | source)
XLA Modules:
  0.0 414.7 jit_solution(12941459928510709711)
XLA Ops:
  7.2 0.7 copy.45
  7.9 0.7 copy.48
  8.6 0.2 copy.49
  8.8 0.2 copy.46
  9.0 8.7 %route.1 = (s32[1024,1]{1,0:T(8,128)S(1)}, s32[1,1024]{1,0:T(1,128)S(1)}, s32[1024,1]{1,0:T(8,128)S(1)}, bf16[1536,768]{1,0:T(8,128)(2,1)}, bf16[32,768]{1,0:T(8,128)(2,1)}) custom-call(s32[1024,1]{1,0:T(8,128)S(1)} %bitcast.58, s32[1,1024]{1,0:T(1,128)S(1)} %bitcast.62, s32[1024,1]{1,0:T(8,128)S(1)} %bitcast.60, s32[1,1024]{1,0:T(1,128)S(1)} %bitcast.64, ...), custom_call_target="tpu_custom_call" | custom-call | flops 3221225472 | bytes 8388608 | tf_op jit(solution)/shard_map/route/pallas_call | solution.py:146
  17.8 0.5 copy-done.6
  18.4 7.4 %all-to-all-start.2 = ((bf16[32,48,768]{2,1,0:T(8,128)(2,1)}), bf16[32,48,768]{2,1,0:T(8,128)(2,1)}, u32[]{:S(2)}, u32[]{:S(2)}) async-start(bf16[32,48,768]{2,1,0:T(8,128)(2,1)} %bitcast.8), calls=%async_computation.2 | async-start | bytes 4718592 | tf_op jit(solution)/shard_map/all_to_all | solution.py:164
  25.8 0.2 all-gather.3.cloned.1.call-start
  26.0 0.5 all-gather.3.cloned.1.call-update
  26.5 0.6 reshape.226.gain_ref
  27.1 0.6 reshape.228.gain_ref
  27.9 0.8 copy.40
  28.9 0.2 fusion.10
  29.0 2.1 fusion.3
  31.1 0.6 copy.51
  31.8 0.2 slice.58
  31.9 0.7 copy-done.13
  32.7 0.7 pad.4.wr_ref
  33.4 8.0 %project.1 = (bf16[768,1024]{1,0:T(8,128)(2,1)}, bf16[1024,2304]{1,0:T(8,128)(2,1)}) custom-call(bf16[1024,768]{1,0:T(8,128)(2,1)} %bitcast.101, f32[1,768]{1,0:T(1,128)} %reshape.226.gain_ref, bf16[768,768]{1,0:T(8,128)(2,1)} %wq_ref.1, bf16[768,768]{1,0:T(8,128)(2,1)} %wk_ref.1, bf16[768,768]{1,0:T(8,128)(2,1)} %wv_ref.1), custom_call_target="tpu_custom_call" | custom-call | flops 3623878656 | bytes 12582912 | tf_op jit(solution)/shard_map/project/pallas_call | solution.py:183
  41.4 2.3 copy-done.5
  43.8 20.8 %attention_forward.1 = (bf16[1024,768]{1,0:T(8,128)(2,1)S(1)}, bf16[2,12,512,512]{3,2,1,0:T(8,128)(2,1)}) custom-call(s32[2]{0:T(128)S(1)} %copy-done.3, bf16[1024,2304]{1,0:T(8,128)(2,1)S(1)} %copy-done.5, bf16[1024,2304]{1,0:T(8,128)(2,1)S(1)} %copy-done.5, bf16[1024,2304]{1,0:T(8,128)(2,1)S(1)} %copy-done.5, f32[12,3,128,128]{3,2,1,0:T(8,128)S(1)} %bitcast.57, ...), custom_call_target="tpu_custom_call" | custom-call | flops 6442450944 | bytes 12582912 | tf_op jit(solution)/shard_map/attention_forward/pallas_call | solution.py:420
  64.5 1.1 copy-done.4
  65.7 12.3 %after_attention.1 = (f32[1024,768]{1,0:T(8,128)}, f32[1024,1]{1,0:T(8,128)}, bf16[1024,768]{1,0:T(8,128)(2,1)}, bf16[1024,768]{1,0:T(8,128)(2,1)}) custom-call(bf16[1024,768]{1,0:T(8,128)(2,1)} %copy-done.4, bf16[1024,768]{1,0:T(8,128)(2,1)} %bitcast.102, bf16[768,768]{1,0:T(8,128)(2,1)} %w_ref.1, f32[1,768]{1,0:T(1,128)} %reshape.228.gain_ref, ...), custom_call_target="tpu_custom_call" | custom-call | flops 4429185024 | bytes 12582912 | tf_op jit(solution)/shard_map/after_attention/pallas_call | solution.py:224
  78.0 5.5 %all-to-all-done.2 = bf16[32,48,768]{2,1,0:T(8,128)(2,1)} async-done(((bf16[32,48,768]{2,1,0:T(8,128)(2,1)}), bf16[32,48,768]{2,1,0:T(8,128)(2,1)}, u32[]{:S(2)}, u32[]{:S(2)}) %all-to-all-start.2) | async-done | bytes 2359328 | tf_op jit(solution)/shard_map/all_to_all | solution.py:164
  83.4 4.0 all-to-all-start.3
  87.5 0.2 reduce.2
  87.7 0.2 compare_reduce_fusion
  88.0 8.4 %all-gather.3.cloned.1.call-done = bf16[1024,768]{1,0:T(8,128)(2,1)} async-done(((bf16[32,768]{1,0:T(8,128)(2,1)}), bf16[1024,768]{1,0:T(8,128)(2,1)}) %all-gather.3.cloned.1.call-update) | async-done | bytes 1572880 | tf_op jit(solution)/shard_map/all_gather | solution.py:979
  96.4 29.5 %all-to-all-done.3 = bf16[32,32,768]{2,1,0:T(8,128)(2,1)S(1)} async-done(((bf16[32,32,768]{2,1,0:T(8,128)(2,1)}), bf16[32,32,768]{2,1,0:T(8,128)(2,1)S(1)}, u32[]{:S(2)}, u32[]{:S(2)}) %all-to-all-start.3) | async-done | bytes 1572896 | tf_op jit(solution)/shard_map/all_to_all | solution.py:164
  125.9 0.9 slice_convert_fusion
  126.8 0.7 fusion.18
  128.1 0.3 conditional.2
  128.4 3.8 all-to-all-start.4
  132.2 0.5 compare_convert_fusion.mine_ref
  132.7 30.5 %expert_rows.2 = (bf16[1024,768]{1,0:T(8,128)(2,1)}, bf16[1024,768]{1,0:T(8,128)(2,1)}, bf16[1024,3072]{1,0:T(8,128)(2,1)}, bf16[1024,3072]{1,0:T(8,128)(2,1)}, ...) custom-call(bf16[1024,768]{1,0:T(8,128)(2,1)} %bitcast.78, ...), custom_call_target="tpu_custom_call" | custom-call | flops 19327352832 | bytes 31457280 | tf_op jit(solution)/shard_map/expert_rows/pallas_call | solution.py:734
  163.2 6.7 %all-to-all-done.4 = bf16[32,32,768]{2,1,0:T(8,128)(2,1)S(1)} async-done(((bf16[32,32,768]{2,1,0:T(8,128)(2,1)}), bf16[32,32,768]{2,1,0:T(8,128)(2,1)S(1)}, u32[]{:S(2)}, u32[]{:S(2)}) %all-to-all-start.4) | async-done | bytes 1572896 | tf_op jit(solution)/shard_map/all_to_all | solution.py:164
  169.9 1.1 copy-done.11
  171.1 4.2 %all-to-all-start.5 = ((bf16[32,32,768]{2,1,0:T(8,128)(2,1)}), bf16[32,32,768]{2,1,0:T(8,128)(2,1)S(1)}, u32[]{:S(2)}, u32[]{:S(2)}) async-start(bf16[32,32,768]{2,1,0:T(8,128)(2,1)} %bitcast.80), calls=%async_computation.5 | async-start | bytes 3145728 | tf_op jit(solution)/shard_map/all_to_all | solution.py:164
  175.3 1.2 slice.53
  176.5 0.2 reduce_window_sum.11
  176.7 1.9 fusion.5
  178.6 1.4 pad_maximum_fusion.1.g_ref
  180.0 30.6 %expert_rows.3 = (bf16[1024,768]{1,0:T(8,128)(2,1)}, bf16[1024,768]{1,0:T(8,128)(2,1)}, bf16[1024,3072]{1,0:T(8,128)(2,1)}, bf16[1024,3072]{1,0:T(8,128)(2,1)}, ...) custom-call(bf16[1024,768]{1,0:T(8,128)(2,1)} %bitcast.79, ...), custom_call_target="tpu_custom_call" | custom-call | flops 19327352832 | bytes 31457280 | tf_op jit(solution)/shard_map/expert_rows/pallas_call | solution.py:734
  210.5 2.5 all-to-all-done.5
  213.0 1.1 copy-done.9
  214.1 3.9 all-to-all-start.6
  218.1 1.0 slice.55
  219.0 0.7 copy-done.12
  219.7 1.6 pad_maximum_fusion
  221.3 27.8 %expert_weights.1 = (f32[1,768,3072]{2,1,0:T(8,128)}, f32[1,3072,768]{2,1,0:T(8,128)}) custom-call(bf16[768,1024]{1,0:T(8,128)(2,1)} %get-tuple-element.147.refs_0_, bf16[768,1024]{1,0:T(8,128)(2,1)} %get-tuple-element.148.refs_1_, bf16[1024,3072]{1,0:T(8,128)(2,1)} %get-tuple-element.149.refs_2_, bf16[1024,3072]{1,0:T(8,128)(2,1)} %get-tuple-element.150.refs_3_, ...), custom_call_target="tpu_custom_call" | custom-call | flops 19327352832 | bytes 44040192 | tf_op jit(solution)/shard_map/expert_weights/pallas_call | solution.py:773
  249.1 6.6 %all-to-all-done.6 = bf16[32,32,768]{2,1,0:T(8,128)(2,1)} async-done(((bf16[32,32,768]{2,1,0:T(8,128)(2,1)}), bf16[32,32,768]{2,1,0:T(8,128)(2,1)}, u32[]{:S(2)}, u32[]{:S(2)}) %all-to-all-start.6) | async-done | bytes 1572896 | tf_op jit(solution)/shard_map/all_to_all | solution.py:164
  255.8 1.2 conditional.3
  255.8 1.2 broadcast.122
  257.0 3.8 all-to-all-start.7
  260.8 0.2 reduce-scatter.2.cloned.1.call-start
  261.0 1.0 slice_add_fusion
  262.0 0.7 copy.43
  262.7 2.5 convolution_convert_fusion
  265.1 14.5 %before_attention.1 = (f32[1024,768]{1,0:T(8,128)}, bf16[1024,768]{1,0:T(8,128)(2,1)}, bf16[4608,128]{1,0:T(8,128)(2,1)}, f32[1,768]{1,0:T(1,128)}) custom-call(s32[1024,1]{1,0:T(8,128)} %copy-done.1, f32[1024,768]{1,0:T(8,128)} %get-tuple-element.159.y_ref.y_any, bf16[1024,768]{1,0:T(8,128)(2,1)} %bitcast.100, f32[1,768]{1,0:T(1,128)} %reshape.228.gain_ref, ...), custom_call_target="tpu_custom_call" | custom-call | flops 3623878656 | bytes 16777216 | tf_op jit(solution)/shard_map/before_attention/pallas_call | solution.py:294
  279.7 46.3 %attention_backward.1 = (f32[1024,768]{1,0:T(8,128)}, bf16[3,6,768,128]{3,2,1,0:T(8,128)(2,1)}, bf16[512,128]{1,0:T(8,128)(2,1)}) custom-call(bf16[1024,2304]{1,0:T(8,128)(2,1)} %get-tuple-element.114.q_ref.k_ref.v_ref, bf16[1024,2304]{1,0:T(8,128)(2,1)} %get-tuple-element.114.q_ref.k_ref.v_ref, bf16[1024,2304]{1,0:T(8,128)(2,1)} %get-tuple-element.114.q_ref.k_ref.v_ref, ...), custom_call_target="tpu_custom_call" | custom-call | flops 12884901888 | bytes 12582912 | tf_op jit(solution)/shard_map/attention_backward/pallas_call | solution.py:608
  326.0 1.4 copy-done.7
  327.4 68.3 %all_sum.1 = (f32[1024,768]{1,0:T(8,128)}, bf16[18944,128]{1,0:T(8,128)(2,1)}) custom-call(s32[1024,1]{1,0:T(8,128)} %copy-done.1, f32[1024,1]{1,0:T(8,128)} %get-tuple-element.120.gate_ref, bf16[1536,768]{1,0:T(8,128)(2,1)} %bitcast.68, f32[1024,768]{1,0:T(8,128)} %get-tuple-element.159.y_ref.y_any, bf16[13824,128]{1,0:T(8,128)(2,1)} %bitcast.72, ...), custom_call_target="tpu_custom_call" | custom-call | tf_op jit(solution)/shard_map/all_sum/pallas_call | solution.py:938
  395.7 10.6 %unpack.1 = (f32[768,768]{1,0:T(8,128)}, f32[768,768]{1,0:T(8,128)}, f32[768,768]{1,0:T(8,128)}, f32[768,768]{1,0:T(8,128)}, f32[32,768]{1,0:T(8,128)}, /*index=...) custom-call(bf16[18944,128]{1,0:T(8,128)(2,1)} %get-tuple-element.172.q_ref.k_ref.v_ref.o_ref.small_ref, ...), custom_call_target="tpu_custom_call" | custom-call | tf_op jit(solution)/shard_map/unpack/pallas_call | solution.py:352
  406.3 1.4 slice_reduce_fusion
  (43 shorter events, 0.5 us)
Async XLA Ops:
  9.0 8.8 %copy-start.2 = (s32[1,1024]{0,1:T(8,128)}, s32[1,1024]{0,1:T(8,128)S(1)}, u32[]{:S(2)}) copy-start(s32[1,1024]{0,1:T(8,128)S(1)} %copy.46) | copy-start | bytes 12292
  17.8 0.6 copy-start.6
  17.8 69.7 %copy-start.1 = (s32[1024,1]{1,0:T(8,128)}, s32[1024,1]{1,0:T(8,128)S(1)}, u32[]{:S(2)}) copy-start(s32[1024,1]{1,0:T(8,128)S(1)} %get-tuple-element.108.code_ref) | copy-start | bytes 12292
  17.8 69.9 %copy-start = (s32[1024,1]{1,0:T(8,128)}, s32[1024,1]{1,0:T(8,128)S(1)}, u32[]{:S(2)}) copy-start(s32[1024,1]{1,0:T(8,128)S(1)} %get-tuple-element.128.rank_ref) | copy-start | bytes 12292
  17.8 8.7 %copy-start.16 = (f32[768]{0:T(1024)S(1)}, f32[768]{0:T(1024)}, u32[]{:S(2)}) copy-start(f32[768]{0:T(1024)} %param.27) | copy-start | bytes 9220
  17.8 9.3 %copy-start.17 = (f32[768]{0:T(1024)S(1)}, f32[768]{0:T(1024)}, u32[]{:S(2)}) copy-start(f32[768]{0:T(1024)} %param.28) | copy-start | bytes 9220
  17.8 9.9 %copy-start.15 = (f32[32,12]{0,1:T(8,128)S(1)}, f32[32,12]{0,1:T(8,128)}, u32[]{:S(2)}) copy-start(f32[32,12]{0,1:T(8,128)} %param.29) | copy-start | bytes 4612
  17.8 10.1 %copy-start.14 = (bf16[768,32]{0,1:T(8,128)(2,1)S(1)}, bf16[768,32]{0,1:T(8,128)(2,1)}, u32[]{:S(2)}) copy-start(bf16[768,32]{0,1:T(8,128)(2,1)} %param.30) | copy-start | bytes 147460
  18.4 65.1 %all-to-all-start.2 = ((bf16[32,48,768]{2,1,0:T(8,128)(2,1)}), bf16[32,48,768]{2,1,0:T(8,128)(2,1)}, u32[]{:S(2)}, u32[]{:S(2)}) async-start(bf16[32,48,768]{2,1,0:T(8,128)(2,1)} %bitcast.8), calls=%async_computation.2 | async-start | bytes 4718592 | tf_op jit(solution)/shard_map/all_to_all | solution.py:164
  25.8 70.6 %all-gather.3.cloned.1.call-start = ((), (), s32[]{:S(2)}) async-start(), calls=%async_computation.10 | async-start | bytes 1622016 | tf_op jit(solution)/shard_map/all_gather | solution.py:979
  31.8 0.9 copy-start.13
  33.4 8.0 %copy-start.3 = (s32[2]{0:T(128)S(1)}, s32[2]{0:T(128)}, u32[]{:S(2)}) copy-start(s32[2]{0:T(128)} %len_ref.1) | copy-start | bytes 28
  41.4 2.3 copy-start.5
  64.5 1.1 copy-start.4
  83.4 42.4 %all-to-all-start.3 = ((bf16[32,32,768]{2,1,0:T(8,128)(2,1)}), bf16[32,32,768]{2,1,0:T(8,128)(2,1)S(1)}, u32[]{:S(2)}, u32[]{:S(2)}) async-start(bf16[32,32,768]{2,1,0:T(8,128)(2,1)} %bitcast.82), calls=%async_computation.3 | async-start | bytes 3145728 | tf_op jit(solution)/shard_map/all_to_all | solution.py:164
  125.9 2.3 copy-start.10
  128.4 41.5 %all-to-all-start.4 = ((bf16[32,32,768]{2,1,0:T(8,128)(2,1)}), bf16[32,32,768]{2,1,0:T(8,128)(2,1)S(1)}, u32[]{:S(2)}, u32[]{:S(2)}) async-start(bf16[32,32,768]{2,1,0:T(8,128)(2,1)} %bitcast.17), calls=%async_computation.4 | async-start | bytes 3145728 | tf_op jit(solution)/shard_map/all_to_all | solution.py:164
  169.9 1.1 copy-start.11
  171.1 41.9 %all-to-all-start.5 = ((bf16[32,32,768]{2,1,0:T(8,128)(2,1)}), bf16[32,32,768]{2,1,0:T(8,128)(2,1)S(1)}, u32[]{:S(2)}, u32[]{:S(2)}) async-start(bf16[32,32,768]{2,1,0:T(8,128)(2,1)} %bitcast.80), calls=%async_computation.5 | async-start | bytes 3145728 | tf_op jit(solution)/shard_map/all_to_all | solution.py:164
  213.0 1.1 copy-start.9
  213.0 5.1 %copy-start.8 = (bf16[1024,768]{1,0:T(8,128)(2,1)S(1)}, bf16[1024,768]{1,0:T(8,128)(2,1)}, u32[]{:S(2)}) copy-start(bf16[1024,768]{1,0:T(8,128)(2,1)} %get-tuple-element.141) | copy-start | bytes 4718596
  214.1 41.6 %all-to-all-start.6 = ((bf16[32,32,768]{2,1,0:T(8,128)(2,1)}), bf16[32,32,768]{2,1,0:T(8,128)(2,1)}, u32[]{:S(2)}, u32[]{:S(2)}) async-start(bf16[32,32,768]{2,1,0:T(8,128)(2,1)} %bitcast.81), calls=%async_computation.6 | async-start | bytes 3145728 | tf_op jit(solution)/shard_map/all_to_all | solution.py:164
  218.0 1.7 copy-start.12
  257.0 68.9 %all-to-all-start.7 = ((bf16[32,48,768]{2,1,0:T(8,128)(2,1)}), bf16[32,48,768]{2,1,0:T(8,128)(2,1)S(1)}, u32[]{:S(2)}, u32[]{:S(2)}) async-start(bf16[32,48,768]{2,1,0:T(8,128)(2,1)} %bitcast.27), calls=%async_computation.7 | async-start | bytes 4718592 | tf_op jit(solution)/shard_map/all_to_all | solution.py:164
  260.8 134.9 %reduce-scatter.2.cloned.1.call-start = ((), (), s32[]{:S(2)}) async-start(), calls=%async_computation.9 | async-start | bytes 811008 | tf_op jit(solution)/shard_map/reduce_scatter | solution.py:1053
  326.0 1.4 copy-start.7
Sparse Core Ops, SparseCore 0:
  30.1 66.2 all-gather.2
  266.7 97.6 reduce-scatter.1

commit v5 on v4

--- a/solution.py
+++ b/solution.py
@@ -48,6 +48,19 @@
     return jnp.where(distance < 8, distance, far) + jnp.where(offset > 0, 16, 0).astype(jnp.int32)
 
 
+def device_place(cores, d):
+    return dict(device_id=(lax.div(d, cores), lax.rem(d, cores)), device_id_type=pl.DeviceIdType.MESH)
+
+
+def partner_of(me, b):
+    bit = lax.rem(lax.div(me, 1 << b), 2)
+    return bit, me + (1 - 2 * bit) * (1 << b)
+
+
+def rows_at(start, length):
+    return pl.ds(pl.multiple_of(start, 16), length)
+
+
 def plan(room):
     if room % 64:
         return ((0, room),), room, 0
@@ -94,61 +107,44 @@
 
 
 def route_kernel(
-    experts, room, eid_c, eid_r, slot_c, slot_r, g_ref, code_c, code_r, rank_c, out, more
+    experts, room, eid_c, eid_r, slot_c, slot_r, g_ref, code_c, code_r, rank_c, flag, out
 ):
     tokens = g_ref.shape[0]
     wide = max(TILE, experts)
     _, cut, extra = plan(room)
     at = lax.broadcasted_iota(jnp.int32, (tokens, tokens), 0)
     to = lax.broadcasted_iota(jnp.int32, (tokens, tokens), 1)
-    before = (to < at).astype(LOW)
-    after = (at < to).astype(LOW)
+
+    ids = eid_r[...]
+    picked = ids == lax.broadcasted_iota(jnp.int32, (wide, tokens), 0)
+    earlier = dot(picked.astype(LOW), (at < to).astype(LOW))
+    place = jnp.sum(jnp.where(picked, earlier, 0.0), axis=0, keepdims=True).astype(jnp.int32)
+    code = jnp.where(slot_r[...] >= 0, ids * room + place, -1)
+    code_r[...] = code
+    spread(code, g_ref[...], out)
 
     ids = eid_c[...]
     picked = ids == lax.broadcasted_iota(jnp.int32, (tokens, wide), 1)
-    place = jnp.sum(jnp.where(picked, dot(before, picked.astype(LOW)), 0.0), axis=1, keepdims=True)
-    place = place.astype(jnp.int32)
+    earlier = dot((to < at).astype(LOW), picked.astype(LOW))
+    place = jnp.sum(jnp.where(picked, earlier, 0.0), axis=1, keepdims=True).astype(jnp.int32)
     kept = slot_c[...] >= 0
     code_c[...] = jnp.where(kept, ids * room + place, -1)
-    over = jnp.broadcast_to(jnp.where(kept & (place >= cut), 1.0, 0.0), (tokens, TILE))
-    rank = jnp.where(over > 0, dot(before, over.astype(LOW)).astype(jnp.int32), -1)
-    rank_c[...] = rank[:, :1]
-    ids = eid_r[...]
-    picked = ids == lax.broadcasted_iota(jnp.int32, (wide, tokens), 0)
-    place = jnp.sum(jnp.where(picked, dot(picked.astype(LOW), after), 0.0), axis=0, keepdims=True)
-    place = place.astype(jnp.int32)
-    kept = slot_r[...] >= 0
-    code = jnp.where(kept, ids * room + place, -1)
-    code_r[...] = code
-    over = jnp.broadcast_to(jnp.where(kept & (place >= cut), 1.0, 0.0), (16, tokens))
-    rank = jnp.where(over > 0, dot(over.astype(LOW), after).astype(jnp.int32), -1)[:1]
-    spread(segment(code, room, 0, cut), g_ref[...], out)
-    if not extra:
-        more[...] = jnp.zeros(more.shape, LOW)
-        return
-    spread(rank, g_ref[...], more.at[:extra])
-    rank = rank_c[...]
-    lane = lax.broadcasted_iota(jnp.int32, (tokens, g_ref.shape[1]), 1)
-    marks = jnp.where((rank == lane) & (lane < extra), eid_c[...] + 1, 0)
-    marks = marks.astype(jnp.float32)
-    marks = jnp.sum(marks, axis=0, keepdims=True)
-    left = jnp.max(jnp.where(rank >= extra, 1.0, 0.0), axis=0, keepdims=True)
-    marks = jnp.where(lane[:1] == extra, left, marks)
-    line = lax.broadcasted_iota(jnp.int32, (more.shape[0] - extra, g_ref.shape[1]), 0)
-    more[extra:] = jnp.where(line == 0, marks, 0.0).astype(LOW)
+    over = kept & (place >= cut)
+    rank_c[...] = jnp.where(over, place - cut, -1)
+    named = jnp.max(jnp.where(picked & over, 1.0, 0.0), axis=0, keepdims=True)
+    named = jnp.sum(named, axis=1, keepdims=True)
+    flag[...] = jnp.broadcast_to(jnp.where(named > 1.0, 1.0, 0.0), flag.shape)
 
 
 def route(expert_ids, slots, upstream, experts, room):
     tokens, width = upstream.shape
     column = jax.ShapeDtypeStruct((tokens, 1), jnp.int32)
     line = jax.ShapeDtypeStruct((1, tokens), jnp.int32)
-    _, cut, extra = plan(room)
     return pl.pallas_call(
         functools.partial(route_kernel, experts, room),
         out_shape=[
-            column, line, column,
-            jax.ShapeDtypeStruct((experts * cut, width), LOW),
-            jax.ShapeDtypeStruct((extra + 16, width), LOW),
+            column, line, column, jax.ShapeDtypeStruct((16, TILE), jnp.float32),
+            jax.ShapeDtypeStruct((experts * room, width), LOW),
         ],
         compiler_params=params(48),
         cost_estimate=cost(2 * experts * room * tokens * width, 8 << 20),
@@ -189,7 +185,7 @@
             jax.ShapeDtypeStruct((width, tokens), LOW),
             jax.ShapeDtypeStruct((tokens, out), LOW),
         ],
-        compiler_params=params(60),
+        compiler_params=params(40),
         cost_estimate=cost(2 * tokens * width * out, 12 << 20),
         name="project",
     )(x, gain, w_query, w_key, w_value)
@@ -317,17 +313,10 @@
 
 
 def unpack_kernel(
-    experts, heads, buckets, q_ref, k_ref, v_ref, o_ref, small_ref, part_ref, gate_ref, rank_ref, *refs
+    experts, heads, buckets, q_ref, k_ref, v_ref, o_ref, small_ref, gq, gk, gv, go, router, gains, table
 ):
-    more, (gq, gk, gv, go, router, gains, table, mixed) = refs[:-8], refs[-8:]
     for packed_ref, out_ref in ((q_ref, gq), (k_ref, gk), (v_ref, gv), (o_ref, go)):
         out_ref[...] = packed_ref[...].astype(jnp.float32)
-    part = part_ref[...]
-    if more:
-        extra_ref, late_ref = more
-        ff = collect(rank_ref[...], extra_ref[...]) + late_ref[...].astype(jnp.float32)
-        part = part + gate_ref[...] * ff
-    mixed[...] = part.astype(LOW)
 
     @pl.when(pl.program_id(0) == 0)
     def _():
@@ -337,15 +326,14 @@
             lanes = slice(c * TILE, (c + 1) * TILE)
             router[:, lanes] = small[c * experts : (c + 1) * experts]
             for n in range(2):
-                at = lines * experts + n * lines + c
+                at = lines * experts + 16 + n * lines + c
                 gains[n : n + 1, lanes] = small[at : at + 1]
-        at = lines * experts + -(-2 * lines // 16) * 16
+        at = lines * experts + 16 + -(-2 * lines // 16) * 16
         table[...] = small[at : at + heads, :buckets]
 
 
-def unpack(packed, part, gate, rank, more, width, experts, heads, buckets, small_rows):
+def unpack(packed, width, experts, heads, buckets, small_rows):
     blocks = width // TILE
-    tokens = part.shape[0]
     source = lambda m: pl.BlockSpec((width, TILE), lambda i: (m * blocks + i, 0))
     column = lambda rows: pl.BlockSpec((rows, TILE), lambda i: (0, i))
     kept = lambda shape: pl.BlockSpec(shape, lambda i: (0, 0))
@@ -353,21 +341,18 @@
         functools.partial(unpack_kernel, experts, heads, buckets),
         grid=(blocks,),
         in_specs=[source(m) for m in range(4)]
-        + [pl.BlockSpec((small_rows, TILE), lambda i: (4 * blocks * width // small_rows, 0))]
-        + [column(tokens), whole((tokens, 1)), whole((tokens, 1))]
-        + [column(m.shape[0]) for m in more],
+        + [pl.BlockSpec((small_rows, TILE), lambda i: (4 * blocks * width // small_rows, 0))],
         out_specs=[column(width)] * 4
-        + [kept((experts, width)), kept((2, width)), kept((heads, buckets)), column(tokens)],
+        + [kept((experts, width)), kept((2, width)), kept((heads, buckets))],
         out_shape=[jax.ShapeDtypeStruct((width, width), jnp.float32)] * 4
         + [
             jax.ShapeDtypeStruct((experts, width), jnp.float32),
             jax.ShapeDtypeStruct((2, width), jnp.float32),
             jax.ShapeDtypeStruct((heads, buckets), jnp.float32),
-            jax.ShapeDtypeStruct((tokens, width), LOW),
-        ],
-        compiler_params=params(60),
+        ],
+        compiler_params=params(32),
         name="unpack",
-    )(*[packed] * 5, part, gate, rank, *more)
+    )(*[packed] * 5)
 
 
 def attention_forward_kernel(len_ref, q_ref, k_ref, v_ref, near_ref, far_ref, o_ref, p_ref, s_ref):
@@ -391,25 +376,27 @@
         after = far_ref[2 * pair + h, 0]
         before = far_ref[2 * pair + h, 1]
         tops = []
+        for i in range(0, tiles, 2):
+            q_i = q_h[i * TILE : (i + 2) * TILE]
+            raw = dot_t(k_h, q_i)
+            for c in range(2):
+                cols = slice((i + c) * TILE, (i + c + 1) * TILE)
+                top = None
+                for j in range(tiles):
+                    x = raw[j * TILE : (j + 1) * TILE, c * TILE : (c + 1) * TILE] * (0.125 * LOG2E)
+                    d = j - i - c
+                    if -1 <= d <= 1:
+                        x = x + near_ref[h, d + 1]
+                    else:
+                        x = x + (after if d > 0 else before)
+                    s_ref[h, j * TILE : (j + 1) * TILE, cols] = x
+                    m = jnp.max(x, axis=0, keepdims=True)
+                    top = m if top is None else jnp.maximum(top, m)
+                tops.append(top)
         for i in range(tiles):
-            q_i = q_h[i * TILE:(i + 1) * TILE]
-            raw = lax.dot_general(k_h, q_i, (((1,), (1,)), ((), ())), preferred_element_type=jnp.float32)
-            top = None
-            for j in range(tiles):
-                x = raw[j * TILE:(j + 1) * TILE] * (0.125 * LOG2E)
-                d = j - i
-                if -1 <= d <= 1:
-                    x = x + near_ref[h, d + 1]
-                else:
-                    x = x + (after if d > 0 else before)
-                s_ref[j * TILE:(j + 1) * TILE, i * TILE:(i + 1) * TILE] = x
-                m = jnp.max(x, axis=0, keepdims=True)
-                top = m if top is None else jnp.maximum(top, m)
-            tops.append(top)
-        for i in range(tiles):
-            e = jnp.exp2(s_ref[:, i * TILE:(i + 1) * TILE] - tops[i])
+            e = jnp.exp2(s_ref[h, :, i * TILE : (i + 1) * TILE] - tops[i])
             total = jnp.sum(e, axis=0, keepdims=True)
-            p_ref[0, h, :, i * TILE:(i + 1) * TILE] = (e * (1.0 / total)).astype(LOW)
+            p_ref[0, h, :, i * TILE : (i + 1) * TILE] = (e * (1.0 / total)).astype(LOW)
         outs.append(lax.dot_general(v_t[h * half:(h + 1) * half], p_ref[0, h], (((1,), (0,)), ((), ())), preferred_element_type=jnp.float32))
     o_ref[...] = jnp.concatenate(outs, axis=0).T.astype(o_ref.dtype)
 
@@ -434,7 +421,7 @@
             jax.ShapeDtypeStruct((rows * seq, width), LOW),
             jax.ShapeDtypeStruct((rows, heads, seq, seq), LOW),
         ],
-        scratch_shapes=[pltpu.VMEM((seq, seq), jnp.float32)],
+        scratch_shapes=[pltpu.VMEM((2, seq, seq), jnp.float32)],
         compiler_params=params(40),
         cost_estimate=cost(flops=4 * rows * heads * seq * seq * head * 4, bytes_accessed=rows * heads * seq * seq * 2, transcendentals=rows * heads * seq * seq),
         name="attention_forward",
@@ -475,22 +462,28 @@
         v_h = jnp.where(mine, v, jnp.zeros_like(v))
         delta = jnp.sum(weighed[h * half : (h + 1) * half], axis=0, keepdims=True)
         far_sum = [jnp.zeros((8, TILE), jnp.float32), jnp.zeros((8, TILE), jnp.float32)]
-        for i in range(tiles):
-            cols = slice(i * TILE, (i + 1) * TILE)
-            dp = dot_t(v_h, do[cols])
-            for j in range(tiles):
-                rws = slice(j * TILE, (j + 1) * TILE)
-                ds = p_ref[0, h, rws, cols].astype(jnp.float32) * (dp[rws] - delta[:, cols])
-                d = j - i
-                if -1 <= d <= 1:
-                    near_ref[h, d + 1] += ds
-                else:
-                    which = 0 if d > 0 else 1
-                    far_sum[which] = far_sum[which] + jnp.sum(ds.reshape(TILE // 8, 8, TILE), axis=0)
-                d_ref[rws, cols] = ds.astype(LOW)
+        for i in range(0, tiles, 2):
+            dp = dot_t(v_h, do[i * TILE : (i + 2) * TILE])
+            for c in range(2):
+                cols = slice((i + c) * TILE, (i + c + 1) * TILE)
+                for j in range(tiles):
+                    rws = slice(j * TILE, (j + 1) * TILE)
+                    part = dp[rws, c * TILE : (c + 1) * TILE] - delta[:, cols]
+                    ds = p_ref[0, h, rws, cols].astype(jnp.float32) * part
+                    d = j - i - c
+                    if -1 <= d <= 1:
+                        near_ref[h, d + 1] += ds
+                    else:
+                        which = 0 if d > 0 else 1
+                        far_sum[which] = far_sum[which] + jnp.sum(
+                            ds.reshape(TILE // 8, 8, TILE), axis=0
+                        )
+                    d_ref[h, rws, cols] = ds.astype(LOW)
         far_ref[h, 0] += far_sum[0]
         far_ref[h, 1] += far_sum[1]
-        ds_all = d_ref[...]
+    for h in range(2):
+        mine = (lane >= h * half) & (lane < (h + 1) * half)
+        ds_all = d_ref[h]
         dq_parts.append(dot(k_t[h * half : (h + 1) * half], ds_all))
         dk_h = dot(ds_all, q)
         dv_h = dot(p_ref[0, h], do)
@@ -628,7 +621,7 @@
         scratch_shapes=[
             pltpu.VMEM((2, 3, TILE, TILE), jnp.float32),
             pltpu.VMEM((2, 2, 8, TILE), jnp.float32),
-            pltpu.VMEM((seq, seq), LOW),
+            pltpu.VMEM((2, seq, seq), LOW),
             pltpu.VMEM((heads, 8, 2 * TILE), jnp.float32),
             pltpu.VMEM((width, 3 * TILE), jnp.float32),
             pltpu.VMEM((rows * seq, width), jnp.float32),
@@ -788,58 +781,53 @@
     )(*args)
 
 
-def device_place(cores, d):
-    return dict(device_id=(lax.div(d, cores), lax.rem(d, cores)), device_id_type=pl.DeviceIdType.MESH)
-
-
-def partner_of(me, b):
-    bit = lax.rem(lax.div(me, 1 << b), 2)
-    return bit, me + (1 - 2 * bit) * (1 << b)
-
-
-def greet(cores, bits, me):
+def split_units(units, weights):
+    total, sizes, done, so_far = sum(weights), [], 0, 0
+    for w in weights:
+        so_far += w
+        end = (2 * units * so_far + total) // (2 * total)
+        sizes.append(end - done)
+        done = end
+    return sizes
+
+
+def sum_parts(n, heights):
+    bits = n.bit_length() - 1
+    upper = list(range(1, bits))
+    orders = [[0] + upper[t:] + upper[:t] for t in range(3)]
+    parts, first = [], 0
+    for ref, rows in enumerate(heights):
+        units = rows // (16 * n)
+        turns = (0, 1, 2, 0, 1, 2) if units >= 18 else (0, 1, 2) if units >= 6 else (2,)
+        at = 0
+        for t, size in zip(turns, split_units(units, [(5, 5, 4)[t] for t in turns])):
+            parts.append((ref, at * 16 * n, first, size * 16, orders[t]))
+            at += size
+            first += size * 16 * n
+    return bits, parts
+
+
+def sum_kernel(cores, n, room, heights, extra, code_ref, gate_ref, rank_ref, ff_any, y_any, *refs):
+    _, cut, _ = plan(room)
+    xs, refs = refs[: len(heights)], refs[len(heights) :]
+    mixed_ref, out_ref, work_ref, got_ref, ff_ref, y_ref, *refs = refs
+    loads = [(ff_any, ff_ref), (y_any, y_ref)]
+    if extra:
+        tail_ref, *refs = refs
+    send, recv, local = refs
+    loads = [pltpu.make_async_copy(a, b, local.at[i]) for i, (a, b) in enumerate(loads)]
+    for copy in loads:
+        copy.start()
+    summed = heights[:-1] if extra else heights
+    bits, parts = sum_parts(n, summed)
+    full = len(parts)
+    if extra:
+        parts = parts + [(len(summed), 0, sum(summed), heights[-1] // n, list(range(bits)))]
+    me = lax.axis_index("grp") * cores + lax.axis_index("exp")
     barrier = pltpu.get_barrier_semaphore()
     for b in range(bits):
         pl.semaphore_signal(barrier, inc=1, **device_place(cores, partner_of(me, b)[1]))
     pl.semaphore_wait(barrier, bits)
-
-
-def rows_at(start, length):
-    return pl.ds(pl.multiple_of(start, 16), length)
-
-
-def sum_parts(n, heights):
-    bits = n.bit_length() - 1
-    upper = list(range(1, bits))
-    parts, first = [], 0
-    for ref, rows in enumerate(heights):
-        units = rows // (16 * n)
-        pieces = max(1, min(units, round(6 * rows / sum(heights))))
-        at = 0
-        for c in range(pieces):
-            size = (units + c) // pieces
-            t = len(parts) % 3
-            parts.append((ref, at * 16 * n, first, size * 16, [0] + upper[t:] + upper[:t]))
-            at += size
-            first += size * 16 * n
-    return bits, parts
-
-
-def sum_kernel(
-    cores, n, room, heights, code_ref, gate_ref, ff_any, y_any, *refs
-):
-    xs = refs[: len(heights)]
-    mixed_ref, out_ref, *rest = refs[len(heights) :]
-    work_ref, got_ref, ff_ref, y_ref, send, recv, local = rest
-    bits, parts = sum_parts(n, heights)
-    me = lax.axis_index("grp") * cores + lax.axis_index("exp")
-    loads = [
-        pltpu.make_async_copy(ff_any, ff_ref, local.at[0]),
-        pltpu.make_async_copy(y_any, y_ref, local.at[1]),
-    ]
-    for copy in loads:
-        copy.start()
-    greet(cores, bits, me)
     base = [first for _, _, first, _, _ in parts]
     got_at = list(base)
 
@@ -848,7 +836,10 @@
         length = step * (n >> (s + 1))
         bit, partner = partner_of(me, order[s])
         start = base[p] + (1 - bit) * length
-        source = xs[ref].at[rows_at(start - first + at, length)] if s == 0 else work_ref.at[rows_at(start, length)]
+        if s == 0:
+            source = xs[ref].at[rows_at(start - first + at, length)]
+        else:
+            source = work_ref.at[rows_at(start, length)]
         return pltpu.make_async_remote_copy(
             src_ref=source, dst_ref=got_ref.at[rows_at(got_at[p], length)],
             send_sem=send.at[p, s], recv_sem=recv.at[p, s], **device_place(cores, partner),
@@ -863,54 +854,60 @@
             **device_place(cores, partner_of(me, order[s])[1]),
         )
 
-    tokens = mixed_ref.shape[0]
+    tokens, width = mixed_ref.shape
     tile = tokens // 4
 
     def mix_tile(i):
-        if i >= 4:
-            return
-        if i == 0:
-            for copy in loads:
-                copy.wait()
         here = slice(i * tile, (i + 1) * tile)
-        ff = collect(segment(code_ref[here, :], room, 0, plan(room)[1]), ff_ref[...])
-        mixed_ref[here, :] = y_ref[here, :] + gate_ref[here, :] * ff
+        ff = collect(segment(code_ref[here, :], room, 0, cut), ff_ref[...])
+        if extra:
+            tail = tail_ref[...]
+            tail = [tail[c * extra : (c + 1) * extra] for c in range(width // TILE)]
+            ff = ff + collect(rank_ref[here, :], jnp.concatenate(tail, axis=1))
+        mixed_ref[here, :] = (y_ref[here, :] + gate_ref[here, :] * ff).astype(LOW)
 
     moving = [halving(p, 0) for p in range(len(parts))]
     for copy in moving:
         copy.start()
     sent = []
     for s in range(bits):
-        mix_tile(s - 1 if s else 9)
         for p, (ref, at, first, step, order) in enumerate(parts):
             length = step * (n >> (s + 1))
             moving[p].wait_recv()
             sent.append(moving[p])
             base[p] = base[p] + partner_of(me, order[s])[0] * length
             source, shift = (xs[ref], at - first) if s == 0 else (work_ref, 0)
-            target = work_ref if s + 1 < bits else out_ref
-
-            def add(i, _, start=base[p], source=source, shift=shift, target=target, arrived=got_at[p], step=step):
+            last = s + 1 == bits
+            target = out_ref if last else work_ref
+            if p >= full and last:
+                target = tail_ref
+
+            def add(
+                i, _, start=base[p], source=source, shift=shift, target=target, arrived=got_at[p],
+                step=step, to=0 if p >= full and last else base[p],
+            ):
                 got = got_ref[rows_at(arrived + i * step, step), :].astype(jnp.float32)
                 mine = source[rows_at(start + shift + i * step, step), :].astype(jnp.float32)
-                target[rows_at(start + i * step, step), :] = (mine + got).astype(LOW)
+                target[rows_at(to + i * step, step), :] = (mine + got).astype(LOW)
                 return 0
 
             lax.fori_loop(0, length // step, add, 0)
             got_at[p] += length
-            if s + 1 < bits:
+            if not last:
                 moving[p] = halving(p, s + 1)
-            else:
+                moving[p].start()
+            elif p < full:
                 moving[p] = doubling(p, s)
-            moving[p].start()
+                moving[p].start()
     for copy in sent:
         copy.wait_send()
+    for copy in loads:
+        copy.wait()
     sent = []
-    for s in reversed(range(bits)):
-        if s == bits - 1:
-            for i in range(bits - 1, 4):
-                mix_tile(i)
-        for p, (ref, at, first, step, order) in enumerate(parts):
+    for turn, s in enumerate(reversed(range(bits))):
+        for i in ((), (), (0,), (1, 2), (3,))[turn] if bits == 5 else range(4 * turn // bits, 4 * (turn + 1) // bits):
+            mix_tile(i)
+        for p, (ref, at, first, step, order) in enumerate(parts[:full]):
             length = step * (n >> (s + 1))
             moving[p].wait_recv()
             sent.append(moving[p])
@@ -922,36 +919,46 @@
         copy.wait_send()
 
 
-def all_sum(xs, code, gate, ff, y, room):
+def all_sum(xs, code, gate, rank, ff, y, room, ff_more):
     cores = lax.axis_size("exp")
     n = lax.axis_size(AXES)
+    extra = plan(room)[2]
     heights = [a.shape[0] for a in xs]
     if any(h % (16 * n) for h in heights):
         xs = [jnp.concatenate(xs[:-1], axis=0), xs[-1]]
         heights = [a.shape[0] for a in xs]
     total = sum(heights)
     bits, parts = sum_parts(n, heights)
+    count = len(parts)
+    rows = total
     tokens, width = y.shape
-    buffer = pltpu.VMEM((total, TILE), LOW)
+    tail = []
+    if extra:
+        xs = xs + [ff_more]
+        heights = heights + [ff_more.shape[0]]
+        rows += ff_more.shape[0]
+        count += 1
+        tail = [pltpu.VMEM((extra * width // TILE, TILE), LOW)]
+    buffer = pltpu.VMEM((rows, TILE), LOW)
     vmem = pl.BlockSpec(memory_space=pltpu.VMEM)
     anywhere = pl.BlockSpec(memory_space=pl.ANY)
     return pl.pallas_call(
-        functools.partial(sum_kernel, cores, n, room, heights),
+        functools.partial(sum_kernel, cores, n, room, heights, extra),
         out_shape=[
-            jax.ShapeDtypeStruct((tokens, width), jnp.float32),
+            jax.ShapeDtypeStruct((tokens, width), LOW),
             jax.ShapeDtypeStruct((total, TILE), LOW),
         ],
-        in_specs=[vmem, vmem, anywhere, anywhere] + [vmem] * len(xs),
+        in_specs=[vmem] * 3 + [anywhere] * 2 + [vmem] * len(xs),
         out_specs=[vmem] * 2,
         scratch_shapes=[
-            buffer, buffer, pltpu.VMEM(ff.shape, LOW), pltpu.VMEM(y.shape, jnp.float32),
-            pltpu.SemaphoreType.DMA((len(parts), 2 * bits)),
-            pltpu.SemaphoreType.DMA((len(parts), 2 * bits)),
+            buffer, buffer, pltpu.VMEM(ff.shape, LOW), pltpu.VMEM(y.shape, jnp.float32), *tail,
+            pltpu.SemaphoreType.DMA((count, 2 * bits)),
+            pltpu.SemaphoreType.DMA((count, 2 * bits)),
             pltpu.SemaphoreType.DMA((2,)),
         ],
         compiler_params=params(60, collective_id=1, has_side_effects=True),
         name="all_sum",
-    )(code, gate, ff, y, *xs)
+    )(code, gate, rank, ff, y, *xs)
 
 
 def local(
@@ -974,9 +981,7 @@
     mine = (jnp.arange(wide, dtype=jnp.int32) == me).astype(jnp.float32).reshape(1, wide)
 
     segments, cut, extra = plan(room)
-    code_c, code_r, rank_c, g_out, g_more = route(expert_ids, slots, g, experts, room)
-    if extra:
-        g_more = lax.all_gather(g_more, AXES, axis=0, tiled=False)
+    code_c, code_r, rank_c, flag, g_out = route(expert_ids, slots, g, experts, room)
     g_in = exchange(g_out, devices)
     code_r, x, w_query, w_key, w_value, w_output, bias_table, w_router = lax.optimization_barrier(
         (code_r, x, w_query, w_key, w_value, w_output, bias_table, w_router)
@@ -990,49 +995,15 @@
         joined, x, w_output, gain_two, expert_ids.reshape(count, 1), router_w, code_r, experts, room
     )
     h_out, g_in = lax.optimization_barrier((h_out, g_in))
-    g_in = g_in.reshape(devices, cut, width)
+    g_in = g_in.reshape(devices, room, width)
     h_in = [exchange(h_out[0], devices)]
-    g_parts = [(g_in, low, high) for low, high in segments]
-    late = None
-    if extra:
-        spare = room - cut
-        h_in[0], g_more = lax.optimization_barrier((h_in[0], g_more))
-        marks = g_more[:, extra, : extra + 1].astype(jnp.float32)
-        late = jnp.any(marks[:, extra] > 0)
-        mine_marks = marks[:, :extra] == (me + 1).astype(jnp.float32)
-        order = jnp.cumsum(mine_marks.astype(jnp.int32), axis=1) - 1
-        chosen = (
-            mine_marks[:, None, :]
-            & (order[:, None, :] == jnp.arange(spare, dtype=jnp.int32)[None, :, None])
-        ).astype(LOW)
-        flat_code, flat_rank = code_c.reshape(-1), rank_c.reshape(-1)
-        flat_expert = flat_code // room
-        rest = jnp.where(
-            flat_rank >= extra,
-            flat_expert * spare + flat_code - flat_expert * room - cut,
-            experts * spare,
-        )
-
-        def send_rest(rest):
-            empty = jnp.zeros((experts * spare, width), LOW)
-            return exchange(empty.at[rest].set(g, mode="drop"), devices)
-
-        g_rest = lax.cond(
-            late, send_rest, lambda rest: jnp.zeros((experts * spare, width), LOW), rest
-        )
-        h_out[1], g_rest = lax.optimization_barrier((h_out[1], g_rest))
-        g_spare = jnp.einsum(
-            "sqr,srw->sqw", chosen, g_more[:, :extra], preferred_element_type=jnp.float32
-        ).astype(LOW) + g_rest.reshape(devices, spare, width)
-        low, high = segments[1]
-        g_parts[1] = (jnp.concatenate([g_in[:, low:], g_spare], axis=1), 0, high - low)
     for h in h_out[1:]:
         h, h_in[-1] = lax.optimization_barrier((h, h_in[-1]))
         h_in.append(exchange(h, devices))
     dx_back, ffs, parts, grad_router = [], [], [], 0.0
     for n, (low, high) in enumerate(segments):
         ff, dx, hid, da, x_t, dff_t, routed = expert_rows(
-            h_in[n], g_parts[n][0], mine, router_w, w_in[0], w_out[0], experts, *g_parts[n][1:]
+            h_in[n], g_in, mine, router_w, w_in[0], w_out[0], experts, low, high
         )
         if n + 1 < len(segments):
             dx, h_in[n + 1] = lax.optimization_barrier((dx, h_in[n + 1]))
@@ -1043,48 +1014,55 @@
         parts.append((x_t, dff_t, hid, da))
         grad_router = grad_router + routed
     grad_in, grad_out = expert_weights(parts)
-    ff = jnp.concatenate(ffs, axis=1) if len(ffs) > 1 else ffs[0]
-    more = []
-    if extra:
-        ff_spare = ff[:, cut:]
-        ff_more = jnp.einsum(
-            "sqr,sqw->srw", chosen, ff_spare, preferred_element_type=jnp.float32
-        ).astype(LOW)
-        ff_more = lax.psum_scatter(
-            ff_more.reshape(devices * extra, width), AXES, scatter_dimension=0, tiled=True
-        )
-        dx_back, ff_spare = lax.optimization_barrier((dx_back, ff_spare))
-
-        def return_rest(spare_rows, rest):
-            back = exchange(spare_rows.reshape(devices * spare, width), devices)
-            return jnp.take(back, rest, axis=0, mode="fill", fill_value=0)
-
-        ff_rest = lax.cond(
-            late, return_rest, lambda *_: jnp.zeros((count, width), LOW), ff_spare, rest
-        )
-        dx_back, ff_rest = lax.optimization_barrier((dx_back, ff_rest))
-        more = [ff_more, ff_rest]
-    ff = ff[:, :cut].reshape(devices * cut, width)
-    dx_back, grad_in, grad_out, ff = lax.optimization_barrier((dx_back, grad_in, grad_out, ff))
-    ff_back = exchange(ff, devices)
     grad_router = grad_router[:experts].reshape(experts, width // TILE, TILE)
     grad_router = jnp.swapaxes(grad_router, 0, 1).reshape(-1, TILE)
+    small = jnp.concatenate([grad_router, flag], axis=0)
+    ff, ff_more = ffs[0], small
+    if extra:
+        half = segments[0][1]
+        ff = jnp.concatenate([ffs[0], ffs[1][:, : cut - half]], axis=1)
+        ff_spare = ffs[1][:, cut - half :]
+        bits = devices.bit_length() - 1
+        ff_more = ff_spare.reshape((2,) * bits + (extra, width // TILE, TILE))
+        order = tuple(reversed(range(bits))) + (bits + 1, bits, bits + 2)
+        ff_more = jnp.transpose(ff_more, order).reshape(-1, TILE)
+    ff = ff.reshape(devices * cut, width)
+    dx_back, grad_in, grad_out, ff, ff_more, small = lax.optimization_barrier(
+        (dx_back, grad_in, grad_out, ff, ff_more, small)
+    )
+    ff_back = exchange(ff, devices)
 
     dy, do, grad_output, grad_gain_two = before_attention(
         dx_back, code_c, y, g, gain_two, w_output, joined, room
     )
     lines = width // TILE
-    small_rows = grad_router.shape[0] + -(-2 * lines // 16) * 16 + -(-heads // 16) * 16
+    small_rows = small.shape[0] + -(-2 * lines // 16) * 16 + -(-heads // 16) * 16
     small_rows = -(-small_rows // (16 * devices)) * 16 * devices
     grad_tokens, packed, small = attention_backward(
         projected, do, joined, weights, normed_t, w_query, w_key, w_value, x, dy, gain_one,
-        grad_router, grad_gain_two, rows, seq, heads, head, small_rows,
+        small, grad_gain_two, rows, seq, heads, head, small_rows,
     )
     mixed, summed = all_sum(
-        [packed.reshape(-1, TILE), grad_output, small], code_c, gate, ff_back, y, room
-    )
-    *grads, router_t, gains, table, mixed = unpack(
-        summed, mixed, gate, rank_c, more, width, experts, heads, buckets, small_rows
+        [packed.reshape(-1, TILE), grad_output, small], code_c, gate, rank_c, ff_back, y, room, ff_more
+    )
+    if extra:
+        crowded = summed[4 * width * width // TILE + lines * experts, 0] > 0
+
+        def mix_all(mixed):
+            del mixed
+            code = code_c.reshape(-1)
+            expert = code // room
+            place = code - expert * room
+            spare = exchange(ff_spare.reshape(-1, width), devices)
+            first = jnp.where((code >= 0) & (place < cut), expert * cut + place, devices * cut)
+            rest = jnp.where(place >= cut, expert * extra + place - cut, devices * extra)
+            take = lambda a, index: jnp.take(a, index, axis=0, mode="fill", fill_value=0)
+            ff = take(ff_back, first) + take(spare, rest)
+            return (y + gate * ff.astype(jnp.float32)).astype(LOW)
+
+        mixed = lax.cond(crowded, mix_all, lambda mixed: mixed, mixed)
+    *grads, router_t, gains, table = unpack(
+        summed, width, experts, heads, buckets, small_rows
     )
     return (
         mixed.reshape(rows, seq, width),

time: 420 us -> 404 us (0.962)
  blocking collectives: 0 us -> 42.1 us
  waiting for transfers between devices: 59.8 us -> 37 us
  Pallas kernels: 278 us -> 262 us
  between operations: 15.2 us -> 1.81 us
  local copies, waits for them, and re-layouts: 20.2 us -> 27.2 us
  starting transfers between devices: 27.5 us -> 22.7 us
  matrix products: 6.49 us -> 2.01 us
    all_to_all x0 -> x1, blocking collectives: none -> 42.1 us  [exchange(): lax.all_to_all(shaped, AXES, split_axis=0, concat_axis=0, tiled=True)]
    all_to_all x6 -> x5, waiting for transfers between devices: 50.8 us -> 37 us  [exchange(): lax.all_to_all(shaped, AXES, split_axis=0, concat_axis=0, tiled=True)]
    unnamed x42 -> x49, local copies, waits for them, and re-layouts: 11.8 us -> 20.9 us
    all_gather x1 -> x0, waiting for transfers between devices: 8.44 us -> none  [local(): g_more = lax.all_gather(g_more, AXES, axis=0, tiled=False)]
    pallas_call x1, Pallas kernels: 10.6 us -> 4.19 us  [unpack(): pl.pallas_call(functools.partial(unpack_kernel, experts, heads, buckets),...]
    dot_general x2 -> x0, matrix products: 4.39 us -> none  [the longest x1 2.46 us: local(): jnp.einsum('sqr,sqw->srw', chosen, ff_spare, preferred_element_type=jnp.f...]
    all_to_all x6 -> x5, starting transfers between devices: 27 us -> 22.7 us  [exchange(): lax.all_to_all(shaped, AXES, split_axis=0, concat_axis=0, tiled=True)]
  transfers between devices with their start and end apart: 8 -> 5, of which waited for: 6 -> 4; matrix products, arithmetic and copies ran while one was open for 4% -> 3% of each run, Pallas kernels for 62% -> 46%
where the time goes in v5:
time: 404 us; the launch traced here: 399 us
  Pallas kernels  262 us (65%)
  blocking collectives  42.1 us (10%)
  waiting for transfers between devices  37 us (9%)
  local copies, waits for them, and re-layouts  27.2 us (7%)
  starting transfers between devices  22.7 us (6%)
    pallas_call x1, Pallas kernels, all_sum(): pl.pallas_call(functools.partial(sum_kernel, cores, n, room, heights, ext...  67.4 us
    pallas_call x2, Pallas kernels, expert_rows(): pl.pallas_call(functools.partial(expert_kernel, experts, chunk), grid=(n...  61.1 us
    pallas_call x1, Pallas kernels, attention_backward(): pl.pallas_call(attention_backward_kernel, grid=(pairs, rows), in_specs=[s...  42.5 us
    all_to_all x1, blocking collectives, exchange(): lax.all_to_all(shaped, AXES, split_axis=0, concat_axis=0, tiled=True)  42.1 us
    all_to_all x5, waiting for transfers between devices, exchange(): lax.all_to_all(shaped, AXES, split_axis=0, concat_axis=0, tiled=True)  37 us
    pallas_call x1, Pallas kernels, expert_weights(): pl.pallas_call(functools.partial(expert_weights_kernel, len(parts)), grid...  27.8 us
    all_to_all x5, starting transfers between devices, exchange(): lax.all_to_all(shaped, AXES, split_axis=0, concat_axis=0, tiled=True)  22.7 us
    pallas_call x1, Pallas kernels, attention_forward(): pl.pallas_call(attention_forward_kernel, grid=(rows, pairs), in_specs=[pl...  21.3 us
  transfers between devices with their start and end apart: 5, of which 4 were waited for; matrix products, arithmetic and copies ran while one was open for 3% of the time, Pallas kernels for 46%

profile of v5, /device:TPU:0, one launch (start us, length us, event | category | flops | bytes accessed | tf_op | source)
XLA Modules:
  0.0 399.1 jit_solution(9008520826103467033)
XLA Ops:
  0.6 0.7 copy.50
  1.3 0.2 copy.51
  1.6 0.0 copy-start.2
  1.6 0.7 copy.53
  2.3 0.2 copy.54
  2.5 0.0 copy-start.4
  2.5 1.4 copy-done.4
  3.9 6.5 %route.1 = (s32[1024,1]{1,0:T(8,128)}, s32[1,1024]{1,0:T(1,128)S(1)}, s32[1024,1]{1,0:T(8,128)S(1)}, f32[16,128]{1,0:T(8,128)S(1)}, bf16[2048,768]{1,0:T(8,128)(2,1)}) custom-call(s32[1024,1]{1,0:T(8,128)S(1)} %bitcast.58, s32[1,1024]{1,0:T(1,128)S(1)} %bitcast.62, s32[1024,1]{1,0:T(8,128)S(1)} %bitcast.60, s32[1,1024]{1,0:T(1,128)S(1)} %bitcast.64, ...), custom_call_target="tpu_custom_call" | custom-call | flops 3221225472 | bytes 8388608 | tf_op jit(solution)/shard_map/route/pallas_call | solution.py:143
  10.4 0.8 copy-done.1
  11.2 0.6 copy-done.13
  11.8 7.6 %all-to-all-start.1 = ((bf16[32,64,768]{2,1,0:T(8,128)(2,1)}), bf16[32,64,768]{2,1,0:T(8,128)(2,1)}, u32[]{:S(2)}, u32[]{:S(2)}) async-start(bf16[32,64,768]{2,1,0:T(8,128)(2,1)} %bitcast.78), calls=%async_computation.1 | async-start | bytes 6291456 | tf_op jit(solution)/shard_map/all_to_all | solution.py:160
  19.4 0.0 copy-start.3
  19.4 0.1 copy.42
  19.5 0.1 copy.43.far_ref
  19.6 0.1 fusion.4
  19.8 0.2 fusion.2
  19.9 2.0 fusion
  21.9 0.6 copy.56
  22.6 0.0 copy-start.19
  22.6 0.0 copy-start.22
  22.6 0.2 slice.42
  22.8 0.6 copy-done.19
  23.4 0.2 copy.44
  23.5 0.6 reshape.216.gain_ref
  24.1 0.7 pad.4.wr_ref
  24.8 1.4 copy-done.5
  26.2 1.3 copy-done.6
  27.5 1.3 copy-done.7
  28.8 1.3 copy-done.8
  30.1 5.0 %project.1 = (bf16[768,1024]{1,0:T(8,128)(2,1)S(1)}, bf16[1024,2304]{1,0:T(8,128)(2,1)S(1)}) custom-call(bf16[1024,768]{1,0:T(8,128)(2,1)S(1)} %bitcast.69, f32[1,768]{1,0:T(1,128)S(1)} %reshape.214.gain_ref, bf16[768,768]{1,0:T(8,128)(2,1)S(1)} %copy-done.6, bf16[768,768]{1,0:T(8,128)(2,1)S(1)} %copy-done.7, bf16[768,768]{1,0:T(8,128)(2,1)S(1)} %copy-done.8), custom_call_target="tpu_custom_call" | custom-call | flops 3623878656 | bytes 12582912 | tf_op jit(solution)/shard_map/project/pallas_call | solution.py:179
  35.0 1.2 copy-done.12
  36.2 21.3 %attention_forward.1 = (bf16[1024,768]{1,0:T(8,128)(2,1)S(1)}, bf16[2,12,512,512]{3,2,1,0:T(8,128)(2,1)}) custom-call(s32[2]{0:T(128)S(1)} %copy-done.9, bf16[1024,2304]{1,0:T(8,128)(2,1)S(1)} %get-tuple-element.108.q_ref.k_ref.v_ref, bf16[1024,2304]{1,0:T(8,128)(2,1)S(1)} %get-tuple-element.108.q_ref.k_ref.v_ref, ...), custom_call_target="tpu_custom_call" | custom-call | flops 6442450944 | bytes 12582912 | tf_op jit(solution)/shard_map/attention_forward/pallas_call | solution.py:407
  57.5 1.1 copy-done.10
  58.7 12.3 %after_attention.1 = (f32[1024,768]{1,0:T(8,128)}, f32[1024,1]{1,0:T(8,128)}, bf16[1024,768]{1,0:T(8,128)(2,1)}, bf16[1024,768]{1,0:T(8,128)(2,1)}) custom-call(bf16[1024,768]{1,0:T(8,128)(2,1)} %copy-done.10, bf16[1024,768]{1,0:T(8,128)(2,1)} %bitcast.67, bf16[768,768]{1,0:T(8,128)(2,1)} %w_ref.1, f32[1,768]{1,0:T(1,128)} %reshape.216.gain_ref, ...), custom_call_target="tpu_custom_call" | custom-call | flops 4429185024 | bytes 12582912 | tf_op jit(solution)/shard_map/after_attention/pallas_call | solution.py:220
  70.9 19.9 %all-to-all-done.1 = bf16[32,64,768]{2,1,0:T(8,128)(2,1)} async-done(((bf16[32,64,768]{2,1,0:T(8,128)(2,1)}), bf16[32,64,768]{2,1,0:T(8,128)(2,1)}, u32[]{:S(2)}, u32[]{:S(2)}) %all-to-all-start.1) | async-done | bytes 3145760 | tf_op jit(solution)/shard_map/all_to_all | solution.py:160
  90.8 42.1 %all_to_all.34 = bf16[32,32,768]{2,1,0:T(8,128)(2,1)} all-to-all(bf16[32,32,768]{2,1,0:T(8,128)(2,1)} %bitcast.86), channel_id=1, replica_groups=mesh['grp'=16,'exp'=2] {'grp','exp'}, dimensions={0} | all-to-all | bytes 3145728 | tf_op jit(solution)/shard_map/all_to_all | solution.py:160
  132.9 3.5 all-to-all-start.3
  136.4 0.5 compare_convert_fusion.mine_ref
  136.9 30.5 %expert_rows.2 = (bf16[1024,768]{1,0:T(8,128)(2,1)}, bf16[1024,768]{1,0:T(8,128)(2,1)}, bf16[1024,3072]{1,0:T(8,128)(2,1)}, bf16[1024,3072]{1,0:T(8,128)(2,1)}, ...) custom-call(bf16[1024,768]{1,0:T(8,128)(2,1)} %bitcast.83, ...), custom_call_target="tpu_custom_call" | custom-call | flops 19327352832 | bytes 31457280 | tf_op jit(solution)/shard_map/expert_rows/pallas_call | solution.py:727
  167.4 6.7 %all-to-all-done.3 = bf16[32,32,768]{2,1,0:T(8,128)(2,1)S(1)} async-done(((bf16[32,32,768]{2,1,0:T(8,128)(2,1)}), bf16[32,32,768]{2,1,0:T(8,128)(2,1)S(1)}, u32[]{:S(2)}, u32[]{:S(2)}) %all-to-all-start.3) | async-done | bytes 1572896 | tf_op jit(solution)/shard_map/all_to_all | solution.py:160
  174.1 1.1 copy-done.17
  175.2 3.8 all-to-all-start.4
  179.0 30.5 %expert_rows.3 = (bf16[1024,768]{1,0:T(8,128)(2,1)}, bf16[1024,768]{1,0:T(8,128)(2,1)}, bf16[1024,3072]{1,0:T(8,128)(2,1)}, bf16[1024,3072]{1,0:T(8,128)(2,1)}, ...) custom-call(bf16[1024,768]{1,0:T(8,128)(2,1)} %bitcast.80, ...), custom_call_target="tpu_custom_call" | custom-call | flops 19327352832 | bytes 31457280 | tf_op jit(solution)/shard_map/expert_rows/pallas_call | solution.py:727
  209.6 7.2 %all-to-all-done.4 = bf16[32,32,768]{2,1,0:T(8,128)(2,1)S(1)} async-done(((bf16[32,32,768]{2,1,0:T(8,128)(2,1)}), bf16[32,32,768]{2,1,0:T(8,128)(2,1)S(1)}, u32[]{:S(2)}, u32[]{:S(2)}) %all-to-all-start.4) | async-done | bytes 1572896 | tf_op jit(solution)/shard_map/all_to_all | solution.py:160
  216.8 1.2 copy-done.16
  217.9 3.9 all-to-all-start.5
  221.8 1.0 slice_add_fusion
  222.8 1.5 fusion.9
  224.3 0.9 reshape.231
  225.2 0.0 copy-start.18
  225.2 1.0 copy.46
  226.3 0.6 pad_maximum_fusion.1.gr_ref
  226.9 1.6 pad_maximum_fusion
  228.5 27.8 %expert_weights.1 = (f32[1,768,3072]{2,1,0:T(8,128)}, f32[1,3072,768]{2,1,0:T(8,128)}) custom-call(bf16[768,1024]{1,0:T(8,128)(2,1)} %get-tuple-element.130.refs_0_, bf16[768,1024]{1,0:T(8,128)(2,1)} %get-tuple-element.131.refs_1_, bf16[1024,3072]{1,0:T(8,128)(2,1)} %get-tuple-element.132.refs_2_, bf16[1024,3072]{1,0:T(8,128)(2,1)} %get-tuple-element.133.refs_3_, ...), custom_call_target="tpu_custom_call" | custom-call | flops 19327352832 | bytes 44040192 | tf_op jit(solution)/shard_map/expert_weights/pallas_call | solution.py:766
  256.3 3.2 all-to-all-done.5
  259.5 3.9 all-to-all-start.6
  263.5 14.5 %before_attention.1 = (f32[1024,768]{1,0:T(8,128)}, bf16[1024,768]{1,0:T(8,128)(2,1)}, bf16[4608,128]{1,0:T(8,128)(2,1)}, f32[1,768]{1,0:T(1,128)}) custom-call(s32[1024,1]{1,0:T(8,128)} %get-tuple-element.102.code_ref, f32[1024,768]{1,0:T(8,128)} %get-tuple-element.146.y_ref.y_any, bf16[1024,768]{1,0:T(8,128)(2,1)} %bitcast.65, ...), custom_call_target="tpu_custom_call" | custom-call | flops 3623878656 | bytes 16777216 | tf_op jit(solution)/shard_map/before_attention/pallas_call | solution.py:290
  278.0 42.5 %attention_backward.1 = (f32[1024,768]{1,0:T(8,128)}, bf16[3,6,768,128]{3,2,1,0:T(8,128)(2,1)}, bf16[512,128]{1,0:T(8,128)(2,1)}) custom-call(bf16[1024,2304]{1,0:T(8,128)(2,1)} %copy-done.11, bf16[1024,2304]{1,0:T(8,128)(2,1)} %copy-done.11, bf16[1024,2304]{1,0:T(8,128)(2,1)} %copy-done.11, bf16[1024,768]{1,0:T(8,128)(2,1)} %get-tuple-element.149.do_ref, ...), custom_call_target="tpu_custom_call" | custom-call | flops 12884901888 | bytes 12582912 | tf_op jit(solution)/shard_map/attention_backward/pallas_call | solution.py:601
  320.5 67.4 %all_sum.1 = (bf16[1024,768]{1,0:T(8,128)(2,1)}, bf16[18944,128]{1,0:T(8,128)(2,1)}) custom-call(s32[1024,1]{1,0:T(8,128)} %get-tuple-element.102.code_ref, f32[1024,1]{1,0:T(8,128)} %get-tuple-element.114.gate_ref, s32[1024,1]{1,0:T(8,128)} %copy-done.1, bf16[1536,768]{1,0:T(8,128)(2,1)S(1)} %bitcast.71, f32[1024,768]{1,0:T(8,128)} %get-tuple-element.146.y_ref.y_any, ...), custom_call_target="tpu_custom_call" | custom-call | tf_op jit(solution)/shard_map/all_sum/pallas_call | solution.py:945
  387.9 2.4 copy-done
  390.2 4.2 %unpack.1 = (f32[768,768]{1,0:T(8,128)}, f32[768,768]{1,0:T(8,128)}, f32[768,768]{1,0:T(8,128)}, f32[768,768]{1,0:T(8,128)}, f32[32,768]{1,0:T(8,128)}, /*index=5*/f32[2,768]{1,0:T(2,128)S(1)}, f32[12,32]{1,0:T(8,128)}) custom-call(bf16[18944,128]{1,0:T(8,128)(2,1)S(1)} %copy-done, bf16[18944,128]{1,0:T(8,128)(2,1)S(1)} %copy-done, ...), custom_call_target="tpu_custom_call" | custom-call | tf_op jit(solution)/shard_map/unpack/pallas_call | solution.py:340
  394.4 0.5 slice.29
  395.0 0.6 slice_reduce_fusion
  396.2 2.7 copy.60
  (32 shorter events, 0.1 us)
Async XLA Ops:
  1.6 8.8 %copy-start.2 = (s32[1,1024]{0,1:T(8,128)}, s32[1,1024]{0,1:T(8,128)S(1)}, u32[]{:S(2)}) copy-start(s32[1,1024]{0,1:T(8,128)S(1)} %copy.51) | copy-start | bytes 12292
  2.5 1.4 copy-start.4
  10.4 0.8 copy-start.1
  11.2 0.6 copy-start.13
  11.2 8.2 %copy-start.21 = (f32[768]{0:T(1024)S(1)}, f32[768]{0:T(1024)}, u32[]{:S(2)}) copy-start(f32[768]{0:T(1024)} %param.25) | copy-start | bytes 9220
  11.2 8.2 %copy-start.20 = (f32[32,12]{0,1:T(8,128)S(1)}, f32[32,12]{0,1:T(8,128)}, u32[]{:S(2)}) copy-start(f32[32,12]{0,1:T(8,128)} %param.27) | copy-start | bytes 4612
  11.8 79.0 %all-to-all-start.1 = ((bf16[32,64,768]{2,1,0:T(8,128)(2,1)}), bf16[32,64,768]{2,1,0:T(8,128)(2,1)}, u32[]{:S(2)}, u32[]{:S(2)}) async-start(bf16[32,64,768]{2,1,0:T(8,128)(2,1)} %bitcast.78), calls=%async_computation.1 | async-start | bytes 6291456 | tf_op jit(solution)/shard_map/all_to_all | solution.py:160
  19.4 5.4 %copy-start.3 = (f32[1,768]{1,0:T(1,128)}, f32[1,768]{1,0:T(1,128)S(1)}, u32[]{:S(2)}) copy-start(f32[1,768]{1,0:T(1,128)S(1)} %reshape.214.gain_ref) | copy-start | bytes 9220
  22.6 0.8 copy-start.19
  22.6 1.0 copy-start.22
  24.8 1.4 copy-start.5
  26.2 1.3 copy-start.6
  27.5 1.3 copy-start.7
  28.8 1.3 copy-start.8
  30.1 6.2 %copy-start.9 = (s32[2]{0:T(128)S(1)}, s32[2]{0:T(128)}, u32[]{:S(2)}) copy-start(s32[2]{0:T(128)} %len_ref.1) | copy-start | bytes 28
  35.0 1.2 copy-start.12
  36.2 21.3 %copy-start.11 = (bf16[1024,2304]{1,0:T(8,128)(2,1)}, bf16[1024,2304]{1,0:T(8,128)(2,1)S(1)}, u32[]{:S(2)}) copy-start(bf16[1024,2304]{1,0:T(8,128)(2,1)S(1)} %get-tuple-element.108.q_ref.k_ref.v_ref) | copy-start | bytes 14155780
  57.5 1.1 copy-start.10
  132.9 41.2 %all-to-all-start.3 = ((bf16[32,32,768]{2,1,0:T(8,128)(2,1)}), bf16[32,32,768]{2,1,0:T(8,128)(2,1)S(1)}, u32[]{:S(2)}, u32[]{:S(2)}) async-start(bf16[32,32,768]{2,1,0:T(8,128)(2,1)} %bitcast.82), calls=%async_computation.3 | async-start | bytes 3145728 | tf_op jit(solution)/shard_map/all_to_all | solution.py:160
  174.1 1.1 copy-start.17
  175.2 41.5 %all-to-all-start.4 = ((bf16[32,32,768]{2,1,0:T(8,128)(2,1)}), bf16[32,32,768]{2,1,0:T(8,128)(2,1)S(1)}, u32[]{:S(2)}, u32[]{:S(2)}) async-start(bf16[32,32,768]{2,1,0:T(8,128)(2,1)} %bitcast.84), calls=%async_computation.4 | async-start | bytes 3145728 | tf_op jit(solution)/shard_map/all_to_all | solution.py:160
  216.8 1.2 copy-start.16
  217.9 41.6 %all-to-all-start.5 = ((bf16[32,32,768]{2,1,0:T(8,128)(2,1)}), bf16[32,32,768]{2,1,0:T(8,128)(2,1)}, u32[]{:S(2)}, u32[]{:S(2)}) async-start(bf16[32,32,768]{2,1,0:T(8,128)(2,1)} %bitcast.81), calls=%async_computation.5 | async-start | bytes 3145728 | tf_op jit(solution)/shard_map/all_to_all | solution.py:160
  225.2 1.7 copy-start.18
  259.5 60.9 %all-to-all-start.6 = ((bf16[32,48,768]{2,1,0:T(8,128)(2,1)}), bf16[32,48,768]{2,1,0:T(8,128)(2,1)S(1)}, u32[]{:S(2)}, u32[]{:S(2)}) async-start(bf16[32,48,768]{2,1,0:T(8,128)(2,1)} %pad_maximum_fusion), calls=%async_computation.6 | async-start | bytes 4718592 | tf_op jit(solution)/shard_map/all_to_all | solution.py:160
  387.9 2.4 copy-start

commit v6 on v5

--- a/solution.py
+++ b/solution.py
@@ -263,20 +263,24 @@
         gw_ref[...] = jnp.zeros_like(gw_ref)
         gg_ref[...] = jnp.zeros_like(gg_ref)
 
-    dh = collect_all(code_ref[...], room, backs)
-    y = y_ref[...]
-    rms = lax.rsqrt(jnp.mean(y * y, axis=-1, keepdims=True) + EPSILON)
-    gg_ref[...] += jnp.sum(dh * y * rms, axis=0, keepdims=True)
-    u = dh * gain_ref[...]
-    dy = (
-        g_ref[...].astype(jnp.float32)
-        + rms * u
-        - y * (rms * rms * rms) * jnp.mean(u * y, axis=-1, keepdims=True)
-    )
-    dy_ref[...] = dy
-    low = dy.astype(LOW)
-    do_ref[...] = dot_t(low, w_ref[...]).astype(LOW)
-    gw_ref[...] += dot(o_ref[...].T, low)
+    step = y_ref.shape[0] // 2
+    blocks = [slice(n * step, (n + 1) * step) for n in range(2)]
+    dhs = [collect_all(code_ref[here, :], room, backs) for here in blocks]
+    lows = []
+    for here, dh in zip(blocks, dhs):
+        y = y_ref[here, :]
+        rms = lax.rsqrt(jnp.mean(y * y, axis=-1, keepdims=True) + EPSILON)
+        gg_ref[...] += jnp.sum(dh * y * rms, axis=0, keepdims=True)
+        u = dh * gain_ref[...]
+        dy = (
+            g_ref[here, :].astype(jnp.float32)
+            + rms * u
+            - y * (rms * rms * rms) * jnp.mean(u * y, axis=-1, keepdims=True)
+        )
+        dy_ref[here, :] = dy
+        lows.append(dy.astype(LOW))
+        do_ref[here, :] = dot_t(lows[-1], w_ref[...]).astype(LOW)
+    gw_ref[...] += dot(o_ref[...].T, jnp.concatenate(lows, axis=0))
 
     @pl.when(i == pl.num_programs(0) - 1)
     def _():
@@ -285,7 +289,7 @@
 
 def before_attention(backs, code, y, g, gain, w_output, joined, room):
     tokens, width = y.shape
-    step = 256
+    step = 512
     rows = lambda w: pl.BlockSpec((step, w), lambda i: (i, 0))
     return pl.pallas_call(
         functools.partial(before_attention_kernel, room, len(backs)),
@@ -313,10 +317,13 @@
 
 
 def unpack_kernel(
-    experts, heads, buckets, q_ref, k_ref, v_ref, o_ref, small_ref, gq, gk, gv, go, router, gains, table
+    experts, heads, buckets, q_ref, k_ref, v_ref, o_ref, small_ref, mix_ref,
+    gq, gk, gv, go, router, gains, table, mixed,
 ):
+    mixed[...] = mix_ref[...]
     for packed_ref, out_ref in ((q_ref, gq), (k_ref, gk), (v_ref, gv), (o_ref, go)):
-        out_ref[...] = packed_ref[...].astype(jnp.float32)
+        for c in range(packed_ref.shape[0]):
+            out_ref[:, c * TILE : (c + 1) * TILE] = packed_ref[c].astype(jnp.float32)
 
     @pl.when(pl.program_id(0) == 0)
     def _():
@@ -332,27 +339,29 @@
         table[...] = small[at : at + heads, :buckets]
 
 
-def unpack(packed, width, experts, heads, buckets, small_rows):
+def unpack(packed, small, mixed, experts, heads, buckets):
+    tokens, width = mixed.shape
     blocks = width // TILE
-    source = lambda m: pl.BlockSpec((width, TILE), lambda i: (m * blocks + i, 0))
-    column = lambda rows: pl.BlockSpec((rows, TILE), lambda i: (0, i))
+    steps = 4
+    source = lambda m: pl.BlockSpec((blocks, width // steps, TILE), lambda i: (m, i, 0))
+    rows = lambda count: pl.BlockSpec((count // steps, width), lambda i: (i, 0))
     kept = lambda shape: pl.BlockSpec(shape, lambda i: (0, 0))
     return pl.pallas_call(
         functools.partial(unpack_kernel, experts, heads, buckets),
-        grid=(blocks,),
-        in_specs=[source(m) for m in range(4)]
-        + [pl.BlockSpec((small_rows, TILE), lambda i: (4 * blocks * width // small_rows, 0))],
-        out_specs=[column(width)] * 4
-        + [kept((experts, width)), kept((2, width)), kept((heads, buckets))],
+        grid=(steps,),
+        in_specs=[source(m) for m in range(4)] + [whole(small.shape), rows(tokens)],
+        out_specs=[rows(width)] * 4
+        + [kept((experts, width)), kept((2, width)), kept((heads, buckets)), rows(tokens)],
         out_shape=[jax.ShapeDtypeStruct((width, width), jnp.float32)] * 4
         + [
             jax.ShapeDtypeStruct((experts, width), jnp.float32),
             jax.ShapeDtypeStruct((2, width), jnp.float32),
             jax.ShapeDtypeStruct((heads, buckets), jnp.float32),
-        ],
-        compiler_params=params(32),
+            jax.ShapeDtypeStruct((tokens, width), LOW),
+        ],
+        compiler_params=params(60),
         name="unpack",
-    )(*[packed] * 5)
+    )(*[packed.reshape(4 * blocks, width, TILE)] * 4, small, mixed)
 
 
 def attention_forward_kernel(len_ref, q_ref, k_ref, v_ref, near_ref, far_ref, o_ref, p_ref, s_ref):
@@ -428,112 +437,103 @@
     )(lengths, projected, projected, projected, near, far)
 
 def attention_backward_kernel(
-    q_ref, k_ref, v_ref, do_ref, o_ref, p_ref, nt_ref, wq_ref, wk_ref, wv_ref, x_ref, dy_ref, gain_ref,
+    rows, q_ref, k_ref, v_ref, do_ref, o_ref, p_ref, nt_ref, wq_ref, wk_ref, wv_ref, x_ref, dy_ref, gain_ref,
     gr_ref, gg2_ref, out_ref, pack_ref, small_ref,
-    near_ref, far_ref, d_ref, lines_ref, acc_ref, dh_ref, gg_ref,
+    near_ref, far_ref, d_ref, lines_ref, dh_ref,
 ):
-    seq = q_ref.shape[0]
+    seq = q_ref.shape[0] // rows
     tiles = seq // TILE
     half = q_ref.shape[1] // 2
     width = x_ref.shape[1]
     pair = pl.program_id(0)
-    row = pl.program_id(1)
     last_pair = pair == pl.num_programs(0) - 1
-    last_row = row == pl.num_programs(1) - 1
     lane = lax.broadcasted_iota(jnp.int32, (seq, 2 * half), 1)
-    q = q_ref[...]
-    k = k_ref[...]
-    k_t = k.T
-    v = v_ref[...]
-    do = do_ref[...]
-    weighed = (do.astype(jnp.float32) * o_ref[...].astype(jnp.float32)).T
-    dq_parts = []
-    dk_all = None
-    dv_all = None
-
-    @pl.when(row == 0)
-    def _():
-        near_ref[...] = jnp.zeros_like(near_ref)
-        far_ref[...] = jnp.zeros_like(far_ref)
-        acc_ref[...] = jnp.zeros_like(acc_ref)
-
-    for h in range(2):
-        mine = (lane >= h * half) & (lane < (h + 1) * half)
-        v_h = jnp.where(mine, v, jnp.zeros_like(v))
-        delta = jnp.sum(weighed[h * half : (h + 1) * half], axis=0, keepdims=True)
-        far_sum = [jnp.zeros((8, TILE), jnp.float32), jnp.zeros((8, TILE), jnp.float32)]
-        for i in range(0, tiles, 2):
-            dp = dot_t(v_h, do[i * TILE : (i + 2) * TILE])
-            for c in range(2):
-                cols = slice((i + c) * TILE, (i + c + 1) * TILE)
-                for j in range(tiles):
-                    rws = slice(j * TILE, (j + 1) * TILE)
-                    part = dp[rws, c * TILE : (c + 1) * TILE] - delta[:, cols]
-                    ds = p_ref[0, h, rws, cols].astype(jnp.float32) * part
-                    d = j - i - c
-                    if -1 <= d <= 1:
-                        near_ref[h, d + 1] += ds
-                    else:
-                        which = 0 if d > 0 else 1
-                        far_sum[which] = far_sum[which] + jnp.sum(
-                            ds.reshape(TILE // 8, 8, TILE), axis=0
-                        )
-                    d_ref[h, rws, cols] = ds.astype(LOW)
-        far_ref[h, 0] += far_sum[0]
-        far_ref[h, 1] += far_sum[1]
-    for h in range(2):
-        mine = (lane >= h * half) & (lane < (h + 1) * half)
-        ds_all = d_ref[h]
-        dq_parts.append(dot(k_t[h * half : (h + 1) * half], ds_all))
-        dk_h = dot(ds_all, q)
-        dv_h = dot(p_ref[0, h], do)
-        dk_all = dk_h if h == 0 else jnp.where(mine, dk_h, dk_all)
-        dv_all = dv_h if h == 0 else jnp.where(mine, dv_h, dv_all)
-
-    dq = (jnp.concatenate(dq_parts, axis=0).T * 0.125).astype(LOW)
-    grads = jnp.concatenate([dq, (dk_all * 0.125).astype(LOW), dv_all.astype(LOW)], axis=1)
-    acc_ref[...] += dot(nt_ref[...], grads)
     weights = jnp.concatenate([wq_ref[...], wk_ref[...], wv_ref[...]], axis=1)
+    near_ref[...] = jnp.zeros_like(near_ref)
+    for row in range(rows):
+        here = slice(row * seq, (row + 1) * seq)
+        v = v_ref[here, :]
+        do = do_ref[here, :]
+        weighed = (do.astype(jnp.float32) * o_ref[here, :].astype(jnp.float32)).T
+        for h in range(2):
+            mine = (lane >= h * half) & (lane < (h + 1) * half)
+            v_h = jnp.where(mine, v, jnp.zeros_like(v))
+            delta = jnp.sum(weighed[h * half : (h + 1) * half], axis=0, keepdims=True)
+            far_sum = [jnp.zeros((8, TILE), jnp.float32), jnp.zeros((8, TILE), jnp.float32)]
+            for i in range(0, tiles, 2):
+                dp = dot_t(v_h, do[i * TILE : (i + 2) * TILE])
+                for c in range(2):
+                    cols = slice((i + c) * TILE, (i + c + 1) * TILE)
+                    for j in range(tiles):
+                        rws = slice(j * TILE, (j + 1) * TILE)
+                        part = dp[rws, c * TILE : (c + 1) * TILE] - delta[:, cols]
+                        ds = p_ref[row, h, rws, cols].astype(jnp.float32) * part
+                        d = j - i - c
+                        if -1 <= d <= 1:
+                            near_ref[row, h, d + 1] += ds
+                        else:
+                            which = 0 if d > 0 else 1
+                            far_sum[which] = far_sum[which] + jnp.sum(
+                                ds.reshape(TILE // 8, 8, TILE), axis=0
+                            )
+                        d_ref[row, h, rws, cols] = ds.astype(LOW)
+            for which in range(2):
+                far_ref[row, h, which] = far_sum[which]
+    grads_all = []
+    for row in range(rows):
+        here = slice(row * seq, (row + 1) * seq)
+        q = q_ref[here, :]
+        do = do_ref[here, :]
+        k_t = k_ref[here, :].T
+        dq_parts = []
+        dk_all = None
+        dv_all = None
+        for h in range(2):
+            mine = (lane >= h * half) & (lane < (h + 1) * half)
+            ds_all = d_ref[row, h]
+            dq_parts.append(dot(k_t[h * half : (h + 1) * half], ds_all))
+            dk_h = dot(ds_all, q)
+            dv_h = dot(p_ref[row, h], do)
+            dk_all = dk_h if h == 0 else jnp.where(mine, dk_h, dk_all)
+            dv_all = dv_h if h == 0 else jnp.where(mine, dv_h, dv_all)
+        dq = (jnp.concatenate(dq_parts, axis=0).T * 0.125).astype(LOW)
+        grads_all.append(
+            jnp.concatenate([dq, (dk_all * 0.125).astype(LOW), dv_all.astype(LOW)], axis=1)
+        )
+    grads = jnp.concatenate(grads_all, axis=0)
+    acc = dot(nt_ref[...], grads)
+    for n in range(3):
+        pack_ref[n, 0] = acc[:, n * TILE : (n + 1) * TILE].astype(LOW)
     dh = dot_t(grads, weights)
-    here = pl.ds(pl.multiple_of(row * seq, seq), seq)
 
     @pl.when(pair == 0)
     def _():
-        dh_ref[here, :] = dh
+        dh_ref[...] = dh
 
     @pl.when(pair > 0)
     def _():
-        dh_ref[here, :] += dh
-
-    @pl.when(last_row)
-    def _():
-        bucket_sums(near_ref, far_ref, lines_ref, 2 * pair)
-        for n in range(3):
-            pack_ref[n, 0] = acc_ref[:, n * TILE : (n + 1) * TILE].astype(LOW)
-
-    @pl.when(last_pair & (row == 0))
-    def _():
-        gg_ref[...] = jnp.zeros_like(gg_ref)
+        dh_ref[...] += dh
+
+    near_ref[0] = sum(near_ref[row] for row in range(rows))
+    far_ref[0] = sum(far_ref[row] for row in range(rows))
+    bucket_sums(near_ref.at[0], far_ref.at[0], lines_ref, 2 * pair)
 
     @pl.when(last_pair)
     def _():
-        total = dh_ref[here, :]
+        total = dh_ref[...]
         x = x_ref[...].astype(jnp.float32)
         rms = lax.rsqrt(jnp.mean(x * x, axis=-1, keepdims=True) + EPSILON)
-        gg_ref[...] += jnp.sum(total * x * rms, axis=0, keepdims=True)
+        gg = jnp.sum(total * x * rms, axis=0, keepdims=True)
         u = total * gain_ref[...]
         out_ref[...] = (
             dy_ref[...]
             + rms * u
             - x * (rms * rms * rms) * jnp.mean(u * x, axis=-1, keepdims=True)
         )
-
-    @pl.when(last_pair & last_row)
-    def _():
         at = gr_ref.shape[0]
         small_ref[:at] = gr_ref[...].astype(LOW)
         lines = width // TILE
-        gains = [gg_ref[:, c * TILE : (c + 1) * TILE] for c in range(lines)]
+        gains = [gg[:, c * TILE : (c + 1) * TILE] for c in range(lines)]
         gains += [gg2_ref[:, c * TILE : (c + 1) * TILE] for c in range(lines)]
         if 2 * lines % 16:
             gains += [jnp.zeros((16 - 2 * lines % 16, TILE), jnp.float32)]
@@ -595,37 +595,35 @@
 ):
     width = heads * head
     pairs = heads // 2
-    spec = lambda off: pl.BlockSpec((seq, 2 * head), lambda p, b: (b, off + p))
-    column = pl.BlockSpec((width, 2 * head), lambda p, b: (0, p))
-    at_end = pl.BlockSpec((seq, width), lambda p, b: (b * (p // (pairs - 1)), 0))
+    tokens = rows * seq
+    spec = lambda off: pl.BlockSpec((tokens, 2 * head), lambda p: (0, off + p))
+    column = pl.BlockSpec((width, 2 * head), lambda p: (0, p))
     return pl.pallas_call(
-        attention_backward_kernel,
-        grid=(pairs, rows),
+        functools.partial(attention_backward_kernel, rows),
+        grid=(pairs,),
         in_specs=[
             spec(0), spec(pairs), spec(2 * pairs), spec(0), spec(0),
-            pl.BlockSpec((1, 2, seq, seq), lambda p, b: (b, p, 0, 0)),
-            pl.BlockSpec((width, seq), lambda p, b: (0, b)),
-            column, column, column, at_end, at_end,
+            pl.BlockSpec((rows, 2, seq, seq), lambda p: (0, p, 0, 0)),
+            whole((width, tokens)),
+            column, column, column, whole((tokens, width)), whole((tokens, width)),
             whole((1, width)), whole(gr.shape), whole(gg2.shape),
         ],
         out_specs=[
-            at_end,
-            pl.BlockSpec((3, 1, width, TILE), lambda p, b: (0, p, 0, 0)),
-            pl.BlockSpec((small_rows, TILE), lambda p, b: (0, 0)),
+            pl.BlockSpec((tokens, width), lambda p: (0, 0)),
+            pl.BlockSpec((3, 1, width, TILE), lambda p: (0, p, 0, 0)),
+            pl.BlockSpec((small_rows, TILE), lambda p: (0, 0)),
         ],
         out_shape=[
-            jax.ShapeDtypeStruct((rows * seq, width), jnp.float32),
+            jax.ShapeDtypeStruct((tokens, width), jnp.float32),
             jax.ShapeDtypeStruct((3, pairs, width, TILE), LOW),
             jax.ShapeDtypeStruct((small_rows, TILE), LOW),
         ],
         scratch_shapes=[
-            pltpu.VMEM((2, 3, TILE, TILE), jnp.float32),
-            pltpu.VMEM((2, 2, 8, TILE), jnp.float32),
-            pltpu.VMEM((2, seq, seq), LOW),
+            pltpu.VMEM((rows, 2, 3, TILE, TILE), jnp.float32),
+            pltpu.VMEM((rows, 2, 2, 8, TILE), jnp.float32),
+            pltpu.VMEM((rows, 2, seq, seq), LOW),
             pltpu.VMEM((heads, 8, 2 * TILE), jnp.float32),
-            pltpu.VMEM((width, 3 * TILE), jnp.float32),
-            pltpu.VMEM((rows * seq, width), jnp.float32),
-            pltpu.VMEM((1, width), jnp.float32),
+            pltpu.VMEM((tokens, width), jnp.float32),
         ],
         compiler_params=params(60),
         cost_estimate=cost(8 * rows * heads * seq * seq * head * 4, rows * heads * seq * seq * 2),
@@ -810,26 +808,40 @@
 def sum_kernel(cores, n, room, heights, extra, code_ref, gate_ref, rank_ref, ff_any, y_any, *refs):
     _, cut, _ = plan(room)
     xs, refs = refs[: len(heights)], refs[len(heights) :]
-    mixed_ref, out_ref, work_ref, got_ref, ff_ref, y_ref, *refs = refs
-    loads = [(ff_any, ff_ref), (y_any, y_ref)]
+    mixed_any, sum_any, small_any, out_ref, work_ref, got_ref, ff_ref, y_ref, mixed_ref, *refs = refs
     if extra:
         tail_ref, *refs = refs
-    send, recv, local = refs
-    loads = [pltpu.make_async_copy(a, b, local.at[i]) for i, (a, b) in enumerate(loads)]
-    for copy in loads:
-        copy.start()
+    send, recv, local, load, store = refs
+    loads = [
+        pltpu.make_async_copy(ff_any, ff_ref, local.at[0]),
+        pltpu.make_async_copy(y_any, y_ref, local.at[1]),
+    ]
     summed = heights[:-1] if extra else heights
     bits, parts = sum_parts(n, summed)
     full = len(parts)
     if extra:
         parts = parts + [(len(summed), 0, sum(summed), heights[-1] // n, list(range(bits)))]
     me = lax.axis_index("grp") * cores + lax.axis_index("exp")
+    base = [first for _, _, first, _, _ in parts]
+    got_at = list(base)
+    kept = []
+    for p, (ref, at, first, step, order) in enumerate(parts):
+        length = step * (n >> 1)
+        start = base[p] + partner_of(me, order[0])[0] * length
+        kept.append(
+            pltpu.make_async_copy(
+                xs[ref].at[rows_at(start - first + at, length)],
+                work_ref.at[rows_at(start, length)],
+                load.at[p],
+            )
+        )
+        kept[p].start()
+    for copy in loads:
+        copy.start()
     barrier = pltpu.get_barrier_semaphore()
     for b in range(bits):
         pl.semaphore_signal(barrier, inc=1, **device_place(cores, partner_of(me, b)[1]))
     pl.semaphore_wait(barrier, bits)
-    base = [first for _, _, first, _, _ in parts]
-    got_at = list(base)
 
     def halving(p, s):
         ref, at, first, step, order = parts[p]
@@ -854,40 +866,69 @@
             **device_place(cores, partner_of(me, order[s])[1]),
         )
 
+    main = sum(summed[:-1])
+
+    def keep_out(p, s, start, length):
+        here = rows_at(start, length)
+        target = sum_any.at[here]
+        if parts[p][0] == len(summed) - 1:
+            target = small_any.at[rows_at(start - main, length)]
+        copy = pltpu.make_async_copy(out_ref.at[here], target, store.at[p, s])
+        copy.start()
+        return copy
+
     tokens, width = mixed_ref.shape
     tile = tokens // 4
-
-    def mix_tile(i):
-        here = slice(i * tile, (i + 1) * tile)
-        ff = collect(segment(code_ref[here, :], room, 0, cut), ff_ref[...])
-        if extra:
-            tail = tail_ref[...]
-            tail = [tail[c * extra : (c + 1) * extra] for c in range(width // TILE)]
-            ff = ff + collect(rank_ref[here, :], jnp.concatenate(tail, axis=1))
-        mixed_ref[here, :] = (y_ref[here, :] + gate_ref[here, :] * ff).astype(LOW)
+    tiles = [slice(i * tile, (i + 1) * tile) for i in range(4)]
+
+    def mix_most():
+        for copy in loads:
+            copy.wait()
+        for here in tiles:
+            ff = collect(segment(code_ref[here, :], room, 0, cut), ff_ref[...])
+            y_ref[here, :] += gate_ref[here, :] * ff
+
+    def mix_rest():
+        stores = []
+        for i, here in enumerate(tiles):
+            total = y_ref[here, :]
+            if extra:
+                tail = tail_ref[...]
+                tail = [tail[c * extra : (c + 1) * extra] for c in range(width // TILE)]
+                more = collect(rank_ref[here, :], jnp.concatenate(tail, axis=1))
+                total = total + gate_ref[here, :] * more
+            mixed_ref[here, :] = total.astype(LOW)
+            stores.append(
+                pltpu.make_async_copy(mixed_ref.at[here], mixed_any.at[here], local.at[2 + i])
+            )
+            stores[i].start()
+        return stores
 
     moving = [halving(p, 0) for p in range(len(parts))]
     for copy in moving:
         copy.start()
-    sent = []
+    sent, stores = [], []
     for s in range(bits):
+        if s == 1:
+            mix_most()
         for p, (ref, at, first, step, order) in enumerate(parts):
             length = step * (n >> (s + 1))
+            if s == 0:
+                kept[p].wait()
             moving[p].wait_recv()
             sent.append(moving[p])
             base[p] = base[p] + partner_of(me, order[s])[0] * length
-            source, shift = (xs[ref], at - first) if s == 0 else (work_ref, 0)
             last = s + 1 == bits
             target = out_ref if last else work_ref
             if p >= full and last:
                 target = tail_ref
 
             def add(
-                i, _, start=base[p], source=source, shift=shift, target=target, arrived=got_at[p],
-                step=step, to=0 if p >= full and last else base[p],
+                i, _, start=base[p], target=target, arrived=got_at[p], step=step,
+                to=0 if p >= full and last else base[p],
             ):
                 got = got_ref[rows_at(arrived + i * step, step), :].astype(jnp.float32)
-                mine = source[rows_at(start + shift + i * step, step), :].astype(jnp.float32)
+                mine = work_ref[rows_at(start + i * step, step), :].astype(jnp.float32)
                 target[rows_at(to + i * step, step), :] = (mine + got).astype(LOW)
                 return 0
 
@@ -899,24 +940,28 @@
             elif p < full:
                 moving[p] = doubling(p, s)
                 moving[p].start()
+                stores.append(keep_out(p, bits, base[p], step))
     for copy in sent:
         copy.wait_send()
-    for copy in loads:
-        copy.wait()
     sent = []
-    for turn, s in enumerate(reversed(range(bits))):
-        for i in ((), (), (0,), (1, 2), (3,))[turn] if bits == 5 else range(4 * turn // bits, 4 * (turn + 1) // bits):
-            mix_tile(i)
+    for s in reversed(range(bits)):
+        if s == min(1, bits - 1):
+            stores += mix_rest()
         for p, (ref, at, first, step, order) in enumerate(parts[:full]):
             length = step * (n >> (s + 1))
             moving[p].wait_recv()
             sent.append(moving[p])
-            base[p] = base[p] - partner_of(me, order[s])[0] * length
+            bit = partner_of(me, order[s])[0]
+            arrived = base[p] + (1 - 2 * bit) * length
+            base[p] = base[p] - bit * length
             if s > 0:
                 moving[p] = doubling(p, s - 1)
                 moving[p].start()
+            stores.append(keep_out(p, s, arrived, length))
     for copy in sent:
         copy.wait_send()
+    for copy in stores:
+        copy.wait()
 
 
 def all_sum(xs, code, gate, rank, ff, y, room, ff_more):
@@ -927,7 +972,7 @@
     if any(h % (16 * n) for h in heights):
         xs = [jnp.concatenate(xs[:-1], axis=0), xs[-1]]
         heights = [a.shape[0] for a in xs]
-    total = sum(heights)
+    total, small = sum(heights), heights[-1]
     bits, parts = sum_parts(n, heights)
     count = len(parts)
     rows = total
@@ -946,15 +991,19 @@
         functools.partial(sum_kernel, cores, n, room, heights, extra),
         out_shape=[
             jax.ShapeDtypeStruct((tokens, width), LOW),
-            jax.ShapeDtypeStruct((total, TILE), LOW),
-        ],
-        in_specs=[vmem] * 3 + [anywhere] * 2 + [vmem] * len(xs),
-        out_specs=[vmem] * 2,
+            jax.ShapeDtypeStruct((total - small, TILE), LOW),
+            jax.ShapeDtypeStruct((small, TILE), LOW),
+        ],
+        in_specs=[vmem] * 3 + [anywhere] * (2 + len(xs)),
+        out_specs=[anywhere] * 3,
         scratch_shapes=[
-            buffer, buffer, pltpu.VMEM(ff.shape, LOW), pltpu.VMEM(y.shape, jnp.float32), *tail,
+            pltpu.VMEM((total, TILE), LOW), buffer, buffer, pltpu.VMEM(ff.shape, LOW),
+            pltpu.VMEM(y.shape, jnp.float32), pltpu.VMEM(y.shape, LOW), *tail,
             pltpu.SemaphoreType.DMA((count, 2 * bits)),
             pltpu.SemaphoreType.DMA((count, 2 * bits)),
-            pltpu.SemaphoreType.DMA((2,)),
+            pltpu.SemaphoreType.DMA((6,)),
+            pltpu.SemaphoreType.DMA((count,)),
+            pltpu.SemaphoreType.DMA((count, bits + 1)),
         ],
         compiler_params=params(60, collective_id=1, has_side_effects=True),
         name="all_sum",
@@ -1042,14 +1091,13 @@
         projected, do, joined, weights, normed_t, w_query, w_key, w_value, x, dy, gain_one,
         small, grad_gain_two, rows, seq, heads, head, small_rows,
     )
-    mixed, summed = all_sum(
+    mixed, summed, small = all_sum(
         [packed.reshape(-1, TILE), grad_output, small], code_c, gate, rank_c, ff_back, y, room, ff_more
     )
     if extra:
-        crowded = summed[4 * width * width // TILE + lines * experts, 0] > 0
-
-        def mix_all(mixed):
-            del mixed
+        crowded = small[lines * experts, 0] > 0
+
+        def mix_all(_):
             code = code_c.reshape(-1)
             expert = code // room
             place = code - expert * room
@@ -1058,12 +1106,10 @@
             rest = jnp.where(place >= cut, expert * extra + place - cut, devices * extra)
             take = lambda a, index: jnp.take(a, index, axis=0, mode="fill", fill_value=0)
             ff = take(ff_back, first) + take(spare, rest)
-            return (y + gate * ff.astype(jnp.float32)).astype(LOW)
-
-        mixed = lax.cond(crowded, mix_all, lambda mixed: mixed, mixed)
-    *grads, router_t, gains, table = unpack(
-        summed, width, experts, heads, buckets, small_rows
-    )
+            return False, (y + gate * ff.astype(jnp.float32)).astype(LOW)
+
+        _, mixed = lax.while_loop(lambda held: held[0], mix_all, (crowded, mixed))
+    *grads, router_t, gains, table, mixed = unpack(summed, small, mixed, experts, heads, buckets)
     return (
         mixed.reshape(rows, seq, width),
         grad_tokens.reshape(rows, seq, width),

time: 404 us -> 397 us (0.983)
  Pallas kernels: 262 us -> 254 us
    pallas_call x1, Pallas kernels: 42.5 us -> 36.7 us  [attention_backward(): pl.pallas_call(functools.partial(attention_backward_kernel, rows), grid=(...]
    pallas_call x1, Pallas kernels: 67.4 us -> 61.9 us  [all_sum(): pl.pallas_call(functools.partial(sum_kernel, cores, n, room, heights, ext...]
    unnamed x49 -> x50, local copies, waits for them, and re-layouts: 20.9 us -> 15.9 us
  transfers between devices with their start and end apart: 5 -> 5, of which waited for: 4 -> 5; matrix products, arithmetic and copies ran while one was open for 3% -> 3% of each run, Pallas kernels for 46% -> 45%
where the time goes in v6:
time: 397 us; the launch traced here: 391 us
  Pallas kernels  254 us (64%)
  blocking collectives  42.1 us (11%)
  waiting for transfers between devices  40.3 us (10%)
  local copies, waits for them, and re-layouts  25 us (6%)
  starting transfers between devices  22.5 us (6%)
  other arithmetic  3.98 us (1%)
    pallas_call x1, Pallas kernels, all_sum(): pl.pallas_call(functools.partial(sum_kernel, cores, n, room, heights, ext...  61.9 us
    pallas_call x2, Pallas kernels, expert_rows(): pl.pallas_call(functools.partial(expert_kernel, experts, chunk), grid=(n...  61.1 us
    all_to_all x1, blocking collectives, exchange(): lax.all_to_all(shaped, AXES, split_axis=0, concat_axis=0, tiled=True)  42.1 us
    all_to_all x5, waiting for transfers between devices, exchange(): lax.all_to_all(shaped, AXES, split_axis=0, concat_axis=0, tiled=True)  40.3 us
    pallas_call x1, Pallas kernels, attention_backward(): pl.pallas_call(functools.partial(attention_backward_kernel, rows), grid=(...  36.7 us
    pallas_call x1, Pallas kernels, expert_weights(): pl.pallas_call(functools.partial(expert_weights_kernel, len(parts)), grid...  27.8 us
    all_to_all x5, starting transfers between devices, exchange(): lax.all_to_all(shaped, AXES, split_axis=0, concat_axis=0, tiled=True)  22.5 us
    pallas_call x1, Pallas kernels, attention_forward(): pl.pallas_call(attention_forward_kernel, grid=(rows, pairs), in_specs=[pl...  21.4 us
  transfers between devices with their start and end apart: 5, of which 5 were waited for; matrix products, arithmetic and copies ran while one was open for 3% of the time, Pallas kernels for 45%

profile of v6, /device:TPU:0, one launch (start us, length us, event | category | flops | bytes accessed | tf_op | source)
XLA Modules:
  0.0 391.5 jit_solution(867755406370208422)
XLA Ops:
  0.6 0.7 copy.50
  1.3 0.2 copy.51
  1.6 0.0 copy-start.2
  1.6 0.7 copy.53
  2.3 0.2 copy.54
  2.5 0.0 copy-start.4
  2.5 1.4 copy-done.4
  3.9 7.2 %route.1 = (s32[1024,1]{1,0:T(8,128)S(1)}, s32[1,1024]{1,0:T(1,128)S(1)}, s32[1024,1]{1,0:T(8,128)S(1)}, f32[16,128]{1,0:T(8,128)S(1)}, bf16[2048,768]{1,0:T(8,128)(2,1)}) custom-call(s32[1024,1]{1,0:T(8,128)S(1)} %bitcast.59, s32[1,1024]{1,0:T(1,128)S(1)} %bitcast.63, s32[1024,1]{1,0:T(8,128)S(1)} %bitcast.61, s32[1,1024]{1,0:T(1,128)S(1)} %bitcast.65, ...), custom_call_target="tpu_custom_call" | custom-call | flops 3221225472 | bytes 8388608 | tf_op jit(solution)/shard_map/route/pallas_call | solution.py:143
  11.2 0.8 copy-done.1
  12.0 0.6 copy-done.13
  12.6 7.6 %all-to-all-start.1 = ((bf16[32,64,768]{2,1,0:T(8,128)(2,1)}), bf16[32,64,768]{2,1,0:T(8,128)(2,1)}, u32[]{:S(2)}, u32[]{:S(2)}) async-start(bf16[32,64,768]{2,1,0:T(8,128)(2,1)} %bitcast.83), calls=%async_computation.1 | async-start | bytes 6291456 | tf_op jit(solution)/shard_map/all_to_all | solution.py:160
  20.2 0.0 copy-start.3
  20.2 0.1 copy.42
  20.4 0.1 copy.43.far_ref
  20.5 0.1 fusion.6
  20.6 0.2 fusion.4
  20.7 2.1 fusion.2
  22.9 0.6 copy.56
  23.5 0.0 copy-start.18
  23.5 0.0 copy-start.21
  23.5 0.2 slice.42
  23.7 0.6 copy-done.18
  24.3 0.2 copy.44
  24.5 0.6 reshape.337.gain_ref
  25.1 0.7 pad.4.wr_ref
  25.8 1.4 copy-done.5
  27.2 1.3 copy-done.6
  28.4 1.3 copy-done.7
  29.7 1.3 copy-done.8
  31.0 4.9 %project.1 = (bf16[768,1024]{1,0:T(8,128)(2,1)S(1)}, bf16[1024,2304]{1,0:T(8,128)(2,1)S(1)}) custom-call(bf16[1024,768]{1,0:T(8,128)(2,1)S(1)} %bitcast.70, f32[1,768]{1,0:T(1,128)S(1)} %reshape.335.gain_ref, bf16[768,768]{1,0:T(8,128)(2,1)S(1)} %copy-done.6, bf16[768,768]{1,0:T(8,128)(2,1)S(1)} %copy-done.7, bf16[768,768]{1,0:T(8,128)(2,1)S(1)} %copy-done.8), custom_call_target="tpu_custom_call" | custom-call | flops 3623878656 | bytes 12582912 | tf_op jit(solution)/shard_map/project/pallas_call | solution.py:179
  35.9 1.2 copy-done.12
  37.1 21.4 %attention_forward.1 = (bf16[1024,768]{1,0:T(8,128)(2,1)S(1)}, bf16[2,12,512,512]{3,2,1,0:T(8,128)(2,1)}) custom-call(s32[2]{0:T(128)S(1)} %copy-done.9, bf16[1024,2304]{1,0:T(8,128)(2,1)S(1)} %get-tuple-element.124.q_ref.k_ref.v_ref, bf16[1024,2304]{1,0:T(8,128)(2,1)S(1)} %get-tuple-element.124.q_ref.k_ref.v_ref, ...), custom_call_target="tpu_custom_call" | custom-call | flops 6442450944 | bytes 12582912 | tf_op jit(solution)/shard_map/attention_forward/pallas_call | solution.py:416
  58.4 1.1 copy-done.10
  59.6 12.3 %after_attention.1 = (f32[1024,768]{1,0:T(8,128)}, f32[1024,1]{1,0:T(8,128)}, bf16[1024,768]{1,0:T(8,128)(2,1)}, bf16[1024,768]{1,0:T(8,128)(2,1)}) custom-call(bf16[1024,768]{1,0:T(8,128)(2,1)} %copy-done.10, bf16[1024,768]{1,0:T(8,128)(2,1)} %bitcast.68, bf16[768,768]{1,0:T(8,128)(2,1)} %w_ref.1, f32[1,768]{1,0:T(1,128)} %reshape.337.gain_ref, ...), custom_call_target="tpu_custom_call" | custom-call | flops 4429185024 | bytes 12582912 | tf_op jit(solution)/shard_map/after_attention/pallas_call | solution.py:220
  71.8 19.8 %all-to-all-done.1 = bf16[32,64,768]{2,1,0:T(8,128)(2,1)} async-done(((bf16[32,64,768]{2,1,0:T(8,128)(2,1)}), bf16[32,64,768]{2,1,0:T(8,128)(2,1)}, u32[]{:S(2)}, u32[]{:S(2)}) %all-to-all-start.1) | async-done | bytes 3145760 | tf_op jit(solution)/shard_map/all_to_all | solution.py:160
  91.6 42.1 %all_to_all.34 = bf16[32,32,768]{2,1,0:T(8,128)(2,1)} all-to-all(bf16[32,32,768]{2,1,0:T(8,128)(2,1)} %bitcast.91), channel_id=1, replica_groups=mesh['grp'=16,'exp'=2] {'grp','exp'}, dimensions={0} | all-to-all | bytes 3145728 | tf_op jit(solution)/shard_map/all_to_all | solution.py:160
  133.7 3.5 all-to-all-start.3
  137.2 0.5 compare_convert_fusion.mine_ref
  137.7 30.5 %expert_rows.2 = (bf16[1024,768]{1,0:T(8,128)(2,1)}, bf16[1024,768]{1,0:T(8,128)(2,1)}, bf16[1024,3072]{1,0:T(8,128)(2,1)}, bf16[1024,3072]{1,0:T(8,128)(2,1)}, ...) custom-call(bf16[1024,768]{1,0:T(8,128)(2,1)} %bitcast.88, ...), custom_call_target="tpu_custom_call" | custom-call | flops 19327352832 | bytes 31457280 | tf_op jit(solution)/shard_map/expert_rows/pallas_call | solution.py:725
  168.2 6.7 %all-to-all-done.3 = bf16[32,32,768]{2,1,0:T(8,128)(2,1)S(1)} async-done(((bf16[32,32,768]{2,1,0:T(8,128)(2,1)}), bf16[32,32,768]{2,1,0:T(8,128)(2,1)S(1)}, u32[]{:S(2)}, u32[]{:S(2)}) %all-to-all-start.3) | async-done | bytes 1572896 | tf_op jit(solution)/shard_map/all_to_all | solution.py:160
  174.9 1.1 copy-done.16
  176.1 3.8 all-to-all-start.4
  179.9 30.5 %expert_rows.3 = (bf16[1024,768]{1,0:T(8,128)(2,1)}, bf16[1024,768]{1,0:T(8,128)(2,1)}, bf16[1024,3072]{1,0:T(8,128)(2,1)}, bf16[1024,3072]{1,0:T(8,128)(2,1)}, ...) custom-call(bf16[1024,768]{1,0:T(8,128)(2,1)} %bitcast.85, ...), custom_call_target="tpu_custom_call" | custom-call | flops 19327352832 | bytes 31457280 | tf_op jit(solution)/shard_map/expert_rows/pallas_call | solution.py:725
  210.4 7.2 %all-to-all-done.4 = bf16[32,32,768]{2,1,0:T(8,128)(2,1)S(1)} async-done(((bf16[32,32,768]{2,1,0:T(8,128)(2,1)}), bf16[32,32,768]{2,1,0:T(8,128)(2,1)S(1)}, u32[]{:S(2)}, u32[]{:S(2)}) %all-to-all-start.4) | async-done | bytes 1572896 | tf_op jit(solution)/shard_map/all_to_all | solution.py:160
  217.6 1.1 copy-done.15
  218.7 3.9 all-to-all-start.5
  222.6 1.0 slice_add_fusion
  223.6 1.5 fusion.11
  225.1 0.9 reshape.352
  226.0 1.1 copy.46
  227.1 0.7 pad_maximum_fusion.1.gr_ref
  227.8 1.6 pad_maximum_fusion
  229.3 27.8 %expert_weights.1 = (f32[1,768,3072]{2,1,0:T(8,128)}, f32[1,3072,768]{2,1,0:T(8,128)}) custom-call(bf16[768,1024]{1,0:T(8,128)(2,1)} %get-tuple-element.146.refs_0_, bf16[768,1024]{1,0:T(8,128)(2,1)} %get-tuple-element.147.refs_1_, bf16[1024,3072]{1,0:T(8,128)(2,1)} %get-tuple-element.148.refs_2_, bf16[1024,3072]{1,0:T(8,128)(2,1)} %get-tuple-element.149.refs_3_, ...), custom_call_target="tpu_custom_call" | custom-call | flops 19327352832 | bytes 44040192 | tf_op jit(solution)/shard_map/expert_weights/pallas_call | solution.py:764
  257.2 3.2 all-to-all-done.5
  260.4 3.8 all-to-all-start.6
  264.1 1.2 copy.48
  265.4 0.2 copy.49
  265.6 12.9 %before_attention.1 = (f32[1024,768]{1,0:T(8,128)}, bf16[1024,768]{1,0:T(8,128)(2,1)}, bf16[4608,128]{1,0:T(8,128)(2,1)}, f32[1,768]{1,0:T(1,128)}) custom-call(s32[1024,1]{1,0:T(8,128)} %copy-done, f32[1024,768]{1,0:T(8,128)} %get-tuple-element.250.y_ref.y_any, bf16[1024,768]{1,0:T(8,128)(2,1)} %bitcast.66, f32[1,768]{1,0:T(1,128)} %reshape.337.gain_ref, ...), custom_call_target="tpu_custom_call" | custom-call | flops 3623878656 | bytes 16777216 | tf_op jit(solution)/shard_map/before_attention/pallas_call | solution.py:294
  278.5 36.7 %attention_backward.1 = (f32[1024,768]{1,0:T(8,128)}, bf16[3,6,768,128]{3,2,1,0:T(8,128)(2,1)}, bf16[512,128]{1,0:T(8,128)(2,1)}) custom-call(bf16[1024,2304]{1,0:T(8,128)(2,1)} %copy-done.11, bf16[1024,2304]{1,0:T(8,128)(2,1)} %copy-done.11, bf16[1024,2304]{1,0:T(8,128)(2,1)} %copy-done.11, bf16[1024,768]{1,0:T(8,128)(2,1)} %get-tuple-element.165.do_ref, ...), custom_call_target="tpu_custom_call" | custom-call | flops 12884901888 | bytes 12582912 | tf_op jit(solution)/shard_map/attention_backward/pallas_call | solution.py:601
  315.2 3.5 all-to-all-done.6
  318.7 61.9 %all_sum.1 = (bf16[1024,768]{1,0:T(8,128)(2,1)}, bf16[18432,128]{1,0:T(8,128)(2,1)}, bf16[512,128]{1,0:T(8,128)(2,1)}) custom-call(s32[1024,1]{1,0:T(8,128)} %copy-done, f32[1024,1]{1,0:T(8,128)} %get-tuple-element.206.gate_ref, s32[1024,1]{1,0:T(8,128)} %copy-done.1, bf16[1536,768]{1,0:T(8,128)(2,1)S(1)} %bitcast.72, ...), custom_call_target="tpu_custom_call" | custom-call | tf_op jit(solution)/shard_map/all_sum/pallas_call | solution.py:990
  380.6 1.2 slice.29
  382.4 7.4 %unpack.1 = (f32[768,768]{1,0:T(8,128)}, f32[768,768]{1,0:T(8,128)}, f32[768,768]{1,0:T(8,128)}, f32[768,768]{1,0:T(8,128)}, f32[32,768]{1,0:T(8,128)}, /*index=...) custom-call(bf16[24,768,128]{2,1,0:T(8,128)(2,1)} %bitcast.74, bf16[24,768,128]{2,1,0:T(8,128)(2,1)} %bitcast.75, ...), custom_call_target="tpu_custom_call" | custom-call | tf_op jit(solution)/shard_map/unpack/pallas_call | solution.py:349
  389.9 1.4 slice_reduce_fusion
  (35 shorter events, 0.1 us)
Async XLA Ops:
  1.6 9.6 %copy-start.2 = (s32[1,1024]{0,1:T(8,128)}, s32[1,1024]{0,1:T(8,128)S(1)}, u32[]{:S(2)}) copy-start(s32[1,1024]{0,1:T(8,128)S(1)} %copy.51) | copy-start | bytes 12292
  2.5 1.4 copy-start.4
  11.2 0.8 copy-start.1
  12.0 0.6 copy-start.13
  12.0 253.4 %copy-start = (s32[1024,1]{1,0:T(8,128)}, s32[1024,1]{1,0:T(8,128)S(1)}, u32[]{:S(2)}) copy-start(s32[1024,1]{1,0:T(8,128)S(1)} %get-tuple-element.207.code_ref) | copy-start | bytes 12292
  12.0 8.2 %copy-start.20 = (f32[768]{0:T(1024)S(1)}, f32[768]{0:T(1024)}, u32[]{:S(2)}) copy-start(f32[768]{0:T(1024)} %param.25) | copy-start | bytes 9220
  12.0 8.2 %copy-start.19 = (f32[32,12]{0,1:T(8,128)S(1)}, f32[32,12]{0,1:T(8,128)}, u32[]{:S(2)}) copy-start(f32[32,12]{0,1:T(8,128)} %param.27) | copy-start | bytes 4612
  12.6 79.1 %all-to-all-start.1 = ((bf16[32,64,768]{2,1,0:T(8,128)(2,1)}), bf16[32,64,768]{2,1,0:T(8,128)(2,1)}, u32[]{:S(2)}, u32[]{:S(2)}) async-start(bf16[32,64,768]{2,1,0:T(8,128)(2,1)} %bitcast.83), calls=%async_computation.1 | async-start | bytes 6291456 | tf_op jit(solution)/shard_map/all_to_all | solution.py:160
  20.2 5.5 %copy-start.3 = (f32[1,768]{1,0:T(1,128)}, f32[1,768]{1,0:T(1,128)S(1)}, u32[]{:S(2)}) copy-start(f32[1,768]{1,0:T(1,128)S(1)} %reshape.335.gain_ref) | copy-start | bytes 9220
  23.5 0.8 copy-start.18
  23.5 1.0 copy-start.21
  25.8 1.4 copy-start.5
  27.2 1.3 copy-start.6
  28.4 1.3 copy-start.7
  29.7 1.3 copy-start.8
  31.0 6.1 %copy-start.9 = (s32[2]{0:T(128)S(1)}, s32[2]{0:T(128)}, u32[]{:S(2)}) copy-start(s32[2]{0:T(128)} %len_ref.1) | copy-start | bytes 28
  35.9 1.2 copy-start.12
  37.1 21.4 %copy-start.11 = (bf16[1024,2304]{1,0:T(8,128)(2,1)}, bf16[1024,2304]{1,0:T(8,128)(2,1)S(1)}, u32[]{:S(2)}) copy-start(bf16[1024,2304]{1,0:T(8,128)(2,1)S(1)} %get-tuple-element.124.q_ref.k_ref.v_ref) | copy-start | bytes 14155780
  58.4 1.1 copy-start.10
  133.7 41.2 %all-to-all-start.3 = ((bf16[32,32,768]{2,1,0:T(8,128)(2,1)}), bf16[32,32,768]{2,1,0:T(8,128)(2,1)S(1)}, u32[]{:S(2)}, u32[]{:S(2)}) async-start(bf16[32,32,768]{2,1,0:T(8,128)(2,1)} %bitcast.87), calls=%async_computation.3 | async-start | bytes 3145728 | tf_op jit(solution)/shard_map/all_to_all | solution.py:160
  174.9 1.1 copy-start.16
  176.1 41.5 %all-to-all-start.4 = ((bf16[32,32,768]{2,1,0:T(8,128)(2,1)}), bf16[32,32,768]{2,1,0:T(8,128)(2,1)S(1)}, u32[]{:S(2)}, u32[]{:S(2)}) async-start(bf16[32,32,768]{2,1,0:T(8,128)(2,1)} %bitcast.89), calls=%async_computation.4 | async-start | bytes 3145728 | tf_op jit(solution)/shard_map/all_to_all | solution.py:160
  217.6 1.1 copy-start.15
  218.7 41.6 %all-to-all-start.5 = ((bf16[32,32,768]{2,1,0:T(8,128)(2,1)}), bf16[32,32,768]{2,1,0:T(8,128)(2,1)}, u32[]{:S(2)}, u32[]{:S(2)}) async-start(bf16[32,32,768]{2,1,0:T(8,128)(2,1)} %bitcast.86), calls=%async_computation.5 | async-start | bytes 3145728 | tf_op jit(solution)/shard_map/all_to_all | solution.py:160
  225.1 2.0 copy-start.14
  226.0 1.7 copy-start.17
  260.4 58.3 %all-to-all-start.6 = ((bf16[32,48,768]{2,1,0:T(8,128)(2,1)}), bf16[32,48,768]{2,1,0:T(8,128)(2,1)S(1)}, u32[]{:S(2)}, u32[]{:S(2)}) async-start(bf16[32,48,768]{2,1,0:T(8,128)(2,1)} %pad_maximum_fusion), calls=%async_computation.6 | async-start | bytes 4718592 | tf_op jit(solution)/shard_map/all_to_all | solution.py:160

commit v7 on v6

--- a/solution.py
+++ b/solution.py
@@ -64,7 +64,14 @@
 def plan(room):
     if room % 64:
         return ((0, room),), room, 0
-    return ((0, room // 2), (room // 2, room)), 3 * room // 4, room // 4
+    half = room // 2
+    return ((half, half + room // 4), (0, half)), 3 * room // 4, room // 4
+
+
+def back_plan(room):
+    if room % 64:
+        return ((0, room),)
+    return ((room // 2, room), (0, room // 2))
 
 
 def segment(code, room, low, high):
@@ -94,7 +101,7 @@
 
 def collect_all(code, room, refs):
     total = None
-    for (low, high), ref in zip(plan(room)[0], refs):
+    for (low, high), ref in zip(back_plan(room), refs):
         part = collect(segment(code, room, low, high), ref[...])
         total = part if total is None else total + part
     return total
@@ -107,7 +114,7 @@
 
 
 def route_kernel(
-    experts, room, eid_c, eid_r, slot_c, slot_r, g_ref, code_c, code_r, rank_c, flag, out
+    experts, room, eid_ref, slot_ref, g_ref, code_c, code_r, rank_c, rank_r, marks, out, more
 ):
     tokens = g_ref.shape[0]
     wide = max(TILE, experts)
@@ -115,44 +122,54 @@
     at = lax.broadcasted_iota(jnp.int32, (tokens, tokens), 0)
     to = lax.broadcasted_iota(jnp.int32, (tokens, tokens), 1)
 
-    ids = eid_r[...]
+    line = lambda ref: jnp.concatenate([ref[i : i + 1] for i in range(ref.shape[0])], axis=1)
+    ids = line(eid_ref)
+    slots = line(slot_ref)
+    both = jnp.concatenate([ids, slots] + [jnp.zeros((6, tokens), jnp.int32)], axis=0)
+    columns = both.astype(jnp.float32).T.astype(jnp.int32)
     picked = ids == lax.broadcasted_iota(jnp.int32, (wide, tokens), 0)
     earlier = dot(picked.astype(LOW), (at < to).astype(LOW))
     place = jnp.sum(jnp.where(picked, earlier, 0.0), axis=0, keepdims=True).astype(jnp.int32)
-    code = jnp.where(slot_r[...] >= 0, ids * room + place, -1)
+    kept = slots >= 0
+    code = jnp.where(kept, ids * room + place, -1)
     code_r[...] = code
-    spread(code, g_ref[...], out)
-
-    ids = eid_c[...]
+    rank = jnp.where(kept & (place >= cut), place - cut, -1)
+    rank_r[...] = rank
+    spread(segment(code, room, 0, cut), g_ref[...], out)
+    spread(rank, g_ref[...], more)
+
+    ids = columns[:, :1]
     picked = ids == lax.broadcasted_iota(jnp.int32, (tokens, wide), 1)
     earlier = dot((to < at).astype(LOW), picked.astype(LOW))
     place = jnp.sum(jnp.where(picked, earlier, 0.0), axis=1, keepdims=True).astype(jnp.int32)
-    kept = slot_c[...] >= 0
+    kept = columns[:, 1:2] >= 0
     code_c[...] = jnp.where(kept, ids * room + place, -1)
     over = kept & (place >= cut)
     rank_c[...] = jnp.where(over, place - cut, -1)
     named = jnp.max(jnp.where(picked & over, 1.0, 0.0), axis=0, keepdims=True)
     named = jnp.sum(named, axis=1, keepdims=True)
-    flag[...] = jnp.broadcast_to(jnp.where(named > 1.0, 1.0, 0.0), flag.shape)
+    owner = jnp.max(jnp.where(over, ids + 1, 0).astype(jnp.float32), axis=0, keepdims=True)
+    lane = lax.broadcasted_iota(jnp.int32, marks.shape, 1)
+    crowded = jnp.where(named > 1.0, 1.0, 0.0)
+    marks[...] = jnp.where(lane == 0, owner, jnp.where(lane == 1, crowded, 0.0))
 
 
 def route(expert_ids, slots, upstream, experts, room):
     tokens, width = upstream.shape
     column = jax.ShapeDtypeStruct((tokens, 1), jnp.int32)
     line = jax.ShapeDtypeStruct((1, tokens), jnp.int32)
+    _, cut, extra = plan(room)
     return pl.pallas_call(
         functools.partial(route_kernel, experts, room),
         out_shape=[
-            column, line, column, jax.ShapeDtypeStruct((16, TILE), jnp.float32),
-            jax.ShapeDtypeStruct((experts * room, width), LOW),
-        ],
-        compiler_params=params(48),
+            column, line, column, line, jax.ShapeDtypeStruct((8, TILE), jnp.float32),
+            jax.ShapeDtypeStruct((experts * cut, width), LOW),
+            jax.ShapeDtypeStruct((max(extra, 16), width), LOW),
+        ],
+        compiler_params=params(60),
         cost_estimate=cost(2 * experts * room * tokens * width, 8 << 20),
         name="route",
-    )(
-        expert_ids.reshape(tokens, 1), expert_ids.reshape(1, tokens),
-        slots.reshape(tokens, 1), slots.reshape(1, tokens), upstream,
-    )
+    )(expert_ids, slots, upstream)
 
 
 def exchange(buffer, devices):
@@ -191,12 +208,60 @@
     )(x, gain, w_query, w_key, w_value)
 
 
+def gather_orders(bits):
+    far = tuple(range(3, bits))
+    return [[(0,), (1,), (2,), far], [(0,), (2,), (1,), far], [(0,), (1,), (2,), far]]
+
+
+def span(order, s, n):
+    for group in order[: s + 1]:
+        n >>= len(group)
+    return n
+
+
+def digit_of(d, group):
+    if isinstance(d, int):
+        return sum(((d >> b) & 1) << i for i, b in enumerate(group))
+    return sum(lax.rem(lax.div(d, 1 << b), 2) * (1 << i) for i, b in enumerate(group))
+
+
+def peer_of(me, group, r):
+    for i, b in enumerate(group):
+        if (r >> i) & 1:
+            me = partner_of(me, b)[1]
+    return me
+
+
+def rank_in(order, d):
+    n = 1 << sum(len(group) for group in order)
+    return sum(digit_of(d, group) * span(order, s, n) for s, group in enumerate(order))
+
+
 def after_attention_kernel(
-    experts, room, o_ref, x_ref, w_ref, gain_ref, eid_ref, wr_ref, code_ref, y_ref, gate_ref, *rest
+    experts, room, cores, n, o_ref, x_ref, w_ref, gain_ref, eid_ref, wr_ref, code_ref, *rest
 ):
-    outs, held = rest[:-1], rest[-1]
+    segments, _, extra = plan(room)
+    if extra:
+        rank_ref, g_ref, mark_ref, *rest = rest
+    y_ref, gate_ref, *rest = rest
+    outs, rest = rest[: len(segments)], rest[len(segments) :]
+    if extra:
+        h_more, g_more, flag_ref, *rest = rest
+        own, moved, marks, send, recv, *rest = rest
+    (held,) = rest
     step = o_ref.shape[0]
     i = pl.program_id(0)
+    bits = n.bit_length() - 1
+    if extra:
+        me = lax.axis_index("grp") * cores + lax.axis_index("exp")
+        barrier = pltpu.get_barrier_semaphore()
+        greeted = [(g, r) for g in gather_orders(bits)[0] for r in range(1, 1 << len(g))]
+
+        @pl.when(i == 0)
+        def _():
+            for group, r in greeted:
+                pl.semaphore_signal(barrier, inc=1, **device_place(cores, peer_of(me, group, r)))
+
     y = x_ref[...].astype(jnp.float32) + dot(o_ref[...], w_ref[...])
     y_ref[...] = y
     rms = lax.rsqrt(jnp.mean(y * y, axis=-1, keepdims=True) + EPSILON)
@@ -204,25 +269,123 @@
     held[pl.ds(pl.multiple_of(i * step, step), step), :] = normed
     router = route_softmax(dot(normed, wr_ref[...]), experts)
     lane = lax.broadcasted_iota(jnp.int32, router.shape, 1)
-    gate_ref[...] = jnp.sum(jnp.where(lane == eid_ref[...], router, 0.0), axis=-1, keepdims=True)
+    expert = lax.div(jnp.maximum(eid_ref[...], 0), room)
+    gate_ref[...] = jnp.sum(jnp.where(lane == expert, router, 0.0), axis=-1, keepdims=True)
 
     @pl.when(i == pl.num_programs(0) - 1)
     def _():
-        spread_all(code_ref[...], room, held[...], outs)
-
-
-def after_attention(joined, x, w_output, gain, expert_ids, w_router, code, experts, room):
+        chunks = []
+        for (low, high), out in zip(segments, outs):
+            dest = segment(code_ref[...], room, low, high)
+            size = min(256, out.shape[0])
+            chunks += [(dest, out, start, size) for start in range(0, out.shape[0], size)]
+
+        def spread_some(count):
+            for dest, out, start, size in chunks[:count]:
+                spread(dest - start, held[...], out.at[start : start + size])
+            del chunks[:count]
+
+        if not extra:
+            spread_some(len(chunks))
+            return
+        single, width = g_ref.shape
+        block = 2 * single
+        orders = gather_orders(bits)
+        phases = len(orders[0])
+        third = width // 3
+        spread(rank_ref[...], held[...], own)
+        base = []
+        for p, order in enumerate(orders):
+            lanes = slice(p * third, (p + 1) * third)
+            base.append(rank_in(order, me) * block)
+            moved[p, rows_at(base[p], single), :] = own[:, lanes]
+            moved[p, rows_at(base[p] + single, single), :] = g_ref[:, lanes]
+        tall = mark_ref.shape[0]
+        marks[pl.ds(pl.multiple_of(rank_in(orders[0], me) * tall, 8), tall), :] = mark_ref[...]
+        pl.semaphore_wait(barrier, len(greeted))
+
+        def doubling(s):
+            copies = []
+            for p, order in enumerate(orders):
+                size = span(order, s, n)
+                for r in range(1, 1 << len(order[s])):
+                    place = device_place(cores, peer_of(me, order[s], r))
+                    here = rows_at(base[p], block * size)
+                    copies.append(
+                        pltpu.make_async_remote_copy(
+                            src_ref=moved.at[p, here], dst_ref=moved.at[p, here],
+                            send_sem=send.at[p, s, r - 1], recv_sem=recv.at[p, s, r - 1], **place,
+                        )
+                    )
+                    if p == 0:
+                        start = lax.div(base[0], block) * tall
+                        here = pl.ds(pl.multiple_of(start, 8), tall * size)
+                        copies.append(
+                            pltpu.make_async_remote_copy(
+                                src_ref=marks.at[here], dst_ref=marks.at[here],
+                                send_sem=send.at[3, s, r - 1], recv_sem=recv.at[3, s, r - 1], **place,
+                            )
+                        )
+            for copy in copies:
+                copy.start()
+            return copies
+
+        sent = []
+        for s in reversed(range(phases)):
+            copies = doubling(s)
+            spread_some(2)
+            for copy in copies:
+                copy.wait_recv()
+            sent += copies
+            for p, order in enumerate(orders):
+                base[p] = base[p] - digit_of(me, order[s]) * block * span(order, s, n)
+        spread_some(len(chunks))
+        for copy in sent:
+            copy.wait_send()
+        for d in range(n):
+            here = slice(d * single, (d + 1) * single)
+            first = rank_in(orders[0], d) * tall
+            keep = marks[first : first + 1, :1] == (me + 1).astype(jnp.float32)
+            for p, order in enumerate(orders):
+                lanes = slice(p * third, (p + 1) * third)
+                at = rank_in(order, d) * block
+                for out, start in ((h_more, at), (g_more, at + single)):
+                    got = moved[p, start : start + single, :].astype(jnp.float32)
+                    out[here, lanes] = jnp.where(keep, got, 0.0).astype(LOW)
+        flag_ref[...] = jnp.broadcast_to(
+            jnp.max(marks[:, 1:2], axis=0, keepdims=True), flag_ref.shape
+        )
+
+
+def after_attention(
+    joined, x, w_output, gain, expert_ids, w_router, code, rank, g_extra, marks, experts, room
+):
     tokens, width = x.shape
     step = 256
+    cores = lax.axis_size("exp")
+    n = lax.axis_size(AXES)
+    bits = n.bit_length() - 1
+    segments, _, extra = plan(room)
     rows = pl.BlockSpec((step, width), lambda i: (i, 0))
     single = pl.BlockSpec((step, 1), lambda i: (i, 0))
     outs = buffers(experts, room, width)
+    more, scratch, options = [], [], {}
+    if extra:
+        more = [rank, g_extra, marks]
+        outs = outs + [jax.ShapeDtypeStruct((n * extra, width), LOW)] * 2
+        outs = outs + [jax.ShapeDtypeStruct((8, TILE), jnp.float32)]
+        scratch = [
+            pltpu.VMEM((extra, width), LOW), pltpu.VMEM((3, 2 * n * extra, width // 3), LOW),
+            pltpu.VMEM((8 * n, TILE), jnp.float32),
+            pltpu.SemaphoreType.DMA((4, 4, (n >> 3) - 1)), pltpu.SemaphoreType.DMA((4, 4, (n >> 3) - 1)),
+        ]
+        options = dict(collective_id=2, has_side_effects=True)
     return pl.pallas_call(
-        functools.partial(after_attention_kernel, experts, room),
+        functools.partial(after_attention_kernel, experts, room, cores, n),
         grid=(tokens // step,),
         in_specs=[
             rows, rows, whole((width, width)), whole((1, width)), single, whole(w_router.shape),
-            whole((1, tokens)),
+            whole((1, tokens)), *[whole(m.shape) for m in more],
         ],
         out_specs=[rows, single] + [pl.BlockSpec(o.shape, lambda i: (0, 0)) for o in outs],
         out_shape=[
@@ -230,11 +393,11 @@
             jax.ShapeDtypeStruct((tokens, 1), jnp.float32),
         ]
         + outs,
-        scratch_shapes=[pltpu.VMEM((tokens, width), LOW)],
-        compiler_params=params(60),
+        scratch_shapes=scratch + [pltpu.VMEM((tokens, width), LOW)],
+        compiler_params=params(60, **options),
         cost_estimate=cost(2 * tokens * width * (width + experts * room), 12 << 20),
         name="after_attention",
-    )(joined, x, w_output, gain, expert_ids, w_router, code)
+    )(joined, x, w_output, gain, expert_ids, w_router, code, *more)
 
 
 def route_softmax(logits, experts):
@@ -333,9 +496,9 @@
             lanes = slice(c * TILE, (c + 1) * TILE)
             router[:, lanes] = small[c * experts : (c + 1) * experts]
             for n in range(2):
-                at = lines * experts + 16 + n * lines + c
+                at = lines * experts + n * lines + c
                 gains[n : n + 1, lanes] = small[at : at + 1]
-        at = lines * experts + 16 + -(-2 * lines // 16) * 16
+        at = lines * experts + -(-2 * lines // 16) * 16
         table[...] = small[at : at + heads, :buckets]
 
 
@@ -646,8 +809,8 @@
     return near, far
 
 
-def expert_kernel(experts, chunk, x_ref, g_ref, mine_ref, wr_ref, wi_any, wo_any,
-                  ff_ref, dx_ref, hid_ref, da_ref, xt_ref, dfft_ref, gr_ref, wi_ref, wo_ref, sem):
+def expert_kernel(experts, chunk, held, x_ref, g_ref, mine_ref, wr_ref, wi_any, wo_any, *refs):
+    ff_ref, dx_ref, hid_ref, da_ref, xt_ref, dfft_ref, gr_ref, wi_ref, wo_ref, sem = refs[held:]
     inner = wi_ref.shape[1]
     first_step = pl.program_id(0) == 0
 
@@ -704,38 +867,55 @@
     dgate = jnp.sum(g * ff.astype(jnp.float32), axis=-1, keepdims=True)
     dlogits = ((gate * dgate) * (mine - router)).astype(LOW)
     dx = dx + lax.dot_general(dlogits, wr_ref[...], (((1,), (1,)), ((), ())), preferred_element_type=jnp.float32)
-    dx_ref[...] = dx.astype(LOW)
+    dx_ref[...] = dx.astype(LOW).reshape(dx_ref.shape)
     x_t = x.T
     xt_ref[...] = x_t
     dfft_ref[...] = dff.T
     gr_ref[...] += dot(dlogits.T, x)
 
-def expert_rows(x, g, mine, wr, wi, wo, experts, low, high, tile=256, chunk=768):
+def expert_rows(x, g, mine, wr, wi, wo, experts, low, high, at=0, total=0, dx=None, tile=256, chunk=768):
     n, width = x.shape
     inner = wi.shape[1]
     sources, room = g.shape[0], high - low
+    total = total or room
     group = max(1, min(sources, tile // room))
     while sources % group or (group * room) % TILE:
         group += 1
     tile = group * room
-    gspec = pl.BlockSpec((group, room, width), lambda i: (i, low // room, 0))
     once = lambda s: pl.BlockSpec(s, lambda i: (0,) * len(s), pipeline_mode=pl.Buffered(1))
     rowspec = lambda w: pl.BlockSpec((tile, w), lambda i: (i, 0))
+    column = pl.BlockSpec((width, tile), lambda i: (0, i))
     anywhere = pl.BlockSpec(memory_space=pl.ANY)
+    held = [] if dx is None else [dx]
     return pl.pallas_call(
-        functools.partial(expert_kernel, experts, chunk),
+        functools.partial(expert_kernel, experts, chunk, len(held)),
         grid=(n // tile,),
-        in_specs=[rowspec(width), gspec, once(mine.shape), once(wr.shape), anywhere, anywhere],
-        out_specs=[rowspec(width), rowspec(width), rowspec(inner), rowspec(inner),
-                   pl.BlockSpec((width, tile), lambda i: (0, i)), pl.BlockSpec((width, tile), lambda i: (0, i)),
-                   pl.BlockSpec((wr.shape[1], width), lambda i: (0, 0))],
-        out_shape=[jax.ShapeDtypeStruct((n, width), LOW)] * 2 + [jax.ShapeDtypeStruct((n, inner), LOW)] * 2
-            + [jax.ShapeDtypeStruct((width, n), LOW)] * 2 + [jax.ShapeDtypeStruct((wr.shape[1], width), jnp.float32)],
-        scratch_shapes=[pltpu.VMEM(wi.shape, LOW), pltpu.VMEM(wo.shape, LOW), pltpu.SemaphoreType.DMA((2, inner // chunk))],
+        in_specs=[
+            rowspec(width), pl.BlockSpec((group, room, width), lambda i: (i, low // room, 0)),
+            once(mine.shape), once(wr.shape), anywhere, anywhere, *[anywhere] * len(held),
+        ],
+        out_specs=[
+            rowspec(width), pl.BlockSpec((group, room, width), lambda i: (i, at // room, 0)),
+            rowspec(inner), rowspec(inner), column, column,
+            pl.BlockSpec((wr.shape[1], width), lambda i: (0, 0)),
+        ],
+        out_shape=[
+            jax.ShapeDtypeStruct((n, width), LOW),
+            jax.ShapeDtypeStruct((sources, total, width), LOW),
+            *[jax.ShapeDtypeStruct((n, inner), LOW)] * 2,
+            *[jax.ShapeDtypeStruct((width, n), LOW)] * 2,
+            jax.ShapeDtypeStruct((wr.shape[1], width), jnp.float32),
+        ],
+        scratch_shapes=[
+            pltpu.VMEM(wi.shape, LOW), pltpu.VMEM(wo.shape, LOW),
+            pltpu.SemaphoreType.DMA((2, inner // chunk)),
+        ],
+        input_output_aliases={6: 1} if held else {},
         compiler_params=params(60),
-        cost_estimate=cost(flops=8 * n * width * inner, bytes_accessed=4 * n * inner + 8 * width * inner, transcendentals=n * inner),
+        cost_estimate=cost(8 * n * width * inner, 4 * n * inner + 8 * width * inner, n * inner),
         name="expert_rows",
-    )(x, g, mine, wr, wi, wo)
+    )(x, g, mine, wr, wi, wo, *held)
+
 
 def expert_weights_kernel(parts, *refs):
     ins, (gi_ref, go_ref) = refs[: 4 * parts], refs[4 * parts :]
@@ -1026,58 +1206,85 @@
     g = cotangent.reshape(count, width)
     gain_one = gain_attn.reshape(1, width)
     gain_two = gain_ffn.reshape(1, width)
-    wide = max(128, experts)
-    mine = (jnp.arange(wide, dtype=jnp.int32) == me).astype(jnp.float32).reshape(1, wide)
+    mine = (jnp.arange(experts, dtype=jnp.int32) == me).astype(jnp.float32).reshape(1, experts)
 
     segments, cut, extra = plan(room)
-    code_c, code_r, rank_c, flag, g_out = route(expert_ids, slots, g, experts, room)
+    code_c, code_r, rank_c, rank_r, marks, g_out, g_extra = route(expert_ids, slots, g, experts, room)
     g_in = exchange(g_out, devices)
-    code_r, x, w_query, w_key, w_value, w_output, bias_table, w_router = lax.optimization_barrier(
-        (code_r, x, w_query, w_key, w_value, w_output, bias_table, w_router)
-    )
-    router_w = jnp.pad(w_router, ((0, 0), (0, wide - experts)))
+    code_r, gain_one, bias_table = lax.optimization_barrier((code_r, gain_one, bias_table))
 
     normed_t, projected = project(x, gain_one, w_query, w_key, w_value)
     near, far = bias_tiles(bias_table)
     joined, weights = attention_forward(lengths, projected, near, far, rows, seq, heads, head)
     y, gate, *h_out = after_attention(
-        joined, x, w_output, gain_two, expert_ids.reshape(count, 1), router_w, code_r, experts, room
+        joined, x, w_output, gain_two, code_c, w_router, code_r, rank_r,
+        g_extra, marks, experts, room,
     )
+    code = code_c.reshape(-1)
+    expert = code // room
+    place = code - expert * room
+    rest = jnp.where((code >= 0) & (place >= cut), expert * extra + place - cut, experts * extra)
+
+    def experts_on(h, g_rows, low, high, *more):
+        return expert_rows(h, g_rows, mine, w_router, w_in[0], w_out[0], experts, low, high, *more)
+
+    parts, grad_router, ff_more, crowded = [], 0.0, None, None
+    if extra:
+        h_more, g_more, flag = h_out[-3:]
+        h_out = h_out[:-3]
+        crowded = flag[0, 0] > 0
     h_out, g_in = lax.optimization_barrier((h_out, g_in))
-    g_in = g_in.reshape(devices, room, width)
+    g_in = g_in.reshape(devices, cut, width)
     h_in = [exchange(h_out[0], devices)]
+    if extra:
+
+        def exchange_rest(_):
+            rms = lax.rsqrt(jnp.mean(y * y, axis=-1, keepdims=True) + EPSILON)
+            h = (y * rms * gain_two).astype(LOW)
+            empty = jnp.zeros((experts * extra, width), LOW)
+            send = lambda a: exchange(empty.at[rest].set(a, mode="drop"), devices)
+            return False, send(h), send(g)
+
+        h_in[0], h_more, g_more = lax.optimization_barrier((h_in[0], h_more, g_more))
+        _, h_more, g_more = lax.while_loop(
+            lambda held: held[0], exchange_rest, (crowded, h_more, g_more)
+        )
+        h_out[1], h_more, g_more = lax.optimization_barrier((h_out[1], h_more, g_more))
     for h in h_out[1:]:
         h, h_in[-1] = lax.optimization_barrier((h, h_in[-1]))
         h_in.append(exchange(h, devices))
-    dx_back, ffs, parts, grad_router = [], [], [], 0.0
-    for n, (low, high) in enumerate(segments):
-        ff, dx, hid, da, x_t, dff_t, routed = expert_rows(
-            h_in[n], g_in, mine, router_w, w_in[0], w_out[0], experts, low, high
+    ffs, dx_back, dx = [], [], None
+    if extra:
+        ff_more, dx, hid, da, x_t, dff_t, routed = experts_on(
+            h_more, g_more.reshape(devices, extra, width), 0, extra, room - cut, 2 * extra
         )
-        if n + 1 < len(segments):
-            dx, h_in[n + 1] = lax.optimization_barrier((dx, h_in[n + 1]))
-        if n:
+        ff_more = ff_more.reshape(devices, extra, width)
+        parts.append((x_t, dff_t, hid, da))
+        grad_router = grad_router + routed
+    for m, (low, high) in enumerate(segments):
+        held = (0, 2 * extra, dx) if extra and not m else ()
+        ff, dx, hid, da, x_t, dff_t, routed = experts_on(h_in[m], g_in, low, high, *held)
+        if m + 1 < len(segments):
+            dx, h_in[m + 1] = lax.optimization_barrier((dx, h_in[m + 1]))
+        if m:
             dx, dx_back[-1] = lax.optimization_barrier((dx, dx_back[-1]))
-        dx_back.append(exchange(dx, devices))
+        dx_back.append(exchange(dx.reshape(-1, width), devices))
         ffs.append(ff.reshape(devices, high - low, width))
         parts.append((x_t, dff_t, hid, da))
         grad_router = grad_router + routed
     grad_in, grad_out = expert_weights(parts)
-    grad_router = grad_router[:experts].reshape(experts, width // TILE, TILE)
-    grad_router = jnp.swapaxes(grad_router, 0, 1).reshape(-1, TILE)
-    small = jnp.concatenate([grad_router, flag], axis=0)
-    ff, ff_more = ffs[0], small
+    grad_router = grad_router.reshape(experts, width // TILE, TILE)
+    small = jnp.swapaxes(grad_router, 0, 1).reshape(-1, TILE)
+    ff, ff_packed = ffs[0], small
     if extra:
-        half = segments[0][1]
-        ff = jnp.concatenate([ffs[0], ffs[1][:, : cut - half]], axis=1)
-        ff_spare = ffs[1][:, cut - half :]
+        ff = jnp.concatenate([ffs[1], ffs[0]], axis=1)
         bits = devices.bit_length() - 1
-        ff_more = ff_spare.reshape((2,) * bits + (extra, width // TILE, TILE))
+        ff_packed = ff_more.reshape((2,) * bits + (extra, width // TILE, TILE))
         order = tuple(reversed(range(bits))) + (bits + 1, bits, bits + 2)
-        ff_more = jnp.transpose(ff_more, order).reshape(-1, TILE)
+        ff_packed = jnp.transpose(ff_packed, order).reshape(-1, TILE)
     ff = ff.reshape(devices * cut, width)
-    dx_back, grad_in, grad_out, ff, ff_more, small = lax.optimization_barrier(
-        (dx_back, grad_in, grad_out, ff, ff_more, small)
+    dx_back, grad_in, grad_out, ff, ff_packed, small = lax.optimization_barrier(
+        (dx_back, grad_in, grad_out, ff, ff_packed, small)
     )
     ff_back = exchange(ff, devices)
 
@@ -1092,18 +1299,13 @@
         small, grad_gain_two, rows, seq, heads, head, small_rows,
     )
     mixed, summed, small = all_sum(
-        [packed.reshape(-1, TILE), grad_output, small], code_c, gate, rank_c, ff_back, y, room, ff_more
+        [packed.reshape(-1, TILE), grad_output, small], code_c, gate, rank_c, ff_back, y, room, ff_packed
     )
     if extra:
-        crowded = small[lines * experts, 0] > 0
 
         def mix_all(_):
-            code = code_c.reshape(-1)
-            expert = code // room
-            place = code - expert * room
-            spare = exchange(ff_spare.reshape(-1, width), devices)
+            spare = exchange(ff_more.reshape(-1, width), devices)
             first = jnp.where((code >= 0) & (place < cut), expert * cut + place, devices * cut)
-            rest = jnp.where(place >= cut, expert * extra + place - cut, devices * extra)
             take = lambda a, index: jnp.take(a, index, axis=0, mode="fill", fill_value=0)
             ff = take(ff_back, first) + take(spare, rest)
             return False, (y + gate * ff.astype(jnp.float32)).astype(LOW)

time: 397 us -> 380 us (0.957)
  blocking collectives: 42.1 us -> 0 us
  Pallas kernels: 254 us -> 284 us
  starting transfers between devices: 22.5 us -> 30 us
  waiting for transfers between devices: 40.3 us -> 32.8 us
  local copies, waits for them, and re-layouts: 25 us -> 18.8 us
    all_to_all x1 -> x0, blocking collectives: 42.1 us -> none  [exchange(): lax.all_to_all(shaped, AXES, split_axis=0, concat_axis=0, tiled=True)]
    pallas_call x3 -> x4, Pallas kernels: 73.3 us -> 104 us  [the longest x3 65.7 us: expert_rows(): pl.pallas_call(functools.partial(expert_kernel, experts, chunk, len(held)...]
    all_to_all x5 -> x6, waiting for transfers between devices: 40.3 us -> 32.8 us  [exchange(): lax.all_to_all(shaped, AXES, split_axis=0, concat_axis=0, tiled=True)]
    all_to_all x5 -> x6, starting transfers between devices: 22.5 us -> 30 us  [exchange(): lax.all_to_all(shaped, AXES, split_axis=0, concat_axis=0, tiled=True)]
    unnamed x50 -> x37, local copies, waits for them, and re-layouts: 15.9 us -> 11.6 us
  transfers between devices with their start and end apart: 5 -> 6, of which waited for: 5 -> 5; matrix products, arithmetic and copies ran while one was open for 3% -> 4% of each run, Pallas kernels for 45% -> 55%
where the time goes in v7:
time: 380 us; the launch traced here: 375 us
  Pallas kernels  284 us (75%)
  waiting for transfers between devices  32.8 us (9%)
  starting transfers between devices  30 us (8%)
  local copies, waits for them, and re-layouts  18.8 us (5%)
  other arithmetic  5.06 us (1%)
    pallas_call x3, Pallas kernels, expert_rows(): pl.pallas_call(functools.partial(expert_kernel, experts, chunk, len(held)...  65.7 us
    pallas_call x1, Pallas kernels, all_sum(): pl.pallas_call(functools.partial(sum_kernel, cores, n, room, heights, ext...  61.7 us
    pallas_call x1, Pallas kernels, after_attention(): pl.pallas_call(functools.partial(after_attention_kernel, experts, room, c...  38 us
    pallas_call x1, Pallas kernels, attention_backward(): pl.pallas_call(functools.partial(attention_backward_kernel, rows), grid=(...  36.8 us
    all_to_all x6, waiting for transfers between devices, exchange(): lax.all_to_all(shaped, AXES, split_axis=0, concat_axis=0, tiled=True)  32.8 us
    all_to_all x6, starting transfers between devices, exchange(): lax.all_to_all(shaped, AXES, split_axis=0, concat_axis=0, tiled=True)  30 us
    pallas_call x1, Pallas kernels, expert_weights(): pl.pallas_call(functools.partial(expert_weights_kernel, len(parts)), grid...  28 us
    pallas_call x1, Pallas kernels, attention_forward(): pl.pallas_call(attention_forward_kernel, grid=(rows, pairs), in_specs=[pl...  21.2 us
  transfers between devices with their start and end apart: 6, of which 5 were waited for; matrix products, arithmetic and copies ran while one was open for 4% of the time, Pallas kernels for 55%

profile of v7, /device:TPU:0, one launch (start us, length us, event | category | flops | bytes accessed | tf_op | source)
XLA Modules:
  0.0 375.2 jit_solution(1652343288130543993)
XLA Ops:
  0.6 7.8 %route.1 = (s32[1024,1]{1,0:T(8,128)}, s32[1,1024]{1,0:T(1,128)}, s32[1024,1]{1,0:T(8,128)}, s32[1,1024]{1,0:T(1,128)}, f32[8,128]{1,0:T(8,128)}, /*index=5*/bf16[1536,768]{1,0:T(8,128)(2,1)}, bf16[16,768]{1,0:T(8,128)(2,1)}) custom-call(s32[2,512]{1,0:T(2,128)} %eid_ref.1, s32[2,512]{1,0:T(2,128)} %slot_ref.1, bf16[1024,768]{1,0:T(8,128)(2,1)} %bitcast.94), custom_call_target="tpu_custom_call" | custom-call | flops 3221225472 | bytes 8388608 | tf_op jit(solution)/shard_map/route/pallas_call | solution.py:162
  8.4 7.6 %all-to-all-start.3 = ((bf16[32,48,768]{2,1,0:T(8,128)(2,1)}), bf16[32,48,768]{2,1,0:T(8,128)(2,1)}, u32[]{:S(2)}, u32[]{:S(2)}) async-start(bf16[32,48,768]{2,1,0:T(8,128)(2,1)} %bitcast.70), calls=%async_computation.3 | async-start | bytes 4718592 | tf_op jit(solution)/shard_map/all_to_all | solution.py:177
  16.0 0.0 copy-done.18
  16.1 0.0 copy-start
  16.1 0.0 copy-done.17
  16.1 0.1 copy.42
  16.2 0.1 copy.43.far_ref
  16.3 0.1 fusion.10
  16.4 0.2 fusion.8
  16.6 2.1 fusion.6
  18.7 0.6 copy.51
  19.3 0.0 copy-start.2
  19.3 0.2 slice.26
  19.5 1.7 copy.44.wr_ref
  21.2 0.7 reshape.298.gain_ref
  21.9 0.0 copy-done
  21.9 0.0 copy-done.2
  21.9 1.4 copy-done.1
  23.3 1.3 copy-done.3
  24.6 1.3 copy-done.4
  25.8 4.9 %project.1 = (bf16[768,1024]{1,0:T(8,128)(2,1)S(1)}, bf16[1024,2304]{1,0:T(8,128)(2,1)S(1)}) custom-call(bf16[1024,768]{1,0:T(8,128)(2,1)S(1)} %bitcast.54, f32[1,768]{1,0:T(1,128)S(1)} %reshape.296.gain_ref, bf16[768,768]{1,0:T(8,128)(2,1)S(1)} %copy-done.2, bf16[768,768]{1,0:T(8,128)(2,1)S(1)} %copy-done.3, bf16[768,768]{1,0:T(8,128)(2,1)S(1)} %copy-done.4), custom_call_target="tpu_custom_call" | custom-call | flops 3623878656 | bytes 12582912 | tf_op jit(solution)/shard_map/project/pallas_call | solution.py:196
  30.7 0.0 copy-start.8
  30.7 1.2 copy-done.8
  31.9 0.0 copy-done.5
  31.9 21.2 %attention_forward.1 = (bf16[1024,768]{1,0:T(8,128)(2,1)S(1)}, bf16[2,12,512,512]{3,2,1,0:T(8,128)(2,1)}) custom-call(s32[2]{0:T(128)S(1)} %copy-done.5, bf16[1024,2304]{1,0:T(8,128)(2,1)S(1)} %get-tuple-element.184.q_ref.k_ref.v_ref, bf16[1024,2304]{1,0:T(8,128)(2,1)S(1)} %get-tuple-element.184.q_ref.k_ref.v_ref, ...), custom_call_target="tpu_custom_call" | custom-call | flops 6442450944 | bytes 12582912 | tf_op jit(solution)/shard_map/attention_forward/pallas_call | solution.py:579
  53.1 0.0 copy-done.7
  53.1 1.1 copy-done.6
  54.3 38.0 %after_attention.1 = (f32[1024,768]{1,0:T(8,128)S(1)}, f32[1024,1]{1,0:T(8,128)}, bf16[512,768]{1,0:T(8,128)(2,1)}, bf16[1024,768]{1,0:T(8,128)(2,1)}, bf16[512,...) custom-call(bf16[1024,768]{1,0:T(8,128)(2,1)} %copy-done.6, bf16[1024,768]{1,0:T(8,128)(2,1)} %bitcast.52, ...), custom_call_target="tpu_custom_call" | custom-call | flops 4429185024 | bytes 12582912 | tf_op jit(solution)/shard_map/after_attention/pallas_call | solution.py:383
  92.3 0.0 all-to-all-done.3
  92.3 3.6 all-to-all-start.4
  95.9 1.2 slice.17
  97.7 1.2 reduce.1
  99.0 17.5 %all-to-all-done.4 = bf16[32,16,768]{2,1,0:T(8,128)(2,1)} async-done(((bf16[32,16,768]{2,1,0:T(8,128)(2,1)}), bf16[32,16,768]{2,1,0:T(8,128)(2,1)}, u32[]{:S(2)}, u32[]{:S(2)}) %all-to-all-start.4) | async-done | bytes 786464 | tf_op jit(solution)/shard_map/all_to_all | solution.py:177
  116.5 0.2 while.20
  116.7 0.0 copy-start.9
  116.7 1.6 copy-done.9
  118.3 7.3 %all-to-all-start.5 = ((bf16[32,32,768]{2,1,0:T(8,128)(2,1)}), bf16[32,32,768]{2,1,0:T(8,128)(2,1)}, u32[]{:S(2)}, u32[]{:S(2)}) async-start(bf16[32,32,768]{2,1,0:T(8,128)(2,1)} %bitcast.71), calls=%async_computation.5 | async-start | bytes 3145728 | tf_op jit(solution)/shard_map/all_to_all | solution.py:177
  125.6 0.5 compare_convert_fusion.mine_ref
  126.1 17.7 %expert_rows.3 = (bf16[512,768]{1,0:T(8,128)(2,1)S(1)}, bf16[32,32,768]{2,1,0:T(8,128)(2,1)}, bf16[512,3072]{1,0:T(8,128)(2,1)}, bf16[512,3072]{1,0:T(8,128)(2,1...) custom-call(bf16[512,768]{1,0:T(8,128)(2,1)} %get-tuple-element.210.x_ref, ...), custom_call_target="tpu_custom_call" | custom-call | flops 9663676416 | bytes 25165824 | tf_op jit(solution)/shard_map/expert_rows/pallas_call | solution.py:890
  143.8 17.7 %expert_rows.4 = (bf16[512,768]{1,0:T(8,128)(2,1)}, bf16[32,32,768]{2,1,0:T(8,128)(2,1)}, bf16[512,3072]{1,0:T(8,128)(2,1)}, bf16[512,3072]{1,0:T(8,128)(2,1)}, ...) custom-call(bf16[512,768]{1,0:T(8,128)(2,1)} %bitcast.21.x_ref, ...), custom_call_target="tpu_custom_call", output_to_operand_aliasing={{1}: (6, {})} | custom-call | flops 9663676416 | bytes 25165824 | tf_op jit(solution)/shard_map/expert_rows/pallas_call | solution.py:890
  161.5 0.1 all-to-all-done.5
  161.6 3.7 all-to-all-start.6
  165.3 30.3 %expert_rows.5 = (bf16[1024,768]{1,0:T(8,128)(2,1)}, bf16[32,32,768]{2,1,0:T(8,128)(2,1)}, bf16[1024,3072]{1,0:T(8,128)(2,1)}, bf16[1024,3072]{1,0:T(8,128)(2,1)...) custom-call(bf16[1024,768]{1,0:T(8,128)(2,1)} %bitcast.27.x_ref, ...), custom_call_target="tpu_custom_call" | custom-call | flops 19327352832 | bytes 31457280 | tf_op jit(solution)/shard_map/expert_rows/pallas_call | solution.py:890
  195.6 7.4 %all-to-all-done.6 = bf16[32,32,768]{2,1,0:T(8,128)(2,1)S(1)} async-done(((bf16[32,32,768]{2,1,0:T(8,128)(2,1)}), bf16[32,32,768]{2,1,0:T(8,128)(2,1)S(1)}, u32[]{:S(2)}, u32[]{:S(2)}) %all-to-all-start.6) | async-done | bytes 1572896 | tf_op jit(solution)/shard_map/all_to_all | solution.py:177
  203.1 1.2 copy-done.12
  204.3 3.9 %all-to-all-start.7 = ((bf16[32,32,768]{2,1,0:T(8,128)(2,1)}), bf16[32,32,768]{2,1,0:T(8,128)(2,1)}, u32[]{:S(2)}, u32[]{:S(2)}) async-start(bf16[32,32,768]{2,1,0:T(8,128)(2,1)} %get-tuple-element.219), calls=%async_computation.7 | async-start | bytes 3145728 | tf_op jit(solution)/shard_map/all_to_all | solution.py:177
  208.2 0.0 copy-start.14
  208.2 0.9 reshape_reshape.3
  209.1 0.0 copy-start.13
  209.1 1.0 copy.48
  210.1 0.0 copy-done.16
  210.2 0.7 copy.49
  210.8 0.0 copy-done.13
  210.8 3.0 pad_maximum_fusion
  213.8 28.0 %expert_weights.1 = (f32[1,768,3072]{2,1,0:T(8,128)}, f32[1,3072,768]{2,1,0:T(8,128)}) custom-call(bf16[768,512]{1,0:T(8,128)(2,1)} %get-tuple-element.220.refs_0_, bf16[768,512]{1,0:T(8,128)(2,1)} %get-tuple-element.221.refs_1_, bf16[512,3072]{1,0:T(8,128)(2,1)} %get-tuple-element.222.refs_2_, bf16[512,3072]{1,0:T(8,128)(2,1)} %get-tuple-element.223.refs_3_, ...), custom_call_target="tpu_custom_call" | custom-call | flops 19327352832 | bytes 44040192 | tf_op jit(solution)/shard_map/expert_weights/pallas_call | solution.py:944
  241.8 4.1 %all-to-all-done.7 = bf16[32,32,768]{2,1,0:T(8,128)(2,1)} async-done(((bf16[32,32,768]{2,1,0:T(8,128)(2,1)}), bf16[32,32,768]{2,1,0:T(8,128)(2,1)}, u32[]{:S(2)}, u32[]{:S(2)}) %all-to-all-start.7) | async-done | bytes 1572896 | tf_op jit(solution)/shard_map/all_to_all | solution.py:177
  245.9 4.0 %all-to-all-start.8 = ((bf16[32,48,768]{2,1,0:T(8,128)(2,1)}), bf16[32,48,768]{2,1,0:T(8,128)(2,1)S(1)}, u32[]{:S(2)}, u32[]{:S(2)}) async-start(bf16[32,48,768]{2,1,0:T(8,128)(2,1)} %pad_maximum_fusion), calls=%async_computation.8 | async-start | bytes 4718592 | tf_op jit(solution)/shard_map/all_to_all | solution.py:177
  249.9 1.2 copy.50
  251.1 12.9 %before_attention.1 = (f32[1024,768]{1,0:T(8,128)}, bf16[1024,768]{1,0:T(8,128)(2,1)}, bf16[4608,128]{1,0:T(8,128)(2,1)}, f32[1,768]{1,0:T(1,128)}) custom-call(s32[1024,1]{1,0:T(8,128)} %get-tuple-element.181.eid_ref.code_ref, f32[1024,768]{1,0:T(8,128)} %copy-done.9, bf16[1024,768]{1,0:T(8,128)(2,1)} %get-tuple-element.436, ...), custom_call_target="tpu_custom_call" | custom-call | flops 3623878656 | bytes 16777216 | tf_op jit(solution)/shard_map/before_attention/pallas_call | solution.py:457
  264.0 36.8 %attention_backward.1 = (f32[1024,768]{1,0:T(8,128)}, bf16[3,6,768,128]{3,2,1,0:T(8,128)(2,1)}, bf16[512,128]{1,0:T(8,128)(2,1)}) custom-call(bf16[1024,2304]{1,0:T(8,128)(2,1)} %copy-done.7, bf16[1024,2304]{1,0:T(8,128)(2,1)} %copy-done.7, bf16[1024,2304]{1,0:T(8,128)(2,1)} %copy-done.7, bf16[1024,768]{1,0:T(8,128)(2,1)} %get-tuple-element.243.do_ref, ...), custom_call_target="tpu_custom_call" | custom-call | flops 12884901888 | bytes 12582912 | tf_op jit(solution)/shard_map/attention_backward/pallas_call | solution.py:764
  300.8 3.7 all-to-all-done.8
  304.4 61.7 %all_sum.1 = (bf16[1024,768]{1,0:T(8,128)(2,1)}, bf16[18432,128]{1,0:T(8,128)(2,1)}, bf16[512,128]{1,0:T(8,128)(2,1)}) custom-call(s32[1024,1]{1,0:T(8,128)} %get-tuple-element.181.eid_ref.code_ref, f32[1024,1]{1,0:T(8,128)} %get-tuple-element.290.gate_ref, s32[1024,1]{1,0:T(8,128)} %get-tuple-element.192.rank_ref, bf16[1536,768]{1,0:T(8,128)(2,1)S(1)} %bitcast.56, ...), custom_call_target="tpu_custom_call" | custom-call | tf_op jit(solution)/shard_map/all_sum/pallas_call | solution.py:1170
  366.1 7.4 %unpack.1 = (f32[768,768]{1,0:T(8,128)}, f32[768,768]{1,0:T(8,128)}, f32[768,768]{1,0:T(8,128)}, f32[768,768]{1,0:T(8,128)}, f32[32,768]{1,0:T(8,128)}, /*index=...) custom-call(bf16[24,768,128]{2,1,0:T(8,128)(2,1)} %bitcast.60, bf16[24,768,128]{2,1,0:T(8,128)(2,1)} %bitcast.61, ...), custom_call_target="tpu_custom_call" | custom-call | tf_op jit(solution)/shard_map/unpack/pallas_call | solution.py:512
  373.6 1.4 slice_reduce_fusion
  (22 shorter events, 0.1 us)
Async XLA Ops:
  8.4 7.6 %copy-start.18 = (f32[768]{0:T(1024)S(1)}, f32[768]{0:T(1024)}, u32[]{:S(2)}) copy-start(f32[768]{0:T(1024)} %param.27) | copy-start | bytes 9220
  8.4 7.6 %copy-start.17 = (f32[32,12]{0,1:T(8,128)S(1)}, f32[32,12]{0,1:T(8,128)}, u32[]{:S(2)}) copy-start(f32[32,12]{0,1:T(8,128)} %param.29) | copy-start | bytes 4612
  8.4 83.8 %all-to-all-start.3 = ((bf16[32,48,768]{2,1,0:T(8,128)(2,1)}), bf16[32,48,768]{2,1,0:T(8,128)(2,1)}, u32[]{:S(2)}, u32[]{:S(2)}) async-start(bf16[32,48,768]{2,1,0:T(8,128)(2,1)} %bitcast.70), calls=%async_computation.3 | async-start | bytes 4718592 | tf_op jit(solution)/shard_map/all_to_all | solution.py:177
  16.1 5.8 %copy-start = (f32[1,768]{1,0:T(1,128)}, f32[1,768]{1,0:T(1,128)S(1)}, u32[]{:S(2)}) copy-start(f32[1,768]{1,0:T(1,128)S(1)} %reshape.296.gain_ref) | copy-start | bytes 9220
  19.3 2.6 copy-start.2
  21.9 1.4 copy-start.1
  23.3 1.3 copy-start.3
  24.6 1.3 copy-start.4
  25.8 6.1 %copy-start.5 = (s32[2]{0:T(128)S(1)}, s32[2]{0:T(128)}, u32[]{:S(2)}) copy-start(s32[2]{0:T(128)} %len_ref.1) | copy-start | bytes 28
  30.7 1.2 copy-start.8
  31.9 21.2 %copy-start.7 = (bf16[1024,2304]{1,0:T(8,128)(2,1)}, bf16[1024,2304]{1,0:T(8,128)(2,1)S(1)}, u32[]{:S(2)}) copy-start(bf16[1024,2304]{1,0:T(8,128)(2,1)S(1)} %get-tuple-element.184.q_ref.k_ref.v_ref) | copy-start | bytes 14155780
  53.1 1.1 copy-start.6
  92.3 24.2 %all-to-all-start.4 = ((bf16[32,16,768]{2,1,0:T(8,128)(2,1)}), bf16[32,16,768]{2,1,0:T(8,128)(2,1)}, u32[]{:S(2)}, u32[]{:S(2)}) async-start(bf16[32,16,768]{2,1,0:T(8,128)(2,1)} %bitcast.77), calls=%async_computation.4 | async-start | bytes 1572864 | tf_op jit(solution)/shard_map/all_to_all | solution.py:177
  116.7 1.6 copy-start.9
  118.3 43.3 %all-to-all-start.5 = ((bf16[32,32,768]{2,1,0:T(8,128)(2,1)}), bf16[32,32,768]{2,1,0:T(8,128)(2,1)}, u32[]{:S(2)}, u32[]{:S(2)}) async-start(bf16[32,32,768]{2,1,0:T(8,128)(2,1)} %bitcast.71), calls=%async_computation.5 | async-start | bytes 3145728 | tf_op jit(solution)/shard_map/all_to_all | solution.py:177
  161.6 41.4 %all-to-all-start.6 = ((bf16[32,32,768]{2,1,0:T(8,128)(2,1)}), bf16[32,32,768]{2,1,0:T(8,128)(2,1)S(1)}, u32[]{:S(2)}, u32[]{:S(2)}) async-start(bf16[32,32,768]{2,1,0:T(8,128)(2,1)} %get-tuple-element.217), calls=%async_computation.6 | async-start | bytes 3145728 | tf_op jit(solution)/shard_map/all_to_all | solution.py:177
  203.1 1.2 copy-start.12
  204.3 41.6 %all-to-all-start.7 = ((bf16[32,32,768]{2,1,0:T(8,128)(2,1)}), bf16[32,32,768]{2,1,0:T(8,128)(2,1)}, u32[]{:S(2)}, u32[]{:S(2)}) async-start(bf16[32,32,768]{2,1,0:T(8,128)(2,1)} %get-tuple-element.219), calls=%async_computation.7 | async-start | bytes 3145728 | tf_op jit(solution)/shard_map/all_to_all | solution.py:177
  208.2 2.0 copy-start.14
  208.2 2.0 copy-start.15
  208.2 1.9 copy-start.16
  209.1 1.8 copy-start.13
  245.9 58.5 %all-to-all-start.8 = ((bf16[32,48,768]{2,1,0:T(8,128)(2,1)}), bf16[32,48,768]{2,1,0:T(8,128)(2,1)S(1)}, u32[]{:S(2)}, u32[]{:S(2)}) async-start(bf16[32,48,768]{2,1,0:T(8,128)(2,1)} %pad_maximum_fusion), calls=%async_computation.8 | async-start | bytes 4718592 | tf_op jit(solution)/shard_map/all_to_all | solution.py:177

commit v8 on v7

--- a/solution.py
+++ b/solution.py
@@ -114,7 +114,7 @@
 
 
 def route_kernel(
-    experts, room, eid_ref, slot_ref, g_ref, code_c, code_r, rank_c, rank_r, marks, out, more
+    experts, room, eid_ref, slot_ref, g_ref, code_r, rank_r, out, more
 ):
     tokens = g_ref.shape[0]
     wide = max(TILE, experts)
@@ -125,8 +125,6 @@
     line = lambda ref: jnp.concatenate([ref[i : i + 1] for i in range(ref.shape[0])], axis=1)
     ids = line(eid_ref)
     slots = line(slot_ref)
-    both = jnp.concatenate([ids, slots] + [jnp.zeros((6, tokens), jnp.int32)], axis=0)
-    columns = both.astype(jnp.float32).T.astype(jnp.int32)
     picked = ids == lax.broadcasted_iota(jnp.int32, (wide, tokens), 0)
     earlier = dot(picked.astype(LOW), (at < to).astype(LOW))
     place = jnp.sum(jnp.where(picked, earlier, 0.0), axis=0, keepdims=True).astype(jnp.int32)
@@ -138,14 +136,19 @@
     spread(segment(code, room, 0, cut), g_ref[...], out)
     spread(rank, g_ref[...], more)
 
-    ids = columns[:, :1]
+
+def columns_kernel(experts, room, code_ref, code_c, rank_c, marks):
+    tokens = code_ref.shape[1]
+    wide = max(TILE, experts)
+    _, cut, _ = plan(room)
+    rows = jnp.concatenate([code_ref[...], jnp.zeros((7, tokens), jnp.int32)], axis=0)
+    code = rows.astype(jnp.float32).T.astype(jnp.int32)[:, :1]
+    code_c[...] = code
+    ids = lax.div(code, room)
+    place = code - ids * room
+    over = (code >= 0) & (place >= cut)
+    rank_c[...] = jnp.where(over, place - cut, -1)
     picked = ids == lax.broadcasted_iota(jnp.int32, (tokens, wide), 1)
-    earlier = dot((to < at).astype(LOW), picked.astype(LOW))
-    place = jnp.sum(jnp.where(picked, earlier, 0.0), axis=1, keepdims=True).astype(jnp.int32)
-    kept = columns[:, 1:2] >= 0
-    code_c[...] = jnp.where(kept, ids * room + place, -1)
-    over = kept & (place >= cut)
-    rank_c[...] = jnp.where(over, place - cut, -1)
     named = jnp.max(jnp.where(picked & over, 1.0, 0.0), axis=0, keepdims=True)
     named = jnp.sum(named, axis=1, keepdims=True)
     owner = jnp.max(jnp.where(over, ids + 1, 0).astype(jnp.float32), axis=0, keepdims=True)
@@ -154,15 +157,25 @@
     marks[...] = jnp.where(lane == 0, owner, jnp.where(lane == 1, crowded, 0.0))
 
 
+def columns(code, experts, room):
+    tokens = code.shape[1]
+    column = jax.ShapeDtypeStruct((tokens, 1), jnp.int32)
+    return pl.pallas_call(
+        functools.partial(columns_kernel, experts, room),
+        out_shape=[column, column, jax.ShapeDtypeStruct((8, TILE), jnp.float32)],
+        compiler_params=params(32),
+        name="columns",
+    )(code)
+
+
 def route(expert_ids, slots, upstream, experts, room):
     tokens, width = upstream.shape
-    column = jax.ShapeDtypeStruct((tokens, 1), jnp.int32)
     line = jax.ShapeDtypeStruct((1, tokens), jnp.int32)
     _, cut, extra = plan(room)
     return pl.pallas_call(
         functools.partial(route_kernel, experts, room),
         out_shape=[
-            column, line, column, line, jax.ShapeDtypeStruct((8, TILE), jnp.float32),
+            line, line,
             jax.ShapeDtypeStruct((experts * cut, width), LOW),
             jax.ShapeDtypeStruct((max(extra, 16), width), LOW),
         ],
@@ -210,7 +223,7 @@
 
 def gather_orders(bits):
     far = tuple(range(3, bits))
-    return [[(0,), (1,), (2,), far], [(0,), (2,), (1,), far], [(0,), (1,), (2,), far]]
+    return [[(0,), (1,), (2,), far], [(0,), (2,), far, (1,)], [(0,), far, (1,), (2,)]]
 
 
 def span(order, s, n):
@@ -481,7 +494,7 @@
 
 def unpack_kernel(
     experts, heads, buckets, q_ref, k_ref, v_ref, o_ref, small_ref, mix_ref,
-    gq, gk, gv, go, router, gains, table, mixed,
+    gq, gk, gv, go, router, gain_one, gain_two, table, mixed,
 ):
     mixed[...] = mix_ref[...]
     for packed_ref, out_ref in ((q_ref, gq), (k_ref, gk), (v_ref, gv), (o_ref, go)):
@@ -495,9 +508,8 @@
         for c in range(lines):
             lanes = slice(c * TILE, (c + 1) * TILE)
             router[:, lanes] = small[c * experts : (c + 1) * experts]
-            for n in range(2):
-                at = lines * experts + n * lines + c
-                gains[n : n + 1, lanes] = small[at : at + 1]
+            for n, gain in enumerate((gain_one, gain_two)):
+                gain[lanes] = small[lines * experts + n * lines + c]
         at = lines * experts + -(-2 * lines // 16) * 16
         table[...] = small[at : at + heads, :buckets]
 
@@ -509,16 +521,18 @@
     source = lambda m: pl.BlockSpec((blocks, width // steps, TILE), lambda i: (m, i, 0))
     rows = lambda count: pl.BlockSpec((count // steps, width), lambda i: (i, 0))
     kept = lambda shape: pl.BlockSpec(shape, lambda i: (0, 0))
+    flat = pl.BlockSpec((width,), lambda i: (0,))
     return pl.pallas_call(
         functools.partial(unpack_kernel, experts, heads, buckets),
         grid=(steps,),
         in_specs=[source(m) for m in range(4)] + [whole(small.shape), rows(tokens)],
         out_specs=[rows(width)] * 4
-        + [kept((experts, width)), kept((2, width)), kept((heads, buckets)), rows(tokens)],
+        + [kept((experts, width)), flat, flat, kept((heads, buckets)), rows(tokens)],
         out_shape=[jax.ShapeDtypeStruct((width, width), jnp.float32)] * 4
         + [
             jax.ShapeDtypeStruct((experts, width), jnp.float32),
-            jax.ShapeDtypeStruct((2, width), jnp.float32),
+            jax.ShapeDtypeStruct((width,), jnp.float32),
+            jax.ShapeDtypeStruct((width,), jnp.float32),
             jax.ShapeDtypeStruct((heads, buckets), jnp.float32),
             jax.ShapeDtypeStruct((tokens, width), LOW),
         ],
@@ -978,7 +992,7 @@
         units = rows // (16 * n)
         turns = (0, 1, 2, 0, 1, 2) if units >= 18 else (0, 1, 2) if units >= 6 else (2,)
         at = 0
-        for t, size in zip(turns, split_units(units, [(5, 5, 4)[t] for t in turns])):
+        for t, size in zip(turns, split_units(units, [(5, 5, 3)[t] for t in turns])):
             parts.append((ref, at * 16 * n, first, size * 16, orders[t]))
             at += size
             first += size * 16 * n
@@ -1209,10 +1223,11 @@
     mine = (jnp.arange(experts, dtype=jnp.int32) == me).astype(jnp.float32).reshape(1, experts)
 
     segments, cut, extra = plan(room)
-    code_c, code_r, rank_c, rank_r, marks, g_out, g_extra = route(expert_ids, slots, g, experts, room)
+    code_r, rank_r, g_out, g_extra = route(expert_ids, slots, g, experts, room)
     g_in = exchange(g_out, devices)
     code_r, gain_one, bias_table = lax.optimization_barrier((code_r, gain_one, bias_table))
 
+    code_c, rank_c, marks = columns(code_r, experts, room)
     normed_t, projected = project(x, gain_one, w_query, w_key, w_value)
     near, far = bias_tiles(bias_table)
     joined, weights = attention_forward(lengths, projected, near, far, rows, seq, heads, head)
@@ -1233,10 +1248,7 @@
         h_more, g_more, flag = h_out[-3:]
         h_out = h_out[:-3]
         crowded = flag[0, 0] > 0
-    h_out, g_in = lax.optimization_barrier((h_out, g_in))
-    g_in = g_in.reshape(devices, cut, width)
-    h_in = [exchange(h_out[0], devices)]
-    if extra:
+        h_more, g_more, g_in = lax.optimization_barrier((h_more, g_more, g_in))
 
         def exchange_rest(_):
             rms = lax.rsqrt(jnp.mean(y * y, axis=-1, keepdims=True) + EPSILON)
@@ -1245,11 +1257,13 @@
             send = lambda a: exchange(empty.at[rest].set(a, mode="drop"), devices)
             return False, send(h), send(g)
 
-        h_in[0], h_more, g_more = lax.optimization_barrier((h_in[0], h_more, g_more))
         _, h_more, g_more = lax.while_loop(
             lambda held: held[0], exchange_rest, (crowded, h_more, g_more)
         )
-        h_out[1], h_more, g_more = lax.optimization_barrier((h_out[1], h_more, g_more))
+        h_out[0], h_more, g_more = lax.optimization_barrier((h_out[0], h_more, g_more))
+    h_out, g_in = lax.optimization_barrier((h_out, g_in))
+    g_in = g_in.reshape(devices, cut, width)
+    h_in = [exchange(h_out[0], devices)]
     for h in h_out[1:]:
         h, h_in[-1] = lax.optimization_barrier((h, h_in[-1]))
         h_in.append(exchange(h, devices))
@@ -1311,12 +1325,12 @@
             return False, (y + gate * ff.astype(jnp.float32)).astype(LOW)
 
         _, mixed = lax.while_loop(lambda held: held[0], mix_all, (crowded, mixed))
-    *grads, router_t, gains, table, mixed = unpack(summed, small, mixed, experts, heads, buckets)
+    *grads, router_t, gain_grad_one, gain_grad_two, table, mixed = unpack(summed, small, mixed, experts, heads, buckets)
     return (
         mixed.reshape(rows, seq, width),
         grad_tokens.reshape(rows, seq, width),
         *grads,
-        gains[0], gains[1], table.T, router_t.T,
+        gain_grad_one, gain_grad_two, table.T, router_t.T,
         grad_in,
         grad_out,
     )

time: 380 us -> 371 us (0.976)
  blocking collectives: 0 us -> 25.4 us
  waiting for transfers between devices: 32.8 us -> 17.1 us
  Pallas kernels: 284 us -> 272 us
  starting transfers between devices: 30 us -> 23.7 us
    all_to_all x0 -> x1, blocking collectives: none -> 25.4 us  [exchange(): lax.all_to_all(shaped, AXES, split_axis=0, concat_axis=0, tiled=True)]
    all_to_all x6 -> x5, waiting for transfers between devices: 32.8 us -> 17.1 us  [exchange(): lax.all_to_all(shaped, AXES, split_axis=0, concat_axis=0, tiled=True)]
    pallas_call x1, Pallas kernels: 38 us -> 30.1 us  [after_attention(): pl.pallas_call(functools.partial(after_attention_kernel, experts, room, c...]
    all_to_all x6 -> x5, starting transfers between devices: 30 us -> 23.7 us  [exchange(): lax.all_to_all(shaped, AXES, split_axis=0, concat_axis=0, tiled=True)]
    unnamed x37 -> x49, local copies, waits for them, and re-layouts: 11.6 us -> 13.7 us
  transfers between devices with their start and end apart: 6 -> 5, of which waited for: 5 -> 4; matrix products, arithmetic and copies ran while one was open for 4% -> 4% of each run, Pallas kernels for 55% -> 55%
where the time goes in v8:
time: 371 us; the launch traced here: 366 us
  Pallas kernels  272 us (73%)
  blocking collectives  25.4 us (7%)
  starting transfers between devices  23.7 us (6%)
  local copies, waits for them, and re-layouts  19.5 us (5%)
  waiting for transfers between devices  17.1 us (5%)
  other arithmetic  4.02 us (1%)
    pallas_call x3, Pallas kernels, expert_rows(): pl.pallas_call(functools.partial(expert_kernel, experts, chunk, len(held)...  65.6 us
    pallas_call x1, Pallas kernels, all_sum(): pl.pallas_call(functools.partial(sum_kernel, cores, n, room, heights, ext...  59.1 us
    pallas_call x1, Pallas kernels, attention_backward(): pl.pallas_call(functools.partial(attention_backward_kernel, rows), grid=(...  36.8 us
    pallas_call x1, Pallas kernels, after_attention(): pl.pallas_call(functools.partial(after_attention_kernel, experts, room, c...  30.1 us
    pallas_call x1, Pallas kernels, expert_weights(): pl.pallas_call(functools.partial(expert_weights_kernel, len(parts)), grid...  28 us
    all_to_all x1, blocking collectives, exchange(): lax.all_to_all(shaped, AXES, split_axis=0, concat_axis=0, tiled=True)  25.4 us
    all_to_all x5, starting transfers between devices, exchange(): lax.all_to_all(shaped, AXES, split_axis=0, concat_axis=0, tiled=True)  23.7 us
    pallas_call x1, Pallas kernels, attention_forward(): pl.pallas_call(attention_forward_kernel, grid=(rows, pairs), in_specs=[pl...  21.2 us
  transfers between devices with their start and end apart: 5, of which 4 were waited for; matrix products, arithmetic and copies ran while one was open for 4% of the time, Pallas kernels for 55%

profile of v8, /device:TPU:0, one launch (start us, length us, event | category | flops | bytes accessed | tf_op | source)
XLA Modules:
  0.0 366.4 jit_solution(13714086822111728666)
XLA Ops:
  0.6 5.8 %route.1 = (s32[1,1024]{1,0:T(1,128)}, s32[1,1024]{1,0:T(1,128)}, bf16[1536,768]{1,0:T(8,128)(2,1)}, bf16[16,768]{1,0:T(8,128)(2,1)}) custom-call(s32[2,512]{1,0:T(2,128)} %eid_ref.1, s32[2,512]{1,0:T(2,128)} %slot_ref.1, bf16[1024,768]{1,0:T(8,128)(2,1)} %bitcast.94), custom_call_target="tpu_custom_call" | custom-call | flops 3221225472 | bytes 8388608 | tf_op jit(solution)/shard_map/route/pallas_call | solution.py:175
  6.5 7.6 %all-to-all-start.3 = ((bf16[32,48,768]{2,1,0:T(8,128)(2,1)}), bf16[32,48,768]{2,1,0:T(8,128)(2,1)}, u32[]{:S(2)}, u32[]{:S(2)}) async-start(bf16[32,48,768]{2,1,0:T(8,128)(2,1)} %bitcast.69), calls=%async_computation.3 | async-start | bytes 4718592 | tf_op jit(solution)/shard_map/all_to_all | solution.py:190
  14.1 0.0 copy-done.24
  14.1 0.0 copy-start.4
  14.1 0.0 copy-done.23
  14.1 0.1 copy.42
  14.2 0.1 copy.43.far_ref
  14.3 0.1 fusion.10
  14.4 0.2 fusion.8
  14.6 2.1 fusion.6
  16.7 0.6 copy.51
  17.3 0.0 copy-start.3
  17.3 0.0 copy-start.6
  17.4 0.2 slice.18
  17.5 0.5 copy-done.3
  18.0 0.7 columns.1
  18.7 0.8 copy-done
  19.5 0.8 copy-done.2
  20.3 0.6 copy-done.9
  20.9 1.6 copy.44.wr_ref
  22.5 0.7 reshape.298.gain_ref
  23.2 0.0 copy-done.4
  23.2 0.0 copy-done.6
  23.2 1.4 copy-done.5
  24.6 1.3 copy-done.7
  25.9 1.3 copy-done.8
  27.2 4.9 %project.1 = (bf16[768,1024]{1,0:T(8,128)(2,1)S(1)}, bf16[1024,2304]{1,0:T(8,128)(2,1)S(1)}) custom-call(bf16[1024,768]{1,0:T(8,128)(2,1)S(1)} %bitcast.54, f32[1,768]{1,0:T(1,128)S(1)} %reshape.295.gain_ref, bf16[768,768]{1,0:T(8,128)(2,1)S(1)} %copy-done.6, bf16[768,768]{1,0:T(8,128)(2,1)S(1)} %copy-done.7, bf16[768,768]{1,0:T(8,128)(2,1)S(1)} %copy-done.8), custom_call_target="tpu_custom_call" | custom-call | flops 3623878656 | bytes 12582912 | tf_op jit(solution)/shard_map/project/pallas_call | solution.py:209
  32.1 1.2 copy-done.13
  33.2 21.2 %attention_forward.1 = (bf16[1024,768]{1,0:T(8,128)(2,1)S(1)}, bf16[2,12,512,512]{3,2,1,0:T(8,128)(2,1)}) custom-call(s32[2]{0:T(128)S(1)} %copy-done.10, bf16[1024,2304]{1,0:T(8,128)(2,1)S(1)} %get-tuple-element.186.q_ref.k_ref.v_ref, bf16[1024,2304]{1,0:T(8,128)(2,1)S(1)} %get-tuple-element.186.q_ref.k_ref.v_ref, ...), custom_call_target="tpu_custom_call" | custom-call | flops 6442450944 | bytes 12582912 | tf_op jit(solution)/shard_map/attention_forward/pallas_call | solution.py:593
  54.4 0.0 copy-done.12
  54.5 1.1 copy-done.11
  55.6 30.1 %after_attention.1 = (f32[1024,768]{1,0:T(8,128)}, f32[1024,1]{1,0:T(8,128)}, bf16[512,768]{1,0:T(8,128)(2,1)}, bf16[1024,768]{1,0:T(8,128)(2,1)}, bf16[512,768]...) custom-call(bf16[1024,768]{1,0:T(8,128)(2,1)} %copy-done.11, bf16[1024,768]{1,0:T(8,128)(2,1)} %bitcast.52, ...), custom_call_target="tpu_custom_call" | custom-call | flops 4429185024 | bytes 12582912 | tf_op jit(solution)/shard_map/after_attention/pallas_call | solution.py:396
  85.7 1.2 slice.11
  87.6 0.2 reduce.1
  87.8 0.0 all-to-all-done.3
  87.8 0.2 while.20
  88.0 25.4 %all_to_all.42 = bf16[32,16,768]{2,1,0:T(8,128)(2,1)} all-to-all(bf16[32,16,768]{2,1,0:T(8,128)(2,1)} %bitcast.76), channel_id=1, replica_groups=mesh['grp'=16,'exp'=2] {'grp','exp'}, dimensions={0} | all-to-all | bytes 1572864 | tf_op jit(solution)/shard_map/all_to_all | solution.py:190
  113.5 4.0 %all-to-all-start.5 = ((bf16[32,32,768]{2,1,0:T(8,128)(2,1)}), bf16[32,32,768]{2,1,0:T(8,128)(2,1)S(1)}, u32[]{:S(2)}, u32[]{:S(2)}) async-start(bf16[32,32,768]{2,1,0:T(8,128)(2,1)} %bitcast.26), calls=%async_computation.5 | async-start | bytes 3145728 | tf_op jit(solution)/shard_map/all_to_all | solution.py:190
  117.5 0.5 compare_convert_fusion.mine_ref
  118.0 17.5 %expert_rows.3 = (bf16[512,768]{1,0:T(8,128)(2,1)S(1)}, bf16[32,32,768]{2,1,0:T(8,128)(2,1)}, bf16[512,3072]{1,0:T(8,128)(2,1)}, bf16[512,3072]{1,0:T(8,128)(2,1...) custom-call(bf16[512,768]{1,0:T(8,128)(2,1)S(1)} %copy-done.26, ...), custom_call_target="tpu_custom_call" | custom-call | flops 9663676416 | bytes 25165824 | tf_op jit(solution)/shard_map/expert_rows/pallas_call | solution.py:904
  135.6 17.7 %expert_rows.4 = (bf16[512,768]{1,0:T(8,128)(2,1)}, bf16[32,32,768]{2,1,0:T(8,128)(2,1)}, bf16[512,3072]{1,0:T(8,128)(2,1)}, bf16[512,3072]{1,0:T(8,128)(2,1)}, ...) custom-call(bf16[512,768]{1,0:T(8,128)(2,1)} %bitcast.77, ...), custom_call_target="tpu_custom_call", output_to_operand_aliasing={{1}: (6, {})} | custom-call | flops 9663676416 | bytes 25165824 | tf_op jit(solution)/shard_map/expert_rows/pallas_call | solution.py:904
  153.3 1.9 all-to-all-done.5
  155.2 1.1 copy-done.18
  156.4 4.2 %all-to-all-start.6 = ((bf16[32,32,768]{2,1,0:T(8,128)(2,1)}), bf16[32,32,768]{2,1,0:T(8,128)(2,1)S(1)}, u32[]{:S(2)}, u32[]{:S(2)}) async-start(bf16[32,32,768]{2,1,0:T(8,128)(2,1)} %get-tuple-element.218), calls=%async_computation.6 | async-start | bytes 3145728 | tf_op jit(solution)/shard_map/all_to_all | solution.py:190
  160.6 30.3 %expert_rows.5 = (bf16[1024,768]{1,0:T(8,128)(2,1)}, bf16[32,32,768]{2,1,0:T(8,128)(2,1)}, bf16[1024,3072]{1,0:T(8,128)(2,1)}, bf16[1024,3072]{1,0:T(8,128)(2,1)...) custom-call(bf16[1024,768]{1,0:T(8,128)(2,1)} %bitcast.71, ...), custom_call_target="tpu_custom_call" | custom-call | flops 19327352832 | bytes 31457280 | tf_op jit(solution)/shard_map/expert_rows/pallas_call | solution.py:904
  190.9 7.4 %all-to-all-done.6 = bf16[32,32,768]{2,1,0:T(8,128)(2,1)S(1)} async-done(((bf16[32,32,768]{2,1,0:T(8,128)(2,1)}), bf16[32,32,768]{2,1,0:T(8,128)(2,1)S(1)}, u32[]{:S(2)}, u32[]{:S(2)}) %all-to-all-start.6) | async-done | bytes 1572896 | tf_op jit(solution)/shard_map/all_to_all | solution.py:190
  198.3 1.1 copy-done.17
  199.4 3.9 %all-to-all-start.7 = ((bf16[32,32,768]{2,1,0:T(8,128)(2,1)}), bf16[32,32,768]{2,1,0:T(8,128)(2,1)}, u32[]{:S(2)}, u32[]{:S(2)}) async-start(bf16[32,32,768]{2,1,0:T(8,128)(2,1)} %get-tuple-element.220), calls=%async_computation.7 | async-start | bytes 3145728 | tf_op jit(solution)/shard_map/all_to_all | solution.py:190
  203.3 0.0 copy-start.20
  203.4 0.9 reshape_reshape.3
  204.3 0.0 copy-start.19
  204.3 1.0 copy.48
  205.3 0.0 copy-done.20
  205.3 0.7 copy.49
  206.0 3.0 pad_maximum_fusion
  209.0 28.0 %expert_weights.1 = (f32[1,768,3072]{2,1,0:T(8,128)}, f32[1,3072,768]{2,1,0:T(8,128)}) custom-call(bf16[768,512]{1,0:T(8,128)(2,1)} %get-tuple-element.221.refs_0_, bf16[768,512]{1,0:T(8,128)(2,1)} %get-tuple-element.222.refs_1_, bf16[512,3072]{1,0:T(8,128)(2,1)} %get-tuple-element.223.refs_2_, bf16[512,3072]{1,0:T(8,128)(2,1)} %get-tuple-element.224.refs_3_, ...), custom_call_target="tpu_custom_call" | custom-call | flops 19327352832 | bytes 44040192 | tf_op jit(solution)/shard_map/expert_weights/pallas_call | solution.py:958
  236.9 4.1 %all-to-all-done.7 = bf16[32,32,768]{2,1,0:T(8,128)(2,1)} async-done(((bf16[32,32,768]{2,1,0:T(8,128)(2,1)}), bf16[32,32,768]{2,1,0:T(8,128)(2,1)}, u32[]{:S(2)}, u32[]{:S(2)}) %all-to-all-start.7) | async-done | bytes 1572896 | tf_op jit(solution)/shard_map/all_to_all | solution.py:190
  241.1 4.0 %all-to-all-start.8 = ((bf16[32,48,768]{2,1,0:T(8,128)(2,1)}), bf16[32,48,768]{2,1,0:T(8,128)(2,1)S(1)}, u32[]{:S(2)}, u32[]{:S(2)}) async-start(bf16[32,48,768]{2,1,0:T(8,128)(2,1)} %pad_maximum_fusion), calls=%async_computation.8 | async-start | bytes 4718592 | tf_op jit(solution)/shard_map/all_to_all | solution.py:190
  245.1 1.2 copy.50
  246.3 12.9 %before_attention.1 = (f32[1024,768]{1,0:T(8,128)}, bf16[1024,768]{1,0:T(8,128)(2,1)}, bf16[4608,128]{1,0:T(8,128)(2,1)}, f32[1,768]{1,0:T(1,128)}) custom-call(s32[1024,1]{1,0:T(8,128)} %copy-done, f32[1024,768]{1,0:T(8,128)} %get-tuple-element.414, bf16[1024,768]{1,0:T(8,128)(2,1)} %get-tuple-element.431, f32[1,768]{1,0:T(1,128)S(1)} %get-tuple-element.430, ...), custom_call_target="tpu_custom_call" | custom-call | flops 3623878656 | bytes 16777216 | tf_op jit(solution)/shard_map/before_attention/pallas_call | solution.py:470
  259.1 36.8 %attention_backward.1 = (f32[1024,768]{1,0:T(8,128)}, bf16[3,6,768,128]{3,2,1,0:T(8,128)(2,1)}, bf16[512,128]{1,0:T(8,128)(2,1)}) custom-call(bf16[1024,2304]{1,0:T(8,128)(2,1)} %copy-done.12, bf16[1024,2304]{1,0:T(8,128)(2,1)} %copy-done.12, bf16[1024,2304]{1,0:T(8,128)(2,1)} %copy-done.12, bf16[1024,768]{1,0:T(8,128)(2,1)} %get-tuple-element.244.do_ref, ...), custom_call_target="tpu_custom_call" | custom-call | flops 12884901888 | bytes 12582912 | tf_op jit(solution)/shard_map/attention_backward/pallas_call | solution.py:778
  295.9 3.7 %all-to-all-done.8 = bf16[32,48,768]{2,1,0:T(8,128)(2,1)S(1)} async-done(((bf16[32,48,768]{2,1,0:T(8,128)(2,1)}), bf16[32,48,768]{2,1,0:T(8,128)(2,1)S(1)}, u32[]{:S(2)}, u32[]{:S(2)}) %all-to-all-start.8) | async-done | bytes 2359328 | tf_op jit(solution)/shard_map/all_to_all | solution.py:190
  299.6 59.1 %all_sum.1 = (bf16[1024,768]{1,0:T(8,128)(2,1)}, bf16[18432,128]{1,0:T(8,128)(2,1)}, bf16[512,128]{1,0:T(8,128)(2,1)}) custom-call(s32[1024,1]{1,0:T(8,128)} %copy-done, f32[1024,1]{1,0:T(8,128)} %get-tuple-element.292.gate_ref, s32[1024,1]{1,0:T(8,128)} %copy-done.2, bf16[1536,768]{1,0:T(8,128)(2,1)S(1)} %bitcast.56, f32[1024,768]{1,0:T(8,128)} %get-tuple-element.414, ...), custom_call_target="tpu_custom_call" | custom-call | tf_op jit(solution)/shard_map/all_sum/pallas_call | solution.py:1184
  358.7 7.4 %unpack.1 = (f32[768,768]{1,0:T(8,128)}, f32[768,768]{1,0:T(8,128)}, f32[768,768]{1,0:T(8,128)}, f32[768,768]{1,0:T(8,128)}, f32[32,768]{1,0:T(8,128)}, /*index=...) custom-call(bf16[24,768,128]{2,1,0:T(8,128)(2,1)} %bitcast.59, ...), custom_call_target="tpu_custom_call" | custom-call | tf_op jit(solution)/shard_map/unpack/pallas_call | solution.py:525
  (33 shorter events, 0.1 us)
Async XLA Ops:
  6.5 7.6 %copy-start.24 = (f32[768]{0:T(1024)S(1)}, f32[768]{0:T(1024)}, u32[]{:S(2)}) copy-start(f32[768]{0:T(1024)} %param.27) | copy-start | bytes 9220
  6.5 7.6 %copy-start.23 = (f32[32,12]{0,1:T(8,128)S(1)}, f32[32,12]{0,1:T(8,128)}, u32[]{:S(2)}) copy-start(f32[32,12]{0,1:T(8,128)} %param.29) | copy-start | bytes 4612
  6.5 81.3 %all-to-all-start.3 = ((bf16[32,48,768]{2,1,0:T(8,128)(2,1)}), bf16[32,48,768]{2,1,0:T(8,128)(2,1)}, u32[]{:S(2)}, u32[]{:S(2)}) async-start(bf16[32,48,768]{2,1,0:T(8,128)(2,1)} %bitcast.69), calls=%async_computation.3 | async-start | bytes 4718592 | tf_op jit(solution)/shard_map/all_to_all | solution.py:190
  14.1 9.1 %copy-start.4 = (f32[1,768]{1,0:T(1,128)}, f32[1,768]{1,0:T(1,128)S(1)}, u32[]{:S(2)}) copy-start(f32[1,768]{1,0:T(1,128)S(1)} %reshape.295.gain_ref) | copy-start | bytes 9220
  17.3 0.7 copy-start.3
  17.3 5.9 %copy-start.6 = (bf16[768,768]{1,0:T(8,128)(2,1)S(1)}, bf16[768,768]{1,0:T(8,128)(2,1)}, u32[]{:S(2)}) copy-start(bf16[768,768]{1,0:T(8,128)(2,1)} %wq_ref.3) | copy-start | bytes 3538948
  18.7 0.8 copy-start
  19.5 0.8 copy-start.2
  20.3 0.6 copy-start.9
  23.2 1.4 copy-start.5
  24.6 1.3 copy-start.7
  25.9 1.3 copy-start.8
  27.1 6.1 %copy-start.10 = (s32[2]{0:T(128)S(1)}, s32[2]{0:T(128)}, u32[]{:S(2)}) copy-start(s32[2]{0:T(128)} %len_ref.1) | copy-start | bytes 28
  32.0 1.2 copy-start.13
  33.2 21.2 %copy-start.12 = (bf16[1024,2304]{1,0:T(8,128)(2,1)}, bf16[1024,2304]{1,0:T(8,128)(2,1)S(1)}, u32[]{:S(2)}) copy-start(bf16[1024,2304]{1,0:T(8,128)(2,1)S(1)} %get-tuple-element.186.q_ref.k_ref.v_ref) | copy-start | bytes 14155780
  54.4 1.1 copy-start.11
  55.6 32.0 %copy-start.1 = (s32[1024,1]{1,0:T(8,128)S(1)}, s32[1024,1]{1,0:T(8,128)}, u32[]{:S(2)}) copy-start(s32[1024,1]{1,0:T(8,128)} %copy-done) | copy-start | bytes 12292
  113.5 4.6 %copy-start.26 = (bf16[512,768]{1,0:T(8,128)(2,1)S(1)}, bf16[512,768]{1,0:T(8,128)(2,1)}, u32[]{:S(2)}) copy-start(bf16[512,768]{1,0:T(8,128)(2,1)} %get-tuple-element.211.x_ref) | copy-start | bytes 2359300
  113.5 41.8 %all-to-all-start.5 = ((bf16[32,32,768]{2,1,0:T(8,128)(2,1)}), bf16[32,32,768]{2,1,0:T(8,128)(2,1)S(1)}, u32[]{:S(2)}, u32[]{:S(2)}) async-start(bf16[32,32,768]{2,1,0:T(8,128)(2,1)} %bitcast.26), calls=%async_computation.5 | async-start | bytes 3145728 | tf_op jit(solution)/shard_map/all_to_all | solution.py:190
  155.2 1.1 copy-start.18
  156.4 41.9 %all-to-all-start.6 = ((bf16[32,32,768]{2,1,0:T(8,128)(2,1)}), bf16[32,32,768]{2,1,0:T(8,128)(2,1)S(1)}, u32[]{:S(2)}, u32[]{:S(2)}) async-start(bf16[32,32,768]{2,1,0:T(8,128)(2,1)} %get-tuple-element.218), calls=%async_computation.6 | async-start | bytes 3145728 | tf_op jit(solution)/shard_map/all_to_all | solution.py:190
  198.3 1.1 copy-start.17
  199.4 41.6 %all-to-all-start.7 = ((bf16[32,32,768]{2,1,0:T(8,128)(2,1)}), bf16[32,32,768]{2,1,0:T(8,128)(2,1)}, u32[]{:S(2)}, u32[]{:S(2)}) async-start(bf16[32,32,768]{2,1,0:T(8,128)(2,1)} %get-tuple-element.220), calls=%async_computation.7 | async-start | bytes 3145728 | tf_op jit(solution)/shard_map/all_to_all | solution.py:190
  203.3 2.0 copy-start.20
  203.3 1.9 copy-start.21
  203.4 1.9 copy-start.22
  204.3 1.7 copy-start.19
  241.1 58.5 %all-to-all-start.8 = ((bf16[32,48,768]{2,1,0:T(8,128)(2,1)}), bf16[32,48,768]{2,1,0:T(8,128)(2,1)S(1)}, u32[]{:S(2)}, u32[]{:S(2)}) async-start(bf16[32,48,768]{2,1,0:T(8,128)(2,1)} %pad_maximum_fusion), calls=%async_computation.8 | async-start | bytes 4718592 | tf_op jit(solution)/shard_map/all_to_all | solution.py:190

commit v9 on v8

--- a/solution.py
+++ b/solution.py
@@ -365,9 +365,7 @@
                 for out, start in ((h_more, at), (g_more, at + single)):
                     got = moved[p, start : start + single, :].astype(jnp.float32)
                     out[here, lanes] = jnp.where(keep, got, 0.0).astype(LOW)
-        flag_ref[...] = jnp.broadcast_to(
-            jnp.max(marks[:, 1:2], axis=0, keepdims=True), flag_ref.shape
-        )
+        flag_ref[0, 0] = jnp.max(marks[:, 1:2]).astype(jnp.int32)
 
 
 def after_attention(
@@ -382,11 +380,11 @@
     rows = pl.BlockSpec((step, width), lambda i: (i, 0))
     single = pl.BlockSpec((step, 1), lambda i: (i, 0))
     outs = buffers(experts, room, width)
-    more, scratch, options = [], [], {}
+    more, scratch, options, flag = [], [], {}, []
     if extra:
         more = [rank, g_extra, marks]
         outs = outs + [jax.ShapeDtypeStruct((n * extra, width), LOW)] * 2
-        outs = outs + [jax.ShapeDtypeStruct((8, TILE), jnp.float32)]
+        flag = [jax.ShapeDtypeStruct((1, 1), jnp.int32)]
         scratch = [
             pltpu.VMEM((extra, width), LOW), pltpu.VMEM((3, 2 * n * extra, width // 3), LOW),
             pltpu.VMEM((8 * n, TILE), jnp.float32),
@@ -400,12 +398,15 @@
             rows, rows, whole((width, width)), whole((1, width)), single, whole(w_router.shape),
             whole((1, tokens)), *[whole(m.shape) for m in more],
         ],
-        out_specs=[rows, single] + [pl.BlockSpec(o.shape, lambda i: (0, 0)) for o in outs],
+        out_specs=[rows, single]
+        + [pl.BlockSpec(o.shape, lambda i: (0, 0)) for o in outs]
+        + [pl.BlockSpec(memory_space=pltpu.SMEM)] * len(flag),
         out_shape=[
             jax.ShapeDtypeStruct((tokens, width), jnp.float32),
             jax.ShapeDtypeStruct((tokens, 1), jnp.float32),
         ]
-        + outs,
+        + outs
+        + flag,
         scratch_shapes=scratch + [pltpu.VMEM((tokens, width), LOW)],
         compiler_params=params(60, **options),
         cost_estimate=cost(2 * tokens * width * (width + experts * room), 12 << 20),

time: 371 us -> 370 us (level)
  no operation moved by 1% of the time
where the time goes in v9:
time: 370 us; the launch traced here: 365 us
  Pallas kernels  273 us (74%)
  blocking collectives  25.4 us (7%)
  starting transfers between devices  23.7 us (6%)
  local copies, waits for them, and re-layouts  18.3 us (5%)
  waiting for transfers between devices  17.1 us (5%)
  other arithmetic  4.02 us (1%)
    pallas_call x3, Pallas kernels, expert_rows(): pl.pallas_call(functools.partial(expert_kernel, experts, chunk, len(held)...  65.6 us
    pallas_call x1, Pallas kernels, all_sum(): pl.pallas_call(functools.partial(sum_kernel, cores, n, room, heights, ext...  59.1 us
    pallas_call x1, Pallas kernels, attention_backward(): pl.pallas_call(functools.partial(attention_backward_kernel, rows), grid=(...  36.8 us
    pallas_call x1, Pallas kernels, after_attention(): pl.pallas_call(functools.partial(after_attention_kernel, experts, room, c...  30.2 us
    pallas_call x1, Pallas kernels, expert_weights(): pl.pallas_call(functools.partial(expert_weights_kernel, len(parts)), grid...  28 us
    all_to_all x1, blocking collectives, exchange(): lax.all_to_all(shaped, AXES, split_axis=0, concat_axis=0, tiled=True)  25.4 us
    all_to_all x5, starting transfers between devices, exchange(): lax.all_to_all(shaped, AXES, split_axis=0, concat_axis=0, tiled=True)  23.7 us
    pallas_call x1, Pallas kernels, attention_forward(): pl.pallas_call(attention_forward_kernel, grid=(rows, pairs), in_specs=[pl...  21.2 us
  transfers between devices with their start and end apart: 5, of which 4 were waited for; matrix products, arithmetic and copies ran while one was open for 4% of the time, Pallas kernels for 55%

profile of v9, /device:TPU:0, one launch (start us, length us, event | category | flops | bytes accessed | tf_op | source)
XLA Modules:
  0.0 365.3 jit_solution(16655685871963364527)
XLA Ops:
  0.6 5.8 %route.1 = (s32[1,1024]{1,0:T(1,128)}, s32[1,1024]{1,0:T(1,128)}, bf16[1536,768]{1,0:T(8,128)(2,1)}, bf16[16,768]{1,0:T(8,128)(2,1)}) custom-call(s32[2,512]{1,0:T(2,128)} %eid_ref.1, s32[2,512]{1,0:T(2,128)} %slot_ref.1, bf16[1024,768]{1,0:T(8,128)(2,1)} %bitcast.94), custom_call_target="tpu_custom_call" | custom-call | flops 3221225472 | bytes 8388608 | tf_op jit(solution)/shard_map/route/pallas_call | solution.py:175
  6.5 7.6 %all-to-all-start.3 = ((bf16[32,48,768]{2,1,0:T(8,128)(2,1)}), bf16[32,48,768]{2,1,0:T(8,128)(2,1)}, u32[]{:S(2)}, u32[]{:S(2)}) async-start(bf16[32,48,768]{2,1,0:T(8,128)(2,1)} %bitcast.69), calls=%async_computation.3 | async-start | bytes 4718592 | tf_op jit(solution)/shard_map/all_to_all | solution.py:190
  14.1 0.0 copy-done.24
  14.1 0.0 copy-start.4
  14.1 0.0 copy-done.23
  14.1 0.1 copy.42
  14.2 0.1 copy.43.far_ref
  14.3 0.1 fusion.10
  14.4 0.2 fusion.8
  14.6 2.1 fusion.6
  16.7 0.6 copy.51
  17.3 0.0 copy-start.3
  17.3 0.0 copy-start.6
  17.4 0.2 slice.14
  17.5 0.5 copy-done.3
  18.0 0.7 columns.1
  18.7 0.8 copy-done
  19.5 0.8 copy-done.2
  20.3 0.6 copy-done.9
  20.9 1.6 copy.44.wr_ref
  22.5 0.7 reshape.298.gain_ref
  23.2 0.0 copy-done.4
  23.2 0.0 copy-done.6
  23.2 1.4 copy-done.5
  24.6 1.3 copy-done.7
  25.9 1.3 copy-done.8
  27.2 4.9 %project.1 = (bf16[768,1024]{1,0:T(8,128)(2,1)S(1)}, bf16[1024,2304]{1,0:T(8,128)(2,1)S(1)}) custom-call(bf16[1024,768]{1,0:T(8,128)(2,1)S(1)} %bitcast.54, f32[1,768]{1,0:T(1,128)S(1)} %reshape.295.gain_ref, bf16[768,768]{1,0:T(8,128)(2,1)S(1)} %copy-done.6, bf16[768,768]{1,0:T(8,128)(2,1)S(1)} %copy-done.7, bf16[768,768]{1,0:T(8,128)(2,1)S(1)} %copy-done.8), custom_call_target="tpu_custom_call" | custom-call | flops 3623878656 | bytes 12582912 | tf_op jit(solution)/shard_map/project/pallas_call | solution.py:209
  32.1 1.2 copy-done.13
  33.2 21.2 %attention_forward.1 = (bf16[1024,768]{1,0:T(8,128)(2,1)S(1)}, bf16[2,12,512,512]{3,2,1,0:T(8,128)(2,1)}) custom-call(s32[2]{0:T(128)S(1)} %copy-done.10, bf16[1024,2304]{1,0:T(8,128)(2,1)S(1)} %get-tuple-element.186.q_ref.k_ref.v_ref, bf16[1024,2304]{1,0:T(8,128)(2,1)S(1)} %get-tuple-element.186.q_ref.k_ref.v_ref, ...), custom_call_target="tpu_custom_call" | custom-call | flops 6442450944 | bytes 12582912 | tf_op jit(solution)/shard_map/attention_forward/pallas_call | solution.py:594
  54.4 0.0 copy-done.12
  54.5 1.1 copy-done.11
  55.6 30.2 %after_attention.1 = (f32[1024,768]{1,0:T(8,128)}, f32[1024,1]{1,0:T(8,128)}, bf16[512,768]{1,0:T(8,128)(2,1)}, bf16[1024,768]{1,0:T(8,128)(2,1)}, bf16[512,768]...) custom-call(bf16[1024,768]{1,0:T(8,128)(2,1)} %copy-done.11, bf16[1024,768]{1,0:T(8,128)(2,1)} %bitcast.52, ...), custom_call_target="tpu_custom_call" | custom-call | flops 4429185024 | bytes 12582912 | tf_op jit(solution)/shard_map/after_attention/pallas_call | solution.py:394
  86.4 0.2 reduce.1
  86.6 0.0 all-to-all-done.3
  86.7 0.2 while.20
  86.9 25.4 %all_to_all.42 = bf16[32,16,768]{2,1,0:T(8,128)(2,1)} all-to-all(bf16[32,16,768]{2,1,0:T(8,128)(2,1)} %bitcast.76), channel_id=1, replica_groups=mesh['grp'=16,'exp'=2] {'grp','exp'}, dimensions={0} | all-to-all | bytes 1572864 | tf_op jit(solution)/shard_map/all_to_all | solution.py:190
  112.3 4.0 %all-to-all-start.5 = ((bf16[32,32,768]{2,1,0:T(8,128)(2,1)}), bf16[32,32,768]{2,1,0:T(8,128)(2,1)S(1)}, u32[]{:S(2)}, u32[]{:S(2)}) async-start(bf16[32,32,768]{2,1,0:T(8,128)(2,1)} %bitcast.26), calls=%async_computation.5 | async-start | bytes 3145728 | tf_op jit(solution)/shard_map/all_to_all | solution.py:190
  116.3 0.5 compare_convert_fusion.mine_ref
  116.9 17.5 %expert_rows.3 = (bf16[512,768]{1,0:T(8,128)(2,1)S(1)}, bf16[32,32,768]{2,1,0:T(8,128)(2,1)}, bf16[512,3072]{1,0:T(8,128)(2,1)}, bf16[512,3072]{1,0:T(8,128)(2,1...) custom-call(bf16[512,768]{1,0:T(8,128)(2,1)S(1)} %copy-done.26, ...), custom_call_target="tpu_custom_call" | custom-call | flops 9663676416 | bytes 25165824 | tf_op jit(solution)/shard_map/expert_rows/pallas_call | solution.py:905
  134.4 17.7 %expert_rows.4 = (bf16[512,768]{1,0:T(8,128)(2,1)}, bf16[32,32,768]{2,1,0:T(8,128)(2,1)}, bf16[512,3072]{1,0:T(8,128)(2,1)}, bf16[512,3072]{1,0:T(8,128)(2,1)}, ...) custom-call(bf16[512,768]{1,0:T(8,128)(2,1)} %bitcast.77, ...), custom_call_target="tpu_custom_call", output_to_operand_aliasing={{1}: (6, {})} | custom-call | flops 9663676416 | bytes 25165824 | tf_op jit(solution)/shard_map/expert_rows/pallas_call | solution.py:905
  152.1 1.9 all-to-all-done.5
  154.1 1.1 copy-done.18
  155.2 4.2 %all-to-all-start.6 = ((bf16[32,32,768]{2,1,0:T(8,128)(2,1)}), bf16[32,32,768]{2,1,0:T(8,128)(2,1)S(1)}, u32[]{:S(2)}, u32[]{:S(2)}) async-start(bf16[32,32,768]{2,1,0:T(8,128)(2,1)} %get-tuple-element.218), calls=%async_computation.6 | async-start | bytes 3145728 | tf_op jit(solution)/shard_map/all_to_all | solution.py:190
  159.4 30.3 %expert_rows.5 = (bf16[1024,768]{1,0:T(8,128)(2,1)}, bf16[32,32,768]{2,1,0:T(8,128)(2,1)}, bf16[1024,3072]{1,0:T(8,128)(2,1)}, bf16[1024,3072]{1,0:T(8,128)(2,1)...) custom-call(bf16[1024,768]{1,0:T(8,128)(2,1)} %bitcast.71, ...), custom_call_target="tpu_custom_call" | custom-call | flops 19327352832 | bytes 31457280 | tf_op jit(solution)/shard_map/expert_rows/pallas_call | solution.py:905
  189.8 7.4 %all-to-all-done.6 = bf16[32,32,768]{2,1,0:T(8,128)(2,1)S(1)} async-done(((bf16[32,32,768]{2,1,0:T(8,128)(2,1)}), bf16[32,32,768]{2,1,0:T(8,128)(2,1)S(1)}, u32[]{:S(2)}, u32[]{:S(2)}) %all-to-all-start.6) | async-done | bytes 1572896 | tf_op jit(solution)/shard_map/all_to_all | solution.py:190
  197.1 1.1 copy-done.17
  198.3 3.9 %all-to-all-start.7 = ((bf16[32,32,768]{2,1,0:T(8,128)(2,1)}), bf16[32,32,768]{2,1,0:T(8,128)(2,1)}, u32[]{:S(2)}, u32[]{:S(2)}) async-start(bf16[32,32,768]{2,1,0:T(8,128)(2,1)} %get-tuple-element.220), calls=%async_computation.7 | async-start | bytes 3145728 | tf_op jit(solution)/shard_map/all_to_all | solution.py:190
  202.2 0.0 copy-start.20
  202.2 0.9 reshape_reshape.3
  203.1 0.0 copy-start.19
  203.1 1.0 copy.48
  204.1 0.0 copy-done.22
  204.2 0.7 copy.49
  204.8 0.0 copy-done.19
  204.8 3.0 pad_maximum_fusion
  207.8 28.0 %expert_weights.1 = (f32[1,768,3072]{2,1,0:T(8,128)}, f32[1,3072,768]{2,1,0:T(8,128)}) custom-call(bf16[768,512]{1,0:T(8,128)(2,1)} %get-tuple-element.221.refs_0_, bf16[768,512]{1,0:T(8,128)(2,1)} %get-tuple-element.222.refs_1_, bf16[512,3072]{1,0:T(8,128)(2,1)} %get-tuple-element.223.refs_2_, bf16[512,3072]{1,0:T(8,128)(2,1)} %get-tuple-element.224.refs_3_, ...), custom_call_target="tpu_custom_call" | custom-call | flops 19327352832 | bytes 44040192 | tf_op jit(solution)/shard_map/expert_weights/pallas_call | solution.py:959
  235.8 4.1 %all-to-all-done.7 = bf16[32,32,768]{2,1,0:T(8,128)(2,1)} async-done(((bf16[32,32,768]{2,1,0:T(8,128)(2,1)}), bf16[32,32,768]{2,1,0:T(8,128)(2,1)}, u32[]{:S(2)}, u32[]{:S(2)}) %all-to-all-start.7) | async-done | bytes 1572896 | tf_op jit(solution)/shard_map/all_to_all | solution.py:190
  239.9 4.0 %all-to-all-start.8 = ((bf16[32,48,768]{2,1,0:T(8,128)(2,1)}), bf16[32,48,768]{2,1,0:T(8,128)(2,1)S(1)}, u32[]{:S(2)}, u32[]{:S(2)}) async-start(bf16[32,48,768]{2,1,0:T(8,128)(2,1)} %pad_maximum_fusion), calls=%async_computation.8 | async-start | bytes 4718592 | tf_op jit(solution)/shard_map/all_to_all | solution.py:190
  243.9 1.2 copy.50
  245.1 12.9 %before_attention.1 = (f32[1024,768]{1,0:T(8,128)}, bf16[1024,768]{1,0:T(8,128)(2,1)}, bf16[4608,128]{1,0:T(8,128)(2,1)}, f32[1,768]{1,0:T(1,128)}) custom-call(s32[1024,1]{1,0:T(8,128)} %copy-done, f32[1024,768]{1,0:T(8,128)} %get-tuple-element.414, bf16[1024,768]{1,0:T(8,128)(2,1)} %get-tuple-element.431, f32[1,768]{1,0:T(1,128)S(1)} %get-tuple-element.430, ...), custom_call_target="tpu_custom_call" | custom-call | flops 3623878656 | bytes 16777216 | tf_op jit(solution)/shard_map/before_attention/pallas_call | solution.py:471
  258.0 36.8 %attention_backward.1 = (f32[1024,768]{1,0:T(8,128)}, bf16[3,6,768,128]{3,2,1,0:T(8,128)(2,1)}, bf16[512,128]{1,0:T(8,128)(2,1)}) custom-call(bf16[1024,2304]{1,0:T(8,128)(2,1)} %copy-done.12, bf16[1024,2304]{1,0:T(8,128)(2,1)} %copy-done.12, bf16[1024,2304]{1,0:T(8,128)(2,1)} %copy-done.12, bf16[1024,768]{1,0:T(8,128)(2,1)} %get-tuple-element.244.do_ref, ...), custom_call_target="tpu_custom_call" | custom-call | flops 12884901888 | bytes 12582912 | tf_op jit(solution)/shard_map/attention_backward/pallas_call | solution.py:779
  294.8 3.7 %all-to-all-done.8 = bf16[32,48,768]{2,1,0:T(8,128)(2,1)S(1)} async-done(((bf16[32,48,768]{2,1,0:T(8,128)(2,1)}), bf16[32,48,768]{2,1,0:T(8,128)(2,1)S(1)}, u32[]{:S(2)}, u32[]{:S(2)}) %all-to-all-start.8) | async-done | bytes 2359328 | tf_op jit(solution)/shard_map/all_to_all | solution.py:190
  298.4 59.1 %all_sum.1 = (bf16[1024,768]{1,0:T(8,128)(2,1)}, bf16[18432,128]{1,0:T(8,128)(2,1)}, bf16[512,128]{1,0:T(8,128)(2,1)}) custom-call(s32[1024,1]{1,0:T(8,128)} %copy-done, f32[1024,1]{1,0:T(8,128)} %get-tuple-element.292.gate_ref, s32[1024,1]{1,0:T(8,128)} %copy-done.2, bf16[1536,768]{1,0:T(8,128)(2,1)S(1)} %bitcast.56, f32[1024,768]{1,0:T(8,128)} %get-tuple-element.414, ...), custom_call_target="tpu_custom_call" | custom-call | tf_op jit(solution)/shard_map/all_sum/pallas_call | solution.py:1185
  357.5 7.4 %unpack.1 = (f32[768,768]{1,0:T(8,128)}, f32[768,768]{1,0:T(8,128)}, f32[768,768]{1,0:T(8,128)}, f32[768,768]{1,0:T(8,128)}, f32[32,768]{1,0:T(8,128)}, /*index=...) custom-call(bf16[24,768,128]{2,1,0:T(8,128)(2,1)} %bitcast.59, ...), custom_call_target="tpu_custom_call" | custom-call | tf_op jit(solution)/shard_map/unpack/pallas_call | solution.py:526
  (32 shorter events, 0.1 us)
Async XLA Ops:
  6.5 7.6 %copy-start.24 = (f32[768]{0:T(1024)S(1)}, f32[768]{0:T(1024)}, u32[]{:S(2)}) copy-start(f32[768]{0:T(1024)} %param.27) | copy-start | bytes 9220
  6.5 7.6 %copy-start.23 = (f32[32,12]{0,1:T(8,128)S(1)}, f32[32,12]{0,1:T(8,128)}, u32[]{:S(2)}) copy-start(f32[32,12]{0,1:T(8,128)} %param.29) | copy-start | bytes 4612
  6.5 80.2 %all-to-all-start.3 = ((bf16[32,48,768]{2,1,0:T(8,128)(2,1)}), bf16[32,48,768]{2,1,0:T(8,128)(2,1)}, u32[]{:S(2)}, u32[]{:S(2)}) async-start(bf16[32,48,768]{2,1,0:T(8,128)(2,1)} %bitcast.69), calls=%async_computation.3 | async-start | bytes 4718592 | tf_op jit(solution)/shard_map/all_to_all | solution.py:190
  14.1 9.1 %copy-start.4 = (f32[1,768]{1,0:T(1,128)}, f32[1,768]{1,0:T(1,128)S(1)}, u32[]{:S(2)}) copy-start(f32[1,768]{1,0:T(1,128)S(1)} %reshape.295.gain_ref) | copy-start | bytes 9220
  17.3 0.7 copy-start.3
  17.3 5.9 %copy-start.6 = (bf16[768,768]{1,0:T(8,128)(2,1)S(1)}, bf16[768,768]{1,0:T(8,128)(2,1)}, u32[]{:S(2)}) copy-start(bf16[768,768]{1,0:T(8,128)(2,1)} %wq_ref.3) | copy-start | bytes 3538948
  18.7 0.8 copy-start
  19.5 0.8 copy-start.2
  20.3 0.6 copy-start.9
  23.2 1.4 copy-start.5
  24.6 1.3 copy-start.7
  25.9 1.3 copy-start.8
  27.1 6.1 %copy-start.10 = (s32[2]{0:T(128)S(1)}, s32[2]{0:T(128)}, u32[]{:S(2)}) copy-start(s32[2]{0:T(128)} %len_ref.1) | copy-start | bytes 28
  32.0 1.2 copy-start.13
  33.2 21.2 %copy-start.12 = (bf16[1024,2304]{1,0:T(8,128)(2,1)}, bf16[1024,2304]{1,0:T(8,128)(2,1)S(1)}, u32[]{:S(2)}) copy-start(bf16[1024,2304]{1,0:T(8,128)(2,1)S(1)} %get-tuple-element.186.q_ref.k_ref.v_ref) | copy-start | bytes 14155780
  54.4 1.1 copy-start.11
  55.6 30.8 %copy-start.1 = (s32[1024,1]{1,0:T(8,128)S(1)}, s32[1024,1]{1,0:T(8,128)}, u32[]{:S(2)}) copy-start(s32[1024,1]{1,0:T(8,128)} %copy-done) | copy-start | bytes 12292
  112.3 4.6 %copy-start.26 = (bf16[512,768]{1,0:T(8,128)(2,1)S(1)}, bf16[512,768]{1,0:T(8,128)(2,1)}, u32[]{:S(2)}) copy-start(bf16[512,768]{1,0:T(8,128)(2,1)} %get-tuple-element.211.x_ref) | copy-start | bytes 2359300
  112.3 41.8 %all-to-all-start.5 = ((bf16[32,32,768]{2,1,0:T(8,128)(2,1)}), bf16[32,32,768]{2,1,0:T(8,128)(2,1)S(1)}, u32[]{:S(2)}, u32[]{:S(2)}) async-start(bf16[32,32,768]{2,1,0:T(8,128)(2,1)} %bitcast.26), calls=%async_computation.5 | async-start | bytes 3145728 | tf_op jit(solution)/shard_map/all_to_all | solution.py:190
  154.1 1.1 copy-start.18
  155.2 41.9 %all-to-all-start.6 = ((bf16[32,32,768]{2,1,0:T(8,128)(2,1)}), bf16[32,32,768]{2,1,0:T(8,128)(2,1)S(1)}, u32[]{:S(2)}, u32[]{:S(2)}) async-start(bf16[32,32,768]{2,1,0:T(8,128)(2,1)} %get-tuple-element.218), calls=%async_computation.6 | async-start | bytes 3145728 | tf_op jit(solution)/shard_map/all_to_all | solution.py:190
  197.1 1.1 copy-start.17
  198.3 41.6 %all-to-all-start.7 = ((bf16[32,32,768]{2,1,0:T(8,128)(2,1)}), bf16[32,32,768]{2,1,0:T(8,128)(2,1)}, u32[]{:S(2)}, u32[]{:S(2)}) async-start(bf16[32,32,768]{2,1,0:T(8,128)(2,1)} %get-tuple-element.220), calls=%async_computation.7 | async-start | bytes 3145728 | tf_op jit(solution)/shard_map/all_to_all | solution.py:190
  202.2 2.0 copy-start.20
  202.2 1.9 copy-start.21
  202.2 1.9 copy-start.22
  203.1 1.7 copy-start.19
  239.9 58.5 %all-to-all-start.8 = ((bf16[32,48,768]{2,1,0:T(8,128)(2,1)}), bf16[32,48,768]{2,1,0:T(8,128)(2,1)S(1)}, u32[]{:S(2)}, u32[]{:S(2)}) async-start(bf16[32,48,768]{2,1,0:T(8,128)(2,1)} %pad_maximum_fusion), calls=%async_computation.8 | async-start | bytes 4718592 | tf_op jit(solution)/shard_map/all_to_all | solution.py:190

commit v10 on v9

--- a/solution.py
+++ b/solution.py
@@ -119,15 +119,23 @@
     tokens = g_ref.shape[0]
     wide = max(TILE, experts)
     _, cut, extra = plan(room)
-    at = lax.broadcasted_iota(jnp.int32, (tokens, tokens), 0)
-    to = lax.broadcasted_iota(jnp.int32, (tokens, tokens), 1)
-
     line = lambda ref: jnp.concatenate([ref[i : i + 1] for i in range(ref.shape[0])], axis=1)
     ids = line(eid_ref)
     slots = line(slot_ref)
     picked = ids == lax.broadcasted_iota(jnp.int32, (wide, tokens), 0)
-    earlier = dot(picked.astype(LOW), (at < to).astype(LOW))
-    place = jnp.sum(jnp.where(picked, earlier, 0.0), axis=0, keepdims=True).astype(jnp.int32)
+    block = 256
+    at = lax.broadcasted_iota(jnp.int32, (block, block), 0)
+    to = lax.broadcasted_iota(jnp.int32, (block, block), 1)
+    before = (at < to).astype(LOW)
+    passed = jnp.zeros((wide, 1), jnp.float32)
+    places = []
+    for start in range(0, tokens, block):
+        here = picked[:, start : start + block]
+        ones = jnp.where(here, 1.0, 0.0)
+        earlier = dot(ones.astype(LOW), before) + passed
+        places.append(jnp.sum(jnp.where(here, earlier, 0.0), axis=0, keepdims=True))
+        passed = passed + jnp.sum(ones, axis=1, keepdims=True)
+    place = jnp.concatenate(places, axis=1).astype(jnp.int32)
     kept = slots >= 0
     code = jnp.where(kept, ids * room + place, -1)
     code_r[...] = code
@@ -1017,6 +1025,9 @@
     if extra:
         parts = parts + [(len(summed), 0, sum(summed), heights[-1] // n, list(range(bits)))]
     me = lax.axis_index("grp") * cores + lax.axis_index("exp")
+    barrier = pltpu.get_barrier_semaphore()
+    for b in range(bits):
+        pl.semaphore_signal(barrier, inc=1, **device_place(cores, partner_of(me, b)[1]))
     base = [first for _, _, first, _, _ in parts]
     got_at = list(base)
     kept = []
@@ -1033,9 +1044,6 @@
         kept[p].start()
     for copy in loads:
         copy.start()
-    barrier = pltpu.get_barrier_semaphore()
-    for b in range(bits):
-        pl.semaphore_signal(barrier, inc=1, **device_place(cores, partner_of(me, b)[1]))
     pl.semaphore_wait(barrier, bits)
 
     def halving(p, s):
@@ -1136,9 +1144,6 @@
                 moving[p] = doubling(p, s)
                 moving[p].start()
                 stores.append(keep_out(p, bits, base[p], step))
-    for copy in sent:
-        copy.wait_send()
-    sent = []
     for s in reversed(range(bits)):
         if s == min(1, bits - 1):
             stores += mix_rest()

time: 370 us -> 370 us (level)
  no operation moved by 1% of the time
where the time goes in v10:
time: 370 us; the launch traced here: 365 us
  Pallas kernels  272 us (74%)
  blocking collectives  25.4 us (7%)
  starting transfers between devices  23.7 us (6%)
  local copies, waits for them, and re-layouts  18.3 us (5%)
  waiting for transfers between devices  17.1 us (5%)
  other arithmetic  4.02 us (1%)
    pallas_call x3, Pallas kernels, expert_rows(): pl.pallas_call(functools.partial(expert_kernel, experts, chunk, len(held)...  65.6 us
    pallas_call x1, Pallas kernels, all_sum(): pl.pallas_call(functools.partial(sum_kernel, cores, n, room, heights, ext...  58.8 us
    pallas_call x1, Pallas kernels, attention_backward(): pl.pallas_call(functools.partial(attention_backward_kernel, rows), grid=(...  36.8 us
    pallas_call x1, Pallas kernels, after_attention(): pl.pallas_call(functools.partial(after_attention_kernel, experts, room, c...  30.2 us
    pallas_call x1, Pallas kernels, expert_weights(): pl.pallas_call(functools.partial(expert_weights_kernel, len(parts)), grid...  28 us
    all_to_all x1, blocking collectives, exchange(): lax.all_to_all(shaped, AXES, split_axis=0, concat_axis=0, tiled=True)  25.4 us
    all_to_all x5, starting transfers between devices, exchange(): lax.all_to_all(shaped, AXES, split_axis=0, concat_axis=0, tiled=True)  23.7 us
    pallas_call x1, Pallas kernels, attention_forward(): pl.pallas_call(attention_forward_kernel, grid=(rows, pairs), in_specs=[pl...  21.2 us
  transfers between devices with their start and end apart: 5, of which 4 were waited for; matrix products, arithmetic and copies ran while one was open for 4% of the time, Pallas kernels for 55%

profile of v10, /device:TPU:0, one launch (start us, length us, event | category | flops | bytes accessed | tf_op | source)
XLA Modules:
  0.0 365.0 jit_solution(16102920027034332273)
XLA Ops:
  0.6 5.8 %route.1 = (s32[1,1024]{1,0:T(1,128)}, s32[1,1024]{1,0:T(1,128)}, bf16[1536,768]{1,0:T(8,128)(2,1)}, bf16[16,768]{1,0:T(8,128)(2,1)}) custom-call(s32[2,512]{1,0:T(2,128)} %eid_ref.1, s32[2,512]{1,0:T(2,128)} %slot_ref.1, bf16[1024,768]{1,0:T(8,128)(2,1)} %bitcast.94), custom_call_target="tpu_custom_call" | custom-call | flops 3221225472 | bytes 8388608 | tf_op jit(solution)/shard_map/route/pallas_call | solution.py:183
  6.4 7.6 %all-to-all-start.3 = ((bf16[32,48,768]{2,1,0:T(8,128)(2,1)}), bf16[32,48,768]{2,1,0:T(8,128)(2,1)}, u32[]{:S(2)}, u32[]{:S(2)}) async-start(bf16[32,48,768]{2,1,0:T(8,128)(2,1)} %bitcast.69), calls=%async_computation.3 | async-start | bytes 4718592 | tf_op jit(solution)/shard_map/all_to_all | solution.py:198
  14.0 0.0 copy-done.24
  14.0 0.0 copy-start.4
  14.1 0.0 copy-done.23
  14.1 0.1 copy.42
  14.2 0.1 copy.43.far_ref
  14.3 0.1 fusion.10
  14.4 0.2 fusion.8
  14.6 2.1 fusion.6
  16.7 0.6 copy.51
  17.3 0.0 copy-start.3
  17.3 0.0 copy-start.6
  17.3 0.2 slice.14
  17.5 0.5 copy-done.3
  18.0 0.7 columns.1
  18.7 0.8 copy-done
  19.5 0.8 copy-done.2
  20.3 0.6 copy-done.9
  20.9 1.6 copy.44.wr_ref
  22.5 0.7 reshape.298.gain_ref
  23.2 0.0 copy-done.4
  23.2 0.0 copy-done.6
  23.2 1.4 copy-done.5
  24.6 1.3 copy-done.7
  25.8 1.3 copy-done.8
  27.1 4.9 %project.1 = (bf16[768,1024]{1,0:T(8,128)(2,1)S(1)}, bf16[1024,2304]{1,0:T(8,128)(2,1)S(1)}) custom-call(bf16[1024,768]{1,0:T(8,128)(2,1)S(1)} %bitcast.54, f32[1,768]{1,0:T(1,128)S(1)} %reshape.295.gain_ref, bf16[768,768]{1,0:T(8,128)(2,1)S(1)} %copy-done.6, bf16[768,768]{1,0:T(8,128)(2,1)S(1)} %copy-done.7, bf16[768,768]{1,0:T(8,128)(2,1)S(1)} %copy-done.8), custom_call_target="tpu_custom_call" | custom-call | flops 3623878656 | bytes 12582912 | tf_op jit(solution)/shard_map/project/pallas_call | solution.py:217
  32.0 0.0 copy-start.13
  32.0 1.2 copy-done.13
  33.2 0.0 copy-done.10
  33.2 21.2 %attention_forward.1 = (bf16[1024,768]{1,0:T(8,128)(2,1)S(1)}, bf16[2,12,512,512]{3,2,1,0:T(8,128)(2,1)}) custom-call(s32[2]{0:T(128)S(1)} %copy-done.10, bf16[1024,2304]{1,0:T(8,128)(2,1)S(1)} %get-tuple-element.186.q_ref.k_ref.v_ref, bf16[1024,2304]{1,0:T(8,128)(2,1)S(1)} %get-tuple-element.186.q_ref.k_ref.v_ref, ...), custom_call_target="tpu_custom_call" | custom-call | flops 6442450944 | bytes 12582912 | tf_op jit(solution)/shard_map/attention_forward/pallas_call | solution.py:602
  54.4 1.1 copy-done.11
  55.6 30.2 %after_attention.1 = (f32[1024,768]{1,0:T(8,128)}, f32[1024,1]{1,0:T(8,128)}, bf16[512,768]{1,0:T(8,128)(2,1)}, bf16[1024,768]{1,0:T(8,128)(2,1)}, bf16[512,768]...) custom-call(bf16[1024,768]{1,0:T(8,128)(2,1)} %copy-done.11, bf16[1024,768]{1,0:T(8,128)(2,1)} %bitcast.52, ...), custom_call_target="tpu_custom_call" | custom-call | flops 4429185024 | bytes 12582912 | tf_op jit(solution)/shard_map/after_attention/pallas_call | solution.py:402
  86.4 0.0 copy-done.1
  86.4 0.2 reduce.1
  86.6 0.0 all-to-all-done.3
  86.6 0.2 while.20
  86.9 25.4 %all_to_all.42 = bf16[32,16,768]{2,1,0:T(8,128)(2,1)} all-to-all(bf16[32,16,768]{2,1,0:T(8,128)(2,1)} %bitcast.76), channel_id=1, replica_groups=mesh['grp'=16,'exp'=2] {'grp','exp'}, dimensions={0} | all-to-all | bytes 1572864 | tf_op jit(solution)/shard_map/all_to_all | solution.py:198
  112.3 4.0 %all-to-all-start.5 = ((bf16[32,32,768]{2,1,0:T(8,128)(2,1)}), bf16[32,32,768]{2,1,0:T(8,128)(2,1)S(1)}, u32[]{:S(2)}, u32[]{:S(2)}) async-start(bf16[32,32,768]{2,1,0:T(8,128)(2,1)} %bitcast.26), calls=%async_computation.5 | async-start | bytes 3145728 | tf_op jit(solution)/shard_map/all_to_all | solution.py:198
  116.3 0.5 compare_convert_fusion.mine_ref
  116.8 17.5 %expert_rows.3 = (bf16[512,768]{1,0:T(8,128)(2,1)S(1)}, bf16[32,32,768]{2,1,0:T(8,128)(2,1)}, bf16[512,3072]{1,0:T(8,128)(2,1)}, bf16[512,3072]{1,0:T(8,128)(2,1...) custom-call(bf16[512,768]{1,0:T(8,128)(2,1)S(1)} %copy-done.26, ...), custom_call_target="tpu_custom_call" | custom-call | flops 9663676416 | bytes 25165824 | tf_op jit(solution)/shard_map/expert_rows/pallas_call | solution.py:913
  134.4 17.7 %expert_rows.4 = (bf16[512,768]{1,0:T(8,128)(2,1)}, bf16[32,32,768]{2,1,0:T(8,128)(2,1)}, bf16[512,3072]{1,0:T(8,128)(2,1)}, bf16[512,3072]{1,0:T(8,128)(2,1)}, ...) custom-call(bf16[512,768]{1,0:T(8,128)(2,1)} %bitcast.77, ...), custom_call_target="tpu_custom_call", output_to_operand_aliasing={{1}: (6, {})} | custom-call | flops 9663676416 | bytes 25165824 | tf_op jit(solution)/shard_map/expert_rows/pallas_call | solution.py:913
  152.1 1.9 all-to-all-done.5
  154.0 1.1 copy-done.18
  155.2 4.2 %all-to-all-start.6 = ((bf16[32,32,768]{2,1,0:T(8,128)(2,1)}), bf16[32,32,768]{2,1,0:T(8,128)(2,1)S(1)}, u32[]{:S(2)}, u32[]{:S(2)}) async-start(bf16[32,32,768]{2,1,0:T(8,128)(2,1)} %get-tuple-element.218), calls=%async_computation.6 | async-start | bytes 3145728 | tf_op jit(solution)/shard_map/all_to_all | solution.py:198
  159.4 30.3 %expert_rows.5 = (bf16[1024,768]{1,0:T(8,128)(2,1)}, bf16[32,32,768]{2,1,0:T(8,128)(2,1)}, bf16[1024,3072]{1,0:T(8,128)(2,1)}, bf16[1024,3072]{1,0:T(8,128)(2,1)...) custom-call(bf16[1024,768]{1,0:T(8,128)(2,1)} %bitcast.71, ...), custom_call_target="tpu_custom_call" | custom-call | flops 19327352832 | bytes 31457280 | tf_op jit(solution)/shard_map/expert_rows/pallas_call | solution.py:913
  189.7 7.4 %all-to-all-done.6 = bf16[32,32,768]{2,1,0:T(8,128)(2,1)S(1)} async-done(((bf16[32,32,768]{2,1,0:T(8,128)(2,1)}), bf16[32,32,768]{2,1,0:T(8,128)(2,1)S(1)}, u32[]{:S(2)}, u32[]{:S(2)}) %all-to-all-start.6) | async-done | bytes 1572896 | tf_op jit(solution)/shard_map/all_to_all | solution.py:198
  197.1 1.1 copy-done.17
  198.2 3.9 %all-to-all-start.7 = ((bf16[32,32,768]{2,1,0:T(8,128)(2,1)}), bf16[32,32,768]{2,1,0:T(8,128)(2,1)}, u32[]{:S(2)}, u32[]{:S(2)}) async-start(bf16[32,32,768]{2,1,0:T(8,128)(2,1)} %get-tuple-element.220), calls=%async_computation.7 | async-start | bytes 3145728 | tf_op jit(solution)/shard_map/all_to_all | solution.py:198
  202.1 0.0 copy-start.20
  202.2 0.9 reshape_reshape.3
  203.1 0.0 copy-start.19
  203.1 1.0 copy.48
  204.2 0.7 copy.49
  204.8 3.0 pad_maximum_fusion
  207.8 28.0 %expert_weights.1 = (f32[1,768,3072]{2,1,0:T(8,128)}, f32[1,3072,768]{2,1,0:T(8,128)}) custom-call(bf16[768,512]{1,0:T(8,128)(2,1)} %get-tuple-element.221.refs_0_, bf16[768,512]{1,0:T(8,128)(2,1)} %get-tuple-element.222.refs_1_, bf16[512,3072]{1,0:T(8,128)(2,1)} %get-tuple-element.223.refs_2_, bf16[512,3072]{1,0:T(8,128)(2,1)} %get-tuple-element.224.refs_3_, ...), custom_call_target="tpu_custom_call" | custom-call | flops 19327352832 | bytes 44040192 | tf_op jit(solution)/shard_map/expert_weights/pallas_call | solution.py:967
  235.7 4.1 %all-to-all-done.7 = bf16[32,32,768]{2,1,0:T(8,128)(2,1)} async-done(((bf16[32,32,768]{2,1,0:T(8,128)(2,1)}), bf16[32,32,768]{2,1,0:T(8,128)(2,1)}, u32[]{:S(2)}, u32[]{:S(2)}) %all-to-all-start.7) | async-done | bytes 1572896 | tf_op jit(solution)/shard_map/all_to_all | solution.py:198
  239.9 4.0 %all-to-all-start.8 = ((bf16[32,48,768]{2,1,0:T(8,128)(2,1)}), bf16[32,48,768]{2,1,0:T(8,128)(2,1)S(1)}, u32[]{:S(2)}, u32[]{:S(2)}) async-start(bf16[32,48,768]{2,1,0:T(8,128)(2,1)} %pad_maximum_fusion), calls=%async_computation.8 | async-start | bytes 4718592 | tf_op jit(solution)/shard_map/all_to_all | solution.py:198
  243.9 1.2 copy.50
  245.1 12.9 %before_attention.1 = (f32[1024,768]{1,0:T(8,128)}, bf16[1024,768]{1,0:T(8,128)(2,1)}, bf16[4608,128]{1,0:T(8,128)(2,1)}, f32[1,768]{1,0:T(1,128)}) custom-call(s32[1024,1]{1,0:T(8,128)} %copy-done, f32[1024,768]{1,0:T(8,128)} %get-tuple-element.414, bf16[1024,768]{1,0:T(8,128)(2,1)} %get-tuple-element.431, f32[1,768]{1,0:T(1,128)S(1)} %get-tuple-element.430, ...), custom_call_target="tpu_custom_call" | custom-call | flops 3623878656 | bytes 16777216 | tf_op jit(solution)/shard_map/before_attention/pallas_call | solution.py:479
  258.0 36.8 %attention_backward.1 = (f32[1024,768]{1,0:T(8,128)}, bf16[3,6,768,128]{3,2,1,0:T(8,128)(2,1)}, bf16[512,128]{1,0:T(8,128)(2,1)}) custom-call(bf16[1024,2304]{1,0:T(8,128)(2,1)} %copy-done.12, bf16[1024,2304]{1,0:T(8,128)(2,1)} %copy-done.12, bf16[1024,2304]{1,0:T(8,128)(2,1)} %copy-done.12, bf16[1024,768]{1,0:T(8,128)(2,1)} %get-tuple-element.244.do_ref, ...), custom_call_target="tpu_custom_call" | custom-call | flops 12884901888 | bytes 12582912 | tf_op jit(solution)/shard_map/attention_backward/pallas_call | solution.py:787
  294.7 3.7 %all-to-all-done.8 = bf16[32,48,768]{2,1,0:T(8,128)(2,1)S(1)} async-done(((bf16[32,48,768]{2,1,0:T(8,128)(2,1)}), bf16[32,48,768]{2,1,0:T(8,128)(2,1)S(1)}, u32[]{:S(2)}, u32[]{:S(2)}) %all-to-all-start.8) | async-done | bytes 2359328 | tf_op jit(solution)/shard_map/all_to_all | solution.py:198
  298.4 58.8 %all_sum.1 = (bf16[1024,768]{1,0:T(8,128)(2,1)}, bf16[18432,128]{1,0:T(8,128)(2,1)}, bf16[512,128]{1,0:T(8,128)(2,1)}) custom-call(s32[1024,1]{1,0:T(8,128)} %copy-done, f32[1024,1]{1,0:T(8,128)} %get-tuple-element.292.gate_ref, s32[1024,1]{1,0:T(8,128)} %copy-done.2, bf16[1536,768]{1,0:T(8,128)(2,1)S(1)} %bitcast.56, f32[1024,768]{1,0:T(8,128)} %get-tuple-element.414, ...), custom_call_target="tpu_custom_call" | custom-call | tf_op jit(solution)/shard_map/all_sum/pallas_call | solution.py:1190
  357.3 7.4 %unpack.1 = (f32[768,768]{1,0:T(8,128)}, f32[768,768]{1,0:T(8,128)}, f32[768,768]{1,0:T(8,128)}, f32[768,768]{1,0:T(8,128)}, f32[32,768]{1,0:T(8,128)}, /*index=...) custom-call(bf16[24,768,128]{2,1,0:T(8,128)(2,1)} %bitcast.59, ...), custom_call_target="tpu_custom_call" | custom-call | tf_op jit(solution)/shard_map/unpack/pallas_call | solution.py:534
  (32 shorter events, 0.1 us)
Async XLA Ops:
  6.4 7.6 %copy-start.24 = (f32[768]{0:T(1024)S(1)}, f32[768]{0:T(1024)}, u32[]{:S(2)}) copy-start(f32[768]{0:T(1024)} %param.27) | copy-start | bytes 9220
  6.4 7.6 %copy-start.23 = (f32[32,12]{0,1:T(8,128)S(1)}, f32[32,12]{0,1:T(8,128)}, u32[]{:S(2)}) copy-start(f32[32,12]{0,1:T(8,128)} %param.29) | copy-start | bytes 4612
  6.4 80.2 %all-to-all-start.3 = ((bf16[32,48,768]{2,1,0:T(8,128)(2,1)}), bf16[32,48,768]{2,1,0:T(8,128)(2,1)}, u32[]{:S(2)}, u32[]{:S(2)}) async-start(bf16[32,48,768]{2,1,0:T(8,128)(2,1)} %bitcast.69), calls=%async_computation.3 | async-start | bytes 4718592 | tf_op jit(solution)/shard_map/all_to_all | solution.py:198
  14.0 9.1 %copy-start.4 = (f32[1,768]{1,0:T(1,128)}, f32[1,768]{1,0:T(1,128)S(1)}, u32[]{:S(2)}) copy-start(f32[1,768]{1,0:T(1,128)S(1)} %reshape.295.gain_ref) | copy-start | bytes 9220
  17.3 0.7 copy-start.3
  17.3 5.9 %copy-start.6 = (bf16[768,768]{1,0:T(8,128)(2,1)S(1)}, bf16[768,768]{1,0:T(8,128)(2,1)}, u32[]{:S(2)}) copy-start(bf16[768,768]{1,0:T(8,128)(2,1)} %wq_ref.3) | copy-start | bytes 3538948
  18.7 0.8 copy-start
  19.5 0.8 copy-start.2
  20.3 0.6 copy-start.9
  23.2 1.4 copy-start.5
  24.6 1.3 copy-start.7
  25.8 1.3 copy-start.8
  27.1 6.1 %copy-start.10 = (s32[2]{0:T(128)S(1)}, s32[2]{0:T(128)}, u32[]{:S(2)}) copy-start(s32[2]{0:T(128)} %len_ref.1) | copy-start | bytes 28
  32.0 1.2 copy-start.13
  33.2 21.2 %copy-start.12 = (bf16[1024,2304]{1,0:T(8,128)(2,1)}, bf16[1024,2304]{1,0:T(8,128)(2,1)S(1)}, u32[]{:S(2)}) copy-start(bf16[1024,2304]{1,0:T(8,128)(2,1)S(1)} %get-tuple-element.186.q_ref.k_ref.v_ref) | copy-start | bytes 14155780
  54.4 1.1 copy-start.11
  55.6 30.8 %copy-start.1 = (s32[1024,1]{1,0:T(8,128)S(1)}, s32[1024,1]{1,0:T(8,128)}, u32[]{:S(2)}) copy-start(s32[1024,1]{1,0:T(8,128)} %copy-done) | copy-start | bytes 12292
  112.3 4.6 %copy-start.26 = (bf16[512,768]{1,0:T(8,128)(2,1)S(1)}, bf16[512,768]{1,0:T(8,128)(2,1)}, u32[]{:S(2)}) copy-start(bf16[512,768]{1,0:T(8,128)(2,1)} %get-tuple-element.211.x_ref) | copy-start | bytes 2359300
  112.3 41.8 %all-to-all-start.5 = ((bf16[32,32,768]{2,1,0:T(8,128)(2,1)}), bf16[32,32,768]{2,1,0:T(8,128)(2,1)S(1)}, u32[]{:S(2)}, u32[]{:S(2)}) async-start(bf16[32,32,768]{2,1,0:T(8,128)(2,1)} %bitcast.26), calls=%async_computation.5 | async-start | bytes 3145728 | tf_op jit(solution)/shard_map/all_to_all | solution.py:198
  154.0 1.1 copy-start.18
  155.2 41.9 %all-to-all-start.6 = ((bf16[32,32,768]{2,1,0:T(8,128)(2,1)}), bf16[32,32,768]{2,1,0:T(8,128)(2,1)S(1)}, u32[]{:S(2)}, u32[]{:S(2)}) async-start(bf16[32,32,768]{2,1,0:T(8,128)(2,1)} %get-tuple-element.218), calls=%async_computation.6 | async-start | bytes 3145728 | tf_op jit(solution)/shard_map/all_to_all | solution.py:198
  197.1 1.1 copy-start.17
  198.2 41.6 %all-to-all-start.7 = ((bf16[32,32,768]{2,1,0:T(8,128)(2,1)}), bf16[32,32,768]{2,1,0:T(8,128)(2,1)}, u32[]{:S(2)}, u32[]{:S(2)}) async-start(bf16[32,32,768]{2,1,0:T(8,128)(2,1)} %get-tuple-element.220), calls=%async_computation.7 | async-start | bytes 3145728 | tf_op jit(solution)/shard_map/all_to_all | solution.py:198
  202.1 2.0 copy-start.20
  202.2 1.9 copy-start.21
  202.2 1.9 copy-start.22
  203.1 1.7 copy-start.19
  239.9 58.5 %all-to-all-start.8 = ((bf16[32,48,768]{2,1,0:T(8,128)(2,1)}), bf16[32,48,768]{2,1,0:T(8,128)(2,1)S(1)}, u32[]{:S(2)}, u32[]{:S(2)}) async-start(bf16[32,48,768]{2,1,0:T(8,128)(2,1)} %pad_maximum_fusion), calls=%async_computation.8 | async-start | bytes 4718592 | tf_op jit(solution)/shard_map/all_to_all | solution.py:198
